TPU v7x, 32 devices: a whole 2x2x4 slice. The times are simulated.
32 devices in a mesh: tile: 16 (over z, y, x), own: 2 (over core).
Axes of the slice: x: 2, y: 2, z: 4, core: 2. Of those that a mesh axis runs over, the one named last changes fastest.
Arguments:
- features: bfloat16 [512, 8, 768], P('tile'), may hold values from -6 to 6
- cotangent: bfloat16 [512, 8, 768], P('tile'), may hold values from -6 to 6
- depth_kernel: float32 [7, 7, 768], replicated, may hold values from -0.875 to 0.875
- ln_gain: float32 [768], replicated, may hold values from 0.1 to 1.9
- weight_up: bfloat16 [768, 3072], P('tile', 'own'), may hold values from -0.21875 to 0.21875
- bias_up: float32 [3072], P('own'), may hold values from -3 to 3
- weight_down: bfloat16 [3072, 768], P('own', 'tile'), may hold values from -0.109375 to 0.109375
- layer_scale: float32 [768], replicated, may hold values from 0.3 to 3
- tissue: int32 [64, 1], P('tile'), may hold values 0 or 1
- lengths: int32 [16], replicated, may hold values from 1 to 4, 32 in all
Outputs:
- block_out: bfloat16 [512, 8, 768], P(('tile', 'own'))
- grad_features: bfloat16 [512, 8, 768], P(('tile', 'own'))
- muon_up: float32 [768, 3072], P('tile', 'own')
- muon_down: float32 [3072, 768], P('own', 'tile')
Inputs may be any that keep to these rules, and one draw needn't show every extreme that they name: `lengths`: patch rows of slide in each strip; they sum to 32, and some strip has exactly 4.
All inputs are finite; a program needn't handle non-finite values. No bound on the sum of `tissue` on one device may be relied on, other than what follows from the above.
Results may differ from a plain program's by a relative error of at most 0.015.
Values may be sent and summed in bfloat16 or wider, within the bound.
No kernel may reach another device: no remote copies, remote signals or barrier semaphores. Data moves between devices by JAX's collectives and lax.ppermute only.
A program may use at most 128 MiB of HBM per device.

v0:
```python
import jax
import jax.numpy as jnp
from jax import lax
from jax.sharding import PartitionSpec as P

KERNEL = 7
PATCH = 8
ITERS_NS = 2


INV_ROOT_TWO = 0.7071067811865476
INV_ROOT_TAU = 0.3989422804014327
NS_A = 3.4445
NS_B = -4.775
NS_C = 2.0315
EPS_NORM = 1e-06
HIGHEST_PREC = lax.Precision.HIGHEST


def padded_2(shard, sides, width):
    for axis, dim in sides:
        devices, length = (lax.axis_size(axis), shard.shape[dim])
        up = [(i, (i + 1) % devices) for i in range(devices - 1)]
        down = [(j, i) for i, j in up]
        last = lax.slice_in_dim(shard, length - width, length, axis=dim)
        initial = lax.slice_in_dim(shard, 0, width, axis=dim)
        before = lax.ppermute(last, axis, up)
        after = lax.ppermute(initial, axis, down)
        shard = jnp.concatenate([before, shard, after], axis=dim)
    return shard


def gelu_exact(hidden):
    return 0.5 * hidden * (1.0 + lax.erf(hidden * INV_ROOT_TWO))


def gelu_slope(hidden):
    return (
        0.5 * (1.0 + lax.erf(hidden * INV_ROOT_TWO))
        + hidden * jnp.exp(-0.5 * hidden * hidden) * INV_ROOT_TAU
    )


def depthwise(framed, kernel):
    margin = kernel.shape[0] // 2
    padded = jnp.pad(framed, ((0, 0), (margin, margin), (0, 0)))
    row_count = framed.shape[0] - 2 * margin
    col_count = framed.shape[1]
    totals = jnp.zeros((row_count, col_count, framed.shape[2]), jnp.float32)
    for row_tap in range(kernel.shape[0]):
        for col_tap in range(kernel.shape[1]):
            totals = (
                totals
                + kernel[row_tap, col_tap]
                * padded[row_tap : row_tap + row_count, col_tap : col_tap + col_count]
            )
    return totals


def layer_norm(mixed, ln_gain):
    average = jnp.mean(mixed, axis=-1, keepdims=True)
    shifted = mixed - average
    variance = jnp.mean(shifted * shifted, axis=-1, keepdims=True)
    inv_std = lax.rsqrt(variance + 1e-06)
    centred = shifted * inv_std
    return (centred, inv_std, (centred * ln_gain).astype(jnp.bfloat16))


def norm_back(grad_normed, centred, inv_std, ln_gain):
    scaled_grad = grad_normed * ln_gain
    first_mean = jnp.mean(scaled_grad, axis=-1, keepdims=True)
    second_mean = jnp.mean(scaled_grad * centred, axis=-1, keepdims=True)
    return inv_std * (scaled_grad - first_mean - centred * second_mean)


def branch_pass(normed_rows, grad_branch, up_full, bias_up, down_full):
    hidden = jnp.dot(normed_rows, up_full, preferred_element_type=jnp.float32) + bias_up
    activation = gelu_exact(hidden).astype(jnp.bfloat16)
    branch = jnp.dot(activation, down_full, preferred_element_type=jnp.float32)
    grad_act = lax.dot_general(
        grad_branch, down_full, (((1,), (1,)), ((), ())), preferred_element_type=jnp.float32
    )
    grad_hidden = (grad_act * gelu_slope(hidden)).astype(jnp.bfloat16)
    grad_normed = lax.dot_general(
        grad_hidden, up_full, (((1,), (1,)), ((), ())), preferred_element_type=jnp.float32
    )
    grad_up = lax.dot_general(
        normed_rows, grad_hidden, (((0,), (0,)), ((), ())), preferred_element_type=jnp.float32
    )
    grad_down_t = lax.dot_general(
        grad_branch, activation, (((0,), (0,)), ((), ())), preferred_element_type=jnp.float32
    )
    return (branch, grad_normed, grad_up, grad_down_t)


def ns_update(block, gram_matrix):
    polynomial = NS_B * gram_matrix + NS_C * jnp.dot(
        gram_matrix, gram_matrix, precision=HIGHEST_PREC, preferred_element_type=jnp.float32
    )
    return NS_A * block + jnp.dot(
        block, polynomial, precision=HIGHEST_PREC, preferred_element_type=jnp.float32
    )


def local_gram(block):
    return lax.dot_general(
        block,
        block,
        (((0,), (0,)), ((), ())),
        precision=HIGHEST_PREC,
        preferred_element_type=jnp.float32,
    )


def newton_schulz(gradient):
    scaled = gradient * lax.rsqrt(jnp.sum(gradient * gradient) + EPS_NORM)
    for sweep_index in range(ITERS_NS):
        scaled = ns_update(scaled, local_gram(scaled))
    return scaled


def rim_rows(source_field, live_rows, margin):
    tail_rows = lax.dynamic_slice_in_dim(source_field, live_rows - margin, margin, 0)
    return jnp.concatenate([source_field[:margin], tail_rows], 0)


def framed_rows(source_field, received, live_rows, margin):
    blank_rows = jnp.zeros((margin,) + source_field.shape[1:], source_field.dtype)
    framed = jnp.concatenate([received[:margin], source_field, blank_rows], 0)
    return lax.dynamic_update_slice_in_dim(framed, received[3 * margin :], live_rows + margin, 0)


def shards(
    features,
    cotangent,
    depth_kernel,
    ln_gain,
    weight_up,
    bias_up,
    weight_down,
    layer_scale,
    tissue,
    lengths,
):
    tile_rows, columns, channels = features.shape
    margin = KERNEL // 2
    tile_index = lax.axis_index("tile")
    own_index = lax.axis_index("own")
    own_count = lax.axis_size("own")
    tile_len = lengths[tile_index]
    live_rows = PATCH * tile_len
    row_live = jnp.arange(tile_rows) < live_rows
    patch_mask = jnp.repeat(jnp.repeat(tissue, PATCH, axis=0), PATCH, axis=1)
    keep_mask = jnp.where(row_live[:, None], patch_mask, 0).astype(jnp.float32)[:, :, None]
    inputs_live = jnp.where(row_live[:, None, None], features, jnp.zeros_like(features))
    received = padded_2(rim_rows(inputs_live, live_rows, margin), (("tile", 0),), margin)
    mixed = depthwise(
        framed_rows(inputs_live, received, live_rows, margin).astype(jnp.float32), depth_kernel
    )
    centred, inv_std, normed = layer_norm(mixed, ln_gain)
    grad_branch = (keep_mask * layer_scale * cotangent.astype(jnp.float32)).astype(jnp.bfloat16)
    up_full = lax.all_gather(weight_up, "tile", axis=0, tiled=True)
    down_full = lax.all_gather(weight_down, "tile", axis=1, tiled=True)
    normed_flat = normed.reshape(-1, channels)
    grad_branch_flat = grad_branch.reshape(-1, channels)
    branch, grad_normed, grad_up, grad_down = branch_pass(
        normed_flat, grad_branch_flat, up_full, bias_up, down_full
    )
    branch_rows = lax.psum_scatter(
        branch.reshape(tile_rows, columns, channels).astype(jnp.bfloat16),
        "own",
        scatter_dimension=0,
        tiled=True,
    ).astype(jnp.float32)
    grad_normed = (
        lax.psum(grad_normed.astype(jnp.bfloat16), "own")
        .astype(jnp.float32)
        .reshape(tile_rows, columns, channels)
    )
    own_share = tile_rows // own_count
    row_offset = own_index * own_share
    mine_live = lax.dynamic_slice_in_dim(row_live, row_offset, own_share, 0)[:, None, None]
    mine_keep = lax.dynamic_slice_in_dim(keep_mask, row_offset, own_share, 0)
    mine_inputs = lax.dynamic_slice_in_dim(features, row_offset, own_share, 0).astype(jnp.float32)
    block_out = jnp.where(
        mine_live, mine_inputs + mine_keep * layer_scale * branch_rows, 0.0
    ).astype(jnp.bfloat16)
    grad_mixed = norm_back(grad_normed, centred, inv_std, ln_gain)
    grad_mixed = jnp.where(row_live[:, None, None], grad_mixed, 0.0)
    received_grad = padded_2(
        rim_rows(grad_mixed, live_rows, margin).astype(jnp.bfloat16), (("tile", 0),), margin
    ).astype(jnp.float32)
    spread = depthwise(
        framed_rows(grad_mixed, received_grad, live_rows, margin), depth_kernel[::-1, ::-1]
    )
    mine_cot = lax.dynamic_slice_in_dim(cotangent, row_offset, own_share, 0).astype(jnp.float32)
    grad_features = jnp.where(
        mine_live, mine_cot + lax.dynamic_slice_in_dim(spread, row_offset, own_share, 0), 0.0
    ).astype(jnp.bfloat16)
    whole_up, whole_down = lax.psum((grad_up, grad_down), "tile")
    ortho_up = newton_schulz(whole_up)
    ortho_down = newton_schulz(whole_down)
    rows_each = channels // lax.axis_size("tile")
    muon_up = lax.dynamic_slice_in_dim(ortho_up, tile_index * rows_each, rows_each, 0)
    muon_down = lax.dynamic_slice_in_dim(ortho_down, tile_index * rows_each, rows_each, 0).T
    return (block_out, grad_features, muon_up, muon_down)


def solution(mesh):
    in_specs = (
        P("tile", None, None),
        P("tile", None, None),
        P(),
        P(),
        P("tile", "own"),
        P("own"),
        P("own", "tile"),
        P(),
        P("tile", None),
        P(),
    )
    out_specs = (
        P(("tile", "own"), None, None),
        P(("tile", "own"), None, None),
        P("tile", "own"),
        P("own", "tile"),
    )
    return jax.shard_map(shards, mesh=mesh, in_specs=in_specs, out_specs=out_specs, check_vma=False)
```

profile of v0, /device:TPU:0, one launch (start us, length us, event | category | flops | bytes accessed | tf_op | source)
XLA Modules:
  0.0 889.3 jit_solution(2092861591822035736)
XLA Ops:
  7.2 0.7 all-gather.3.cloned.1.call-update
  7.9 0.7 all-gather.5.cloned.1.call-update
  8.7 1.2 dynamic_slice.28
  10.6 1.1 broadcast_select_fusion
  11.7 4.8 collective-permute-start
  16.6 1.3 collective-permute-start.1
  17.9 0.7 broadcast_in_dim.77
  18.7 1.5 slice_reduce_fusion.48
  20.4 1.4 slice_reduce_fusion.47
  22.0 1.7 slice_reduce_fusion.46
  24.0 6.9 fusion.237
  31.4 0.2 multiply_reduce_fusion.2
  31.6 44.2 %all-gather.3.cloned.1.call-done = bf16[768,1536]{1,0:T(8,128)(2,1)} async-done(((bf16[48,1536]{1,0:T(8,128)(2,1)}), bf16[768,1536]{1,0:T(8,128)(2,1)}) %all-gather.3.cloned.1.call-update) | async-done | bytes 2359312 | tf_op jit(solution)/shard_map/all_gather | solution.py:162
  75.9 3.7 multiply_convert_fusion
  79.6 60.2 %all-gather.5.cloned.1.call-done = bf16[1536,768]{0,1:T(8,128)(2,1)} async-done(((bf16[1536,48]{0,1:T(8,128)(2,1)}), bf16[1536,768]{0,1:T(8,128)(2,1)}) %all-gather.5.cloned.1.call-update) | async-done | bytes 2359312 | tf_op jit(solution)/shard_map/all_gather | solution.py:163
  139.8 3.2 fusion.28
  143.0 1.6 convolution_convert_fusion
  144.7 3.2 fusion.37
  148.0 3.1 fusion.227
  151.1 3.0 fusion.230
  154.1 8.0 all-reduce.6.cloned.1.call-done
  162.1 1.2 fusion.45
  163.3 1.3 fusion.44
  164.6 1.3 fusion.43
  165.9 1.3 collective-permute-start.3
  167.2 16.2 %collective-permute-start.2 = (bf16[3,8,768]{2,1,0:T(8,128)(2,1)S(1)}, bf16[3,8,768]{2,1,0:T(8,128)(2,1)S(1)}, u32[]{:S(2)}, u32[]{:S(2)}) collective-permute-start(bf16[3,8,768]{2,1,0:T(8,128)(2,1)S(1)} %get-tuple-element.63), channel_id=1, source_target_pairs={{0,2},{2,4},{4,6},{6,8},{8,10},{10,12},{12,14},{14,16},{16,18},{18... | collective-permute-start | bytes 110600 | tf_op jit(solution)/shard_map/ppermute | solution.py:27
  183.5 0.6 constant_dynamic-slice_fusion.1
  184.1 0.6 dynamic_slice.29
  184.8 0.1 maximum_maximum_fusion
  185.0 2.1 fusion.215
  187.1 6.4 fusion.197
  193.5 2.5 fusion.221
  196.0 265.9 %all-reduce.8.cloned.1.call-done = (f32[768,1536]{1,0:T(8,128)}, f32[768,1536]{1,0:T(8,128)}) async-done(((f32[768,1536]{1,0:T(8,128)}, f32[768,1536]{1,0:T(8,128)}), (f32[768,1536]{1,0:T(8,128)}, f32[768,1536]{1,0:T(8,128)})) %all-reduce.8.cloned.1.call-update) | async-done | bytes 9437200 | tf_op jit(solution)/shard_map/psum | solution.py:200
  461.9 5.6 multiply_reduce_fusion
  468.2 29.8 %fusion.22 = f32[1536,1536]{1,0:T(8,128)S(1)} fusion(f32[768,1536]{1,0:T(8,128)} %get-tuple-element.53, f32[]{:T(128)S(6)} %rsqrt.15), kind=kOutput, calls=%fused_computation.112 | convolution fusion | flops 21744451584 | bytes 14155780 | tf_op jit(solution)/shard_map/dot_general | solution.py:106
  498.0 48.1 %convolution_multiply_fusion.3 = f32[1536,1536]{1,0:T(8,128)} fusion(f32[1536,1536]{1,0:T(8,128)S(1)} %fusion.22), kind=kOutput, calls=%fused_computation.87 | convolution fusion | flops 43488903168 | bytes 18874368 | tf_op jit(solution)/shard_map/dot_general | solution.py:97
  546.1 26.1 %multiply_add_fusion.1 = f32[768,1536]{1,0:T(8,128)S(1)} fusion(f32[768,1536]{1,0:T(8,128)S(1)} %bitcast.57, f32[1536,1536]{1,0:T(8,128)} %convolution_multiply_fusion.3, f32[1536,1536]{1,0:T(8,128)S(1)} %fusion.22, f32[]{:T(128)S(6)} %rsqrt.15), kind=kOutput, calls=%fused_computation.106 | convolution fusion | flops 21752709120 | bytes 28311556 | tf_op jit(solution)/shard_map/dot_general | solution.py:100
  572.3 27.5 %fusion.240 = f32[1536,1536]{1,0:T(8,128)S(1)} fusion(f32[768,1536]{1,0:T(8,128)S(1)} %multiply_add_fusion.1), kind=kOutput, calls=%fused_computation.426 | convolution fusion | flops 21743271936 | bytes 14155776 | tf_op jit(solution)/shard_map/dot_general | solution.py:106
  599.8 48.1 %convolution_multiply_fusion.2 = f32[1536,1536]{1,0:T(8,128)} fusion(f32[1536,1536]{1,0:T(8,128)S(1)} %fusion.240), kind=kOutput, calls=%fused_computation.86 | convolution fusion | flops 43488903168 | bytes 18874368 | tf_op jit(solution)/shard_map/dot_general | solution.py:97
  647.9 26.3 %fusion.6 = f32[768,1536]{1,0:T(8,128)} fusion(f32[768,1536]{1,0:T(8,128)S(1)} %multiply_add_fusion.1, f32[1536,1536]{1,0:T(8,128)} %convolution_multiply_fusion.2, f32[1536,1536]{1,0:T(8,128)S(1)} %fusion.240), kind=kOutput, calls=%fused_computation.94 | convolution fusion | flops 21747990528 | bytes 28311552 | tf_op jit(solution)/shard_map/dot_general | solution.py:100
  674.9 29.8 %fusion.18 = f32[1536,1536]{1,0:T(8,128)S(1)} fusion(f32[768,1536]{1,0:T(8,128)} %get-tuple-element.54, f32[]{:T(128)S(6)} %rsqrt.16), kind=kOutput, calls=%fused_computation.108 | convolution fusion | flops 21744451584 | bytes 14155780 | tf_op jit(solution)/shard_map/dot_general | solution.py:106
  704.7 48.1 %convolution_multiply_fusion.1 = f32[1536,1536]{1,0:T(8,128)} fusion(f32[1536,1536]{1,0:T(8,128)S(1)} %fusion.18), kind=kOutput, calls=%fused_computation.85 | convolution fusion | flops 43488903168 | bytes 18874368 | tf_op jit(solution)/shard_map/dot_general | solution.py:97
  752.8 26.1 %multiply_add_fusion = f32[768,1536]{1,0:T(8,128)S(1)} fusion(f32[1536,1536]{1,0:T(8,128)} %convolution_multiply_fusion.1, f32[1536,1536]{1,0:T(8,128)S(1)} %fusion.18, f32[768,1536]{1,0:T(8,128)S(1)} %bitcast.55, f32[]{:T(128)S(6)} %rsqrt.16), kind=kOutput, calls=%fused_computation.100 | convolution fusion | flops 21752709120 | bytes 28311556 | tf_op jit(solution)/shard_map/dot_general | solution.py:100
  778.9 27.3 %fusion.241 = f32[1536,1536]{1,0:T(8,128)S(1)} fusion(f32[768,1536]{1,0:T(8,128)S(1)} %multiply_add_fusion), kind=kOutput, calls=%fused_computation.427 | convolution fusion | flops 21743271936 | bytes 14155776 | tf_op jit(solution)/shard_map/dot_general | solution.py:106
  806.2 48.1 %convolution_multiply_fusion = f32[1536,1536]{1,0:T(8,128)} fusion(f32[1536,1536]{1,0:T(8,128)S(1)} %fusion.241), kind=kOutput, calls=%fused_computation.84 | convolution fusion | flops 43488903168 | bytes 18874368 | tf_op jit(solution)/shard_map/dot_general | solution.py:97
  854.3 25.8 %fusion = f32[768,1536]{1,0:T(8,128)S(1)} fusion(f32[768,1536]{1,0:T(8,128)S(1)} %multiply_add_fusion, f32[1536,1536]{1,0:T(8,128)} %convolution_multiply_fusion, f32[1536,1536]{1,0:T(8,128)S(1)} %fusion.241), kind=kOutput, calls=%fused_computation.88 | convolution fusion | flops 21747990528 | bytes 28311552 | tf_op jit(solution)/shard_map/dot_general | solution.py:100
  880.1 1.8 dynamic-slice_add_fusion.2
  881.9 0.8 fusion.226
  (132 shorter events, 1.2 us)
Async XLA Ops:
  7.2 68.7 %all-gather.3.cloned.1.call-start = ((), (), s32[]{:S(2)}) async-start(), calls=%async_computation.1 | async-start | bytes 2506752 | tf_op jit(solution)/shard_map/all_gather | solution.py:162
  7.9 131.9 %all-gather.5.cloned.1.call-start = ((), (), s32[]{:S(2)}) async-start(), calls=%async_computation.2 | async-start | bytes 2506752 | tf_op jit(solution)/shard_map/all_gather | solution.py:163
  8.6 153.4 %all-reduce.6.cloned.1.call-start = ((), (), s32[]{:S(2)}) async-start(), calls=%async_computation.4 | async-start | bytes 786432 | tf_op jit(solution)/shard_map/psum | solution.py:176
  11.7 12.1 %collective-permute-start = (bf16[3,8,768]{2,1,0:T(8,128)(2,1)S(1)}, bf16[3,8,768]{2,1,0:T(8,128)(2,1)S(1)}, u32[]{:S(2)}, u32[]{:S(2)}) collective-permute-start(bf16[3,8,768]{2,1,0:T(8,128)(2,1)S(1)} %get-tuple-element.66), channel_id=1, source_target_pairs={{0,2},{2,4},{4,6},{6,8},{8,10},{10,12},{12,14},{14,16},{16,18},{18... | collective-permute-start | bytes 110600 | tf_op jit(solution)/shard_map/ppermute | solution.py:27
  16.6 7.3 collective-permute-start.1
  20.2 10.8 %copy-start.5 = (f32[768]{0:T(1024)}, f32[768]{0:T(1024)S(1)}, u32[]{:S(2)}) copy-start(f32[768]{0:T(1024)S(1)} %get-tuple-element.5) | copy-start | bytes 9220
  20.2 10.8 %copy-start.6 = (f32[768]{0:T(1024)}, f32[768]{0:T(1024)S(1)}, u32[]{:S(2)}) copy-start(f32[768]{0:T(1024)S(1)} %get-tuple-element.6) | copy-start | bytes 9220
  20.2 10.7 %copy-start.7 = (f32[768]{0:T(1024)}, f32[768]{0:T(1024)S(1)}, u32[]{:S(2)}) copy-start(f32[768]{0:T(1024)S(1)} %get-tuple-element.7) | copy-start | bytes 9220
  20.2 10.7 %copy-start.8 = (f32[768]{0:T(1024)}, f32[768]{0:T(1024)S(1)}, u32[]{:S(2)}) copy-start(f32[768]{0:T(1024)S(1)} %get-tuple-element.8) | copy-start | bytes 9220
  20.2 10.7 %copy-start.9 = (f32[768]{0:T(1024)}, f32[768]{0:T(1024)S(1)}, u32[]{:S(2)}) copy-start(f32[768]{0:T(1024)S(1)} %get-tuple-element.9) | copy-start | bytes 9220
  20.3 10.7 %copy-start.10 = (f32[768]{0:T(1024)}, f32[768]{0:T(1024)S(1)}, u32[]{:S(2)}) copy-start(f32[768]{0:T(1024)S(1)} %get-tuple-element.10) | copy-start | bytes 9220
  20.3 10.7 %copy-start.11 = (f32[768]{0:T(1024)}, f32[768]{0:T(1024)S(1)}, u32[]{:S(2)}) copy-start(f32[768]{0:T(1024)S(1)} %get-tuple-element.11) | copy-start | bytes 9220
  20.3 10.7 %copy-start.12 = (f32[768]{0:T(1024)}, f32[768]{0:T(1024)S(1)}, u32[]{:S(2)}) copy-start(f32[768]{0:T(1024)S(1)} %get-tuple-element.12) | copy-start | bytes 9220
  20.3 10.7 %copy-start.13 = (f32[768]{0:T(1024)}, f32[768]{0:T(1024)S(1)}, u32[]{:S(2)}) copy-start(f32[768]{0:T(1024)S(1)} %get-tuple-element.13) | copy-start | bytes 9220
  20.3 10.7 %copy-start.14 = (f32[768]{0:T(1024)}, f32[768]{0:T(1024)S(1)}, u32[]{:S(2)}) copy-start(f32[768]{0:T(1024)S(1)} %get-tuple-element.14) | copy-start | bytes 9220
  20.3 10.7 %copy-start.15 = (f32[768]{0:T(1024)}, f32[768]{0:T(1024)S(1)}, u32[]{:S(2)}) copy-start(f32[768]{0:T(1024)S(1)} %get-tuple-element.15) | copy-start | bytes 9220
  20.3 10.7 %copy-start.16 = (f32[768]{0:T(1024)}, f32[768]{0:T(1024)S(1)}, u32[]{:S(2)}) copy-start(f32[768]{0:T(1024)S(1)} %get-tuple-element.16) | copy-start | bytes 9220
  20.3 10.7 %copy-start.17 = (f32[768]{0:T(1024)}, f32[768]{0:T(1024)S(1)}, u32[]{:S(2)}) copy-start(f32[768]{0:T(1024)S(1)} %get-tuple-element.17) | copy-start | bytes 9220
  20.3 10.7 %copy-start.18 = (f32[768]{0:T(1024)}, f32[768]{0:T(1024)S(1)}, u32[]{:S(2)}) copy-start(f32[768]{0:T(1024)S(1)} %get-tuple-element.18) | copy-start | bytes 9220
  20.3 10.7 %copy-start.19 = (f32[768]{0:T(1024)}, f32[768]{0:T(1024)S(1)}, u32[]{:S(2)}) copy-start(f32[768]{0:T(1024)S(1)} %get-tuple-element.19) | copy-start | bytes 9220
  20.4 10.7 %copy-start.20 = (f32[768]{0:T(1024)}, f32[768]{0:T(1024)S(1)}, u32[]{:S(2)}) copy-start(f32[768]{0:T(1024)S(1)} %get-tuple-element.20) | copy-start | bytes 9220
  20.4 10.7 %copy-start.21 = (f32[768]{0:T(1024)}, f32[768]{0:T(1024)S(1)}, u32[]{:S(2)}) copy-start(f32[768]{0:T(1024)S(1)} %get-tuple-element.21) | copy-start | bytes 9220
  20.4 10.7 %copy-start.22 = (f32[768]{0:T(1024)}, f32[768]{0:T(1024)S(1)}, u32[]{:S(2)}) copy-start(f32[768]{0:T(1024)S(1)} %get-tuple-element.22) | copy-start | bytes 9220
  21.8 9.4 %copy-start.23 = (f32[768]{0:T(1024)}, f32[768]{0:T(1024)S(1)}, u32[]{:S(2)}) copy-start(f32[768]{0:T(1024)S(1)} %get-tuple-element.24) | copy-start | bytes 9220
  21.8 9.4 %copy-start.24 = (f32[768]{0:T(1024)}, f32[768]{0:T(1024)S(1)}, u32[]{:S(2)}) copy-start(f32[768]{0:T(1024)S(1)} %get-tuple-element.25) | copy-start | bytes 9220
  21.8 9.4 %copy-start.25 = (f32[768]{0:T(1024)}, f32[768]{0:T(1024)S(1)}, u32[]{:S(2)}) copy-start(f32[768]{0:T(1024)S(1)} %get-tuple-element.26) | copy-start | bytes 9220
  21.8 9.4 %copy-start.26 = (f32[768]{0:T(1024)}, f32[768]{0:T(1024)S(1)}, u32[]{:S(2)}) copy-start(f32[768]{0:T(1024)S(1)} %get-tuple-element.27) | copy-start | bytes 9220
  21.8 9.4 %copy-start.27 = (f32[768]{0:T(1024)}, f32[768]{0:T(1024)S(1)}, u32[]{:S(2)}) copy-start(f32[768]{0:T(1024)S(1)} %get-tuple-element.28) | copy-start | bytes 9220
  21.8 9.4 %copy-start.28 = (f32[768]{0:T(1024)}, f32[768]{0:T(1024)S(1)}, u32[]{:S(2)}) copy-start(f32[768]{0:T(1024)S(1)} %get-tuple-element.29) | copy-start | bytes 9220
  21.8 9.4 %copy-start.29 = (f32[768]{0:T(1024)}, f32[768]{0:T(1024)S(1)}, u32[]{:S(2)}) copy-start(f32[768]{0:T(1024)S(1)} %get-tuple-element.30) | copy-start | bytes 9220
  21.8 9.4 %copy-start.30 = (f32[768]{0:T(1024)}, f32[768]{0:T(1024)S(1)}, u32[]{:S(2)}) copy-start(f32[768]{0:T(1024)S(1)} %get-tuple-element.31) | copy-start | bytes 9220
  21.8 9.4 %copy-start.31 = (f32[768]{0:T(1024)}, f32[768]{0:T(1024)S(1)}, u32[]{:S(2)}) copy-start(f32[768]{0:T(1024)S(1)} %get-tuple-element.32) | copy-start | bytes 9220
  21.8 9.4 %copy-start.32 = (f32[768]{0:T(1024)}, f32[768]{0:T(1024)S(1)}, u32[]{:S(2)}) copy-start(f32[768]{0:T(1024)S(1)} %get-tuple-element.33) | copy-start | bytes 9220
  21.9 9.4 %copy-start.33 = (f32[768]{0:T(1024)}, f32[768]{0:T(1024)S(1)}, u32[]{:S(2)}) copy-start(f32[768]{0:T(1024)S(1)} %get-tuple-element.34) | copy-start | bytes 9220
  21.9 9.4 %copy-start.34 = (f32[768]{0:T(1024)}, f32[768]{0:T(1024)S(1)}, u32[]{:S(2)}) copy-start(f32[768]{0:T(1024)S(1)} %get-tuple-element.35) | copy-start | bytes 9220
  23.9 51.9 %copy-start.1 = (f32[768]{0:T(1024)S(1)}, f32[768]{0:T(1024)}, u32[]{:S(2)}) copy-start(f32[768]{0:T(1024)} %param.13) | copy-start | bytes 9220
  23.9 51.9 %copy-start.44 = (f32[1536]{0:T(1024)S(1)}, f32[1536]{0:T(1024)}, u32[]{:S(2)}) copy-start(f32[1536]{0:T(1024)} %param.15) | copy-start | bytes 18436
  31.3 108.5 %copy-start = (bf16[32,8,768]{2,1,0:T(8,128)(2,1)S(1)}, bf16[32,8,768]{2,1,0:T(8,128)(2,1)}, u32[]{:S(2)}) copy-start(bf16[32,8,768]{2,1,0:T(8,128)(2,1)} %param.11) | copy-start | bytes 1179652
  31.4 108.4 %copy-start.2 = (f32[768]{0:T(1024)S(1)}, f32[768]{0:T(1024)}, u32[]{:S(2)}) copy-start(f32[768]{0:T(1024)} %param.17) | copy-start | bytes 9220
  144.6 48.9 %reduce-scatter.2.cloned.1.call-start = ((), (), s32[]{:S(2)}) async-start(), calls=%async_computation.3 | async-start | bytes 589824 | tf_op jit(solution)/shard_map/reduce_scatter | solution.py:169
  147.9 314.0 %all-reduce.8.cloned.1.call-start = ((), (), s32[]{:S(2)}) async-start(), calls=%async_computation.5 | async-start | bytes 18874368 | tf_op jit(solution)/shard_map/psum | solution.py:200
  165.9 18.8 %collective-permute-start.3 = (bf16[3,8,768]{2,1,0:T(8,128)(2,1)S(1)}, bf16[3,8,768]{2,1,0:T(8,128)(2,1)S(1)}, u32[]{:S(2)}, u32[]{:S(2)}) collective-permute-start(bf16[3,8,768]{2,1,0:T(8,128)(2,1)S(1)} %get-tuple-element.64), channel_id=1, source_target_pairs={{2,0},{4,2},{6,4},{8,6},{10,8},{12,10},{14,12},{16,14},{18,16},{20... | collective-permute-start | bytes 110600 | tf_op jit(solution)/shard_map/ppermute | solution.py:28
  167.2 17.6 %collective-permute-start.2 = (bf16[3,8,768]{2,1,0:T(8,128)(2,1)S(1)}, bf16[3,8,768]{2,1,0:T(8,128)(2,1)S(1)}, u32[]{:S(2)}, u32[]{:S(2)}) collective-permute-start(bf16[3,8,768]{2,1,0:T(8,128)(2,1)S(1)} %get-tuple-element.63), channel_id=1, source_target_pairs={{0,2},{2,4},{4,6},{6,8},{8,10},{10,12},{12,14},{14,16},{16,18},{18... | collective-permute-start | bytes 110600 | tf_op jit(solution)/shard_map/ppermute | solution.py:27
  468.2 77.9 %slice-start.2 = ((s8[4718592]{0:T(1024)(128)(4,1)}), s8[4194304]{0:T(1024)(128)(4,1)S(1)}, s32[]{:S(2)}) async-start(s8[4718592]{0:T(1024)(128)(4,1)} %bitcast.56), calls=%async_computation.8 | async-start | bytes 8388608
  498.0 48.1 %slice-start.3 = ((s8[4718592]{0:T(1024)(128)(4,1)}), s8[524288]{0:T(1024)(128)(4,1)S(1)}, s32[]{:S(2)}) async-start(s8[4718592]{0:T(1024)(128)(4,1)} %bitcast.56), calls=%async_computation.9 | async-start | bytes 1048576
  572.2 75.6 %copy-start.42 = (f32[768,1536]{1,0:T(8,128)}, f32[768,1536]{1,0:T(8,128)S(1)}, u32[]{:S(2)}) copy-start(f32[768,1536]{1,0:T(8,128)S(1)} %multiply_add_fusion.1) | copy-start | bytes 14155780
  674.9 77.9 %slice-start = ((s8[4718592]{0:T(1024)(128)(4,1)}), s8[4194304]{0:T(1024)(128)(4,1)S(1)}, s32[]{:S(2)}) async-start(s8[4718592]{0:T(1024)(128)(4,1)} %bitcast.54), calls=%async_computation.6 | async-start | bytes 8388608
  704.6 48.1 %slice-start.1 = ((s8[4718592]{0:T(1024)(128)(4,1)}), s8[524288]{0:T(1024)(128)(4,1)S(1)}, s32[]{:S(2)}) async-start(s8[4718592]{0:T(1024)(128)(4,1)} %bitcast.54), calls=%async_computation.7 | async-start | bytes 1048576
  (10 other events, 82.3 us)
Sparse Core Ops, SparseCore 0:
  10.8 65.0 all-gather.2
  78.6 61.0 all-gather.4
  144.8 17.2 all-reduce.5
  164.3 8.9 reduce-scatter.1
  179.4 282.4 all-reduce.7
where the time goes:
time: 897 us; the launch traced here: 889 us
  matrix products  429 us (48%)
  waiting for transfers between devices  380 us (42%)
  other arithmetic  31.6 us (4%)
  starting transfers between devices  23.9 us (3%)
  between operations  17 us (2%)
    psum x1, waiting for transfers between devices, shards(): whole_up, whole_down = lax.psum((grad_up, grad_down), 'tile')  266 us
    dot_general x4, matrix products, ns_update(): jnp.dot(gram_matrix, gram_matrix, precision=HIGHEST_PREC, preferred_eleme...  192 us
    dot_general x4, matrix products, local_gram(): lax.dot_general(block, block, (((0,), (0,)), ((), ())), precision=HIGHEST...  114 us
    dot_general x4, matrix products, ns_update(): jnp.dot(block, polynomial, precision=HIGHEST_PREC, preferred_element_type...  104 us
    all_gather x1, waiting for transfers between devices, shards(): down_full = lax.all_gather(weight_down, 'tile', axis=1, tiled=True)  60.2 us
    all_gather x1, waiting for transfers between devices, shards(): up_full = lax.all_gather(weight_up, 'tile', axis=0, tiled=True)  44.2 us
    ppermute x2, starting transfers between devices, padded_2(): before = lax.ppermute(last, axis, up)  21.1 us
  transfers between devices with their start and end apart: 9, of which 4 were waited for; matrix products, arithmetic and copies ran while one was open for 5% of the time, Pallas kernels for 0%

commit v1 on v0

v1 whole, which is shorter than its diff:
```python
import jax
import jax.numpy as jnp
from jax import lax
from jax.sharding import PartitionSpec as P

KERNEL = 7
PATCH = 8
PLANE = 4

INV_ROOT_TWO = 0.7071067811865476
INV_ROOT_TAU = 0.3989422804014327
NS_A = 3.4445
NS_B = -4.775
NS_C = 2.0315
EPS_NORM = 1e-06
F32 = jnp.float32
BF16 = jnp.bfloat16


def swap(value, axis, bit):
    return lax.ppermute(value, axis, [(i, i ^ bit) for i in range(lax.axis_size(axis))])


def neighbours(first, last):
    devices = lax.axis_size("tile")
    up = [(i, i + 1) for i in range(devices - 1)]
    down = [(i + 1, i) for i in range(devices - 1)]
    return lax.ppermute(last, "tile", up), lax.ppermute(first, "tile", down)


def in_order(blocks, index):
    bit = 1
    while bit < len(blocks):
        odd = (index // bit) % 2 == 1
        blocks = [jnp.where(odd, blocks[s ^ bit], blocks[s]) for s in range(len(blocks))]
        bit *= 2
    return blocks


def depthwise(framed, kernel):
    margin = kernel.shape[0] // 2
    padded = jnp.pad(framed, ((0, 0), (margin, margin), (0, 0)))
    row_count = framed.shape[0] - 2 * margin
    col_count = framed.shape[1]
    totals = jnp.zeros((row_count, col_count, framed.shape[2]), F32)
    for row_tap in range(kernel.shape[0]):
        for col_tap in range(kernel.shape[1]):
            totals = (
                totals
                + kernel[row_tap, col_tap]
                * padded[row_tap : row_tap + row_count, col_tap : col_tap + col_count]
            )
    return totals


def layer_norm(mixed, ln_gain):
    average = jnp.mean(mixed, axis=-1, keepdims=True)
    shifted = mixed - average
    variance = jnp.mean(shifted * shifted, axis=-1, keepdims=True)
    inv_std = lax.rsqrt(variance + 1e-06)
    centred = shifted * inv_std
    return (centred, inv_std, (centred * ln_gain).astype(BF16))


def norm_back(grad_normed, centred, inv_std, ln_gain):
    scaled_grad = grad_normed * ln_gain
    first_mean = jnp.mean(scaled_grad, axis=-1, keepdims=True)
    second_mean = jnp.mean(scaled_grad * centred, axis=-1, keepdims=True)
    return inv_std * (scaled_grad - first_mean - centred * second_mean)


def framed_share(field, live_rows, offset, share, margin):
    tail_rows = lax.dynamic_slice_in_dim(field, live_rows - margin, margin, 0)
    before, after = neighbours(field[:margin], tail_rows)
    blank_rows = jnp.zeros((margin,) + field.shape[1:], field.dtype)
    framed = jnp.concatenate([before, field, blank_rows], 0)
    framed = lax.dynamic_update_slice_in_dim(framed, after, live_rows + margin, 0)
    return lax.dynamic_slice_in_dim(framed, offset, share + 2 * margin, 0).astype(F32)


def dot(left, right, contract, precision=None):
    return lax.dot_general(
        left, right, (contract, ((), ())), precision=precision, preferred_element_type=F32
    )


def orthogonal_rows(grad_t, starts, height):
    high = lax.Precision.HIGH
    plain = ((1,), (0,))
    gram = dot(grad_t, grad_t, ((0,), (0,)))
    channels = gram.shape[0]
    diagonal = lax.broadcasted_iota(jnp.int32, gram.shape, 0) == lax.broadcasted_iota(
        jnp.int32, gram.shape, 1
    )
    scale = lax.rsqrt(jnp.sum(jnp.where(diagonal, gram, 0.0)) + EPS_NORM)
    gram = gram * (scale * scale)
    first = NS_B * gram + NS_C * dot(gram, gram, plain, high)
    half = NS_A * gram + dot(gram, first, plain, high)
    second_gram = NS_A * half + dot(half, first, plain, high)

    def rows(matrix):
        return jnp.concatenate([lax.dynamic_slice_in_dim(matrix, s, height, 0) for s in starts], 0)

    gram_rows = rows(second_gram)
    second = NS_B * gram_rows + NS_C * dot(gram_rows, second_gram, plain, high)
    column = lax.broadcasted_iota(jnp.int32, second.shape, 1)
    row = jnp.concatenate([s + jnp.arange(height) for s in starts])[:, None]
    both = (
        jnp.where(row == column, NS_A * NS_A, 0.0)
        + NS_A * (rows(first) + second)
        + dot(second, first, plain, high)
    ) * scale
    top = both.astype(BF16)
    rest = (both - top.astype(F32)).astype(BF16)
    across = ((1,), (1,))
    return dot(top, grad_t, across) + dot(rest, grad_t, across)


def shards(
    features,
    cotangent,
    depth_kernel,
    ln_gain,
    weight_up,
    bias_up,
    weight_down,
    layer_scale,
    tissue,
    lengths,
):
    tile_rows, columns, channels = features.shape
    margin = KERNEL // 2
    tiles = lax.axis_size("tile")
    owners = lax.axis_size("own")
    lines = tiles // PLANE
    tile = lax.axis_index("tile")
    own = lax.axis_index("own")
    place, line = tile % PLANE, tile // PLANE
    share = tile_rows // owners
    offset = own * share
    tokens = share * columns
    live_rows = PATCH * lengths[tile]
    row_live = jnp.arange(tile_rows) < live_rows
    mine_live = (offset + jnp.arange(share) < live_rows)[:, None, None]
    mine_tissue = jnp.repeat(tissue, PATCH, axis=0)
    mine_tissue = lax.dynamic_slice_in_dim(mine_tissue, offset, share, 0)
    mine_tissue = jnp.repeat(mine_tissue, PATCH, axis=1)[:, :, None]
    keep_scale = jnp.where(mine_live & (mine_tissue > 0), layer_scale, 0.0)
    mine_cot = lax.dynamic_slice_in_dim(cotangent, offset, share, 0).astype(F32)
    mine_inputs = lax.dynamic_slice_in_dim(features, offset, share, 0).astype(F32)

    units = weight_up.shape[1] // PLANE
    both_weights = jnp.stack([weight_up, weight_down.T])
    pieces = []
    for s in range(PLANE):
        piece = lax.dynamic_slice_in_dim(both_weights, (place ^ s) * units, units, 2)
        pieces.append(swap(piece, "tile", s) if s else piece)
    piece = jnp.concatenate(in_order(pieces, place), 1)
    pieces = [swap(piece, "tile", PLANE * s) if s else piece for s in range(lines)]
    weights = jnp.concatenate(in_order(pieces, line), 1)
    up, down_t = weights[0], weights[1]
    bias = lax.dynamic_slice_in_dim(bias_up, place * units, units, 0)

    def gather(mine):
        mine = mine.reshape(tokens, channels)
        mine = jnp.concatenate([mine] + [swap(mine, "tile", s) for s in range(1, PLANE)], 0)
        return jnp.concatenate([mine] + [swap(mine, "own", s) for s in range(1, owners)], 0)

    def scatter(partial):
        partial = partial.reshape(owners, PLANE * tokens, channels)
        total = partial[0]
        for s in range(1, owners):
            total = total + swap(partial[s].astype(BF16), "own", s).astype(F32)
        total = total.reshape(PLANE, tokens, channels)
        mine = total[0]
        for s in range(1, PLANE):
            mine = mine + swap(total[s].astype(BF16), "tile", s).astype(F32)
        return mine.reshape(share, columns, channels)

    grad_branch = gather((keep_scale * mine_cot).astype(BF16))
    inputs_live = jnp.where(row_live[:, None, None], features, jnp.zeros_like(features))
    mixed = depthwise(framed_share(inputs_live, live_rows, offset, share, margin), depth_kernel)
    centred, inv_std, normed = layer_norm(mixed, ln_gain)
    normed = gather(normed)

    plain, across, over_tokens = ((1,), (0,)), ((1,), (1,)), ((0,), (0,))
    hidden = dot(normed, up, plain) + bias
    cdf = 0.5 * (1.0 + lax.erf(hidden * INV_ROOT_TWO))
    act = (hidden * cdf).astype(BF16)
    slope = cdf + hidden * jnp.exp(-0.5 * hidden * hidden) * INV_ROOT_TAU
    grad_hidden = (dot(grad_branch, down_t, plain) * slope).astype(BF16)

    parts = jnp.concatenate(
        [dot(grad_hidden, normed, over_tokens), dot(act, grad_branch, over_tokens)], 0
    ).astype(BF16)
    kept = 2 * units // lines
    grad_t = lax.dynamic_slice_in_dim(parts, line * kept, kept, 0).astype(F32)
    for s in range(1, lines):
        part = lax.dynamic_slice_in_dim(parts, (line ^ s) * kept, kept, 0)
        grad_t = grad_t + swap(part, "tile", PLANE * s).astype(F32)
    grad_t = grad_t.astype(BF16)

    grad_normed = scatter(dot(grad_hidden, up, across))
    branch = scatter(dot(act, down_t, across))
    block_out = jnp.where(mine_live, mine_inputs + keep_scale * branch, 0.0).astype(BF16)

    half_lines = lines // 2
    blocks = [swap(grad_t, "tile", PLANE * s) if s else grad_t for s in range(half_lines)]
    block = jnp.concatenate(in_order(blocks, line % half_lines), 0)
    blocks = [swap(block, "tile", s) if s else block for s in range(PLANE)]
    whole_t = jnp.concatenate(in_order(blocks, place), 0)

    grad_mixed = jnp.where(mine_live, norm_back(grad_normed, centred, inv_std, ln_gain), 0.0)
    grad_mixed = grad_mixed.astype(BF16)
    grad_mixed = [swap(grad_mixed, "own", s) if s else grad_mixed for s in range(owners)]
    grad_mixed = jnp.concatenate(in_order(grad_mixed, own), 0)
    spread = depthwise(
        framed_share(grad_mixed, live_rows, offset, share, margin), depth_kernel[::-1, ::-1]
    )
    grad_features = jnp.where(mine_live, mine_cot + spread, 0.0).astype(BF16)

    height = channels // tiles
    other = tile ^ (PLANE * half_lines)
    ortho = orthogonal_rows(whole_t, (tile * height, other * height), height)
    mine, theirs = ortho[:height], swap(ortho[height:].astype(BF16), "tile", PLANE * half_lines)
    theirs = theirs.astype(F32)
    expands = line < half_lines
    muon_up = jnp.where(expands, mine, theirs)
    muon_down = jnp.where(expands, theirs, mine).T
    return (block_out, grad_features, muon_up, muon_down)


def solution(mesh):
    in_specs = (
        P("tile", None, None),
        P("tile", None, None),
        P(),
        P(),
        P("tile", "own"),
        P("own"),
        P("own", "tile"),
        P(),
        P("tile", None),
        P(),
    )
    out_specs = (
        P(("tile", "own"), None, None),
        P(("tile", "own"), None, None),
        P("tile", "own"),
        P("own", "tile"),
    )
    return jax.shard_map(shards, mesh=mesh, in_specs=in_specs, out_specs=out_specs, check_vma=False)
```

time: 897 us -> 194 us (0.22)
  matrix products: 429 us -> 22.1 us
  waiting for transfers between devices: 380 us -> 79.8 us
  starting transfers between devices: 23.9 us -> 54.5 us
  between operations: 17 us -> 3.9 us
    dot_general x18 -> x14, matrix products: 429 us -> 22.1 us  [dot(): lax.dot_general(left, right, (contract, ((), ())), precision=precision, p...]
    psum x2 -> x0, waiting for transfers between devices: 274 us -> none  [the longest x1 266 us: shards(): whole_up, whole_down = lax.psum((grad_up, grad_down), 'tile')]
    all_gather x2 -> x0, waiting for transfers between devices: 104 us -> none  [the longest x1 60.2 us: shards(): down_full = lax.all_gather(weight_down, 'tile', axis=1, tiled=True)]
    ppermute x4 -> x35, waiting for transfers between devices: 0.01 us -> 79.8 us  [the longest x31 76 us: swap(): lax.ppermute(value, axis, [(i, i ^ bit) for i in range(lax.axis_size(axis...]
    ppermute x4 -> x35, starting transfers between devices: 23.7 us -> 54.5 us  [the longest x31 44.8 us: swap(): lax.ppermute(value, axis, [(i, i ^ bit) for i in range(lax.axis_size(axis...]
  transfers between devices with their start and end apart: 9 -> 35, of which waited for: 4 -> 13; matrix products, arithmetic and copies ran while one was open for 5% -> 23% of each run, Pallas kernels for 0% -> 0%
where the time goes in v1:
time: 194 us; the launch traced here: 193 us
  waiting for transfers between devices  79.8 us (41%)
  starting transfers between devices  54.5 us (28%)
  other arithmetic  24.9 us (13%)
  matrix products  22.1 us (11%)
  local copies, waits for them, and re-layouts  7.83 us (4%)
  between operations  3.9 us (2%)
    ppermute x31, waiting for transfers between devices, swap(): lax.ppermute(value, axis, [(i, i ^ bit) for i in range(lax.axis_size(axis...  76 us
    ppermute x31, starting transfers between devices, swap(): lax.ppermute(value, axis, [(i, i ^ bit) for i in range(lax.axis_size(axis...  44.8 us
    dot_general x14, matrix products, dot(): lax.dot_general(left, right, (contract, ((), ())), precision=precision, p...  22.1 us
    ppermute x4, starting transfers between devices, neighbours(): return (lax.ppermute(last, 'tile', up), lax.ppermute(first, 'tile', down))  9.78 us
    reduce_sum x1, other arithmetic, layer_norm(): average = jnp.mean(mixed, axis=-1, keepdims=True)  4.88 us
    convert_element_type x1, other arithmetic, shards(): grad_features = jnp.where(mine_live, mine_cot + spread, 0.0).astype(BF16)  4.27 us
  transfers between devices with their start and end apart: 35, of which 13 were waited for; matrix products, arithmetic and copies ran while one was open for 23% of the time, Pallas kernels for 0%

profile of v1, /device:TPU:0, one launch (start us, length us, event | category | flops | bytes accessed | tf_op | source)
XLA Modules:
  0.0 193.1 jit_solution(12181999434519300607)
XLA Ops:
  1.5 1.2 dynamic_slice.61
  5.0 4.0 %collective-permute-start.18 = (bf16[128,768]{1,0:T(8,128)(2,1)S(1)}, bf16[128,768]{1,0:T(8,128)(2,1)S(1)}, u32[]{:S(2)}, u32[]{:S(2)}) collective-permute-start(bf16[128,768]{1,0:T(8,128)(2,1)S(1)} %get-tuple-element.58), channel_id=1, source_target_pairs={{0,6},{2,4},{4,2},{6,0},{8,14},{10,12},{12,10},{14,8},{16,22},{18,... | collective-permute-start | bytes 589832 | tf_op jit(solution)/shard_map/ppermute | solution.py:21
  10.6 2.8 %collective-permute-start.6 = (bf16[2,48,384]{2,1,0:T(8,128)(2,1)S(1)}, bf16[2,48,384]{2,1,0:T(8,128)(2,1)S(1)}, u32[]{:S(2)}, u32[]{:S(2)}) collective-permute-start(bf16[2,48,384]{2,1,0:T(8,128)(2,1)S(1)} %get-tuple-element.101), channel_id=1, source_target_pairs={{0,6},{2,4},{4,2},{6,0},{8,14},{10,12},{12,10},{14,8},{16,22},{18,... | collective-permute-start | bytes 221192 | tf_op jit(solution)/shard_map/ppermute | solution.py:21
  14.6 2.4 %collective-permute-start = (bf16[3,8,768]{2,1,0:T(8,128)(2,1)S(1)}, bf16[3,8,768]{2,1,0:T(8,128)(2,1)S(1)}, u32[]{:S(2)}, u32[]{:S(2)}) collective-permute-start(bf16[3,8,768]{2,1,0:T(8,128)(2,1)S(1)} %get-tuple-element.96), channel_id=1, source_target_pairs={{0,2},{2,4},{4,6},{6,8},{8,10},{10,12},{12,14},{14,16},{16,18},{18... | collective-permute-start | bytes 110600 | tf_op jit(solution)/shard_map/ppermute | solution.py:28
  19.8 1.3 collective-permute-start.1
  21.7 3.9 %collective-permute-done.1 = bf16[3,8,768]{2,1,0:T(8,128)(2,1)S(1)} collective-permute-done((bf16[3,8,768]{2,1,0:T(8,128)(2,1)S(1)}, bf16[3,8,768]{2,1,0:T(8,128)(2,1)S(1)}, u32[]{:S(2)}, u32[]{:S(2)}) %collective-permute-start.1) | collective-permute-done | bytes 36896 | tf_op jit(solution)/shard_map/ppermute | solution.py:28
  25.6 2.2 %collective-permute-start.7 = (bf16[2,48,384]{2,1,0:T(8,128)(2,1)S(1)}, bf16[2,48,384]{2,1,0:T(8,128)(2,1)S(1)}, u32[]{:S(2)}, u32[]{:S(2)}) collective-permute-start(bf16[2,48,384]{2,1,0:T(8,128)(2,1)S(1)} %get-tuple-element.102), channel_id=1, source_target_pairs={{0,4},{2,6},{4,0},{6,2},{8,12},{10,14},{12,8},{14,10},{16,20},{18,... | collective-permute-start | bytes 221192 | tf_op jit(solution)/shard_map/ppermute | solution.py:21
  27.9 4.9 %fusion.236 = (f32[16,8]{1,0:T(8,128)S(1)}, f32[16,8,768]{2,1,0:T(8,128)S(1)}) fusion(f32[768]{0:T(1024)} %get-tuple-element.51, f32[768]{0:T(1024)} %get-tuple-element.52, f32[768]{0:T(1024)S(1)} %get-tuple-element.5, f32[22,8,768]{2,1,0:T(8,128)S(1)} %dynamic-slice_convert_fusion.1, f32[768]{0:T(1024)S(1)} %get-tuple-element.6, ...), kind=kLoop, calls=%fused_computation.499 | loop fusion | flops 9633664 | bytes 3877376 | tf_op jit(solution)/shard_map/reduce_sum | solution.py:57
  33.5 3.7 %collective-permute-start.16 = (bf16[128,768]{1,0:T(8,128)(2,1)S(1)}, bf16[128,768]{1,0:T(8,128)(2,1)S(1)}, u32[]{:S(2)}, u32[]{:S(2)}) collective-permute-start(bf16[128,768]{1,0:T(8,128)(2,1)S(1)} %get-tuple-element.58), channel_id=1, source_target_pairs={{0,2},{2,0},{4,6},{6,4},{8,10},{10,8},{12,14},{14,12},{16,18},{18,... | collective-permute-start | bytes 589832 | tf_op jit(solution)/shard_map/ppermute | solution.py:21
  37.2 1.5 collective-permute-start.3
  38.9 4.1 %collective-permute-done.16 = bf16[128,768]{1,0:T(8,128)(2,1)S(1)} collective-permute-done((bf16[128,768]{1,0:T(8,128)(2,1)S(1)}, bf16[128,768]{1,0:T(8,128)(2,1)S(1)}, u32[]{:S(2)}, u32[]{:S(2)}) %collective-permute-start.16) | collective-permute-done | bytes 196640 | tf_op jit(solution)/shard_map/ppermute | solution.py:21
  43.0 2.0 %collective-permute-start.2 = (bf16[128,768]{1,0:T(8,128)(2,1)S(1)}, bf16[128,768]{1,0:T(8,128)(2,1)S(1)}, u32[]{:S(2)}, u32[]{:S(2)}) collective-permute-start(bf16[128,768]{1,0:T(8,128)(2,1)S(1)} %get-tuple-element.66), channel_id=1, source_target_pairs={{0,2},{2,0},{4,6},{6,4},{8,10},{10,8},{12,14},{14,12},{16,18},{18,... | collective-permute-start | bytes 589832 | tf_op jit(solution)/shard_map/ppermute | solution.py:21
  45.0 1.6 collective-permute-start.11
  46.7 1.1 collective-permute-start.10
  47.9 1.8 collective-permute-start.9
  50.4 6.2 %collective-permute-done.11 = bf16[2,192,384]{2,1,0:T(8,128)(2,1)S(1)} collective-permute-done((bf16[2,192,384]{2,1,0:T(8,128)(2,1)S(1)}, bf16[2,192,384]{2,1,0:T(8,128)(2,1)S(1)}, u32[]{:S(2)}, u32[]{:S(2)}) %collective-permute-start.11) | collective-permute-done | bytes 294944 | tf_op jit(solution)/shard_map/ppermute | solution.py:21
  56.6 9.0 %collective-permute-done.10 = bf16[2,192,384]{2,1,0:T(8,128)(2,1)S(1)} collective-permute-done((bf16[2,192,384]{2,1,0:T(8,128)(2,1)S(1)}, bf16[2,192,384]{2,1,0:T(8,128)(2,1)S(1)}, u32[]{:S(2)}, u32[]{:S(2)}) %collective-permute-start.10) | collective-permute-done | bytes 294944 | tf_op jit(solution)/shard_map/ppermute | solution.py:21
  66.3 1.1 multiply_convert_fusion
  67.4 1.3 fusion.13
  70.4 1.2 fusion.214
  71.5 3.8 %collective-permute-start.27 = (bf16[192,768]{1,0:T(8,128)(2,1)S(1)}, bf16[192,768]{1,0:T(8,128)(2,1)S(1)}, u32[]{:S(2)}, u32[]{:S(2)}) collective-permute-start(bf16[192,768]{1,0:T(8,128)(2,1)S(1)} %get-tuple-element.77), channel_id=1, source_target_pairs={{0,8},{2,10},{4,12},{6,14},{8,0},{10,2},{12,4},{14,6},{16,24},{18,... | collective-permute-start | bytes 884744 | tf_op jit(solution)/shard_map/ppermute | solution.py:21
  76.4 1.4 collective-permute-start.29
  79.0 4.2 %collective-permute-done.27 = bf16[192,768]{1,0:T(8,128)(2,1)S(1)} collective-permute-done((bf16[192,768]{1,0:T(8,128)(2,1)S(1)}, bf16[192,768]{1,0:T(8,128)(2,1)S(1)}, u32[]{:S(2)}, u32[]{:S(2)}) %collective-permute-start.27) | collective-permute-done | bytes 294944 | tf_op jit(solution)/shard_map/ppermute | solution.py:21
  83.1 14.2 %collective-permute-done.28 = bf16[192,768]{1,0:T(8,128)(2,1)S(1)} collective-permute-done((bf16[192,768]{1,0:T(8,128)(2,1)S(1)}, bf16[192,768]{1,0:T(8,128)(2,1)S(1)}, u32[]{:S(2)}, u32[]{:S(2)}) %collective-permute-start.28) | collective-permute-done | bytes 294944 | tf_op jit(solution)/shard_map/ppermute | solution.py:21
  97.8 3.8 %collective-permute-start.30 = (bf16[192,768]{1,0:T(8,128)(2,1)S(1)}, bf16[192,768]{1,0:T(8,128)(2,1)S(1)}, u32[]{:S(2)}, u32[]{:S(2)}) collective-permute-start(bf16[192,768]{1,0:T(8,128)(2,1)S(1)} %add_convert_fusion), channel_id=1, source_target_pairs={{0,8},{2,10},{4,12},{6,14},{8,0},{10,2},{12,4},{14,6},{16,24},{18,... | collective-permute-start | bytes 884744 | tf_op jit(solution)/shard_map/ppermute | solution.py:21
  102.7 4.3 %collective-permute-done.30 = bf16[192,768]{1,0:T(8,128)(2,1)S(1)} collective-permute-done((bf16[192,768]{1,0:T(8,128)(2,1)S(1)}, bf16[192,768]{1,0:T(8,128)(2,1)S(1)}, u32[]{:S(2)}, u32[]{:S(2)}) %collective-permute-start.30) | collective-permute-done | bytes 294944 | tf_op jit(solution)/shard_map/ppermute | solution.py:21
  108.7 1.8 collective-permute-start.21
  110.5 1.4 collective-permute-start.23
  113.2 15.3 %collective-permute-done.21 = bf16[128,768]{1,0:T(8,128)(2,1)S(1)} collective-permute-done((bf16[128,768]{1,0:T(8,128)(2,1)S(1)}, bf16[128,768]{1,0:T(8,128)(2,1)S(1)}, u32[]{:S(2)}, u32[]{:S(2)}) %collective-permute-start.21) | collective-permute-done | bytes 196640 | tf_op jit(solution)/shard_map/ppermute | solution.py:21
  128.9 3.8 %collective-permute-done.23 = bf16[128,768]{1,0:T(8,128)(2,1)S(1)} collective-permute-done((bf16[128,768]{1,0:T(8,128)(2,1)S(1)}, bf16[128,768]{1,0:T(8,128)(2,1)S(1)}, u32[]{:S(2)}, u32[]{:S(2)}) %collective-permute-start.23) | collective-permute-done | bytes 196640 | tf_op jit(solution)/shard_map/ppermute | solution.py:21
  132.6 1.4 collective-permute-start.15
  135.1 1.3 div.54
  137.3 3.0 %collective-permute-start.31 = (bf16[384,768]{1,0:T(8,128)(2,1)}, bf16[384,768]{1,0:T(8,128)(2,1)}, u32[]{:S(2)}, u32[]{:S(2)}) collective-permute-start(bf16[384,768]{1,0:T(8,128)(2,1)} %pad_maximum_fusion.4), channel_id=1, source_target_pairs={{0,6},{2,4},{4,2},{6,0},{8,14},{10,12},{12,10},{14,8},{16,22},{18,... | collective-permute-start | bytes 1769480 | tf_op jit(solution)/shard_map/ppermute | solution.py:21
  140.3 1.4 collective-permute-done.15
  141.8 10.7 %collective-permute-done.14 = bf16[128,768]{1,0:T(8,128)(2,1)} collective-permute-done((bf16[128,768]{1,0:T(8,128)(2,1)S(1)}, bf16[128,768]{1,0:T(8,128)(2,1)}, u32[]{:S(2)}, u32[]{:S(2)}) %collective-permute-start.14) | collective-permute-done | bytes 196640 | tf_op jit(solution)/shard_map/ppermute | solution.py:21
  152.5 2.1 %select_convert_fusion = (bf16[16,8,768]{2,1,0:T(8,128)(2,1)S(1)}, bf16[16,8,768]{2,1,0:T(8,128)(2,1)}) fusion(f32[128,768]{1,0:T(8,128)S(1)} %get-tuple-element.54, f32[16,8,768]{2,1,0:T(8,128)S(1)} %get-tuple-element.68, f32[16,8]{1,0:T(8,128)S(1)} %broadcast_multiply_fusion, f32[16,8]{1,0:T(8,128)} %div.54, f32[768]{0:T(1024)} %param.13, ...), kind=kLoop, calls=%fused_computation.363 | loop fusion | flops 2064384 | bytes 2367524 | tf_op jit(solution)/shard_map/convert_element_type | solution.py:214
  154.7 1.3 collective-permute-done.24
  156.1 1.3 collective-permute-start.26
  157.4 4.8 %collective-permute-start.25 = (bf16[3,8,768]{2,1,0:T(8,128)(2,1)S(1)}, bf16[3,8,768]{2,1,0:T(8,128)(2,1)S(1)}, u32[]{:S(2)}, u32[]{:S(2)}) collective-permute-start(bf16[3,8,768]{2,1,0:T(8,128)(2,1)S(1)} %get-tuple-element.104), channel_id=1, source_target_pairs={{0,2},{2,4},{4,6},{6,8},{8,10},{10,12},{12,14},{14,16},{16,18},{18... | collective-permute-start | bytes 110600 | tf_op jit(solution)/shard_map/ppermute | solution.py:28
  162.2 2.0 %broadcast_select_fusion.7 = (bf16[384,768]{1,0:T(8,128)(2,1)S(1)}, bf16[384,768]{1,0:T(8,128)(2,1)S(1)}, bf16[384,768]{1,0:T(8,128)(2,1)S(1)}, bf16[384,768]{1,0:T(8,128)(2,1)S(1)}) fusion(pred[]{:T(512)S(6)} %eq.44, bf16[384,768]{1,0:T(8,128)(2,1)} %collective-permute-done.31, bf16[384,768]{1,0:T(8,128)(2,1)} %collective-permute-done.32, pred[]{:T(512)S(6)} %eq.45, ...), kind=kLoop, calls=%fused_computation.139 | loop fusion | flops 3538944 | bytes 4718594 | tf_op jit(solution)/shard_map/jit(_where)/select_n | solution.py:35
  164.3 2.6 %select_reduce_fusion = (f32[]{:T(128)}, f32[768,768]{1,0:T(8,128)S(1)}) fusion(bf16[384,768]{1,0:T(8,128)(2,1)S(1)} %get-tuple-element.76, bf16[384,768]{1,0:T(8,128)(2,1)S(1)} %get-tuple-element.75, bf16[384,768]{1,0:T(8,128)(2,1)S(1)} %get-tuple-element.74, bf16[384,768]{1,0:T(8,128)(2,1)S(1)} %get-tuple-element.73), kind=kOutput, calls=%fused_computation.90 | convolution fusion | flops 1823145984 | bytes 4718596 | tf_op jit(solution)/shard_map/dot_general | solution.py:82
  167.6 3.2 %multiply_add_fusion.2 = f32[768,768]{1,0:T(8,128)S(1)} fusion(f32[768,768]{1,0:T(8,128)S(1)} %get-tuple-element.110, f32[]{:T(128)S(6)} %mul.1199), kind=kOutput, calls=%fused_computation.89 | convolution fusion | flops 2720858112 | bytes 4718596 | tf_op jit(solution)/shard_map/dot_general | solution.py:82
  170.8 3.2 %multiply_add_fusion.1 = f32[768,768]{1,0:T(8,128)S(1)} fusion(f32[768,768]{1,0:T(8,128)S(1)} %get-tuple-element.110, f32[768,768]{1,0:T(8,128)S(1)} %multiply_add_fusion.2, f32[]{:T(128)S(6)} %mul.1199), kind=kOutput, calls=%fused_computation.88 | convolution fusion | flops 2720268288 | bytes 7077892 | tf_op jit(solution)/shard_map/dot_general | solution.py:82
  174.0 3.2 %multiply_add_fusion = f32[768,768]{1,0:T(8,128)S(1)} fusion(f32[768,768]{1,0:T(8,128)S(1)} %multiply_add_fusion.1, f32[768,768]{1,0:T(8,128)S(1)} %multiply_add_fusion.2), kind=kOutput, calls=%fused_computation.87 | convolution fusion | flops 2719088640 | bytes 7077888 | tf_op jit(solution)/shard_map/dot_general | solution.py:82
  177.3 1.2 fusion.16
  182.0 3.4 %collective-permute-start.34 = (bf16[48,1536]{1,0:T(8,128)(2,1)S(1)}, bf16[48,1536]{1,0:T(8,128)(2,1)S(1)}, u32[]{:S(2)}, u32[]{:S(2)}) collective-permute-start(bf16[48,1536]{1,0:T(8,128)(2,1)S(1)} %slice.1799), channel_id=1, source_target_pairs={{0,16},{2,18},{4,20},{6,22},{8,24},{10,26},{12,28},{14,30},{16,0},... | collective-permute-start | bytes 442376 | tf_op jit(solution)/shard_map/ppermute | solution.py:21
  186.7 4.3 %fusion.21 = bf16[16,8,768]{2,1,0:T(8,128)(2,1)} fusion(f32[22,8,768]{2,1,0:T(8,128)S(1)} %dynamic-slice_convert_fusion, f32[768]{0:T(1024)} %get-tuple-element.51, f32[768]{0:T(1024)} %get-tuple-element.52, f32[768]{0:T(1024)S(1)} %copy-done.15, f32[768]{0:T(1024)S(1)} %copy-done.17, f32[768]{0:T(1024)S(1)} %copy-done.19, f32[768]{0:T(1024)S(1)} %copy-done.21, ...), kind=kLoop, calls=%fused_computation.156 | loop fusion | flops 9928704 | bytes 3876884 | tf_op jit(solution)/shard_map/convert_element_type | solution.py:220
  190.9 1.3 collective-permute-done.34
  (285 shorter events, 26.0 us)
Async XLA Ops:
  0.6 16.4 %copy-start.10 = (f32[7,7,768]{2,1,0:T(8,128)S(1)}, f32[7,7,768]{2,1,0:T(8,128)}, u32[]{:S(2)}) copy-start(f32[7,7,768]{2,1,0:T(8,128)} %param.12) | copy-start | bytes 451588
  5.0 41.6 %collective-permute-start.18 = (bf16[128,768]{1,0:T(8,128)(2,1)S(1)}, bf16[128,768]{1,0:T(8,128)(2,1)S(1)}, u32[]{:S(2)}, u32[]{:S(2)}) collective-permute-start(bf16[128,768]{1,0:T(8,128)(2,1)S(1)} %get-tuple-element.58), channel_id=1, source_target_pairs={{0,6},{2,4},{4,2},{6,0},{8,14},{10,12},{12,10},{14,8},{16,22},{18,... | collective-permute-start | bytes 589832 | tf_op jit(solution)/shard_map/ppermute | solution.py:21
  9.0 36.0 %collective-permute-start.17 = (bf16[128,768]{1,0:T(8,128)(2,1)S(1)}, bf16[128,768]{1,0:T(8,128)(2,1)S(1)}, u32[]{:S(2)}, u32[]{:S(2)}) collective-permute-start(bf16[128,768]{1,0:T(8,128)(2,1)S(1)} %get-tuple-element.58), channel_id=1, source_target_pairs={{0,4},{2,6},{4,0},{6,2},{8,12},{10,14},{12,8},{14,10},{16,20},{18,... | collective-permute-start | bytes 589832 | tf_op jit(solution)/shard_map/ppermute | solution.py:21
  10.4 23.1 %collective-permute-start.8 = (bf16[2,48,384]{2,1,0:T(8,128)(2,1)S(1)}, bf16[2,48,384]{2,1,0:T(8,128)(2,1)S(1)}, u32[]{:S(2)}, u32[]{:S(2)}) collective-permute-start(bf16[2,48,384]{2,1,0:T(8,128)(2,1)S(1)} %get-tuple-element.100), channel_id=1, source_target_pairs={{0,2},{2,0},{4,6},{6,4},{8,10},{10,8},{12,14},{14,12},{16,18},{18,... | collective-permute-start | bytes 221192 | tf_op jit(solution)/shard_map/ppermute | solution.py:21
  10.6 26.6 %collective-permute-start.6 = (bf16[2,48,384]{2,1,0:T(8,128)(2,1)S(1)}, bf16[2,48,384]{2,1,0:T(8,128)(2,1)S(1)}, u32[]{:S(2)}, u32[]{:S(2)}) collective-permute-start(bf16[2,48,384]{2,1,0:T(8,128)(2,1)S(1)} %get-tuple-element.101), channel_id=1, source_target_pairs={{0,6},{2,4},{4,2},{6,0},{8,14},{10,12},{12,10},{14,8},{16,22},{18,... | collective-permute-start | bytes 221192 | tf_op jit(solution)/shard_map/ppermute | solution.py:21
  14.6 5.2 %collective-permute-start = (bf16[3,8,768]{2,1,0:T(8,128)(2,1)S(1)}, bf16[3,8,768]{2,1,0:T(8,128)(2,1)S(1)}, u32[]{:S(2)}, u32[]{:S(2)}) collective-permute-start(bf16[3,8,768]{2,1,0:T(8,128)(2,1)S(1)} %get-tuple-element.96), channel_id=1, source_target_pairs={{0,2},{2,4},{4,6},{6,8},{8,10},{10,12},{12,14},{14,16},{16,18},{18... | collective-permute-start | bytes 110600 | tf_op jit(solution)/shard_map/ppermute | solution.py:28
  17.2 15.5 %copy-start.12 = (f32[768]{0:T(1024)}, f32[768]{0:T(1024)S(1)}, u32[]{:S(2)}) copy-start(f32[768]{0:T(1024)S(1)} %get-tuple-element.4) | copy-start | bytes 9220
  17.2 15.5 %copy-start.14 = (f32[768]{0:T(1024)}, f32[768]{0:T(1024)S(1)}, u32[]{:S(2)}) copy-start(f32[768]{0:T(1024)S(1)} %get-tuple-element.5) | copy-start | bytes 9220
  17.2 15.5 %copy-start.16 = (f32[768]{0:T(1024)}, f32[768]{0:T(1024)S(1)}, u32[]{:S(2)}) copy-start(f32[768]{0:T(1024)S(1)} %get-tuple-element.6) | copy-start | bytes 9220
  17.2 15.5 %copy-start.18 = (f32[768]{0:T(1024)}, f32[768]{0:T(1024)S(1)}, u32[]{:S(2)}) copy-start(f32[768]{0:T(1024)S(1)} %get-tuple-element.7) | copy-start | bytes 9220
  17.2 15.5 %copy-start.20 = (f32[768]{0:T(1024)}, f32[768]{0:T(1024)S(1)}, u32[]{:S(2)}) copy-start(f32[768]{0:T(1024)S(1)} %get-tuple-element.8) | copy-start | bytes 9220
  17.2 15.5 %copy-start.22 = (f32[768]{0:T(1024)}, f32[768]{0:T(1024)S(1)}, u32[]{:S(2)}) copy-start(f32[768]{0:T(1024)S(1)} %get-tuple-element.9) | copy-start | bytes 9220
  17.3 15.5 %copy-start.24 = (f32[768]{0:T(1024)}, f32[768]{0:T(1024)S(1)}, u32[]{:S(2)}) copy-start(f32[768]{0:T(1024)S(1)} %get-tuple-element.10) | copy-start | bytes 9220
  17.3 15.5 %copy-start.26 = (f32[768]{0:T(1024)}, f32[768]{0:T(1024)S(1)}, u32[]{:S(2)}) copy-start(f32[768]{0:T(1024)S(1)} %get-tuple-element.11) | copy-start | bytes 9220
  17.3 15.5 %copy-start.28 = (f32[768]{0:T(1024)}, f32[768]{0:T(1024)S(1)}, u32[]{:S(2)}) copy-start(f32[768]{0:T(1024)S(1)} %get-tuple-element.12) | copy-start | bytes 9220
  17.3 15.5 %copy-start.30 = (f32[768]{0:T(1024)}, f32[768]{0:T(1024)S(1)}, u32[]{:S(2)}) copy-start(f32[768]{0:T(1024)S(1)} %get-tuple-element.13) | copy-start | bytes 9220
  17.3 15.5 %copy-start.32 = (f32[768]{0:T(1024)}, f32[768]{0:T(1024)S(1)}, u32[]{:S(2)}) copy-start(f32[768]{0:T(1024)S(1)} %get-tuple-element.14) | copy-start | bytes 9220
  19.8 5.8 %collective-permute-start.1 = (bf16[3,8,768]{2,1,0:T(8,128)(2,1)S(1)}, bf16[3,8,768]{2,1,0:T(8,128)(2,1)S(1)}, u32[]{:S(2)}, u32[]{:S(2)}) collective-permute-start(bf16[3,8,768]{2,1,0:T(8,128)(2,1)S(1)} %get-tuple-element.95), channel_id=1, source_target_pairs={{2,0},{4,2},{6,4},{8,6},{10,8},{12,10},{14,12},{16,14},{18,16},{20... | collective-permute-start | bytes 110600 | tf_op jit(solution)/shard_map/ppermute | solution.py:28
  25.6 11.6 %collective-permute-start.7 = (bf16[2,48,384]{2,1,0:T(8,128)(2,1)S(1)}, bf16[2,48,384]{2,1,0:T(8,128)(2,1)S(1)}, u32[]{:S(2)}, u32[]{:S(2)}) collective-permute-start(bf16[2,48,384]{2,1,0:T(8,128)(2,1)S(1)} %get-tuple-element.102), channel_id=1, source_target_pairs={{0,4},{2,6},{4,0},{6,2},{8,12},{10,14},{12,8},{14,10},{16,20},{18,... | collective-permute-start | bytes 221192 | tf_op jit(solution)/shard_map/ppermute | solution.py:21
  33.5 9.5 %collective-permute-start.16 = (bf16[128,768]{1,0:T(8,128)(2,1)S(1)}, bf16[128,768]{1,0:T(8,128)(2,1)S(1)}, u32[]{:S(2)}, u32[]{:S(2)}) collective-permute-start(bf16[128,768]{1,0:T(8,128)(2,1)S(1)} %get-tuple-element.58), channel_id=1, source_target_pairs={{0,2},{2,0},{4,6},{6,4},{8,10},{10,8},{12,14},{14,12},{16,18},{18,... | collective-permute-start | bytes 589832 | tf_op jit(solution)/shard_map/ppermute | solution.py:21
  37.2 10.7 %collective-permute-start.4 = (bf16[128,768]{1,0:T(8,128)(2,1)S(1)}, bf16[128,768]{1,0:T(8,128)(2,1)S(1)}, u32[]{:S(2)}, u32[]{:S(2)}) collective-permute-start(bf16[128,768]{1,0:T(8,128)(2,1)S(1)} %get-tuple-element.66), channel_id=1, source_target_pairs={{0,6},{2,4},{4,2},{6,0},{8,14},{10,12},{12,10},{14,8},{16,22},{18,... | collective-permute-start | bytes 589832 | tf_op jit(solution)/shard_map/ppermute | solution.py:21
  37.2 12.5 %collective-permute-start.3 = (bf16[128,768]{1,0:T(8,128)(2,1)S(1)}, bf16[128,768]{1,0:T(8,128)(2,1)S(1)}, u32[]{:S(2)}, u32[]{:S(2)}) collective-permute-start(bf16[128,768]{1,0:T(8,128)(2,1)S(1)} %get-tuple-element.66), channel_id=1, source_target_pairs={{0,4},{2,6},{4,0},{6,2},{8,12},{10,14},{12,8},{14,10},{16,20},{18,... | collective-permute-start | bytes 589832 | tf_op jit(solution)/shard_map/ppermute | solution.py:21
  43.0 6.7 %collective-permute-start.2 = (bf16[128,768]{1,0:T(8,128)(2,1)S(1)}, bf16[128,768]{1,0:T(8,128)(2,1)S(1)}, u32[]{:S(2)}, u32[]{:S(2)}) collective-permute-start(bf16[128,768]{1,0:T(8,128)(2,1)S(1)} %get-tuple-element.66), channel_id=1, source_target_pairs={{0,2},{2,0},{4,6},{6,4},{8,10},{10,8},{12,14},{14,12},{16,18},{18,... | collective-permute-start | bytes 589832 | tf_op jit(solution)/shard_map/ppermute | solution.py:21
  45.0 11.6 %collective-permute-start.11 = (bf16[2,192,384]{2,1,0:T(8,128)(2,1)S(1)}, bf16[2,192,384]{2,1,0:T(8,128)(2,1)S(1)}, u32[]{:S(2)}, u32[]{:S(2)}) collective-permute-start(bf16[2,192,384]{2,1,0:T(8,128)(2,1)S(1)} %pad_maximum_fusion.5), channel_id=1, source_target_pairs={{0,8},{2,10},{4,12},{6,14},{8,0},{10,2},{12,4},{14,6},{16,24},{18,... | collective-permute-start | bytes 884744 | tf_op jit(solution)/shard_map/ppermute | solution.py:21
  46.7 18.9 %collective-permute-start.10 = (bf16[2,192,384]{2,1,0:T(8,128)(2,1)S(1)}, bf16[2,192,384]{2,1,0:T(8,128)(2,1)S(1)}, u32[]{:S(2)}, u32[]{:S(2)}) collective-permute-start(bf16[2,192,384]{2,1,0:T(8,128)(2,1)S(1)} %pad_maximum_fusion.5), channel_id=1, source_target_pairs={{0,16},{2,18},{4,20},{6,22},{8,24},{10,26},{12,28},{14,30},{16,0},... | collective-permute-start | bytes 884744 | tf_op jit(solution)/shard_map/ppermute | solution.py:21
  47.9 17.7 %collective-permute-start.9 = (bf16[2,192,384]{2,1,0:T(8,128)(2,1)S(1)}, bf16[2,192,384]{2,1,0:T(8,128)(2,1)S(1)}, u32[]{:S(2)}, u32[]{:S(2)}) collective-permute-start(bf16[2,192,384]{2,1,0:T(8,128)(2,1)S(1)} %pad_maximum_fusion.5), channel_id=1, source_target_pairs={{0,24},{2,26},{4,28},{6,30},{8,16},{10,18},{12,20},{14,22},{16,8},... | collective-permute-start | bytes 884744 | tf_op jit(solution)/shard_map/ppermute | solution.py:21
  49.7 16.5 %collective-permute-start.19 = (bf16[512,768]{1,0:T(8,128)(2,1)S(1)}, bf16[512,768]{1,0:T(8,128)(2,1)S(1)}, u32[]{:S(2)}, u32[]{:S(2)}) collective-permute-start(bf16[512,768]{1,0:T(8,128)(2,1)S(1)} %pad_maximum_fusion.3), channel_id=1, source_target_pairs={{0,1},{1,0},{2,3},{3,2},{4,5},{5,4},{6,7},{7,6},{8,9},{9,8},{10,11... | collective-permute-start | bytes 2359304 | tf_op jit(solution)/shard_map/ppermute | solution.py:21
  49.8 16.5 %collective-permute-start.5 = (bf16[512,768]{1,0:T(8,128)(2,1)S(1)}, bf16[512,768]{1,0:T(8,128)(2,1)S(1)}, u32[]{:S(2)}, u32[]{:S(2)}) collective-permute-start(bf16[512,768]{1,0:T(8,128)(2,1)S(1)} %pad_maximum_fusion.2), channel_id=1, source_target_pairs={{0,1},{1,0},{2,3},{3,2},{4,5},{5,4},{6,7},{7,6},{8,9},{9,8},{10,11... | collective-permute-start | bytes 2359304 | tf_op jit(solution)/shard_map/ppermute | solution.py:21
  71.5 11.6 %collective-permute-start.27 = (bf16[192,768]{1,0:T(8,128)(2,1)S(1)}, bf16[192,768]{1,0:T(8,128)(2,1)S(1)}, u32[]{:S(2)}, u32[]{:S(2)}) collective-permute-start(bf16[192,768]{1,0:T(8,128)(2,1)S(1)} %get-tuple-element.77), channel_id=1, source_target_pairs={{0,8},{2,10},{4,12},{6,14},{8,0},{10,2},{12,4},{14,6},{16,24},{18,... | collective-permute-start | bytes 884744 | tf_op jit(solution)/shard_map/ppermute | solution.py:21
  75.3 22.0 %collective-permute-start.28 = (bf16[192,768]{1,0:T(8,128)(2,1)S(1)}, bf16[192,768]{1,0:T(8,128)(2,1)S(1)}, u32[]{:S(2)}, u32[]{:S(2)}) collective-permute-start(bf16[192,768]{1,0:T(8,128)(2,1)S(1)} %get-tuple-element.78), channel_id=1, source_target_pairs={{0,16},{2,18},{4,20},{6,22},{8,24},{10,26},{12,28},{14,30},{16,0},... | collective-permute-start | bytes 884744 | tf_op jit(solution)/shard_map/ppermute | solution.py:21
  76.4 21.0 %collective-permute-start.29 = (bf16[192,768]{1,0:T(8,128)(2,1)S(1)}, bf16[192,768]{1,0:T(8,128)(2,1)S(1)}, u32[]{:S(2)}, u32[]{:S(2)}) collective-permute-start(bf16[192,768]{1,0:T(8,128)(2,1)S(1)} %get-tuple-element.79), channel_id=1, source_target_pairs={{0,24},{2,26},{4,28},{6,30},{8,16},{10,18},{12,20},{14,22},{16,8},... | collective-permute-start | bytes 884744 | tf_op jit(solution)/shard_map/ppermute | solution.py:21
  78.9 29.6 %collective-permute-start.20 = (bf16[512,768]{1,0:T(8,128)(2,1)S(1)}, bf16[512,768]{1,0:T(8,128)(2,1)S(1)}, u32[]{:S(2)}, u32[]{:S(2)}) collective-permute-start(bf16[512,768]{1,0:T(8,128)(2,1)S(1)} %slice.1797), channel_id=1, source_target_pairs={{0,1},{1,0},{2,3},{3,2},{4,5},{5,4},{6,7},{7,6},{8,9},{9,8},{10,11... | collective-permute-start | bytes 2359304 | tf_op jit(solution)/shard_map/ppermute | solution.py:21
  97.8 9.2 %collective-permute-start.30 = (bf16[192,768]{1,0:T(8,128)(2,1)S(1)}, bf16[192,768]{1,0:T(8,128)(2,1)S(1)}, u32[]{:S(2)}, u32[]{:S(2)}) collective-permute-start(bf16[192,768]{1,0:T(8,128)(2,1)S(1)} %add_convert_fusion), channel_id=1, source_target_pairs={{0,8},{2,10},{4,12},{6,14},{8,0},{10,2},{12,4},{14,6},{16,24},{18,... | collective-permute-start | bytes 884744 | tf_op jit(solution)/shard_map/ppermute | solution.py:21
  102.6 9.4 %collective-permute-start.12 = (bf16[512,768]{1,0:T(8,128)(2,1)S(1)}, bf16[512,768]{1,0:T(8,128)(2,1)S(1)}, u32[]{:S(2)}, u32[]{:S(2)}) collective-permute-start(bf16[512,768]{1,0:T(8,128)(2,1)S(1)} %slice.1798), channel_id=1, source_target_pairs={{0,1},{1,0},{2,3},{3,2},{4,5},{5,4},{6,7},{7,6},{8,9},{9,8},{10,11... | collective-permute-start | bytes 2359304 | tf_op jit(solution)/shard_map/ppermute | solution.py:21
  107.9 54.3 %collective-permute-start.33 = (bf16[384,768]{1,0:T(8,128)(2,1)}, bf16[384,768]{1,0:T(8,128)(2,1)}, u32[]{:S(2)}, u32[]{:S(2)}) collective-permute-start(bf16[384,768]{1,0:T(8,128)(2,1)} %pad_maximum_fusion.4), channel_id=1, source_target_pairs={{0,2},{2,0},{4,6},{6,4},{8,10},{10,8},{12,14},{14,12},{16,18},{18,... | collective-permute-start | bytes 1769480 | tf_op jit(solution)/shard_map/ppermute | solution.py:21
  108.2 54.0 %collective-permute-start.32 = (bf16[384,768]{1,0:T(8,128)(2,1)}, bf16[384,768]{1,0:T(8,128)(2,1)}, u32[]{:S(2)}, u32[]{:S(2)}) collective-permute-start(bf16[384,768]{1,0:T(8,128)(2,1)} %pad_maximum_fusion.4), channel_id=1, source_target_pairs={{0,4},{2,6},{4,0},{6,2},{8,12},{10,14},{12,8},{14,10},{16,20},{18,... | collective-permute-start | bytes 1769480 | tf_op jit(solution)/shard_map/ppermute | solution.py:21
  108.7 19.9 %collective-permute-start.21 = (bf16[128,768]{1,0:T(8,128)(2,1)S(1)}, bf16[128,768]{1,0:T(8,128)(2,1)S(1)}, u32[]{:S(2)}, u32[]{:S(2)}) collective-permute-start(bf16[128,768]{1,0:T(8,128)(2,1)S(1)} %get-tuple-element.83), channel_id=1, source_target_pairs={{0,2},{2,0},{4,6},{6,4},{8,10},{10,8},{12,14},{14,12},{16,18},{18,... | collective-permute-start | bytes 589832 | tf_op jit(solution)/shard_map/ppermute | solution.py:21
  110.5 22.1 %collective-permute-start.23 = (bf16[128,768]{1,0:T(8,128)(2,1)S(1)}, bf16[128,768]{1,0:T(8,128)(2,1)S(1)}, u32[]{:S(2)}, u32[]{:S(2)}) collective-permute-start(bf16[128,768]{1,0:T(8,128)(2,1)S(1)} %get-tuple-element.84), channel_id=1, source_target_pairs={{0,6},{2,4},{4,2},{6,0},{8,14},{10,12},{12,10},{14,8},{16,22},{18,... | collective-permute-start | bytes 589832 | tf_op jit(solution)/shard_map/ppermute | solution.py:21
  112.0 22.1 %collective-permute-start.22 = (bf16[128,768]{1,0:T(8,128)(2,1)S(1)}, bf16[128,768]{1,0:T(8,128)(2,1)S(1)}, u32[]{:S(2)}, u32[]{:S(2)}) collective-permute-start(bf16[128,768]{1,0:T(8,128)(2,1)S(1)} %get-tuple-element.85), channel_id=1, source_target_pairs={{0,4},{2,6},{4,0},{6,2},{8,12},{10,14},{12,8},{14,10},{16,20},{18,... | collective-permute-start | bytes 589832 | tf_op jit(solution)/shard_map/ppermute | solution.py:21
  112.4 40.0 %copy-start = (bf16[32,8,768]{2,1,0:T(8,128)(2,1)S(1)}, bf16[32,8,768]{2,1,0:T(8,128)(2,1)}, u32[]{:S(2)}) copy-start(bf16[32,8,768]{2,1,0:T(8,128)(2,1)} %param.10) | copy-start | bytes 1179652
  128.6 8.7 %collective-permute-start.13 = (bf16[128,768]{1,0:T(8,128)(2,1)}, bf16[128,768]{1,0:T(8,128)(2,1)}, u32[]{:S(2)}, u32[]{:S(2)}) collective-permute-start(bf16[128,768]{1,0:T(8,128)(2,1)} %get-tuple-element.86), channel_id=1, source_target_pairs={{0,2},{2,0},{4,6},{6,4},{8,10},{10,8},{12,14},{14,12},{16,18},{18,... | collective-permute-start | bytes 589832 | tf_op jit(solution)/shard_map/ppermute | solution.py:21
  132.6 9.1 %collective-permute-start.15 = (bf16[128,768]{1,0:T(8,128)(2,1)}, bf16[128,768]{1,0:T(8,128)(2,1)}, u32[]{:S(2)}, u32[]{:S(2)}) collective-permute-start(bf16[128,768]{1,0:T(8,128)(2,1)} %get-tuple-element.87), channel_id=1, source_target_pairs={{0,6},{2,4},{4,2},{6,0},{8,14},{10,12},{12,10},{14,8},{16,22},{18,... | collective-permute-start | bytes 589832 | tf_op jit(solution)/shard_map/ppermute | solution.py:21
  134.1 18.4 %collective-permute-start.14 = (bf16[128,768]{1,0:T(8,128)(2,1)S(1)}, bf16[128,768]{1,0:T(8,128)(2,1)}, u32[]{:S(2)}, u32[]{:S(2)}) collective-permute-start(bf16[128,768]{1,0:T(8,128)(2,1)S(1)} %get-tuple-element.88), channel_id=1, source_target_pairs={{0,4},{2,6},{4,0},{6,2},{8,12},{10,14},{12,8},{14,10},{16,20},{18,... | collective-permute-start | bytes 589832 | tf_op jit(solution)/shard_map/ppermute | solution.py:21
  137.3 24.9 %collective-permute-start.31 = (bf16[384,768]{1,0:T(8,128)(2,1)}, bf16[384,768]{1,0:T(8,128)(2,1)}, u32[]{:S(2)}, u32[]{:S(2)}) collective-permute-start(bf16[384,768]{1,0:T(8,128)(2,1)} %pad_maximum_fusion.4), channel_id=1, source_target_pairs={{0,6},{2,4},{4,2},{6,0},{8,14},{10,12},{12,10},{14,8},{16,22},{18,... | collective-permute-start | bytes 1769480 | tf_op jit(solution)/shard_map/ppermute | solution.py:21
  154.6 1.4 collective-permute-start.24
  156.1 30.1 %collective-permute-start.26 = (bf16[3,8,768]{2,1,0:T(8,128)(2,1)S(1)}, bf16[3,8,768]{2,1,0:T(8,128)(2,1)S(1)}, u32[]{:S(2)}, u32[]{:S(2)}) collective-permute-start(bf16[3,8,768]{2,1,0:T(8,128)(2,1)S(1)} %get-tuple-element.103), channel_id=1, source_target_pairs={{2,0},{4,2},{6,4},{8,6},{10,8},{12,10},{14,12},{16,14},{18,16},{20... | collective-permute-start | bytes 110600 | tf_op jit(solution)/shard_map/ppermute | solution.py:28
  157.4 28.1 %collective-permute-start.25 = (bf16[3,8,768]{2,1,0:T(8,128)(2,1)S(1)}, bf16[3,8,768]{2,1,0:T(8,128)(2,1)S(1)}, u32[]{:S(2)}, u32[]{:S(2)}) collective-permute-start(bf16[3,8,768]{2,1,0:T(8,128)(2,1)S(1)} %get-tuple-element.104), channel_id=1, source_target_pairs={{0,2},{2,4},{4,6},{6,8},{8,10},{10,12},{12,14},{14,16},{16,18},{18... | collective-permute-start | bytes 110600 | tf_op jit(solution)/shard_map/ppermute | solution.py:28
  182.0 10.2 %collective-permute-start.34 = (bf16[48,1536]{1,0:T(8,128)(2,1)S(1)}, bf16[48,1536]{1,0:T(8,128)(2,1)S(1)}, u32[]{:S(2)}, u32[]{:S(2)}) collective-permute-start(bf16[48,1536]{1,0:T(8,128)(2,1)S(1)} %slice.1799), channel_id=1, source_target_pairs={{0,16},{2,18},{4,20},{6,22},{8,24},{10,26},{12,28},{14,30},{16,0},... | collective-permute-start | bytes 442376 | tf_op jit(solution)/shard_map/ppermute | solution.py:21
  (78 other events, 662.4 us)

commit v2 on v1

--- a/solution.py
+++ b/solution.py
@@ -26,6 +26,10 @@
     up = [(i, i + 1) for i in range(devices - 1)]
     down = [(i + 1, i) for i in range(devices - 1)]
     return lax.ppermute(last, "tile", up), lax.ppermute(first, "tile", down)
+
+
+def exchange(blocks, groups):
+    return lax.all_to_all(blocks, "tile", 0, 0, axis_index_groups=groups)
 
 
 def in_order(blocks, index):
@@ -149,33 +153,32 @@
     mine_cot = lax.dynamic_slice_in_dim(cotangent, offset, share, 0).astype(F32)
     mine_inputs = lax.dynamic_slice_in_dim(features, offset, share, 0).astype(F32)
 
+    planes = [[i * PLANE + j for j in range(PLANE)] for i in range(lines)]
+    columns_z = [[i * PLANE + j for i in range(lines)] for j in range(PLANE)]
+    height = channels // tiles
     units = weight_up.shape[1] // PLANE
     both_weights = jnp.stack([weight_up, weight_down.T])
-    pieces = []
-    for s in range(PLANE):
-        piece = lax.dynamic_slice_in_dim(both_weights, (place ^ s) * units, units, 2)
-        pieces.append(swap(piece, "tile", s) if s else piece)
-    piece = jnp.concatenate(in_order(pieces, place), 1)
-    pieces = [swap(piece, "tile", PLANE * s) if s else piece for s in range(lines)]
-    weights = jnp.concatenate(in_order(pieces, line), 1)
-    up, down_t = weights[0], weights[1]
+    pieces = both_weights.reshape(2, height, PLANE, units).transpose(2, 0, 1, 3)
+    pieces = exchange(pieces, planes)
+    pieces = pieces.transpose(1, 0, 2, 3).reshape(2, PLANE * height, units)
+    pieces = exchange(jnp.broadcast_to(pieces, (lines,) + pieces.shape), columns_z)
+    up = pieces[:, 0].reshape(channels, units)
+    down_t = pieces[:, 1].reshape(channels, units)
     bias = lax.dynamic_slice_in_dim(bias_up, place * units, units, 0)
 
     def gather(mine):
         mine = mine.reshape(tokens, channels)
-        mine = jnp.concatenate([mine] + [swap(mine, "tile", s) for s in range(1, PLANE)], 0)
+        mine = exchange(jnp.broadcast_to(mine, (PLANE,) + mine.shape), planes)
+        mine = mine.reshape(PLANE * tokens, channels)
         return jnp.concatenate([mine] + [swap(mine, "own", s) for s in range(1, owners)], 0)
 
-    def scatter(partial):
-        partial = partial.reshape(owners, PLANE * tokens, channels)
-        total = partial[0]
+    def scatter(partials):
+        partials = jnp.stack(partials).reshape(2, owners, PLANE, tokens, channels)
+        total = partials[:, 0]
         for s in range(1, owners):
-            total = total + swap(partial[s].astype(BF16), "own", s).astype(F32)
-        total = total.reshape(PLANE, tokens, channels)
-        mine = total[0]
-        for s in range(1, PLANE):
-            mine = mine + swap(total[s].astype(BF16), "tile", s).astype(F32)
-        return mine.reshape(share, columns, channels)
+            total = total + swap(partials[:, s].astype(BF16), "own", s).astype(F32)
+        total = exchange(total.astype(BF16).transpose(1, 0, 2, 3), planes).astype(F32)
+        return jnp.sum(total, 0).reshape(2, share, columns, channels)
 
     grad_branch = gather((keep_scale * mine_cot).astype(BF16))
     inputs_live = jnp.where(row_live[:, None, None], features, jnp.zeros_like(features))
@@ -194,21 +197,17 @@
         [dot(grad_hidden, normed, over_tokens), dot(act, grad_branch, over_tokens)], 0
     ).astype(BF16)
     kept = 2 * units // lines
-    grad_t = lax.dynamic_slice_in_dim(parts, line * kept, kept, 0).astype(F32)
-    for s in range(1, lines):
-        part = lax.dynamic_slice_in_dim(parts, (line ^ s) * kept, kept, 0)
-        grad_t = grad_t + swap(part, "tile", PLANE * s).astype(F32)
-    grad_t = grad_t.astype(BF16)
-
-    grad_normed = scatter(dot(grad_hidden, up, across))
-    branch = scatter(dot(act, down_t, across))
+    parts = exchange(parts.reshape(lines, kept, channels), columns_z)
+    grad_t = jnp.sum(parts.astype(F32), 0).astype(BF16)
+
+    grad_normed, branch = scatter([dot(grad_hidden, up, across), dot(act, down_t, across)])
     block_out = jnp.where(mine_live, mine_inputs + keep_scale * branch, 0.0).astype(BF16)
 
     half_lines = lines // 2
     blocks = [swap(grad_t, "tile", PLANE * s) if s else grad_t for s in range(half_lines)]
     block = jnp.concatenate(in_order(blocks, line % half_lines), 0)
-    blocks = [swap(block, "tile", s) if s else block for s in range(PLANE)]
-    whole_t = jnp.concatenate(in_order(blocks, place), 0)
+    blocks = exchange(jnp.broadcast_to(block, (PLANE,) + block.shape), planes)
+    whole_t = blocks.reshape(-1, channels)
 
     grad_mixed = jnp.where(mine_live, norm_back(grad_normed, centred, inv_std, ln_gain), 0.0)
     grad_mixed = grad_mixed.astype(BF16)
@@ -219,7 +218,6 @@
     )
     grad_features = jnp.where(mine_live, mine_cot + spread, 0.0).astype(BF16)
 
-    height = channels // tiles
     other = tile ^ (PLANE * half_lines)
     ortho = orthogonal_rows(whole_t, (tile * height, other * height), height)
     mine, theirs = ortho[:height], swap(ortho[height:].astype(BF16), "tile", PLANE * half_lines)

time: 194 us -> 223 us (1.15)
  waiting for transfers between devices: 79.8 us -> 104 us
  starting transfers between devices: 54.5 us -> 43.1 us
  matrix products: 22.1 us -> 29.6 us
  local copies, waits for them, and re-layouts: 7.83 us -> 15.1 us
    all_to_all x0 -> x7, waiting for transfers between devices: none -> 79.6 us  [exchange(): return lax.all_to_all(blocks, 'tile', 0, 0, axis_index_groups=groups)]
    ppermute x31 -> x6, waiting for transfers between devices: 76 us -> 12.2 us  [swap(): lax.ppermute(value, axis, [(i, i ^ bit) for i in range(lax.axis_size(axis...]
    ppermute x31 -> x6, starting transfers between devices: 44.8 us -> 0.66 us  [swap(): lax.ppermute(value, axis, [(i, i ^ bit) for i in range(lax.axis_size(axis...]
    all_to_all x0 -> x7, starting transfers between devices: none -> 31.2 us  [exchange(): return lax.all_to_all(blocks, 'tile', 0, 0, axis_index_groups=groups)]
    ppermute x4, waiting for transfers between devices: 3.88 us -> 12.7 us  [neighbours(): return (lax.ppermute(last, 'tile', up), lax.ppermute(first, 'tile', down))]
    dot_general x14, matrix products: 22.1 us -> 29.6 us  [dot(): lax.dot_general(left, right, (contract, ((), ())), precision=precision, p...]
    broadcast_in_dim x0 -> x4, local copies, waits for them, and re-layouts: none -> 4.75 us  [the longest x2 1.86 us: gather(): mine = exchange(jnp.broadcast_to(mine, (PLANE,) + mine.shape), planes)]
    reduce_sum x0 -> x2, other arithmetic: none -> 3.23 us  [the longest x1 1.71 us: scatter(): return jnp.sum(total, 0).reshape(2, share, columns, channels)]
  transfers between devices with their start and end apart: 35 -> 17, of which waited for: 13 -> 10; matrix products, arithmetic and copies ran while one was open for 23% -> 16% of each run, Pallas kernels for 0% -> 0%
where the time goes in v2:
time: 223 us; the launch traced here: 222 us
  waiting for transfers between devices  104 us (47%)
  starting transfers between devices  43.1 us (19%)
  matrix products  29.6 us (13%)
  other arithmetic  26.2 us (12%)
  local copies, waits for them, and re-layouts  15.1 us (7%)
  between operations  3.86 us (2%)
    all_to_all x7, waiting for transfers between devices, exchange(): return lax.all_to_all(blocks, 'tile', 0, 0, axis_index_groups=groups)  79.6 us
    all_to_all x7, starting transfers between devices, exchange(): return lax.all_to_all(blocks, 'tile', 0, 0, axis_index_groups=groups)  31.2 us
    dot_general x14, matrix products, dot(): lax.dot_general(left, right, (contract, ((), ())), precision=precision, p...  29.6 us
    ppermute x4, waiting for transfers between devices, neighbours(): return (lax.ppermute(last, 'tile', up), lax.ppermute(first, 'tile', down))  12.7 us
    ppermute x6, waiting for transfers between devices, swap(): lax.ppermute(value, axis, [(i, i ^ bit) for i in range(lax.axis_size(axis...  12.2 us
    ppermute x4, starting transfers between devices, neighbours(): return (lax.ppermute(last, 'tile', up), lax.ppermute(first, 'tile', down))  11.2 us
    reduce_sum x1, other arithmetic, layer_norm(): average = jnp.mean(mixed, axis=-1, keepdims=True)  4.72 us
  transfers between devices with their start and end apart: 17, of which 10 were waited for; matrix products, arithmetic and copies ran while one was open for 16% of the time, Pallas kernels for 0%

profile of v2, /device:TPU:0, one launch (start us, length us, event | category | flops | bytes accessed | tf_op | source)
XLA Modules:
  0.0 222.3 jit_solution(8854069493886129927)
XLA Ops:
  0.7 1.0 stack.14
  1.7 0.9 stack.15
  3.6 5.2 %all-to-all-start.1 = ((bf16[4,2,48,384]{3,2,1,0:T(8,128)(2,1)}), bf16[4,2,48,384]{3,2,1,0:T(8,128)(2,1)S(1)}, u32[]{:S(2)}, u32[]{:S(2)}) async-start(bf16[4,2,48,384]{3,2,1,0:T(8,128)(2,1)} %copy.21), calls=%async_computation.1 | async-start | bytes 589824 | tf_op jit(solution)/shard_map/all_to_all | solution.py:32
  10.2 1.3 collective-permute-start.2
  11.5 4.6 %collective-permute-start.1 = (bf16[3,8,768]{2,1,0:T(8,128)(2,1)S(1)}, bf16[3,8,768]{2,1,0:T(8,128)(2,1)S(1)}, u32[]{:S(2)}, u32[]{:S(2)}) collective-permute-start(bf16[3,8,768]{2,1,0:T(8,128)(2,1)S(1)} %get-tuple-element.72), channel_id=1, source_target_pairs={{0,2},{2,4},{4,6},{6,8},{8,10},{10,12},{12,14},{14,16},{16,18},{18... | collective-permute-start | bytes 110600 | tf_op jit(solution)/shard_map/ppermute | solution.py:28
  20.3 4.7 %fusion.220 = (f32[16,8]{1,0:T(8,128)S(1)}, f32[16,8,768]{2,1,0:T(8,128)S(1)}) fusion(f32[768]{0:T(1024)} %get-tuple-element.51, f32[768]{0:T(1024)} %get-tuple-element.52, f32[768]{0:T(1024)S(1)} %get-tuple-element.5, f32[22,8,768]{2,1,0:T(8,128)S(1)} %dynamic-slice_convert_fusion.1, f32[768]{0:T(1024)S(1)} %get-tuple-element.6, ...), kind=kLoop, calls=%fused_computation.439 | loop fusion | flops 9633664 | bytes 3877376 | tf_op jit(solution)/shard_map/reduce_sum | solution.py:61
  25.5 0.9 broadcast_in_dim.91
  26.4 6.0 %all-to-all-start = ((bf16[4,128,768]{2,1,0:T(8,128)(2,1)}), bf16[4,128,768]{2,1,0:T(8,128)(2,1)}, u32[]{:S(2)}, u32[]{:S(2)}) async-start(bf16[4,128,768]{2,1,0:T(8,128)(2,1)} %broadcast_in_dim.91), calls=%async_computation | async-start | bytes 1572864 | tf_op jit(solution)/shard_map/all_to_all | solution.py:32
  32.7 9.5 %all-to-all-done = bf16[4,128,768]{2,1,0:T(8,128)(2,1)} async-done(((bf16[4,128,768]{2,1,0:T(8,128)(2,1)}), bf16[4,128,768]{2,1,0:T(8,128)(2,1)}, u32[]{:S(2)}, u32[]{:S(2)}) %all-to-all-start) | async-done | bytes 786464 | tf_op jit(solution)/shard_map/all_to_all | solution.py:32
  42.2 0.9 broadcast_in_dim.95
  43.1 3.5 %all-to-all-start.3 = ((bf16[4,128,768]{2,1,0:T(8,128)(2,1)}), bf16[4,128,768]{2,1,0:T(8,128)(2,1)S(1)}, u32[]{:S(2)}, u32[]{:S(2)}) async-start(bf16[4,128,768]{2,1,0:T(8,128)(2,1)} %broadcast_in_dim.95), calls=%async_computation.3 | async-start | bytes 1572864 | tf_op jit(solution)/shard_map/all_to_all | solution.py:32
  46.7 9.5 %all-to-all-done.3 = bf16[4,128,768]{2,1,0:T(8,128)(2,1)S(1)} async-done(((bf16[4,128,768]{2,1,0:T(8,128)(2,1)}), bf16[4,128,768]{2,1,0:T(8,128)(2,1)S(1)}, u32[]{:S(2)}, u32[]{:S(2)}) %all-to-all-start.3) | async-done | bytes 786464 | tf_op jit(solution)/shard_map/all_to_all | solution.py:32
  56.2 1.2 broadcast_in_dim.92
  57.4 5.1 %all-to-all-start.2 = ((bf16[4,2,192,384]{3,2,1,0:T(8,128)(2,1)}), bf16[4,2,192,384]{3,2,1,0:T(8,128)(2,1)S(1)}, u32[]{:S(2)}, u32[]{:S(2)}) async-start(bf16[4,2,192,384]{3,2,1,0:T(8,128)(2,1)} %broadcast_in_dim.92), calls=%async_computation.2 | async-start | bytes 2359296 | tf_op jit(solution)/shard_map/all_to_all | solution.py:32
  63.8 25.6 %all-to-all-done.2 = bf16[4,2,192,384]{3,2,1,0:T(8,128)(2,1)S(1)} async-done(((bf16[4,2,192,384]{3,2,1,0:T(8,128)(2,1)}), bf16[4,2,192,384]{3,2,1,0:T(8,128)(2,1)S(1)}, u32[]{:S(2)}, u32[]{:S(2)}) %all-to-all-start.2) | async-done | bytes 1179680 | tf_op jit(solution)/shard_map/all_to_all | solution.py:32
  89.6 1.1 multiply_convert_fusion
  90.7 1.0 convolution_bitcast_fusion
  91.7 2.7 %fusion.13 = bf16[1024,384]{1,0:T(8,128)(2,1)S(1)} fusion(f32[1024,384]{1,0:T(8,128)S(1)} %get-tuple-element.76, bf16[768,384]{1,0:T(8,128)(2,1)S(1)} %bitcast.97, bf16[512,768]{1,0:T(8,128)(2,1)} %collective-permute-done, bf16[512,768]{1,0:T(8,128)(2,1)} %bitcast.3), kind=kOutput, calls=%fused_computation.111 | convolution fusion | flops 611057664 | bytes 4521984 | tf_op jit(solution)/shard_map/dot_general | solution.py:86
  94.4 1.0 convolution_bitcast_fusion.1
  95.4 1.6 fusion.14
  97.6 2.3 %convolution_convert_fusion = bf16[384,768]{1,0:T(8,128)(2,1)S(1)} fusion(bf16[1024,384]{1,0:T(8,128)(2,1)S(1)} %get-tuple-element.75, bf16[512,768]{1,0:T(8,128)(2,1)} %collective-permute-done, bf16[512,768]{1,0:T(8,128)(2,1)} %bitcast.3), kind=kOutput, calls=%fused_computation.119 | convolution fusion | flops 607420416 | bytes 2949120 | tf_op jit(solution)/shard_map/dot_general | solution.py:86
  100.7 1.1 pad_maximum_fusion.3
  101.8 4.3 %all-to-all-start.5 = ((bf16[4,192,768]{2,1,0:T(8,128)(2,1)}), bf16[4,192,768]{2,1,0:T(8,128)(2,1)}, u32[]{:S(2)}, u32[]{:S(2)}) async-start(bf16[4,192,768]{2,1,0:T(8,128)(2,1)} %bitcast.93), calls=%async_computation.5 | async-start | bytes 2359296 | tf_op jit(solution)/shard_map/all_to_all | solution.py:32
  106.1 2.2 %fusion.15 = bf16[4,2,128,768]{3,2,0,1:T(8,128)(2,1)S(1)} fusion(bf16[2,4,128,768]{3,2,1,0:T(8,128)(2,1)} %collective-permute-done.4, f32[1,2,4,128,768]{4,3,2,1,0:T(8,128)S(1)} %convolution_bitcast_fusion, f32[1,2,4,128,768]{4,3,2,1,0:T(8,128)} %copy-done), kind=kLoop, calls=%fused_computation.113 | loop fusion | flops 3145728 | bytes 9437184 | tf_op jit(solution)/shard_map/transpose | solution.py:180
  108.4 1.3 copy.24
  109.6 25.9 %all-to-all-done.5 = bf16[4,192,768]{2,1,0:T(8,128)(2,1)} async-done(((bf16[4,192,768]{2,1,0:T(8,128)(2,1)}), bf16[4,192,768]{2,1,0:T(8,128)(2,1)}, u32[]{:S(2)}, u32[]{:S(2)}) %all-to-all-start.5) | async-done | bytes 1179680 | tf_op jit(solution)/shard_map/all_to_all | solution.py:32
  135.6 3.6 %all-to-all-start.4 = ((bf16[4,2,128,768]{3,2,1,0:T(8,128)(2,1)}), bf16[4,2,128,768]{3,2,1,0:T(8,128)(2,1)S(1)}, u32[]{:S(2)}, u32[]{:S(2)}) async-start(bf16[4,2,128,768]{3,2,1,0:T(8,128)(2,1)} %copy.24), calls=%async_computation.4 | async-start | bytes 3145728 | tf_op jit(solution)/shard_map/all_to_all | solution.py:32
  139.1 1.5 reduce_sum.71
  140.8 8.4 %collective-permute-done.8 = bf16[192,768]{1,0:T(8,128)(2,1)S(1)} collective-permute-done((bf16[192,768]{1,0:T(8,128)(2,1)S(1)}, bf16[192,768]{1,0:T(8,128)(2,1)S(1)}, u32[]{:S(2)}, u32[]{:S(2)}) %collective-permute-start.8) | collective-permute-done | bytes 294944 | tf_op jit(solution)/shard_map/ppermute | solution.py:21
  149.3 9.1 %all-to-all-done.4 = bf16[4,2,128,768]{3,2,1,0:T(8,128)(2,1)S(1)} async-done(((bf16[4,2,128,768]{3,2,1,0:T(8,128)(2,1)}), bf16[4,2,128,768]{3,2,1,0:T(8,128)(2,1)S(1)}, u32[]{:S(2)}, u32[]{:S(2)}) %all-to-all-start.4) | async-done | bytes 1572896 | tf_op jit(solution)/shard_map/all_to_all | solution.py:32
  158.4 1.7 broadcast_in_dim.98
  160.2 3.6 %all-to-all-start.6 = ((bf16[4,384,768]{2,1,0:T(8,128)(2,1)}), bf16[4,384,768]{2,1,0:T(8,128)(2,1)S(1)}, u32[]{:S(2)}, u32[]{:S(2)}) async-start(bf16[4,384,768]{2,1,0:T(8,128)(2,1)} %broadcast_in_dim.98), calls=%async_computation.6 | async-start | bytes 4718592 | tf_op jit(solution)/shard_map/all_to_all | solution.py:32
  163.9 1.7 convert_reduce_fusion
  167.0 1.3 div.27
  169.1 2.0 select_convert_fusion
  171.1 1.6 collective-permute-done.5
  172.7 1.0 broadcast_select_fusion.4
  173.7 3.9 %collective-permute-start.6 = (bf16[3,8,768]{2,1,0:T(8,128)(2,1)S(1)}, bf16[3,8,768]{2,1,0:T(8,128)(2,1)S(1)}, u32[]{:S(2)}, u32[]{:S(2)}) collective-permute-start(bf16[3,8,768]{2,1,0:T(8,128)(2,1)S(1)} %get-tuple-element.74), channel_id=1, source_target_pairs={{0,2},{2,4},{4,6},{6,8},{8,10},{10,12},{12,14},{14,16},{16,18},{18... | collective-permute-start | bytes 110600 | tf_op jit(solution)/shard_map/ppermute | solution.py:28
  177.7 1.5 collective-permute-start.7
  179.2 11.2 %collective-permute-done.6 = bf16[3,8,768]{2,1,0:T(8,128)(2,1)S(1)} collective-permute-done((bf16[3,8,768]{2,1,0:T(8,128)(2,1)S(1)}, bf16[3,8,768]{2,1,0:T(8,128)(2,1)S(1)}, u32[]{:S(2)}, u32[]{:S(2)}) %collective-permute-start.6) | collective-permute-done | bytes 36896 | tf_op jit(solution)/shard_map/ppermute | solution.py:28
  191.1 1.5 collective-permute-done.7
  192.6 4.1 %fusion.5 = (f32[]{:T(128)}, f32[768,768,1]{1,0,2:T(8,128)}) fusion(bf16[4,384,768]{2,1,0:T(8,128)(2,1)S(1)} %all-to-all-done.6), kind=kOutput, calls=%fused_computation.97 | convolution fusion | flops 1813708800 | bytes 4718596 | tf_op jit(solution)/shard_map/dot_general | solution.py:86
  197.3 6.5 %multiply_add_fusion.2 = f32[768,768]{1,0:T(8,128)S(1)} fusion(f32[768,768,1]{1,0,2:T(8,128)} %get-tuple-element.78, f32[]{:T(128)S(6)} %mul.1170), kind=kOutput, calls=%fused_computation.100 | convolution fusion | flops 2720858112 | bytes 4718596 | tf_op jit(solution)/shard_map/dot_general | solution.py:86
  203.8 3.2 %multiply_add_fusion.1 = f32[768,768]{1,0:T(8,128)S(1)} fusion(f32[768,768,1]{1,0,2:T(8,128)S(1)} %copy-done.2, f32[768,768]{1,0:T(8,128)S(1)} %multiply_add_fusion.2, f32[]{:T(128)S(6)} %mul.1170), kind=kOutput, calls=%fused_computation.99 | convolution fusion | flops 2720268288 | bytes 7077892 | tf_op jit(solution)/shard_map/dot_general | solution.py:86
  207.1 3.2 %multiply_add_fusion = f32[768,768]{1,0:T(8,128)S(1)} fusion(f32[768,768]{1,0:T(8,128)S(1)} %multiply_add_fusion.1, f32[768,768]{1,0:T(8,128)S(1)} %multiply_add_fusion.2), kind=kOutput, calls=%fused_computation.98 | convolution fusion | flops 2719088640 | bytes 7077888 | tf_op jit(solution)/shard_map/dot_general | solution.py:86
  211.3 1.2 fusion.19
  215.1 4.3 %fusion.21 = bf16[16,8,768]{2,1,0:T(8,128)(2,1)} fusion(f32[22,8,768]{2,1,0:T(8,128)S(1)} %dynamic-slice_convert_fusion, f32[768]{0:T(1024)} %get-tuple-element.51, f32[768]{0:T(1024)} %get-tuple-element.52, f32[768]{0:T(1024)S(1)} %copy-done.14, f32[768]{0:T(1024)S(1)} %copy-done.16, f32[768]{0:T(1024)S(1)} %copy-done.18, f32[768]{0:T(1024)S(1)} %copy-done.20, ...), kind=kLoop, calls=%fused_computation.135 | loop fusion | flops 9928704 | bytes 3876884 | tf_op jit(solution)/shard_map/convert_element_type | solution.py:219
  219.3 2.1 collective-permute-done.9
  (247 shorter events, 15.9 us)
Async XLA Ops:
  0.6 9.4 %copy-start.3 = (bf16[32,8,768]{2,1,0:T(8,128)(2,1)S(1)}, bf16[32,8,768]{2,1,0:T(8,128)(2,1)}, u32[]{:S(2)}) copy-start(bf16[32,8,768]{2,1,0:T(8,128)(2,1)} %param.10) | copy-start | bytes 1179652
  0.7 15.4 %copy-start.8 = (f32[7,7,768]{2,1,0:T(8,128)S(1)}, f32[7,7,768]{2,1,0:T(8,128)}, u32[]{:S(2)}) copy-start(f32[7,7,768]{2,1,0:T(8,128)} %param.12) | copy-start | bytes 451588
  0.7 16.1 %copy-start.91 = (s32[4,1]{0,1:T(1,128)S(1)}, s32[4,1]{0,1:T(1,128)}, u32[]{:S(2)}) copy-start(s32[4,1]{0,1:T(1,128)} %param.18) | copy-start | bytes 52
  0.7 17.4 %copy-start.89 = (f32[768]{0:T(1024)S(1)}, f32[768]{0:T(1024)}, u32[]{:S(2)}) copy-start(f32[768]{0:T(1024)} %param.17) | copy-start | bytes 9220
  0.7 17.4 %copy-start.6 = (bf16[32,8,768]{2,1,0:T(8,128)(2,1)S(1)}, bf16[32,8,768]{2,1,0:T(8,128)(2,1)}, u32[]{:S(2)}) copy-start(bf16[32,8,768]{2,1,0:T(8,128)(2,1)} %param.11) | copy-start | bytes 1179652
  3.6 21.8 %all-to-all-start.1 = ((bf16[4,2,48,384]{3,2,1,0:T(8,128)(2,1)}), bf16[4,2,48,384]{3,2,1,0:T(8,128)(2,1)S(1)}, u32[]{:S(2)}, u32[]{:S(2)}) async-start(bf16[4,2,48,384]{3,2,1,0:T(8,128)(2,1)} %copy.21), calls=%async_computation.1 | async-start | bytes 589824 | tf_op jit(solution)/shard_map/all_to_all | solution.py:32
  10.2 10.0 %collective-permute-start.2 = (bf16[3,8,768]{2,1,0:T(8,128)(2,1)S(1)}, bf16[3,8,768]{2,1,0:T(8,128)(2,1)S(1)}, u32[]{:S(2)}, u32[]{:S(2)}) collective-permute-start(bf16[3,8,768]{2,1,0:T(8,128)(2,1)S(1)} %get-tuple-element.71), channel_id=1, source_target_pairs={{2,0},{4,2},{6,4},{8,6},{10,8},{12,10},{14,12},{16,14},{18,16},{20... | collective-permute-start | bytes 110600 | tf_op jit(solution)/shard_map/ppermute | solution.py:28
  11.5 8.0 %collective-permute-start.1 = (bf16[3,8,768]{2,1,0:T(8,128)(2,1)S(1)}, bf16[3,8,768]{2,1,0:T(8,128)(2,1)S(1)}, u32[]{:S(2)}, u32[]{:S(2)}) collective-permute-start(bf16[3,8,768]{2,1,0:T(8,128)(2,1)S(1)} %get-tuple-element.72), channel_id=1, source_target_pairs={{0,2},{2,4},{4,6},{6,8},{8,10},{10,12},{12,14},{14,16},{16,18},{18... | collective-permute-start | bytes 110600 | tf_op jit(solution)/shard_map/ppermute | solution.py:28
  16.3 8.8 %copy-start.13 = (f32[768]{0:T(1024)}, f32[768]{0:T(1024)S(1)}, u32[]{:S(2)}) copy-start(f32[768]{0:T(1024)S(1)} %get-tuple-element.5) | copy-start | bytes 9220
  16.3 8.8 %copy-start.15 = (f32[768]{0:T(1024)}, f32[768]{0:T(1024)S(1)}, u32[]{:S(2)}) copy-start(f32[768]{0:T(1024)S(1)} %get-tuple-element.6) | copy-start | bytes 9220
  16.3 8.8 %copy-start.17 = (f32[768]{0:T(1024)}, f32[768]{0:T(1024)S(1)}, u32[]{:S(2)}) copy-start(f32[768]{0:T(1024)S(1)} %get-tuple-element.7) | copy-start | bytes 9220
  16.3 8.8 %copy-start.19 = (f32[768]{0:T(1024)}, f32[768]{0:T(1024)S(1)}, u32[]{:S(2)}) copy-start(f32[768]{0:T(1024)S(1)} %get-tuple-element.8) | copy-start | bytes 9220
  16.3 8.8 %copy-start.21 = (f32[768]{0:T(1024)}, f32[768]{0:T(1024)S(1)}, u32[]{:S(2)}) copy-start(f32[768]{0:T(1024)S(1)} %get-tuple-element.9) | copy-start | bytes 9220
  16.3 8.8 %copy-start.23 = (f32[768]{0:T(1024)}, f32[768]{0:T(1024)S(1)}, u32[]{:S(2)}) copy-start(f32[768]{0:T(1024)S(1)} %get-tuple-element.10) | copy-start | bytes 9220
  16.3 8.8 %copy-start.25 = (f32[768]{0:T(1024)}, f32[768]{0:T(1024)S(1)}, u32[]{:S(2)}) copy-start(f32[768]{0:T(1024)S(1)} %get-tuple-element.11) | copy-start | bytes 9220
  16.3 8.8 %copy-start.27 = (f32[768]{0:T(1024)}, f32[768]{0:T(1024)S(1)}, u32[]{:S(2)}) copy-start(f32[768]{0:T(1024)S(1)} %get-tuple-element.12) | copy-start | bytes 9220
  16.3 8.8 %copy-start.29 = (f32[768]{0:T(1024)}, f32[768]{0:T(1024)S(1)}, u32[]{:S(2)}) copy-start(f32[768]{0:T(1024)S(1)} %get-tuple-element.13) | copy-start | bytes 9220
  16.4 8.8 %copy-start.31 = (f32[768]{0:T(1024)}, f32[768]{0:T(1024)S(1)}, u32[]{:S(2)}) copy-start(f32[768]{0:T(1024)S(1)} %get-tuple-element.14) | copy-start | bytes 9220
  16.4 8.8 %copy-start.33 = (f32[768]{0:T(1024)}, f32[768]{0:T(1024)S(1)}, u32[]{:S(2)}) copy-start(f32[768]{0:T(1024)S(1)} %get-tuple-element.15) | copy-start | bytes 9220
  16.4 8.8 %copy-start.35 = (f32[768]{0:T(1024)}, f32[768]{0:T(1024)S(1)}, u32[]{:S(2)}) copy-start(f32[768]{0:T(1024)S(1)} %get-tuple-element.16) | copy-start | bytes 9220
  16.4 8.8 %copy-start.37 = (f32[768]{0:T(1024)}, f32[768]{0:T(1024)S(1)}, u32[]{:S(2)}) copy-start(f32[768]{0:T(1024)S(1)} %get-tuple-element.17) | copy-start | bytes 9220
  16.4 8.8 %copy-start.39 = (f32[768]{0:T(1024)}, f32[768]{0:T(1024)S(1)}, u32[]{:S(2)}) copy-start(f32[768]{0:T(1024)S(1)} %get-tuple-element.18) | copy-start | bytes 9220
  16.4 8.8 %copy-start.41 = (f32[768]{0:T(1024)}, f32[768]{0:T(1024)S(1)}, u32[]{:S(2)}) copy-start(f32[768]{0:T(1024)S(1)} %get-tuple-element.19) | copy-start | bytes 9220
  16.4 8.8 %copy-start.43 = (f32[768]{0:T(1024)}, f32[768]{0:T(1024)S(1)}, u32[]{:S(2)}) copy-start(f32[768]{0:T(1024)S(1)} %get-tuple-element.20) | copy-start | bytes 9220
  16.4 8.8 %copy-start.45 = (f32[768]{0:T(1024)}, f32[768]{0:T(1024)S(1)}, u32[]{:S(2)}) copy-start(f32[768]{0:T(1024)S(1)} %get-tuple-element.21) | copy-start | bytes 9220
  16.4 8.8 %copy-start.47 = (f32[768]{0:T(1024)}, f32[768]{0:T(1024)S(1)}, u32[]{:S(2)}) copy-start(f32[768]{0:T(1024)S(1)} %get-tuple-element.22) | copy-start | bytes 9220
  16.6 8.6 %copy-start.49 = (f32[768]{0:T(1024)}, f32[768]{0:T(1024)S(1)}, u32[]{:S(2)}) copy-start(f32[768]{0:T(1024)S(1)} %get-tuple-element.23) | copy-start | bytes 9220
  16.6 8.6 %copy-start.51 = (f32[768]{0:T(1024)}, f32[768]{0:T(1024)S(1)}, u32[]{:S(2)}) copy-start(f32[768]{0:T(1024)S(1)} %get-tuple-element.24) | copy-start | bytes 9220
  16.6 8.6 %copy-start.53 = (f32[768]{0:T(1024)}, f32[768]{0:T(1024)S(1)}, u32[]{:S(2)}) copy-start(f32[768]{0:T(1024)S(1)} %get-tuple-element.25) | copy-start | bytes 9220
  16.6 8.6 %copy-start.55 = (f32[768]{0:T(1024)}, f32[768]{0:T(1024)S(1)}, u32[]{:S(2)}) copy-start(f32[768]{0:T(1024)S(1)} %get-tuple-element.26) | copy-start | bytes 9220
  16.7 8.6 %copy-start.57 = (f32[768]{0:T(1024)}, f32[768]{0:T(1024)S(1)}, u32[]{:S(2)}) copy-start(f32[768]{0:T(1024)S(1)} %get-tuple-element.27) | copy-start | bytes 9220
  16.7 8.6 %copy-start.59 = (f32[768]{0:T(1024)}, f32[768]{0:T(1024)S(1)}, u32[]{:S(2)}) copy-start(f32[768]{0:T(1024)S(1)} %get-tuple-element.28) | copy-start | bytes 9220
  16.7 8.6 %copy-start.61 = (f32[768]{0:T(1024)}, f32[768]{0:T(1024)S(1)}, u32[]{:S(2)}) copy-start(f32[768]{0:T(1024)S(1)} %get-tuple-element.29) | copy-start | bytes 9220
  26.4 15.8 %all-to-all-start = ((bf16[4,128,768]{2,1,0:T(8,128)(2,1)}), bf16[4,128,768]{2,1,0:T(8,128)(2,1)}, u32[]{:S(2)}, u32[]{:S(2)}) async-start(bf16[4,128,768]{2,1,0:T(8,128)(2,1)} %broadcast_in_dim.91), calls=%async_computation | async-start | bytes 1572864 | tf_op jit(solution)/shard_map/all_to_all | solution.py:32
  43.1 13.1 %all-to-all-start.3 = ((bf16[4,128,768]{2,1,0:T(8,128)(2,1)}), bf16[4,128,768]{2,1,0:T(8,128)(2,1)S(1)}, u32[]{:S(2)}, u32[]{:S(2)}) async-start(bf16[4,128,768]{2,1,0:T(8,128)(2,1)} %broadcast_in_dim.95), calls=%async_computation.3 | async-start | bytes 1572864 | tf_op jit(solution)/shard_map/all_to_all | solution.py:32
  56.2 33.4 %copy-start.4 = (bf16[4,128,768]{2,1,0:T(8,128)(2,1)}, bf16[4,128,768]{2,1,0:T(8,128)(2,1)S(1)}, u32[]{:S(2)}) copy-start(bf16[4,128,768]{2,1,0:T(8,128)(2,1)S(1)} %all-to-all-done.3) | copy-start | bytes 2359300
  57.4 32.0 %all-to-all-start.2 = ((bf16[4,2,192,384]{3,2,1,0:T(8,128)(2,1)}), bf16[4,2,192,384]{3,2,1,0:T(8,128)(2,1)S(1)}, u32[]{:S(2)}, u32[]{:S(2)}) async-start(bf16[4,2,192,384]{3,2,1,0:T(8,128)(2,1)} %broadcast_in_dim.92), calls=%async_computation.2 | async-start | bytes 2359296 | tf_op jit(solution)/shard_map/all_to_all | solution.py:32
  62.6 27.0 %collective-permute-start.3 = (bf16[512,768]{1,0:T(8,128)(2,1)S(1)}, bf16[512,768]{1,0:T(8,128)(2,1)S(1)}, u32[]{:S(2)}, u32[]{:S(2)}) collective-permute-start(bf16[512,768]{1,0:T(8,128)(2,1)S(1)} %bitcast.99), channel_id=1, source_target_pairs={{0,1},{1,0},{2,3},{3,2},{4,5},{5,4},{6,7},{7,6},{8,9},{9,8},{10,11... | collective-permute-start | bytes 2359304 | tf_op jit(solution)/shard_map/ppermute | solution.py:21
  63.3 28.4 %collective-permute-start = (bf16[512,768]{1,0:T(8,128)(2,1)}, bf16[512,768]{1,0:T(8,128)(2,1)}, u32[]{:S(2)}, u32[]{:S(2)}) collective-permute-start(bf16[512,768]{1,0:T(8,128)(2,1)} %bitcast.3), channel_id=1, source_target_pairs={{0,1},{1,0},{2,3},{3,2},{4,5},{5,4},{6,7},{7,6},{8,9},{9,8},{10,11... | collective-permute-start | bytes 2359304 | tf_op jit(solution)/shard_map/ppermute | solution.py:21
  97.5 8.6 %collective-permute-start.4 = (bf16[2,4,128,768]{3,2,1,0:T(8,128)(2,1)}, bf16[2,4,128,768]{3,2,1,0:T(8,128)(2,1)}, u32[]{:S(2)}, u32[]{:S(2)}) collective-permute-start(bf16[2,4,128,768]{3,2,1,0:T(8,128)(2,1)} %fusion.14), channel_id=1, source_target_pairs={{0,1},{1,0},{2,3},{3,2},{4,5},{5,4},{6,7},{7,6},{8,9},{9,8},{10,11... | collective-permute-start | bytes 4718600 | tf_op jit(solution)/shard_map/ppermute | solution.py:21
  101.8 33.7 %all-to-all-start.5 = ((bf16[4,192,768]{2,1,0:T(8,128)(2,1)}), bf16[4,192,768]{2,1,0:T(8,128)(2,1)}, u32[]{:S(2)}, u32[]{:S(2)}) async-start(bf16[4,192,768]{2,1,0:T(8,128)(2,1)} %bitcast.93), calls=%async_computation.5 | async-start | bytes 2359296 | tf_op jit(solution)/shard_map/all_to_all | solution.py:32
  135.6 22.8 %all-to-all-start.4 = ((bf16[4,2,128,768]{3,2,1,0:T(8,128)(2,1)}), bf16[4,2,128,768]{3,2,1,0:T(8,128)(2,1)S(1)}, u32[]{:S(2)}, u32[]{:S(2)}) async-start(bf16[4,2,128,768]{3,2,1,0:T(8,128)(2,1)} %copy.24), calls=%async_computation.4 | async-start | bytes 3145728 | tf_op jit(solution)/shard_map/all_to_all | solution.py:32
  140.7 8.5 %collective-permute-start.8 = (bf16[192,768]{1,0:T(8,128)(2,1)S(1)}, bf16[192,768]{1,0:T(8,128)(2,1)S(1)}, u32[]{:S(2)}, u32[]{:S(2)}) collective-permute-start(bf16[192,768]{1,0:T(8,128)(2,1)S(1)} %reduce_sum.71), channel_id=1, source_target_pairs={{0,8},{2,10},{4,12},{6,14},{8,0},{10,2},{12,4},{14,6},{16,24},{18,... | collective-permute-start | bytes 884744 | tf_op jit(solution)/shard_map/ppermute | solution.py:21
  160.2 32.4 %all-to-all-start.6 = ((bf16[4,384,768]{2,1,0:T(8,128)(2,1)}), bf16[4,384,768]{2,1,0:T(8,128)(2,1)S(1)}, u32[]{:S(2)}, u32[]{:S(2)}) async-start(bf16[4,384,768]{2,1,0:T(8,128)(2,1)} %broadcast_in_dim.98), calls=%async_computation.6 | async-start | bytes 4718592 | tf_op jit(solution)/shard_map/all_to_all | solution.py:32
  171.1 1.7 collective-permute-start.5
  173.7 16.6 %collective-permute-start.6 = (bf16[3,8,768]{2,1,0:T(8,128)(2,1)S(1)}, bf16[3,8,768]{2,1,0:T(8,128)(2,1)S(1)}, u32[]{:S(2)}, u32[]{:S(2)}) collective-permute-start(bf16[3,8,768]{2,1,0:T(8,128)(2,1)S(1)} %get-tuple-element.74), channel_id=1, source_target_pairs={{0,2},{2,4},{4,6},{6,8},{8,10},{10,12},{12,14},{14,16},{16,18},{18... | collective-permute-start | bytes 110600 | tf_op jit(solution)/shard_map/ppermute | solution.py:28
  177.7 14.9 %collective-permute-start.7 = (bf16[3,8,768]{2,1,0:T(8,128)(2,1)S(1)}, bf16[3,8,768]{2,1,0:T(8,128)(2,1)S(1)}, u32[]{:S(2)}, u32[]{:S(2)}) collective-permute-start(bf16[3,8,768]{2,1,0:T(8,128)(2,1)S(1)} %get-tuple-element.73), channel_id=1, source_target_pairs={{2,0},{4,2},{6,4},{8,6},{10,8},{12,10},{14,12},{16,14},{18,16},{20... | collective-permute-start | bytes 110600 | tf_op jit(solution)/shard_map/ppermute | solution.py:28
  214.6 6.9 %collective-permute-start.9 = (bf16[48,1536]{1,0:T(8,128)(2,1)S(1)}, bf16[48,1536]{1,0:T(8,128)(2,1)S(1)}, u32[]{:S(2)}, u32[]{:S(2)}) collective-permute-start(bf16[48,1536]{1,0:T(8,128)(2,1)S(1)} %slice.1722), channel_id=1, source_target_pairs={{0,16},{2,18},{4,20},{6,22},{8,24},{10,26},{12,28},{14,30},{16,0},... | collective-permute-start | bytes 442376 | tf_op jit(solution)/shard_map/ppermute | solution.py:21
  (64 other events, 202.0 us)

commit v3 on v1

v3 whole, which is shorter than its diff:
```python
import jax
import jax.numpy as jnp
from jax import lax
from jax.experimental import pallas as pl
from jax.experimental.pallas import tpu as pltpu
from jax.sharding import PartitionSpec as P

KERNEL = 7
PATCH = 8
COLS = 8
MARGIN = KERNEL // 2
RIM = MARGIN + 1
PLANE = 4
LANES = 128
CHUNK = 8

INV_ROOT_TWO = 0.7071067811865476
INV_ROOT_TAU = 0.3989422804014327
NS_A = 3.4445
NS_B = -4.775
NS_C = 2.0315
EPS_NORM = 1e-06
F32 = jnp.float32
BF16 = jnp.bfloat16


def swap(value, axis, bit):
    return lax.ppermute(value, axis, [(i, i ^ bit) for i in range(lax.axis_size(axis))])


def neighbours(first, last):
    devices = lax.axis_size("tile")
    up = [(i, i + 1) for i in range(devices - 1)]
    down = [(i + 1, i) for i in range(devices - 1)]
    return lax.ppermute(last, "tile", up), lax.ppermute(first, "tile", down)


def in_order(blocks, index):
    bit = 1
    while bit < len(blocks):
        odd = (index & bit) != 0
        blocks = [jnp.where(odd, blocks[s ^ bit], blocks[s]) for s in range(len(blocks))]
        bit *= 2
    return blocks


def call(kernel, out_shape, scratch, flops, *operands, scalars=1):
    smem = pl.BlockSpec(memory_space=pltpu.SMEM)
    vmem = pl.BlockSpec(memory_space=pltpu.VMEM)
    return pl.pallas_call(
        kernel,
        out_shape=out_shape,
        in_specs=[smem] * scalars + [vmem] * (len(operands) - scalars),
        out_specs=[vmem] * len(out_shape),
        scratch_shapes=scratch,
        compiler_params=pltpu.CompilerParams(vmem_limit_bytes=40 * 2**20),
        cost_estimate=pl.CostEstimate(flops=flops, bytes_accessed=2**20, transcendentals=0),
    )(*operands)


def convolve(framed, kernel_ref, offset, out_ref, flipped):
    share, columns, channels = out_ref.shape
    chunk = min(CHUNK, share)
    lane_steps = channels // LANES
    column = lax.broadcasted_iota(jnp.int32, (chunk + 2 * MARGIN, columns, LANES), 1)

    def step(index, carry):
        lanes = pl.ds(pl.multiple_of((index % lane_steps) * LANES, LANES), LANES)
        first = (index // lane_steps) * chunk
        rows = framed[pl.ds(offset + first, chunk + 2 * MARGIN), :, lanes]
        total = jnp.zeros((chunk, columns, LANES), F32)
        for col_tap in range(KERNEL):
            reach = col_tap - MARGIN
            moved = rows
            if reach:
                moved = pltpu.roll(rows, (-reach) % columns, 1)
                inside = (column + reach >= 0) & (column + reach < columns)
                moved = jnp.where(inside, moved, 0.0)
            for row_tap in range(KERNEL):
                tap = row_tap * KERNEL + col_tap
                tap = KERNEL * KERNEL - 1 - tap if flipped else tap
                weight = kernel_ref[pl.ds(tap, 1), lanes][None]
                total = total + weight * moved[row_tap : row_tap + chunk]
        out_ref[pl.ds(first, chunk), :, lanes] = total
        return carry

    lax.fori_loop(0, lane_steps * (share // chunk), step, 0)


def place_strip(framed, pieces, before_ref, after_ref, live_rows):
    columns, channels = framed.shape[1:]

    def rows_of(ref):
        value = ref[...].astype(F32)
        return value.reshape(value.shape[0] // columns, columns, channels)

    for start, ref in pieces:
        rows = rows_of(ref)
        framed[pl.ds(start + MARGIN, rows.shape[0])] = rows
    framed[pl.ds(framed.shape[0] - MARGIN, MARGIN)] = jnp.zeros((MARGIN, columns, channels), F32)
    framed[pl.ds(0, MARGIN)] = rows_of(before_ref)[RIM - MARGIN :]
    framed[pl.ds(live_rows + MARGIN, MARGIN)] = rows_of(after_ref)[:MARGIN]


def forward_kernel(
    scalars, strip, before, after, taps, gain, normed, centred_out, inverse, framed, mixed
):
    place_strip(framed, [(0, strip)], before, after, scalars[0])
    convolve(framed, taps, scalars[1], mixed, False)
    value = mixed[...].reshape(normed.shape)
    channels = value.shape[1]
    shifted = value - jnp.sum(value, 1, keepdims=True) / channels
    variance = jnp.sum(shifted * shifted, 1, keepdims=True) / channels
    inv_std = lax.rsqrt(variance + 1e-06)
    centred = shifted * inv_std
    centred_out[...] = centred
    inverse[...] = jnp.broadcast_to(inv_std, inverse.shape)
    normed[...] = (centred * gain[...]).astype(BF16)


def middle_kernel(
    scalars, strip, total, one, two, three, centred, inverse, gain, layer_scale, grad_mixed, block_out
):
    tokens, channels = grad_mixed.shape
    start = pl.multiple_of(scalars[1] * COLS, 16)
    row = scalars[1] + lax.broadcasted_iota(jnp.int32, (tokens, 1), 0) // COLS
    keep = jnp.zeros((tokens, 1), F32)
    for patch in range(strip.shape[0] // (COLS * PATCH)):
        keep = jnp.where(row // PATCH == patch, scalars[2 + patch].astype(F32), keep)
    live = row < scalars[0]

    def summed(which):
        value = total[which].astype(F32)
        for ref in (one, two, three):
            value = value + ref[which].astype(F32)
        return value

    inputs = strip[pl.ds(start, tokens), :].astype(F32)
    block = inputs + keep * layer_scale[...] * summed(1)
    block_out[...] = jnp.where(live, block, 0.0).astype(BF16)
    scaled_grad = summed(0) * gain[...]
    first_mean = jnp.sum(scaled_grad, 1, keepdims=True) / channels
    second_mean = jnp.sum(scaled_grad * centred[...], 1, keepdims=True) / channels
    value = inverse[:, :1] * (scaled_grad - first_mean - centred[...] * second_mean)
    grad_mixed[...] = jnp.where(live, value, 0.0).astype(BF16)


def weights_kernel(scalars, *refs):
    *pieces, up, down_t = refs
    rows = pieces[0].shape[1]
    for s, piece in enumerate(pieces):
        start = pl.multiple_of((scalars[0] ^ s) * rows, rows)
        up[pl.ds(start, rows), :] = piece[0]
        down_t[pl.ds(start, rows), :] = piece[1]


def backward_kernel(scalars, cotangent, before, after, taps, *rest):
    *pieces, grad_features, framed, spread = rest
    tokens = grad_features.shape[0]
    share = spread.shape[0]
    own = scalars[1] // share
    placed = [((own ^ s) * share, piece) for s, piece in enumerate(pieces)]
    place_strip(framed, placed, before, after, scalars[0])
    convolve(framed, taps, scalars[1], spread, True)
    start = pl.multiple_of(scalars[1] * COLS, 16)
    value = cotangent[pl.ds(start, tokens), :].astype(F32) + spread[...].reshape(grad_features.shape)
    row = scalars[1] + lax.broadcasted_iota(jnp.int32, (tokens, 1), 0) // COLS
    grad_features[...] = jnp.where(row < scalars[0], value, 0.0).astype(BF16)


def dot(left, right, contract, precision=None):
    return lax.dot_general(
        left, right, (contract, ((), ())), precision=precision, preferred_element_type=F32
    )


def member_bits(entry, turn, group):
    bits = group.bit_length() - 1
    return sum(1 << ((i + turn) % bits) for i in range(bits) if entry >> i & 1)


def hidden_block(member, group):
    return (member & (PLANE - 1)) * (group // PLANE) + (member >> (PLANE.bit_length() - 1))


def ortho_kernel(scalars, *refs):
    *gathered, mine, theirs, whole, gram, first, half = refs
    channels = whole.shape[1]
    if len(gathered) == 1:
        whole[...] = gathered[0][...]
    else:
        group, third, _ = gathered[0].shape
        for turn, ref in enumerate(gathered):
            for e in range(group):
                block = hidden_block(scalars[2] ^ member_bits(e, turn, group), group)
                start = pl.multiple_of((block * 3 + turn) * third, third)
                whole[pl.ds(start, third), :] = ref[e]

    plain = ((1,), (0,))
    steps = [pl.ds(i, 256) for i in range(0, channels, 256)]
    value = whole[...]
    squares = jnp.zeros((1, 1), F32)
    for rows in steps:
        product = dot(value[:, rows.start : rows.start + 256], value, ((0,), (0,)))
        row = rows.start + lax.broadcasted_iota(jnp.int32, product.shape, 0)
        column = lax.broadcasted_iota(jnp.int32, product.shape, 1)
        on_diagonal = jnp.where(row == column, product, 0.0)
        squares = squares + jnp.sum(jnp.sum(on_diagonal, 1, keepdims=True), 0, keepdims=True)
        gram[rows, :] = product
    scale = lax.rsqrt(squares + EPS_NORM)
    gram[...] = gram[...] * (scale * scale)

    low = gram[...].astype(BF16)
    for rows in steps:
        first[rows, :] = NS_B * gram[rows, :] + NS_C * dot(low[rows.start : rows.start + 256], low, plain)
    first_low = first[...].astype(BF16)
    for rows in steps:
        product = dot(low[rows.start : rows.start + 256], first_low, plain)
        half[rows, :] = NS_A * gram[rows, :] + product
    half_low = half[...].astype(BF16)
    for rows in steps:
        product = dot(half_low[rows.start : rows.start + 256], first_low, plain)
        gram[rows, :] = NS_A * half[rows, :] + product

    height = mine.shape[0]
    picked = -(-2 * height // 16) * 16
    row = lax.broadcasted_iota(jnp.int32, (picked, channels), 0)
    column = lax.broadcasted_iota(jnp.int32, (picked, channels), 1)
    wanted = jnp.where(row < height, scalars[0] + row, scalars[1] + row - height)
    chosen = (column == wanted) & (row < 2 * height)
    pick = jnp.where(chosen, 1.0, 0.0).astype(BF16)

    def halves(matrix):
        top = matrix.astype(BF16)
        return top, (matrix - top.astype(F32)).astype(BF16)

    def rows_of(matrix):
        top, rest = halves(matrix)
        return dot(pick, top, plain) + dot(pick, rest, plain)

    second_gram = gram[...]
    gram_rows = rows_of(second_gram)
    second = NS_B * gram_rows
    second = second + NS_C * dot(gram_rows.astype(BF16), second_gram.astype(BF16), plain)
    both = (
        jnp.where(chosen, NS_A * NS_A, 0.0)
        + NS_A * (rows_of(first[...]) + second)
        + dot(second.astype(BF16), first_low, plain)
    ) * scale
    top, rest = halves(both)
    across = ((1,), (1,))
    for start in range(0, value.shape[0], 256):
        step = min(256, value.shape[0] - start)
        piece = value[start : start + step]
        out = dot(top, piece, across) + dot(rest, piece, across)
        mine[:, start : start + step] = out[:height]
        theirs[:, start : start + step] = out[height : 2 * height].astype(BF16)


def shards(
    features,
    cotangent,
    depth_kernel,
    ln_gain,
    weight_up,
    bias_up,
    weight_down,
    layer_scale,
    tissue,
    lengths,
):
    tile_rows, columns, channels = features.shape
    tiles = lax.axis_size("tile")
    owners = lax.axis_size("own")
    lines = tiles // PLANE
    half_lines = lines // 2
    tile = lax.axis_index("tile")
    own = lax.axis_index("own")
    place, line = tile & (PLANE - 1), tile >> (PLANE.bit_length() - 1)
    share = tile_rows // owners
    offset = own * share
    tokens = share * columns
    live_rows = PATCH * lengths[tile]
    row = offset + jnp.arange(share)
    keep = jnp.repeat(tissue[:, 0], PATCH, axis=0)
    keep = lax.dynamic_slice_in_dim(keep, offset, share, 0) * (row < live_rows)
    mine_cot = lax.dynamic_slice_in_dim(cotangent, offset, share, 0).astype(F32)
    grad_branch = (keep.astype(F32)[:, None, None] * layer_scale * mine_cot).astype(BF16)
    scalars = jnp.concatenate([jnp.stack([live_rows, offset]), tissue[:, 0]])
    scalars = scalars.astype(jnp.int32)
    strip = features.reshape(tile_rows * columns, channels)
    taps = depth_kernel.reshape(KERNEL * KERNEL, channels)
    gain, scale = ln_gain[None], layer_scale[None]
    frame = pltpu.VMEM((tile_rows + 2 * MARGIN, columns, channels), F32)
    wide = pltpu.VMEM((share, columns, channels), F32)
    rim = RIM * columns

    units = weight_up.shape[1] // PLANE
    both_weights = jnp.stack([weight_up, weight_down.T])
    pieces = []
    for s in range(PLANE):
        piece = lax.dynamic_slice_in_dim(both_weights, (place ^ s) * units, units, 2)
        pieces.append(swap(piece, "tile", s) if s else piece)
    piece = jnp.concatenate(in_order(pieces, place), 1)

    tail = lax.dynamic_slice_in_dim(strip, (live_rows - RIM) * columns, rim, 0)
    before, after = neighbours(strip[:rim], tail)
    piece, before, after = lax.optimization_barrier((piece, before, after))
    pieces = [swap(piece, "tile", PLANE * s) if s else piece for s in range(lines)]
    up, down_t = call(
        weights_kernel,
        [jax.ShapeDtypeStruct((channels, units), BF16)] * 2,
        [],
        10 * 10**9,
        line[None], *pieces,
    )
    bias = lax.dynamic_slice_in_dim(bias_up, place * units, units, 0)

    def gather(mine):
        mine = jnp.concatenate([mine] + [swap(mine, "tile", s) for s in range(1, PLANE)], 0)
        return jnp.concatenate([mine] + [swap(mine, "own", s) for s in range(1, owners)], 0)

    grad_branch = gather(grad_branch.reshape(tokens, channels))
    normed, centred, inverse = call(
        forward_kernel,
        [
            jax.ShapeDtypeStruct((tokens, channels), BF16),
            jax.ShapeDtypeStruct((tokens, channels), F32),
            jax.ShapeDtypeStruct((tokens, LANES), F32),
        ],
        [frame, wide],
        10**6,
        scalars, strip, before, after, taps, gain,
    )
    normed = gather(normed)

    plain, across, over_tokens = ((1,), (0,)), ((1,), (1,)), ((0,), (0,))
    hidden = dot(normed, up, plain) + bias
    cdf = 0.5 * (1.0 + lax.erf(hidden * INV_ROOT_TWO))
    act = (hidden * cdf).astype(BF16)
    slope = cdf + hidden * jnp.exp(-0.5 * hidden * hidden) * INV_ROOT_TAU
    grad_hidden = (dot(grad_branch, down_t, plain) * slope).astype(BF16)

    parts = jnp.concatenate(
        [dot(grad_hidden, normed, over_tokens), dot(act, grad_branch, over_tokens)], 0
    ).astype(BF16)
    parts, grad_hidden, act = lax.optimization_barrier((parts, grad_hidden, act))
    kept = 2 * units // lines
    grad_t = lax.dynamic_slice_in_dim(parts, line * kept, kept, 0).astype(F32)
    arrived = []
    for s in range(1, lines):
        part = lax.dynamic_slice_in_dim(parts, (line ^ s) * kept, kept, 0)
        arrived.append(swap(part, "tile", PLANE * s))

    partial = jnp.stack([dot(grad_hidden, up, across), dot(act, down_t, across)])
    partial = partial.reshape(2, owners, PLANE, tokens, channels)
    total = partial[:, 0]
    for s in range(1, owners):
        total = total + swap(partial[:, s].astype(BF16), "own", s).astype(F32)
    total = total.astype(BF16)
    moved = [swap(total[:, s], "tile", s) for s in range(1, PLANE)]
    grad_mixed, block_out = call(
        middle_kernel,
        [jax.ShapeDtypeStruct((tokens, channels), BF16)] * 2,
        [],
        10**6,
        scalars, strip, total[:, 0], *moved, centred, inverse, gain, scale,
    )

    grad_t = (grad_t + sum(part.astype(F32) for part in arrived)).astype(BF16)
    group = PLANE * half_lines
    bits = [1 << i for i in range(group.bit_length() - 1)]
    third = kept // 3
    thirds = []
    for turn in range(3):
        held = grad_t[turn * third : (turn + 1) * third][None]
        order = bits[turn:] + bits[:turn]
        for bit in order:
            held = jnp.concatenate([held, swap(held, "tile", bit)], 0)
        thirds.append(held)

    halves = [grad_mixed] + [swap(grad_mixed, "own", s) for s in range(1, owners)]
    stacked = jnp.stack(halves)
    head = lax.dynamic_slice_in_dim(stacked, own, 1, 0)[0, :rim]
    last = live_rows - RIM
    tail = lax.dynamic_slice(
        stacked, ((last >> (share.bit_length() - 1)) ^ own, (last & (share - 1)) * columns, 0), (1, rim, channels)
    )[0]
    before, after = neighbours(head, tail)
    (grad_features,) = call(
        backward_kernel,
        [jax.ShapeDtypeStruct((tokens, channels), BF16)],
        [frame, wide],
        10**6,
        scalars, cotangent.reshape(strip.shape), before, after, taps, *halves,
    )

    height = channels // tiles
    other = tile ^ (PLANE * half_lines)
    square = pltpu.VMEM((channels, channels), F32)
    thirds, grad_features = lax.optimization_barrier((thirds, grad_features))
    if third % 16:
        entries = [(e, turn) for turn in range(3) for e in range(group)]
        slots = [
            hidden_block((tile & (group - 1)) ^ member_bits(e, turn, group), group) * 3 + turn
            for e, turn in entries
        ]
        ordered = jnp.zeros((3 * group, third, channels), BF16)
        ordered = ordered.at[jnp.stack(slots)].set(jnp.concatenate(thirds, 0))
        thirds = [ordered.reshape(-1, channels)]
    mine, theirs = call(
        ortho_kernel,
        [
            jax.ShapeDtypeStruct((height, weight_up.shape[1]), F32),
            jax.ShapeDtypeStruct((height, weight_up.shape[1]), BF16),
        ],
        [pltpu.VMEM((weight_up.shape[1], channels), BF16), square, square, square],
        10 * 10**9,
        jnp.stack([tile * height, other * height, tile & (group - 1)]), *thirds,
    )
    theirs = swap(theirs, "tile", PLANE * half_lines)
    theirs = theirs.astype(F32)
    expands = line < half_lines
    muon_up = jnp.where(expands, mine, theirs)
    muon_down = jnp.where(expands, theirs, mine).T
    shape = (share, columns, channels)
    return (block_out.reshape(shape), grad_features.reshape(shape), muon_up, muon_down)


def solution(mesh):
    in_specs = (
        P("tile", None, None),
        P("tile", None, None),
        P(),
        P(),
        P("tile", "own"),
        P("own"),
        P("own", "tile"),
        P(),
        P("tile", None),
        P(),
    )
    out_specs = (
        P(("tile", "own"), None, None),
        P(("tile", "own"), None, None),
        P("tile", "own"),
        P("own", "tile"),
    )
    return jax.shard_map(shards, mesh=mesh, in_specs=in_specs, out_specs=out_specs, check_vma=False)
```

time: 194 us -> 172 us (0.89)
  Pallas kernels: 0 us -> 16.9 us
  matrix products: 22.1 us -> 6.02 us
  waiting for transfers between devices: 79.8 us -> 67 us
  other arithmetic: 24.9 us -> 14.8 us
  starting transfers between devices: 54.5 us -> 57.9 us
  between operations: 3.9 us -> 1.81 us
    ppermute x31 -> x32, waiting for transfers between devices: 76 us -> 58.8 us  [swap(): lax.ppermute(value, axis, [(i, i ^ bit) for i in range(lax.axis_size(axis...]
    pallas_call x0 -> x5, Pallas kernels: none -> 16.9 us  [call(): pl.pallas_call(kernel, out_shape=out_shape, in_specs=[smem] * scalars + [...]
    dot_general x14 -> x6, matrix products: 22.1 us -> 6.02 us  [dot(): lax.dot_general(left, right, (contract, ((), ())), precision=precision, p...]
    reduce_sum x4 -> x0, other arithmetic: 6.15 us -> none  [the longest x1 4.88 us: layer_norm(): average = jnp.mean(mixed, axis=-1, keepdims=True)]
    ppermute x4, waiting for transfers between devices: 3.88 us -> 8.19 us  [neighbours(): return (lax.ppermute(last, 'tile', up), lax.ppermute(first, 'tile', down))]
    ppermute x31 -> x32, starting transfers between devices: 44.8 us -> 49 us  [swap(): lax.ppermute(value, axis, [(i, i ^ bit) for i in range(lax.axis_size(axis...]
    concatenate x5 -> x10, other arithmetic: 2.4 us -> 5.76 us  [the longest x9 5.69 us: shards(): held = jnp.concatenate([held, swap(held, 'tile', bit)], 0)]
    select_n x7 -> x2, other arithmetic: 2.64 us -> 0.1 us  [in_order(): jnp.where(odd, blocks[s ^ bit], blocks[s])]
  transfers between devices with their start and end apart: 35 -> 36, of which waited for: 13 -> 15; matrix products, arithmetic and copies ran while one was open for 23% -> 8% of each run, Pallas kernels for 0% -> 3%
where the time goes in v3:
time: 172 us; the launch traced here: 171 us
  waiting for transfers between devices  67 us (39%)
  starting transfers between devices  57.9 us (34%)
  Pallas kernels  16.9 us (10%)
  other arithmetic  14.8 us (9%)
  local copies, waits for them, and re-layouts  6.72 us (4%)
  matrix products  6.02 us (4%)
  between operations  1.81 us (1%)
    ppermute x32, waiting for transfers between devices, swap(): lax.ppermute(value, axis, [(i, i ^ bit) for i in range(lax.axis_size(axis...  58.8 us
    ppermute x32, starting transfers between devices, swap(): lax.ppermute(value, axis, [(i, i ^ bit) for i in range(lax.axis_size(axis...  49 us
    pallas_call x5, Pallas kernels, call(): pl.pallas_call(kernel, out_shape=out_shape, in_specs=[smem] * scalars + [...  16.9 us
    ppermute x4, starting transfers between devices, neighbours(): return (lax.ppermute(last, 'tile', up), lax.ppermute(first, 'tile', down))  8.86 us
    ppermute x4, waiting for transfers between devices, neighbours(): return (lax.ppermute(last, 'tile', up), lax.ppermute(first, 'tile', down))  8.19 us
    dot_general x6, matrix products, dot(): lax.dot_general(left, right, (contract, ((), ())), precision=precision, p...  6.02 us
    concatenate x9, other arithmetic, shards(): held = jnp.concatenate([held, swap(held, 'tile', bit)], 0)  5.69 us
  transfers between devices with their start and end apart: 36, of which 15 were waited for; matrix products, arithmetic and copies ran while one was open for 8% of the time, Pallas kernels for 3%

profile of v3, /device:TPU:0, one launch (start us, length us, event | category | flops | bytes accessed | tf_op | source)
XLA Modules:
  0.0 171.2 jit_solution(8027646375055589640)
XLA Ops:
  1.6 1.2 dynamic_slice.45
  5.3 3.0 %collective-permute-start = (bf16[128,768]{1,0:T(8,128)(2,1)S(1)}, bf16[128,768]{1,0:T(8,128)(2,1)S(1)}, u32[]{:S(2)}, u32[]{:S(2)}) collective-permute-start(bf16[128,768]{1,0:T(8,128)(2,1)S(1)} %get-tuple-element.43), channel_id=1, source_target_pairs={{0,2},{2,0},{4,6},{6,4},{8,10},{10,8},{12,14},{14,12},{16,18},{18,... | collective-permute-start | bytes 589832 | tf_op jit(solution)/shard_map/ppermute | solution.py:28
  8.3 1.5 collective-permute-start.1
  10.8 2.0 %collective-permute-start.5 = (bf16[2,48,384]{2,1,0:T(8,128)(2,1)S(1)}, bf16[2,48,384]{2,1,0:T(8,128)(2,1)S(1)}, u32[]{:S(2)}, u32[]{:S(2)}) collective-permute-start(bf16[2,48,384]{2,1,0:T(8,128)(2,1)S(1)} %get-tuple-element.65), channel_id=1, source_target_pairs={{0,4},{2,6},{4,0},{6,2},{8,12},{10,14},{12,8},{14,10},{16,20},{18,... | collective-permute-start | bytes 221192 | tf_op jit(solution)/shard_map/ppermute | solution.py:28
  12.7 1.5 collective-permute-start.6
  16.9 1.4 collective-permute-start.2
  18.3 2.5 %collective-permute-start.7 = (bf16[32,768]{1,0:T(8,128)(2,1)S(1)}, bf16[32,768]{1,0:T(8,128)(2,1)S(1)}, u32[]{:S(2)}, u32[]{:S(2)}) collective-permute-start(bf16[32,768]{1,0:T(8,128)(2,1)S(1)} %constant_dynamic-slice_fusion.3), channel_id=1, source_target_pairs={{0,2},{2,4},{4,6},{6,8},{8,10},{10,12},{12,14},{14,16},{16,18},{18... | collective-permute-start | bytes 147464 | tf_op jit(solution)/shard_map/ppermute | solution.py:35
  20.8 1.3 collective-permute-start.8
  22.5 4.5 %collective-permute-done.8.after = bf16[32,768]{1,0:T(8,128)(2,1)S(1)} collective-permute-done((bf16[32,768]{1,0:T(8,128)(2,1)S(1)}, bf16[32,768]{1,0:T(8,128)(2,1)S(1)}, u32[]{:S(2)}, u32[]{:S(2)}) %collective-permute-start.8) | collective-permute-done | bytes 49184 | tf_op jit(solution)/shard_map/ppermute | solution.py:35
  27.1 2.8 %shard_map.130 = (bf16[128,768]{1,0:T(8,128)(2,1)S(1)}, f32[128,768]{1,0:T(8,128)S(1)}, f32[128,128]{1,0:T(8,128)S(1)}) custom-call(s32[6]{0:T(128)S(1)} %pad_add_fusion.scalars, bf16[256,768]{1,0:T(8,128)(2,1)S(1)} %bitcast.65, bf16[32,768]{1,0:T(8,128)(2,1)S(1)} %collective-permute-done.7.before, bf16[32,768]{1,0:T(8,128)(2,1)S(1)} %collective-permute-done.8.after, ...), custom_call_target="tpu_custom_call" | custom-call | flops 1000000 | bytes 1048576 | tf_op jit(solution)/shard_map/pallas_call | solution.py:50
  29.9 3.0 %collective-permute-start.12 = (bf16[128,768]{1,0:T(8,128)(2,1)S(1)}, bf16[128,768]{1,0:T(8,128)(2,1)S(1)}, u32[]{:S(2)}, u32[]{:S(2)}) collective-permute-start(bf16[128,768]{1,0:T(8,128)(2,1)S(1)} %get-tuple-element.27), channel_id=1, source_target_pairs={{0,2},{2,0},{4,6},{6,4},{8,10},{10,8},{12,14},{14,12},{16,18},{18,... | collective-permute-start | bytes 589832 | tf_op jit(solution)/shard_map/ppermute | solution.py:28
  32.9 2.5 %collective-permute-start.13 = (bf16[128,768]{1,0:T(8,128)(2,1)S(1)}, bf16[128,768]{1,0:T(8,128)(2,1)S(1)}, u32[]{:S(2)}, u32[]{:S(2)}) collective-permute-start(bf16[128,768]{1,0:T(8,128)(2,1)S(1)} %get-tuple-element.27), channel_id=1, source_target_pairs={{0,4},{2,6},{4,0},{6,2},{8,12},{10,14},{12,8},{14,10},{16,20},{18,... | collective-permute-start | bytes 589832 | tf_op jit(solution)/shard_map/ppermute | solution.py:28
  35.5 2.7 %collective-permute-start.10 = (bf16[2,192,384]{2,1,0:T(8,128)(2,1)S(1)}, bf16[2,192,384]{2,1,0:T(8,128)(2,1)S(1)}, u32[]{:S(2)}, u32[]{:S(2)}) collective-permute-start(bf16[2,192,384]{2,1,0:T(8,128)(2,1)S(1)} %pad_maximum_fusion.10.refs_0_), channel_id=1, source_target_pairs={{0,16},{2,18},{4,20},{6,22},{8,24},{10,26},{12,28},{14,30},{16,0},... | collective-permute-start | bytes 884744 | tf_op jit(solution)/shard_map/ppermute | solution.py:28
  38.2 1.4 collective-permute-start.11
  40.7 1.4 collective-permute-done.14
  42.3 12.6 %collective-permute-done.10.refs_2_ = bf16[2,192,384]{2,1,0:T(8,128)(2,1)S(1)} collective-permute-done((bf16[2,192,384]{2,1,0:T(8,128)(2,1)S(1)}, bf16[2,192,384]{2,1,0:T(8,128)(2,1)S(1)}, u32[]{:S(2)}, u32[]{:S(2)}) %collective-permute-start.10) | collective-permute-done | bytes 294944 | tf_op jit(solution)/shard_map/ppermute | solution.py:28
  55.5 1.1 multiply_convert_fusion
  56.6 1.3 fusion.10
  62.3 1.6 fusion.11
  64.0 5.4 %collective-permute-start.20 = (bf16[192,768]{1,0:T(8,128)(2,1)S(1)}, bf16[192,768]{1,0:T(8,128)(2,1)S(1)}, u32[]{:S(2)}, u32[]{:S(2)}) collective-permute-start(bf16[192,768]{1,0:T(8,128)(2,1)S(1)} %get-tuple-element.50), channel_id=1, source_target_pairs={{0,8},{2,10},{4,12},{6,14},{8,0},{10,2},{12,4},{14,6},{16,24},{18,... | collective-permute-start | bytes 884744 | tf_op jit(solution)/shard_map/ppermute | solution.py:28
  69.4 1.8 %collective-permute-start.21 = (bf16[192,768]{1,0:T(8,128)(2,1)S(1)}, bf16[192,768]{1,0:T(8,128)(2,1)}, u32[]{:S(2)}, u32[]{:S(2)}) collective-permute-start(bf16[192,768]{1,0:T(8,128)(2,1)S(1)} %get-tuple-element.52), channel_id=1, source_target_pairs={{0,16},{2,18},{4,20},{6,22},{8,24},{10,26},{12,28},{14,30},{16,0},... | collective-permute-start | bytes 884744 | tf_op jit(solution)/shard_map/ppermute | solution.py:28
  71.2 1.4 collective-permute-start.22
  72.6 10.7 %collective-permute-done.20 = bf16[192,768]{1,0:T(8,128)(2,1)S(1)} collective-permute-done((bf16[192,768]{1,0:T(8,128)(2,1)S(1)}, bf16[192,768]{1,0:T(8,128)(2,1)S(1)}, u32[]{:S(2)}, u32[]{:S(2)}) %collective-permute-start.20) | collective-permute-done | bytes 294944 | tf_op jit(solution)/shard_map/ppermute | solution.py:28
  83.3 9.6 %collective-permute-done.21 = bf16[192,768]{1,0:T(8,128)(2,1)} collective-permute-done((bf16[192,768]{1,0:T(8,128)(2,1)S(1)}, bf16[192,768]{1,0:T(8,128)(2,1)}, u32[]{:S(2)}, u32[]{:S(2)}) %collective-permute-start.21) | collective-permute-done | bytes 294944 | tf_op jit(solution)/shard_map/ppermute | solution.py:28
  92.9 1.2 add_convert_fusion
  94.1 6.2 %collective-permute-start.29 = (bf16[1,64,768]{2,1,0:T(8,128)(2,1)S(1)}, bf16[1,64,768]{2,1,0:T(8,128)(2,1)S(1)}, u32[]{:S(2)}, u32[]{:S(2)}) collective-permute-start(bf16[1,64,768]{2,1,0:T(8,128)(2,1)S(1)} %get-tuple-element.57), channel_id=1, source_target_pairs={{0,8},{2,10},{4,12},{6,14},{8,0},{10,2},{12,4},{14,6},{16,24},{18,... | collective-permute-start | bytes 294920 | tf_op jit(solution)/shard_map/ppermute | solution.py:28
  100.4 1.5 collective-permute-start.26
  101.9 1.7 collective-permute-start.23
  105.0 1.7 collective-permute-start.27
  108.5 2.3 %fusion.3 = bf16[2,4,128,768]{3,2,0,1:T(8,128)(2,1)S(1)} fusion(f32[1,2,4,128,768]{4,3,0,2,1:T(8,128)} %bitcast.73, f32[1,2,4,128,768]{4,3,0,2,1:T(8,128)S(1)} %bitcast.71, bf16[2,4,128,768]{3,2,0,1:T(8,128)(2,1)} %collective-permute-done.16), kind=kLoop, calls=%fused_computation.5 | loop fusion | flops 3145728 | bytes 9437184 | tf_op jit(solution)/shard_map/convert_element_type | solution.py:360
  111.8 1.2 collective-permute-start.17
  113.0 1.7 collective-permute-start.18
  116.1 1.2 collective-permute-start.31
  118.1 1.8 %collective-permute-start.28 = (bf16[4,64,768]{2,1,0:T(8,128)(2,1)}, bf16[4,64,768]{2,1,0:T(8,128)(2,1)}, u32[]{:S(2)}, u32[]{:S(2)}) collective-permute-start(bf16[4,64,768]{2,1,0:T(8,128)(2,1)} %pad_maximum_fusion.8), channel_id=1, source_target_pairs={{0,2},{2,0},{4,6},{6,4},{8,10},{10,8},{12,14},{14,12},{16,18},{18,... | collective-permute-start | bytes 1179656 | tf_op jit(solution)/shard_map/ppermute | solution.py:28
  120.6 3.5 %collective-permute-done.17.one = bf16[2,128,768]{2,1,0:T(8,128)(2,1)S(1)} collective-permute-done((bf16[2,128,768]{2,1,0:T(8,128)(2,1)}, bf16[2,128,768]{2,1,0:T(8,128)(2,1)S(1)}, u32[]{:S(2)}, u32[]{:S(2)}) %collective-permute-start.17) | collective-permute-done | bytes 393248 | tf_op jit(solution)/shard_map/ppermute | solution.py:28
  124.4 8.9 %collective-permute-done.18.two = bf16[2,128,768]{2,1,0:T(8,128)(2,1)S(1)} collective-permute-done((bf16[2,128,768]{2,1,0:T(8,128)(2,1)}, bf16[2,128,768]{2,1,0:T(8,128)(2,1)S(1)}, u32[]{:S(2)}, u32[]{:S(2)}) %collective-permute-start.18) | collective-permute-done | bytes 393248 | tf_op jit(solution)/shard_map/ppermute | solution.py:28
  133.4 1.7 %shard_map.131 = (bf16[128,768]{1,0:T(8,128)(2,1)S(1)}, bf16[128,768]{1,0:T(8,128)(2,1)}) custom-call(s32[6]{0:T(128)S(1)} %pad_add_fusion.scalars, bf16[256,768]{1,0:T(8,128)(2,1)S(1)} %bitcast.66, bf16[2,128,768]{2,1,0:T(8,128)(2,1)S(1)} %get-tuple-element.49.total, bf16[2,128,768]{2,1,0:T(8,128)(2,1)S(1)} %collective-permute-done.17.one, ...), custom_call_target="tpu_custom_call" | custom-call | flops 1000000 | bytes 1048576 | tf_op jit(solution)/shard_map/pallas_call | solution.py:50
  135.1 3.6 %collective-permute-done.31 = bf16[4,64,768]{2,1,0:T(8,128)(2,1)} collective-permute-done((bf16[4,64,768]{2,1,0:T(8,128)(2,1)}, bf16[4,64,768]{2,1,0:T(8,128)(2,1)}, u32[]{:S(2)}, u32[]{:S(2)}) %collective-permute-start.31) | collective-permute-done | bytes 393248 | tf_op jit(solution)/shard_map/ppermute | solution.py:28
  138.7 1.1 pad_maximum_fusion.6.refs_2_
  139.8 1.1 pad_maximum_fusion.5.refs_1_
  141.0 3.6 %collective-permute-start.33 = (bf16[32,768]{1,0:T(8,128)(2,1)S(1)}, bf16[32,768]{1,0:T(8,128)(2,1)S(1)}, u32[]{:S(2)}, u32[]{:S(2)}) collective-permute-start(bf16[32,768]{1,0:T(8,128)(2,1)S(1)} %get-tuple-element.56), channel_id=1, source_target_pairs={{0,2},{2,4},{4,6},{6,8},{8,10},{10,12},{12,14},{14,16},{16,18},{18... | collective-permute-start | bytes 147464 | tf_op jit(solution)/shard_map/ppermute | solution.py:35
  144.6 1.5 collective-permute-start.34
  146.1 1.1 pad_maximum_fusion.4.refs_0_
  147.2 3.4 %collective-permute-done.34.after = bf16[32,768]{1,0:T(8,128)(2,1)S(1)} collective-permute-done((bf16[32,768]{1,0:T(8,128)(2,1)S(1)}, bf16[32,768]{1,0:T(8,128)(2,1)S(1)}, u32[]{:S(2)}, u32[]{:S(2)}) %collective-permute-start.34) | collective-permute-done | bytes 49184 | tf_op jit(solution)/shard_map/ppermute | solution.py:35
  150.6 3.3 %shard_map.132 = bf16[128,768]{1,0:T(8,128)(2,1)} custom-call(s32[6]{0:T(128)S(1)} %pad_add_fusion.scalars, bf16[256,768]{1,0:T(8,128)(2,1)S(1)} %bitcast.67, bf16[32,768]{1,0:T(8,128)(2,1)S(1)} %collective-permute-done.33.before, bf16[32,768]{1,0:T(8,128)(2,1)S(1)} %collective-permute-done.34.after, f32[49,768]{1,0:T(8,128)S(1)} %reshape.71.taps, ...), custom_call_target="tpu_custom_call" | custom-call | flops 1000000 | bytes 1048576 | tf_op jit(solution)/shard_map/pallas_call | solution.py:50
  153.9 9.0 %shard_map.133 = (f32[48,1536]{1,0:T(8,128)S(1)}, bf16[48,1536]{1,0:T(8,128)(2,1)S(1)}) custom-call(s32[3]{0:T(128)S(1)} %pad_add_fusion.1.scalars, bf16[8,64,768]{2,1,0:T(8,128)(2,1)S(1)} %pad_maximum_fusion.4.refs_0_, bf16[8,64,768]{2,1,0:T(8,128)(2,1)S(1)} %pad_maximum_fusion.5.refs_1_, bf16[8,64,768]{2,1,0:T(8,128)(2,1)S(1)} %pad_maximum_fusion.6.refs_2_), custom_call_target="tpu_custom_call" | custom-call | flops 10000000000 | bytes 1048576 | tf_op jit(solution)/shard_map/pallas_call | solution.py:50
  162.9 1.4 collective-permute-start.35
  164.3 6.0 %collective-permute-done.35 = bf16[48,1536]{1,0:T(8,128)(2,1)S(1)} collective-permute-done((bf16[48,1536]{1,0:T(8,128)(2,1)S(1)}, bf16[48,1536]{1,0:T(8,128)(2,1)S(1)}, u32[]{:S(2)}, u32[]{:S(2)}) %collective-permute-start.35) | collective-permute-done | bytes 147488 | tf_op jit(solution)/shard_map/ppermute | solution.py:28
  (110 shorter events, 21.6 us)
Async XLA Ops:
  0.6 16.2 %copy-start.13 = (s32[4,1]{0,1:T(1,128)S(1)}, s32[4,1]{0,1:T(1,128)}, u32[]{:S(2)}) copy-start(s32[4,1]{0,1:T(1,128)} %param.18) | copy-start | bytes 52
  0.6 21.5 %copy-start.9 = (bf16[48,1536]{1,0:T(8,128)(2,1)S(1)}, bf16[48,1536]{1,0:T(8,128)(2,1)}, u32[]{:S(2)}) copy-start(bf16[48,1536]{1,0:T(8,128)(2,1)} %param.14) | copy-start | bytes 442372
  0.7 21.5 %copy-start.10 = (bf16[1536,48]{0,1:T(8,128)(2,1)S(1)}, bf16[1536,48]{0,1:T(8,128)(2,1)}, u32[]{:S(2)}) copy-start(bf16[1536,48]{0,1:T(8,128)(2,1)} %param.16) | copy-start | bytes 442372
  0.7 15.3 %copy-start = (bf16[32,8,768]{2,1,0:T(8,128)(2,1)S(1)}, bf16[32,8,768]{2,1,0:T(8,128)(2,1)}, u32[]{:S(2)}) copy-start(bf16[32,8,768]{2,1,0:T(8,128)(2,1)} %param.10) | copy-start | bytes 1179652
  0.7 15.3 %copy-start.12 = (f32[768]{0:T(1024)S(1)}, f32[768]{0:T(1024)}, u32[]{:S(2)}) copy-start(f32[768]{0:T(1024)} %param.13) | copy-start | bytes 9220
  5.3 30.1 %collective-permute-start = (bf16[128,768]{1,0:T(8,128)(2,1)S(1)}, bf16[128,768]{1,0:T(8,128)(2,1)S(1)}, u32[]{:S(2)}, u32[]{:S(2)}) collective-permute-start(bf16[128,768]{1,0:T(8,128)(2,1)S(1)} %get-tuple-element.43), channel_id=1, source_target_pairs={{0,2},{2,0},{4,6},{6,4},{8,10},{10,8},{12,14},{14,12},{16,18},{18,... | collective-permute-start | bytes 589832 | tf_op jit(solution)/shard_map/ppermute | solution.py:28
  8.3 27.2 %collective-permute-start.1 = (bf16[128,768]{1,0:T(8,128)(2,1)S(1)}, bf16[128,768]{1,0:T(8,128)(2,1)S(1)}, u32[]{:S(2)}, u32[]{:S(2)}) collective-permute-start(bf16[128,768]{1,0:T(8,128)(2,1)S(1)} %get-tuple-element.43), channel_id=1, source_target_pairs={{0,4},{2,6},{4,0},{6,2},{8,12},{10,14},{12,8},{14,10},{16,20},{18,... | collective-permute-start | bytes 589832 | tf_op jit(solution)/shard_map/ppermute | solution.py:28
  10.7 6.2 %collective-permute-start.4 = (bf16[2,48,384]{2,1,0:T(8,128)(2,1)S(1)}, bf16[2,48,384]{2,1,0:T(8,128)(2,1)S(1)}, u32[]{:S(2)}, u32[]{:S(2)}) collective-permute-start(bf16[2,48,384]{2,1,0:T(8,128)(2,1)S(1)} %get-tuple-element.64), channel_id=1, source_target_pairs={{0,6},{2,4},{4,2},{6,0},{8,14},{10,12},{12,10},{14,8},{16,22},{18,... | collective-permute-start | bytes 221192 | tf_op jit(solution)/shard_map/ppermute | solution.py:28
  10.8 7.5 %collective-permute-start.5 = (bf16[2,48,384]{2,1,0:T(8,128)(2,1)S(1)}, bf16[2,48,384]{2,1,0:T(8,128)(2,1)S(1)}, u32[]{:S(2)}, u32[]{:S(2)}) collective-permute-start(bf16[2,48,384]{2,1,0:T(8,128)(2,1)S(1)} %get-tuple-element.65), channel_id=1, source_target_pairs={{0,4},{2,6},{4,0},{6,2},{8,12},{10,14},{12,8},{14,10},{16,20},{18,... | collective-permute-start | bytes 221192 | tf_op jit(solution)/shard_map/ppermute | solution.py:28
  12.7 8.0 %collective-permute-start.6 = (bf16[2,48,384]{2,1,0:T(8,128)(2,1)S(1)}, bf16[2,48,384]{2,1,0:T(8,128)(2,1)S(1)}, u32[]{:S(2)}, u32[]{:S(2)}) collective-permute-start(bf16[2,48,384]{2,1,0:T(8,128)(2,1)S(1)} %get-tuple-element.63), channel_id=1, source_target_pairs={{0,2},{2,0},{4,6},{6,4},{8,10},{10,8},{12,14},{14,12},{16,18},{18,... | collective-permute-start | bytes 221192 | tf_op jit(solution)/shard_map/ppermute | solution.py:28
  16.9 21.3 %collective-permute-start.2 = (bf16[128,768]{1,0:T(8,128)(2,1)S(1)}, bf16[128,768]{1,0:T(8,128)(2,1)S(1)}, u32[]{:S(2)}, u32[]{:S(2)}) collective-permute-start(bf16[128,768]{1,0:T(8,128)(2,1)S(1)} %get-tuple-element.43), channel_id=1, source_target_pairs={{0,6},{2,4},{4,2},{6,0},{8,14},{10,12},{12,10},{14,8},{16,22},{18,... | collective-permute-start | bytes 589832 | tf_op jit(solution)/shard_map/ppermute | solution.py:28
  18.3 4.2 %collective-permute-start.7 = (bf16[32,768]{1,0:T(8,128)(2,1)S(1)}, bf16[32,768]{1,0:T(8,128)(2,1)S(1)}, u32[]{:S(2)}, u32[]{:S(2)}) collective-permute-start(bf16[32,768]{1,0:T(8,128)(2,1)S(1)} %constant_dynamic-slice_fusion.3), channel_id=1, source_target_pairs={{0,2},{2,4},{4,6},{6,8},{8,10},{10,12},{12,14},{14,16},{16,18},{18... | collective-permute-start | bytes 147464 | tf_op jit(solution)/shard_map/ppermute | solution.py:35
  20.8 6.3 %collective-permute-start.8 = (bf16[32,768]{1,0:T(8,128)(2,1)S(1)}, bf16[32,768]{1,0:T(8,128)(2,1)S(1)}, u32[]{:S(2)}, u32[]{:S(2)}) collective-permute-start(bf16[32,768]{1,0:T(8,128)(2,1)S(1)} %slice_bitcast_fusion.7), channel_id=1, source_target_pairs={{2,0},{4,2},{6,4},{8,6},{10,8},{12,10},{14,12},{16,14},{18,16},{20... | collective-permute-start | bytes 147464 | tf_op jit(solution)/shard_map/ppermute | solution.py:35
  29.9 9.8 %collective-permute-start.12 = (bf16[128,768]{1,0:T(8,128)(2,1)S(1)}, bf16[128,768]{1,0:T(8,128)(2,1)S(1)}, u32[]{:S(2)}, u32[]{:S(2)}) collective-permute-start(bf16[128,768]{1,0:T(8,128)(2,1)S(1)} %get-tuple-element.27), channel_id=1, source_target_pairs={{0,2},{2,0},{4,6},{6,4},{8,10},{10,8},{12,14},{14,12},{16,18},{18,... | collective-permute-start | bytes 589832 | tf_op jit(solution)/shard_map/ppermute | solution.py:28
  32.9 7.8 %collective-permute-start.13 = (bf16[128,768]{1,0:T(8,128)(2,1)S(1)}, bf16[128,768]{1,0:T(8,128)(2,1)S(1)}, u32[]{:S(2)}, u32[]{:S(2)}) collective-permute-start(bf16[128,768]{1,0:T(8,128)(2,1)S(1)} %get-tuple-element.27), channel_id=1, source_target_pairs={{0,4},{2,6},{4,0},{6,2},{8,12},{10,14},{12,8},{14,10},{16,20},{18,... | collective-permute-start | bytes 589832 | tf_op jit(solution)/shard_map/ppermute | solution.py:28
  35.4 6.6 %collective-permute-start.14 = (bf16[128,768]{1,0:T(8,128)(2,1)S(1)}, bf16[128,768]{1,0:T(8,128)(2,1)S(1)}, u32[]{:S(2)}, u32[]{:S(2)}) collective-permute-start(bf16[128,768]{1,0:T(8,128)(2,1)S(1)} %get-tuple-element.27), channel_id=1, source_target_pairs={{0,6},{2,4},{4,2},{6,0},{8,14},{10,12},{12,10},{14,8},{16,22},{18,... | collective-permute-start | bytes 589832 | tf_op jit(solution)/shard_map/ppermute | solution.py:28
  35.5 19.4 %collective-permute-start.10 = (bf16[2,192,384]{2,1,0:T(8,128)(2,1)S(1)}, bf16[2,192,384]{2,1,0:T(8,128)(2,1)S(1)}, u32[]{:S(2)}, u32[]{:S(2)}) collective-permute-start(bf16[2,192,384]{2,1,0:T(8,128)(2,1)S(1)} %pad_maximum_fusion.10.refs_0_), channel_id=1, source_target_pairs={{0,16},{2,18},{4,20},{6,22},{8,24},{10,26},{12,28},{14,30},{16,0},... | collective-permute-start | bytes 884744 | tf_op jit(solution)/shard_map/ppermute | solution.py:28
  38.2 16.7 %collective-permute-start.11 = (bf16[2,192,384]{2,1,0:T(8,128)(2,1)S(1)}, bf16[2,192,384]{2,1,0:T(8,128)(2,1)S(1)}, u32[]{:S(2)}, u32[]{:S(2)}) collective-permute-start(bf16[2,192,384]{2,1,0:T(8,128)(2,1)S(1)} %pad_maximum_fusion.10.refs_0_), channel_id=1, source_target_pairs={{0,24},{2,26},{4,28},{6,30},{8,16},{10,18},{12,20},{14,22},{16,8},... | collective-permute-start | bytes 884744 | tf_op jit(solution)/shard_map/ppermute | solution.py:28
  39.7 15.6 %collective-permute-start.9 = (bf16[2,192,384]{2,1,0:T(8,128)(2,1)S(1)}, bf16[2,192,384]{2,1,0:T(8,128)(2,1)S(1)}, u32[]{:S(2)}, u32[]{:S(2)}) collective-permute-start(bf16[2,192,384]{2,1,0:T(8,128)(2,1)S(1)} %pad_maximum_fusion.10.refs_0_), channel_id=1, source_target_pairs={{0,8},{2,10},{4,12},{6,14},{8,0},{10,2},{12,4},{14,6},{16,24},{18,... | collective-permute-start | bytes 884744 | tf_op jit(solution)/shard_map/ppermute | solution.py:28
  40.7 14.7 %collective-permute-start.3 = (bf16[512,768]{1,0:T(8,128)(2,1)S(1)}, bf16[512,768]{1,0:T(8,128)(2,1)S(1)}, u32[]{:S(2)}, u32[]{:S(2)}) collective-permute-start(bf16[512,768]{1,0:T(8,128)(2,1)S(1)} %pad_maximum_fusion.2), channel_id=1, source_target_pairs={{0,1},{1,0},{2,3},{3,2},{4,5},{5,4},{6,7},{7,6},{8,9},{9,8},{10,11... | collective-permute-start | bytes 2359304 | tf_op jit(solution)/shard_map/ppermute | solution.py:28
  42.1 13.4 %collective-permute-start.15 = (bf16[512,768]{1,0:T(8,128)(2,1)S(1)}, bf16[512,768]{1,0:T(8,128)(2,1)S(1)}, u32[]{:S(2)}, u32[]{:S(2)}) collective-permute-start(bf16[512,768]{1,0:T(8,128)(2,1)S(1)} %pad_maximum_fusion.3), channel_id=1, source_target_pairs={{0,1},{1,0},{2,3},{3,2},{4,5},{5,4},{6,7},{7,6},{8,9},{9,8},{10,11... | collective-permute-start | bytes 2359304 | tf_op jit(solution)/shard_map/ppermute | solution.py:28
  61.7 2.2 %copy-start.4 = (f32[1024,768]{1,0:T(8,128)}, f32[1024,768]{1,0:T(8,128)S(1)}, u32[]{:S(2)}) copy-start(f32[1024,768]{1,0:T(8,128)S(1)} %fusion.25) | copy-start | bytes 9437188
  63.9 44.6 %collective-permute-start.16 = (bf16[2,4,128,768]{3,2,0,1:T(8,128)(2,1)}, bf16[2,4,128,768]{3,2,0,1:T(8,128)(2,1)}, u32[]{:S(2)}, u32[]{:S(2)}) collective-permute-start(bf16[2,4,128,768]{3,2,0,1:T(8,128)(2,1)} %fusion.11), channel_id=1, source_target_pairs={{0,1},{1,0},{2,3},{3,2},{4,5},{5,4},{6,7},{7,6},{8,9},{9,8},{10,11... | collective-permute-start | bytes 4718600 | tf_op jit(solution)/shard_map/ppermute | solution.py:28
  64.0 19.4 %collective-permute-start.20 = (bf16[192,768]{1,0:T(8,128)(2,1)S(1)}, bf16[192,768]{1,0:T(8,128)(2,1)S(1)}, u32[]{:S(2)}, u32[]{:S(2)}) collective-permute-start(bf16[192,768]{1,0:T(8,128)(2,1)S(1)} %get-tuple-element.50), channel_id=1, source_target_pairs={{0,8},{2,10},{4,12},{6,14},{8,0},{10,2},{12,4},{14,6},{16,24},{18,... | collective-permute-start | bytes 884744 | tf_op jit(solution)/shard_map/ppermute | solution.py:28
  69.4 23.5 %collective-permute-start.21 = (bf16[192,768]{1,0:T(8,128)(2,1)S(1)}, bf16[192,768]{1,0:T(8,128)(2,1)}, u32[]{:S(2)}, u32[]{:S(2)}) collective-permute-start(bf16[192,768]{1,0:T(8,128)(2,1)S(1)} %get-tuple-element.52), channel_id=1, source_target_pairs={{0,16},{2,18},{4,20},{6,22},{8,24},{10,26},{12,28},{14,30},{16,0},... | collective-permute-start | bytes 884744 | tf_op jit(solution)/shard_map/ppermute | solution.py:28
  71.2 21.7 %collective-permute-start.22 = (bf16[192,768]{1,0:T(8,128)(2,1)S(1)}, bf16[192,768]{1,0:T(8,128)(2,1)}, u32[]{:S(2)}, u32[]{:S(2)}) collective-permute-start(bf16[192,768]{1,0:T(8,128)(2,1)S(1)} %get-tuple-element.51), channel_id=1, source_target_pairs={{0,24},{2,26},{4,28},{6,30},{8,16},{10,18},{12,20},{14,22},{16,8},... | collective-permute-start | bytes 884744 | tf_op jit(solution)/shard_map/ppermute | solution.py:28
  72.6 35.9 %copy-start.3 = (f32[1024,768]{1,0:T(8,128)S(1)}, f32[1024,768]{1,0:T(8,128)}, u32[]{:S(2)}) copy-start(f32[1024,768]{1,0:T(8,128)} %copy-done.2) | copy-start | bytes 9437188
  94.1 9.4 %collective-permute-start.29 = (bf16[1,64,768]{2,1,0:T(8,128)(2,1)S(1)}, bf16[1,64,768]{2,1,0:T(8,128)(2,1)S(1)}, u32[]{:S(2)}, u32[]{:S(2)}) collective-permute-start(bf16[1,64,768]{2,1,0:T(8,128)(2,1)S(1)} %get-tuple-element.57), channel_id=1, source_target_pairs={{0,8},{2,10},{4,12},{6,14},{8,0},{10,2},{12,4},{14,6},{16,24},{18,... | collective-permute-start | bytes 294920 | tf_op jit(solution)/shard_map/ppermute | solution.py:28
  100.4 4.6 %collective-permute-start.26 = (bf16[1,64,768]{2,1,0:T(8,128)(2,1)S(1)}, bf16[1,64,768]{2,1,0:T(8,128)(2,1)S(1)}, u32[]{:S(2)}, u32[]{:S(2)}) collective-permute-start(bf16[1,64,768]{2,1,0:T(8,128)(2,1)S(1)} %get-tuple-element.58), channel_id=1, source_target_pairs={{0,4},{2,6},{4,0},{6,2},{8,12},{10,14},{12,8},{14,10},{16,20},{18,... | collective-permute-start | bytes 294920 | tf_op jit(solution)/shard_map/ppermute | solution.py:28
  101.9 5.6 %collective-permute-start.23 = (bf16[1,64,768]{2,1,0:T(8,128)(2,1)S(1)}, bf16[1,64,768]{2,1,0:T(8,128)(2,1)S(1)}, u32[]{:S(2)}, u32[]{:S(2)}) collective-permute-start(bf16[1,64,768]{2,1,0:T(8,128)(2,1)S(1)} %get-tuple-element.59), channel_id=1, source_target_pairs={{0,2},{2,0},{4,6},{6,4},{8,10},{10,8},{12,14},{14,12},{16,18},{18,... | collective-permute-start | bytes 294920 | tf_op jit(solution)/shard_map/ppermute | solution.py:28
  103.6 11.1 %collective-permute-start.30 = (bf16[2,64,768]{2,1,0:T(8,128)(2,1)S(1)}, bf16[2,64,768]{2,1,0:T(8,128)(2,1)S(1)}, u32[]{:S(2)}, u32[]{:S(2)}) collective-permute-start(bf16[2,64,768]{2,1,0:T(8,128)(2,1)S(1)} %pad_maximum_fusion.13), channel_id=1, source_target_pairs={{0,2},{2,0},{4,6},{6,4},{8,10},{10,8},{12,14},{14,12},{16,18},{18,... | collective-permute-start | bytes 589832 | tf_op jit(solution)/shard_map/ppermute | solution.py:28
  105.0 11.1 %collective-permute-start.27 = (bf16[2,64,768]{2,1,0:T(8,128)(2,1)S(1)}, bf16[2,64,768]{2,1,0:T(8,128)(2,1)S(1)}, u32[]{:S(2)}, u32[]{:S(2)}) collective-permute-start(bf16[2,64,768]{2,1,0:T(8,128)(2,1)S(1)} %pad_maximum_fusion.12), channel_id=1, source_target_pairs={{0,8},{2,10},{4,12},{6,14},{8,0},{10,2},{12,4},{14,6},{16,24},{18,... | collective-permute-start | bytes 589832 | tf_op jit(solution)/shard_map/ppermute | solution.py:28
  107.5 10.5 %collective-permute-start.24 = (bf16[2,64,768]{2,1,0:T(8,128)(2,1)S(1)}, bf16[2,64,768]{2,1,0:T(8,128)(2,1)S(1)}, u32[]{:S(2)}, u32[]{:S(2)}) collective-permute-start(bf16[2,64,768]{2,1,0:T(8,128)(2,1)S(1)} %pad_maximum_fusion.11), channel_id=1, source_target_pairs={{0,4},{2,6},{4,0},{6,2},{8,12},{10,14},{12,8},{14,10},{16,20},{18,... | collective-permute-start | bytes 589832 | tf_op jit(solution)/shard_map/ppermute | solution.py:28
  111.8 12.6 %copy-start.11 = (f32[768]{0:T(1024)S(1)}, f32[768]{0:T(1024)}, u32[]{:S(2)}) copy-start(f32[768]{0:T(1024)} %param.17) | copy-start | bytes 9220
  111.8 12.3 %collective-permute-start.17 = (bf16[2,128,768]{2,1,0:T(8,128)(2,1)}, bf16[2,128,768]{2,1,0:T(8,128)(2,1)S(1)}, u32[]{:S(2)}, u32[]{:S(2)}) collective-permute-start(bf16[2,128,768]{2,1,0:T(8,128)(2,1)} %get-tuple-element.48), channel_id=1, source_target_pairs={{0,2},{2,0},{4,6},{6,4},{8,10},{10,8},{12,14},{14,12},{16,18},{18,... | collective-permute-start | bytes 1179656 | tf_op jit(solution)/shard_map/ppermute | solution.py:28
  113.0 20.3 %collective-permute-start.18 = (bf16[2,128,768]{2,1,0:T(8,128)(2,1)}, bf16[2,128,768]{2,1,0:T(8,128)(2,1)S(1)}, u32[]{:S(2)}, u32[]{:S(2)}) collective-permute-start(bf16[2,128,768]{2,1,0:T(8,128)(2,1)} %get-tuple-element.47), channel_id=1, source_target_pairs={{0,4},{2,6},{4,0},{6,2},{8,12},{10,14},{12,8},{14,10},{16,20},{18,... | collective-permute-start | bytes 1179656 | tf_op jit(solution)/shard_map/ppermute | solution.py:28
  114.7 3.4 %copy-start.7 = (bf16[2,64,768]{2,1,0:T(8,128)(2,1)}, bf16[2,64,768]{2,1,0:T(8,128)(2,1)S(1)}, u32[]{:S(2)}) copy-start(bf16[2,64,768]{2,1,0:T(8,128)(2,1)S(1)} %collective-permute-done.30) | copy-start | bytes 589828
  114.7 18.6 %collective-permute-start.19 = (bf16[2,128,768]{2,1,0:T(8,128)(2,1)}, bf16[2,128,768]{2,1,0:T(8,128)(2,1)S(1)}, u32[]{:S(2)}, u32[]{:S(2)}) collective-permute-start(bf16[2,128,768]{2,1,0:T(8,128)(2,1)} %get-tuple-element.46), channel_id=1, source_target_pairs={{0,6},{2,4},{4,2},{6,0},{8,14},{10,12},{12,10},{14,8},{16,22},{18,... | collective-permute-start | bytes 1179656 | tf_op jit(solution)/shard_map/ppermute | solution.py:28
  116.1 22.6 %collective-permute-start.31 = (bf16[4,64,768]{2,1,0:T(8,128)(2,1)}, bf16[4,64,768]{2,1,0:T(8,128)(2,1)}, u32[]{:S(2)}, u32[]{:S(2)}) collective-permute-start(bf16[4,64,768]{2,1,0:T(8,128)(2,1)} %pad_maximum_fusion.9), channel_id=1, source_target_pairs={{0,4},{2,6},{4,0},{6,2},{8,12},{10,14},{12,8},{14,10},{16,20},{18,... | collective-permute-start | bytes 1179656 | tf_op jit(solution)/shard_map/ppermute | solution.py:28
  118.1 21.7 %collective-permute-start.28 = (bf16[4,64,768]{2,1,0:T(8,128)(2,1)}, bf16[4,64,768]{2,1,0:T(8,128)(2,1)}, u32[]{:S(2)}, u32[]{:S(2)}) collective-permute-start(bf16[4,64,768]{2,1,0:T(8,128)(2,1)} %pad_maximum_fusion.8), channel_id=1, source_target_pairs={{0,2},{2,0},{4,6},{6,4},{8,10},{10,8},{12,14},{14,12},{16,18},{18,... | collective-permute-start | bytes 1179656 | tf_op jit(solution)/shard_map/ppermute | solution.py:28
  124.1 22.0 %collective-permute-start.25 = (bf16[4,64,768]{2,1,0:T(8,128)(2,1)}, bf16[4,64,768]{2,1,0:T(8,128)(2,1)}, u32[]{:S(2)}, u32[]{:S(2)}) collective-permute-start(bf16[4,64,768]{2,1,0:T(8,128)(2,1)} %pad_maximum_fusion.7), channel_id=1, source_target_pairs={{0,8},{2,10},{4,12},{6,14},{8,0},{10,2},{12,4},{14,6},{16,24},{18,... | collective-permute-start | bytes 1179656 | tf_op jit(solution)/shard_map/ppermute | solution.py:28
  124.4 14.2 %copy-start.8 = (bf16[2,64,768]{2,1,0:T(8,128)(2,1)S(1)}, bf16[2,64,768]{2,1,0:T(8,128)(2,1)}, u32[]{:S(2)}) copy-start(bf16[2,64,768]{2,1,0:T(8,128)(2,1)} %copy-done.7) | copy-start | bytes 589828
  133.3 6.4 %copy-start.6 = (bf16[2,64,768]{2,1,0:T(8,128)(2,1)S(1)}, bf16[2,64,768]{2,1,0:T(8,128)(2,1)}, u32[]{:S(2)}) copy-start(bf16[2,64,768]{2,1,0:T(8,128)(2,1)} %copy-done.5) | copy-start | bytes 589828
  135.1 5.8 %collective-permute-start.32 = (bf16[128,768]{1,0:T(8,128)(2,1)S(1)}, bf16[128,768]{1,0:T(8,128)(2,1)S(1)}, u32[]{:S(2)}, u32[]{:S(2)}) collective-permute-start(bf16[128,768]{1,0:T(8,128)(2,1)S(1)} %get-tuple-element.35.rest_0_), channel_id=1, source_target_pairs={{0,1},{1,0},{2,3},{3,2},{4,5},{5,4},{6,7},{7,6},{8,9},{9,8},{10,11... | collective-permute-start | bytes 589832 | tf_op jit(solution)/shard_map/ppermute | solution.py:28
  139.7 10.8 %copy-start.1 = (bf16[32,8,768]{2,1,0:T(8,128)(2,1)S(1)}, bf16[32,8,768]{2,1,0:T(8,128)(2,1)}, u32[]{:S(2)}) copy-start(bf16[32,8,768]{2,1,0:T(8,128)(2,1)} %param.11) | copy-start | bytes 1179652
  141.0 6.2 %collective-permute-start.33 = (bf16[32,768]{1,0:T(8,128)(2,1)S(1)}, bf16[32,768]{1,0:T(8,128)(2,1)S(1)}, u32[]{:S(2)}, u32[]{:S(2)}) collective-permute-start(bf16[32,768]{1,0:T(8,128)(2,1)S(1)} %get-tuple-element.56), channel_id=1, source_target_pairs={{0,2},{2,4},{4,6},{6,8},{8,10},{10,12},{12,14},{14,16},{16,18},{18... | collective-permute-start | bytes 147464 | tf_op jit(solution)/shard_map/ppermute | solution.py:35
  144.6 6.0 %collective-permute-start.34 = (bf16[32,768]{1,0:T(8,128)(2,1)S(1)}, bf16[32,768]{1,0:T(8,128)(2,1)S(1)}, u32[]{:S(2)}, u32[]{:S(2)}) collective-permute-start(bf16[32,768]{1,0:T(8,128)(2,1)S(1)} %get-tuple-element.55), channel_id=1, source_target_pairs={{2,0},{4,2},{6,4},{8,6},{10,8},{12,10},{14,12},{16,14},{18,16},{20... | collective-permute-start | bytes 147464 | tf_op jit(solution)/shard_map/ppermute | solution.py:35
  162.9 7.5 %collective-permute-start.35 = (bf16[48,1536]{1,0:T(8,128)(2,1)S(1)}, bf16[48,1536]{1,0:T(8,128)(2,1)S(1)}, u32[]{:S(2)}, u32[]{:S(2)}) collective-permute-start(bf16[48,1536]{1,0:T(8,128)(2,1)S(1)} %get-tuple-element.41), channel_id=1, source_target_pairs={{0,16},{2,18},{4,20},{6,22},{8,24},{10,26},{12,28},{14,30},{16,0},... | collective-permute-start | bytes 442376 | tf_op jit(solution)/shard_map/ppermute | solution.py:28
  (2 other events, 3.6 us)

commit v4 on v3

--- a/solution.py
+++ b/solution.py
@@ -102,20 +102,45 @@
     framed[pl.ds(live_rows + MARGIN, MARGIN)] = rows_of(after_ref)[:MARGIN]
 
 
+def kept_rows(scalars, tokens, patches):
+    row = scalars[1] + lax.broadcasted_iota(jnp.int32, (tokens, 1), 0) // COLS
+    keep = jnp.zeros((tokens, 1), F32)
+    for patch in range(patches):
+        keep = jnp.where(row // PATCH == patch, scalars[2 + patch].astype(F32), keep)
+    live = row < scalars[0]
+    return live, jnp.where(live, keep, 0.0)
+
+
 def forward_kernel(
-    scalars, strip, before, after, taps, gain, normed, centred_out, inverse, framed, mixed
+    scalars,
+    strip,
+    cotangent,
+    before,
+    after,
+    taps,
+    gain,
+    layer_scale,
+    sent,
+    centred_out,
+    inverse,
+    framed,
+    mixed,
 ):
     place_strip(framed, [(0, strip)], before, after, scalars[0])
     convolve(framed, taps, scalars[1], mixed, False)
-    value = mixed[...].reshape(normed.shape)
-    channels = value.shape[1]
+    tokens, channels = centred_out.shape
+    value = mixed[...].reshape(tokens, channels)
     shifted = value - jnp.sum(value, 1, keepdims=True) / channels
     variance = jnp.sum(shifted * shifted, 1, keepdims=True) / channels
     inv_std = lax.rsqrt(variance + 1e-06)
     centred = shifted * inv_std
     centred_out[...] = centred
     inverse[...] = jnp.broadcast_to(inv_std, inverse.shape)
-    normed[...] = (centred * gain[...]).astype(BF16)
+    sent[0] = (centred * gain[...]).astype(BF16)
+    _, keep = kept_rows(scalars, tokens, strip.shape[0] // (COLS * PATCH))
+    start = pl.multiple_of(scalars[1] * COLS, 16)
+    grad_out = cotangent[pl.ds(start, tokens), :].astype(F32)
+    sent[1] = (keep * layer_scale[...] * grad_out).astype(BF16)
 
 
 def middle_kernel(
@@ -123,11 +148,7 @@
 ):
     tokens, channels = grad_mixed.shape
     start = pl.multiple_of(scalars[1] * COLS, 16)
-    row = scalars[1] + lax.broadcasted_iota(jnp.int32, (tokens, 1), 0) // COLS
-    keep = jnp.zeros((tokens, 1), F32)
-    for patch in range(strip.shape[0] // (COLS * PATCH)):
-        keep = jnp.where(row // PATCH == patch, scalars[2 + patch].astype(F32), keep)
-    live = row < scalars[0]
+    live, keep = kept_rows(scalars, tokens, strip.shape[0] // (COLS * PATCH))
 
     def summed(which):
         value = total[which].astype(F32)
@@ -145,13 +166,14 @@
     grad_mixed[...] = jnp.where(live, value, 0.0).astype(BF16)
 
 
-def weights_kernel(scalars, *refs):
-    *pieces, up, down_t = refs
-    rows = pieces[0].shape[1]
-    for s, piece in enumerate(pieces):
-        start = pl.multiple_of((scalars[0] ^ s) * rows, rows)
-        up[pl.ds(start, rows), :] = piece[0]
-        down_t[pl.ds(start, rows), :] = piece[1]
+def weights_kernel(scalars, held, up, down_t):
+    lines, _, rows, _ = held.shape
+    bits = lines.bit_length() - 1
+    for e in range(lines):
+        apart = sum(lines >> (i + 1) for i in range(bits) if e >> i & 1)
+        start = pl.multiple_of((scalars[0] ^ apart) * rows, rows)
+        up[pl.ds(start, rows), :] = held[e, 0]
+        down_t[pl.ds(start, rows), :] = held[e, 1]
 
 
 def backward_kernel(scalars, cotangent, before, after, taps, *rest):
@@ -190,11 +212,13 @@
         whole[...] = gathered[0][...]
     else:
         group, third, _ = gathered[0].shape
-        for turn, ref in enumerate(gathered):
+        group *= 2
+        for turn in range(3):
             for e in range(group):
                 block = hidden_block(scalars[2] ^ member_bits(e, turn, group), group)
                 start = pl.multiple_of((block * 3 + turn) * third, third)
-                whole[pl.ds(start, third), :] = ref[e]
+                later, entry = divmod(e, group // 2)
+                whole[pl.ds(start, third), :] = gathered[2 * turn + later][entry]
 
     plain = ((1,), (0,))
     steps = [pl.ds(i, 256) for i in range(0, channels, 256)]
@@ -274,6 +298,7 @@
     owners = lax.axis_size("own")
     lines = tiles // PLANE
     half_lines = lines // 2
+    line_bits = [1 << i for i in range(lines.bit_length() - 1)]
     tile = lax.axis_index("tile")
     own = lax.axis_index("own")
     place, line = tile & (PLANE - 1), tile >> (PLANE.bit_length() - 1)
@@ -281,11 +306,6 @@
     offset = own * share
     tokens = share * columns
     live_rows = PATCH * lengths[tile]
-    row = offset + jnp.arange(share)
-    keep = jnp.repeat(tissue[:, 0], PATCH, axis=0)
-    keep = lax.dynamic_slice_in_dim(keep, offset, share, 0) * (row < live_rows)
-    mine_cot = lax.dynamic_slice_in_dim(cotangent, offset, share, 0).astype(F32)
-    grad_branch = (keep.astype(F32)[:, None, None] * layer_scale * mine_cot).astype(BF16)
     scalars = jnp.concatenate([jnp.stack([live_rows, offset]), tissue[:, 0]])
     scalars = scalars.astype(jnp.int32)
     strip = features.reshape(tile_rows * columns, channels)
@@ -306,33 +326,32 @@
     tail = lax.dynamic_slice_in_dim(strip, (live_rows - RIM) * columns, rim, 0)
     before, after = neighbours(strip[:rim], tail)
     piece, before, after = lax.optimization_barrier((piece, before, after))
-    pieces = [swap(piece, "tile", PLANE * s) if s else piece for s in range(lines)]
+    held = piece[None]
+    for bit in line_bits[::-1]:
+        held = jnp.concatenate([held, swap(held, "tile", PLANE * bit)], 0)
     up, down_t = call(
         weights_kernel,
         [jax.ShapeDtypeStruct((channels, units), BF16)] * 2,
         [],
         10 * 10**9,
-        line[None], *pieces,
+        line[None], held,
     )
     bias = lax.dynamic_slice_in_dim(bias_up, place * units, units, 0)
 
-    def gather(mine):
-        mine = jnp.concatenate([mine] + [swap(mine, "tile", s) for s in range(1, PLANE)], 0)
-        return jnp.concatenate([mine] + [swap(mine, "own", s) for s in range(1, owners)], 0)
-
-    grad_branch = gather(grad_branch.reshape(tokens, channels))
-    normed, centred, inverse = call(
+    sent, centred, inverse = call(
         forward_kernel,
         [
-            jax.ShapeDtypeStruct((tokens, channels), BF16),
+            jax.ShapeDtypeStruct((2, tokens, channels), BF16),
             jax.ShapeDtypeStruct((tokens, channels), F32),
             jax.ShapeDtypeStruct((tokens, LANES), F32),
         ],
         [frame, wide],
         10**6,
-        scalars, strip, before, after, taps, gain,
-    )
-    normed = gather(normed)
+        scalars, strip, cotangent.reshape(strip.shape), before, after, taps, gain, scale,
+    )
+    mine = jnp.concatenate([sent] + [swap(sent, "tile", s) for s in range(1, PLANE)], 1)
+    both = jnp.concatenate([mine] + [swap(mine, "own", s) for s in range(1, owners)], 1)
+    normed, grad_branch = both[0], both[1]
 
     plain, across, over_tokens = ((1,), (0,)), ((1,), (1,)), ((0,), (0,))
     hidden = dot(normed, up, plain) + bias
@@ -346,11 +365,20 @@
     ).astype(BF16)
     parts, grad_hidden, act = lax.optimization_barrier((parts, grad_hidden, act))
     kept = 2 * units // lines
-    grad_t = lax.dynamic_slice_in_dim(parts, line * kept, kept, 0).astype(F32)
-    arrived = []
-    for s in range(1, lines):
-        part = lax.dynamic_slice_in_dim(parts, (line ^ s) * kept, kept, 0)
-        arrived.append(swap(part, "tile", PLANE * s))
+    reduced = parts.reshape(lines, kept, channels)
+
+    def split(blocks, bit):
+        blocks = blocks.reshape(-1, 2, kept, channels)
+        which = jnp.where((line & bit) != 0, 1, 0)
+        mine = lax.dynamic_slice_in_dim(blocks, which, 1, 1)
+        other = lax.dynamic_slice_in_dim(blocks, 1 - which, 1, 1)
+        return mine[:, 0].astype(F32), other[:, 0].astype(BF16)
+
+    for bit in line_bits[:-1]:
+        reduced, other = split(reduced, bit)
+        reduced = reduced + swap(other, "tile", PLANE * bit).astype(F32)
+    reduced, other = split(reduced, line_bits[-1])
+    arrived = swap(other, "tile", PLANE * line_bits[-1])
 
     partial = jnp.stack([dot(grad_hidden, up, across), dot(act, down_t, across)])
     partial = partial.reshape(2, owners, PLANE, tokens, channels)
@@ -367,7 +395,8 @@
         scalars, strip, total[:, 0], *moved, centred, inverse, gain, scale,
     )
 
-    grad_t = (grad_t + sum(part.astype(F32) for part in arrived)).astype(BF16)
+    arrived, grad_mixed = lax.optimization_barrier((arrived, grad_mixed))
+    grad_t = (reduced + arrived.astype(F32)).astype(BF16)[0]
     group = PLANE * half_lines
     bits = [1 << i for i in range(group.bit_length() - 1)]
     third = kept // 3
@@ -375,9 +404,9 @@
     for turn in range(3):
         held = grad_t[turn * third : (turn + 1) * third][None]
         order = bits[turn:] + bits[:turn]
-        for bit in order:
+        for bit in order[:-1]:
             held = jnp.concatenate([held, swap(held, "tile", bit)], 0)
-        thirds.append(held)
+        thirds += [held, swap(held, "tile", order[-1])]
 
     halves = [grad_mixed] + [swap(grad_mixed, "own", s) for s in range(1, owners)]
     stacked = jnp.stack(halves)

time: 172 us -> 152 us (0.88)
  waiting for transfers between devices: 67 us -> 56.6 us
  starting transfers between devices: 57.9 us -> 49.5 us
  other arithmetic: 14.8 us -> 12 us
    ppermute x32 -> x26, waiting for transfers between devices: 58.8 us -> 48.5 us  [swap(): lax.ppermute(value, axis, [(i, i ^ bit) for i in range(lax.axis_size(axis...]
    ppermute x32 -> x26, starting transfers between devices: 49 us -> 40.4 us  [swap(): lax.ppermute(value, axis, [(i, i ^ bit) for i in range(lax.axis_size(axis...]
    concatenate x9 -> x6, other arithmetic: 5.69 us -> 0.18 us  [shards(): held = jnp.concatenate([held, swap(held, 'tile', bit)], 0)]
    concatenate x2 -> x3, other arithmetic: 0.11 us -> 3.39 us  [the longest x2 2.09 us: shards(): held = jnp.concatenate([held, swap(held, 'tile', PLANE * bit)], 0)]
  transfers between devices with their start and end apart: 36 -> 30, of which waited for: 15 -> 15; matrix products, arithmetic and copies ran while one was open for 8% -> 7% of each run, Pallas kernels for 3% -> 5%
where the time goes in v4:
time: 152 us; the launch traced here: 151 us
  waiting for transfers between devices  56.6 us (37%)
  starting transfers between devices  49.5 us (33%)
  Pallas kernels  17.1 us (11%)
  other arithmetic  12 us (8%)
  local copies, waits for them, and re-layouts  8.16 us (5%)
  matrix products  6 us (4%)
  between operations  1.74 us (1%)
    ppermute x26, waiting for transfers between devices, swap(): lax.ppermute(value, axis, [(i, i ^ bit) for i in range(lax.axis_size(axis...  48.5 us
    ppermute x26, starting transfers between devices, swap(): lax.ppermute(value, axis, [(i, i ^ bit) for i in range(lax.axis_size(axis...  40.4 us
    pallas_call x5, Pallas kernels, call(): pl.pallas_call(kernel, out_shape=out_shape, in_specs=[smem] * scalars + [...  17.1 us
    ppermute x4, starting transfers between devices, neighbours(): return (lax.ppermute(last, 'tile', up), lax.ppermute(first, 'tile', down))  9.09 us
    ppermute x4, waiting for transfers between devices, neighbours(): return (lax.ppermute(last, 'tile', up), lax.ppermute(first, 'tile', down))  8.12 us
    dot_general x6, matrix products, dot(): lax.dot_general(left, right, (contract, ((), ())), precision=precision, p...  6 us
  transfers between devices with their start and end apart: 30, of which 15 were waited for; matrix products, arithmetic and copies ran while one was open for 7% of the time, Pallas kernels for 5%

profile of v4, /device:TPU:0, one launch (start us, length us, event | category | flops | bytes accessed | tf_op | source)
XLA Modules:
  0.0 151.1 jit_solution(8735678675374237024)
XLA Ops:
  1.7 3.0 %collective-permute-start.1 = (bf16[2,48,384]{2,1,0:T(8,128)(2,1)S(1)}, bf16[2,48,384]{2,1,0:T(8,128)(2,1)S(1)}, u32[]{:S(2)}, u32[]{:S(2)}) collective-permute-start(bf16[2,48,384]{2,1,0:T(8,128)(2,1)S(1)} %get-tuple-element.70), channel_id=1, source_target_pairs={{0,4},{2,6},{4,0},{6,2},{8,12},{10,14},{12,8},{14,10},{16,20},{18,... | collective-permute-start | bytes 221192 | tf_op jit(solution)/shard_map/ppermute | solution.py:28
  4.8 1.4 collective-permute-start
  6.3 1.2 dynamic_slice.35
  9.0 3.8 %collective-permute-start.3 = (bf16[32,768]{1,0:T(8,128)(2,1)S(1)}, bf16[32,768]{1,0:T(8,128)(2,1)S(1)}, u32[]{:S(2)}, u32[]{:S(2)}) collective-permute-start(bf16[32,768]{1,0:T(8,128)(2,1)S(1)} %constant_dynamic-slice_fusion), channel_id=1, source_target_pairs={{0,2},{2,4},{4,6},{6,8},{8,10},{10,12},{12,14},{14,16},{16,18},{18... | collective-permute-start | bytes 147464 | tf_op jit(solution)/shard_map/ppermute | solution.py:35
  13.6 1.3 collective-permute-start.4
  15.9 3.7 %collective-permute-done.4.after = bf16[32,768]{1,0:T(8,128)(2,1)S(1)} collective-permute-done((bf16[32,768]{1,0:T(8,128)(2,1)S(1)}, bf16[32,768]{1,0:T(8,128)(2,1)S(1)}, u32[]{:S(2)}, u32[]{:S(2)}) %collective-permute-start.4) | collective-permute-done | bytes 49184 | tf_op jit(solution)/shard_map/ppermute | solution.py:35
  19.6 6.0 %collective-permute-start.9 = (bf16[1,2,192,384]{3,2,1,0:T(8,128)(2,1)S(1)}, bf16[1,2,192,384]{3,2,1,0:T(8,128)(2,1)S(1)}, u32[]{:S(2)}, u32[]{:S(2)}) collective-permute-start(bf16[1,2,192,384]{3,2,1,0:T(8,128)(2,1)S(1)} %bitcast.89), channel_id=1, source_target_pairs={{0,16},{2,18},{4,20},{6,22},{8,24},{10,26},{12,28},{14,30},{16,0},... | collective-permute-start | bytes 884744 | tf_op jit(solution)/shard_map/ppermute | solution.py:28
  25.8 2.9 %shard_map.129 = (bf16[2,128,768]{2,1,0:T(8,128)(2,1)S(1)}, f32[128,768]{1,0:T(8,128)S(1)}, f32[128,128]{1,0:T(8,128)S(1)}) custom-call(s32[6]{0:T(128)S(1)} %pad_add_fusion.scalars, bf16[256,768]{1,0:T(8,128)(2,1)S(1)} %bitcast.77, bf16[256,768]{1,0:T(8,128)(2,1)S(1)} %bitcast.79, bf16[32,768]{1,0:T(8,128)(2,1)S(1)} %collective-permute-done.3.before, ...), custom_call_target="tpu_custom_call" | custom-call | flops 1000000 | bytes 1048576 | tf_op jit(solution)/shard_map/pallas_call | solution.py:50
  28.8 1.9 %collective-permute-start.6 = (bf16[2,128,768]{2,1,0:T(8,128)(2,1)S(1)}, bf16[2,128,768]{2,1,0:T(8,128)(2,1)S(1)}, u32[]{:S(2)}, u32[]{:S(2)}) collective-permute-start(bf16[2,128,768]{2,1,0:T(8,128)(2,1)S(1)} %get-tuple-element.30), channel_id=1, source_target_pairs={{0,4},{2,6},{4,0},{6,2},{8,12},{10,14},{12,8},{14,10},{16,20},{18,... | collective-permute-start | bytes 1179656 | tf_op jit(solution)/shard_map/ppermute | solution.py:28
  30.7 1.5 %collective-permute-start.7 = (bf16[2,128,768]{2,1,0:T(8,128)(2,1)S(1)}, bf16[2,128,768]{2,1,0:T(8,128)(2,1)S(1)}, u32[]{:S(2)}, u32[]{:S(2)}) collective-permute-start(bf16[2,128,768]{2,1,0:T(8,128)(2,1)S(1)} %get-tuple-element.30), channel_id=1, source_target_pairs={{0,6},{2,4},{4,2},{6,0},{8,14},{10,12},{12,10},{14,8},{16,22},{18,... | collective-permute-start | bytes 1179656 | tf_op jit(solution)/shard_map/ppermute | solution.py:28
  32.3 1.8 %collective-permute-done.9 = bf16[1,2,192,384]{3,2,1,0:T(8,128)(2,1)S(1)} collective-permute-done((bf16[1,2,192,384]{3,2,1,0:T(8,128)(2,1)S(1)}, bf16[1,2,192,384]{3,2,1,0:T(8,128)(2,1)S(1)}, u32[]{:S(2)}, u32[]{:S(2)}) %collective-permute-start.9) | collective-permute-done | bytes 294944 | tf_op jit(solution)/shard_map/ppermute | solution.py:28
  35.0 2.0 %collective-permute-start.10 = (bf16[2,2,192,384]{3,2,1,0:T(8,128)(2,1)}, bf16[2,2,192,384]{3,2,1,0:T(8,128)(2,1)}, u32[]{:S(2)}, u32[]{:S(2)}) collective-permute-start(bf16[2,2,192,384]{3,2,1,0:T(8,128)(2,1)} %pad_maximum_fusion.4), channel_id=1, source_target_pairs={{0,8},{2,10},{4,12},{6,14},{8,0},{10,2},{12,4},{14,6},{16,24},{18,... | collective-permute-start | bytes 1769480 | tf_op jit(solution)/shard_map/ppermute | solution.py:28
  36.9 1.7 %collective-permute-done.5 = bf16[2,128,768]{2,1,0:T(8,128)(2,1)S(1)} collective-permute-done((bf16[2,128,768]{2,1,0:T(8,128)(2,1)S(1)}, bf16[2,128,768]{2,1,0:T(8,128)(2,1)S(1)}, u32[]{:S(2)}, u32[]{:S(2)}) %collective-permute-start.5) | collective-permute-done | bytes 393248 | tf_op jit(solution)/shard_map/ppermute | solution.py:28
  38.6 6.3 %collective-permute-done.6 = bf16[2,128,768]{2,1,0:T(8,128)(2,1)S(1)} collective-permute-done((bf16[2,128,768]{2,1,0:T(8,128)(2,1)S(1)}, bf16[2,128,768]{2,1,0:T(8,128)(2,1)S(1)}, u32[]{:S(2)}, u32[]{:S(2)}) %collective-permute-start.6) | collective-permute-done | bytes 393248 | tf_op jit(solution)/shard_map/ppermute | solution.py:28
  44.9 1.3 pad_maximum_fusion.1
  47.3 1.7 %collective-permute-done.10 = bf16[2,2,192,384]{3,2,1,0:T(8,128)(2,1)} collective-permute-done((bf16[2,2,192,384]{3,2,1,0:T(8,128)(2,1)}, bf16[2,2,192,384]{3,2,1,0:T(8,128)(2,1)}, u32[]{:S(2)}, u32[]{:S(2)}) %collective-permute-start.10) | collective-permute-done | bytes 589856 | tf_op jit(solution)/shard_map/ppermute | solution.py:28
  49.0 1.2 pad_maximum_fusion.2.held
  50.4 1.5 %constant_dynamic-update-slice_fusion = bf16[2,1024,768]{2,1,0:T(8,128)(2,1)S(1)} fusion(bf16[2,1024,768]{2,1,0:T(8,128)(2,1)S(1)} %constant_dynamic-update-slice_fusion.1, bf16[2,512,768]{2,1,0:T(8,128)(2,1)} %collective-permute-done.8), kind=kLoop, calls=%fused_computation.76 | loop fusion | bytes 3145728 | tf_op jit(solution)/shard_map/concatenate | solution.py:353
  51.9 1.1 multiply_convert_fusion
  53.8 1.3 fusion.10
  58.0 1.7 %copy-done.3 = f32[1024,768]{1,0:T(8,128)} copy-done((f32[1024,768]{1,0:T(8,128)}, f32[1024,768]{1,0:T(8,128)S(1)}, u32[]{:S(2)}) %copy-start.3) | copy-done | bytes 3145752
  59.7 1.4 fusion.11
  62.0 1.7 %collective-permute-start.15 = (bf16[2,192,768]{2,1,0:T(8,128)(2,1)}, bf16[2,192,768]{2,1,0:T(8,128)(2,1)}, u32[]{:S(2)}, u32[]{:S(2)}) collective-permute-start(bf16[2,192,768]{2,1,0:T(8,128)(2,1)} %dynamic-slice_bitcast_fusion), channel_id=1, source_target_pairs={{0,8},{2,10},{4,12},{6,14},{8,0},{10,2},{12,4},{14,6},{16,24},{18,... | collective-permute-start | bytes 1769480 | tf_op jit(solution)/shard_map/ppermute | solution.py:28
  63.7 14.3 %collective-permute-done.15 = bf16[2,192,768]{2,1,0:T(8,128)(2,1)} collective-permute-done((bf16[2,192,768]{2,1,0:T(8,128)(2,1)}, bf16[2,192,768]{2,1,0:T(8,128)(2,1)}, u32[]{:S(2)}, u32[]{:S(2)}) %collective-permute-start.15) | collective-permute-done | bytes 589856 | tf_op jit(solution)/shard_map/ppermute | solution.py:28
  78.0 1.2 convert_add_fusion
  79.3 2.7 %fusion.3 = bf16[2,4,128,768]{3,2,0,1:T(8,128)(2,1)S(1)} fusion(f32[1,2,4,128,768]{4,3,0,2,1:T(8,128)} %bitcast.84, f32[1,2,4,128,768]{4,3,0,2,1:T(8,128)} %bitcast.86, bf16[2,4,128,768]{3,2,0,1:T(8,128)(2,1)} %collective-permute-done.11), kind=kLoop, calls=%fused_computation.5 | loop fusion | flops 3145728 | bytes 9437184 | tf_op jit(solution)/shard_map/convert_element_type | solution.py:388
  82.1 2.1 %collective-permute-start.12 = (bf16[2,128,768]{2,1,0:T(8,128)(2,1)S(1)}, bf16[2,128,768]{2,1,0:T(8,128)(2,1)S(1)}, u32[]{:S(2)}, u32[]{:S(2)}) collective-permute-start(bf16[2,128,768]{2,1,0:T(8,128)(2,1)S(1)} %get-tuple-element.56), channel_id=1, source_target_pairs={{0,2},{2,0},{4,6},{6,4},{8,10},{10,8},{12,14},{14,12},{16,18},{18,... | collective-permute-start | bytes 1179656 | tf_op jit(solution)/shard_map/ppermute | solution.py:28
  84.2 1.1 collective-permute-start.13
  86.0 3.1 %collective-permute-start.16 = (bf16[1,192,768]{2,1,0:T(8,128)(2,1)S(1)}, bf16[1,192,768]{2,1,0:T(8,128)(2,1)S(1)}, u32[]{:S(2)}, u32[]{:S(2)}) collective-permute-start(bf16[1,192,768]{2,1,0:T(8,128)(2,1)S(1)} %dynamic-slice_convert_fusion), channel_id=1, source_target_pairs={{0,16},{2,18},{4,20},{6,22},{8,24},{10,26},{12,28},{14,30},{16,0},... | collective-permute-start | bytes 884744 | tf_op jit(solution)/shard_map/ppermute | solution.py:28
  89.1 5.1 %collective-permute-done.12.one = bf16[2,128,768]{2,1,0:T(8,128)(2,1)S(1)} collective-permute-done((bf16[2,128,768]{2,1,0:T(8,128)(2,1)S(1)}, bf16[2,128,768]{2,1,0:T(8,128)(2,1)S(1)}, u32[]{:S(2)}, u32[]{:S(2)}) %collective-permute-start.12) | collective-permute-done | bytes 393248 | tf_op jit(solution)/shard_map/ppermute | solution.py:28
  94.2 7.7 %collective-permute-done.13.two = bf16[2,128,768]{2,1,0:T(8,128)(2,1)S(1)} collective-permute-done((bf16[2,128,768]{2,1,0:T(8,128)(2,1)S(1)}, bf16[2,128,768]{2,1,0:T(8,128)(2,1)S(1)}, u32[]{:S(2)}, u32[]{:S(2)}) %collective-permute-start.13) | collective-permute-done | bytes 393248 | tf_op jit(solution)/shard_map/ppermute | solution.py:28
  101.8 1.4 collective-permute-done.14.three
  103.2 1.7 %shard_map.131 = (bf16[128,768]{1,0:T(8,128)(2,1)S(1)}, bf16[128,768]{1,0:T(8,128)(2,1)}) custom-call(s32[6]{0:T(128)S(1)} %pad_add_fusion.scalars, bf16[256,768]{1,0:T(8,128)(2,1)S(1)} %bitcast.78, bf16[2,128,768]{2,1,0:T(8,128)(2,1)S(1)} %get-tuple-element.57.total, bf16[2,128,768]{2,1,0:T(8,128)(2,1)S(1)} %collective-permute-done.12.one, ...), custom_call_target="tpu_custom_call" | custom-call | flops 1000000 | bytes 1048576 | tf_op jit(solution)/shard_map/pallas_call | solution.py:50
  105.9 1.5 collective-permute-start.20
  107.4 1.5 collective-permute-start.23
  109.7 1.2 collective-permute-start.18
  110.9 1.6 %collective-permute-start.21 = (bf16[2,64,768]{2,1,0:T(8,128)(2,1)S(1)}, bf16[2,64,768]{2,1,0:T(8,128)(2,1)S(1)}, u32[]{:S(2)}, u32[]{:S(2)}) collective-permute-start(bf16[2,64,768]{2,1,0:T(8,128)(2,1)S(1)} %pad_maximum_fusion.10), channel_id=1, source_target_pairs={{0,8},{2,10},{4,12},{6,14},{8,0},{10,2},{12,4},{14,6},{16,24},{18,... | collective-permute-start | bytes 589832 | tf_op jit(solution)/shard_map/ppermute | solution.py:28
  112.5 1.3 collective-permute-start.24
  113.8 2.5 %collective-permute-done.18 = bf16[2,64,768]{2,1,0:T(8,128)(2,1)S(1)} collective-permute-done((bf16[2,64,768]{2,1,0:T(8,128)(2,1)S(1)}, bf16[2,64,768]{2,1,0:T(8,128)(2,1)S(1)}, u32[]{:S(2)}, u32[]{:S(2)}) %collective-permute-start.18) | collective-permute-done | bytes 196640 | tf_op jit(solution)/shard_map/ppermute | solution.py:28
  118.5 1.8 %collective-permute-start.25 = (bf16[4,64,768]{2,1,0:T(8,128)(2,1)S(1)}, bf16[4,64,768]{2,1,0:T(8,128)(2,1)S(1)}, u32[]{:S(2)}, u32[]{:S(2)}) collective-permute-start(bf16[4,64,768]{2,1,0:T(8,128)(2,1)S(1)} %pad_maximum_fusion.7.refs_4_), channel_id=1, source_target_pairs={{0,4},{2,6},{4,0},{6,2},{8,12},{10,14},{12,8},{14,10},{16,20},{18,... | collective-permute-start | bytes 1179656 | tf_op jit(solution)/shard_map/ppermute | solution.py:28
  120.4 2.5 %collective-permute-start.27 = (bf16[32,768]{1,0:T(8,128)(2,1)S(1)}, bf16[32,768]{1,0:T(8,128)(2,1)S(1)}, u32[]{:S(2)}, u32[]{:S(2)}) collective-permute-start(bf16[32,768]{1,0:T(8,128)(2,1)S(1)} %get-tuple-element.61), channel_id=1, source_target_pairs={{0,2},{2,4},{4,6},{6,8},{8,10},{10,12},{12,14},{14,16},{16,18},{18... | collective-permute-start | bytes 147464 | tf_op jit(solution)/shard_map/ppermute | solution.py:35
  123.0 1.5 collective-permute-start.28
  124.5 2.5 %collective-permute-done.27.before = bf16[32,768]{1,0:T(8,128)(2,1)S(1)} collective-permute-done((bf16[32,768]{1,0:T(8,128)(2,1)S(1)}, bf16[32,768]{1,0:T(8,128)(2,1)S(1)}, u32[]{:S(2)}, u32[]{:S(2)}) %collective-permute-start.27) | collective-permute-done | bytes 49184 | tf_op jit(solution)/shard_map/ppermute | solution.py:35
  127.0 2.0 %collective-permute-done.28.after = bf16[32,768]{1,0:T(8,128)(2,1)S(1)} collective-permute-done((bf16[32,768]{1,0:T(8,128)(2,1)S(1)}, bf16[32,768]{1,0:T(8,128)(2,1)S(1)}, u32[]{:S(2)}, u32[]{:S(2)}) %collective-permute-start.28) | collective-permute-done | bytes 49184 | tf_op jit(solution)/shard_map/ppermute | solution.py:35
  128.9 3.3 %shard_map.132 = bf16[128,768]{1,0:T(8,128)(2,1)} custom-call(s32[6]{0:T(128)S(1)} %pad_add_fusion.scalars, bf16[256,768]{1,0:T(8,128)(2,1)S(1)} %bitcast.80, bf16[32,768]{1,0:T(8,128)(2,1)S(1)} %collective-permute-done.27.before, bf16[32,768]{1,0:T(8,128)(2,1)S(1)} %collective-permute-done.28.after, f32[49,768]{1,0:T(8,128)S(1)} %reshape.62.taps, ...), custom_call_target="tpu_custom_call" | custom-call | flops 1000000 | bytes 1048576 | tf_op jit(solution)/shard_map/pallas_call | solution.py:50
  132.3 9.0 %shard_map.133 = (f32[48,1536]{1,0:T(8,128)S(1)}, bf16[48,1536]{1,0:T(8,128)(2,1)S(1)}) custom-call(s32[3]{0:T(128)S(1)} %pad_add_fusion.1.scalars, bf16[4,64,768]{2,1,0:T(8,128)(2,1)S(1)} %pad_maximum_fusion.5.refs_0_, bf16[4,64,768]{2,1,0:T(8,128)(2,1)S(1)} %collective-permute-done.19.refs_1_, bf16[4,64,768]{2,1,0:T(8,128)(2,1)S(1)} %pad_maximum_fusion.6.refs_2_, ...), custom_call_target="tpu_custom_call" | custom-call | flops 10000000000 | bytes 1048576 | tf_op jit(solution)/shard_map/pallas_call | solution.py:50
  141.3 4.3 %collective-permute-start.29 = (bf16[48,1536]{1,0:T(8,128)(2,1)S(1)}, bf16[48,1536]{1,0:T(8,128)(2,1)S(1)}, u32[]{:S(2)}, u32[]{:S(2)}) collective-permute-start(bf16[48,1536]{1,0:T(8,128)(2,1)S(1)} %get-tuple-element.51), channel_id=1, source_target_pairs={{0,16},{2,18},{4,20},{6,22},{8,24},{10,26},{12,28},{14,30},{16,0},... | collective-permute-start | bytes 442376 | tf_op jit(solution)/shard_map/ppermute | solution.py:28
  145.5 4.7 %collective-permute-done.29 = bf16[48,1536]{1,0:T(8,128)(2,1)S(1)} collective-permute-done((bf16[48,1536]{1,0:T(8,128)(2,1)S(1)}, bf16[48,1536]{1,0:T(8,128)(2,1)S(1)}, u32[]{:S(2)}, u32[]{:S(2)}) %collective-permute-start.29) | collective-permute-done | bytes 147488 | tf_op jit(solution)/shard_map/ppermute | solution.py:28
  (81 shorter events, 16.3 us)
Async XLA Ops:
  0.6 25.1 %copy-start = (bf16[32,8,768]{2,1,0:T(8,128)(2,1)S(1)}, bf16[32,8,768]{2,1,0:T(8,128)(2,1)}, u32[]{:S(2)}) copy-start(bf16[32,8,768]{2,1,0:T(8,128)(2,1)} %param.10) | copy-start | bytes 1179652
  0.6 25.0 %copy-start.9 = (s32[4,1]{0,1:T(1,128)S(1)}, s32[4,1]{0,1:T(1,128)}, u32[]{:S(2)}) copy-start(s32[4,1]{0,1:T(1,128)} %param.18) | copy-start | bytes 52
  0.7 25.0 %copy-start.6 = (f32[7,7,768]{2,1,0:T(8,128)S(1)}, f32[7,7,768]{2,1,0:T(8,128)}, u32[]{:S(2)}) copy-start(f32[7,7,768]{2,1,0:T(8,128)} %param.12) | copy-start | bytes 451588
  0.7 25.0 %copy-start.7 = (f32[768]{0:T(1024)S(1)}, f32[768]{0:T(1024)}, u32[]{:S(2)}) copy-start(f32[768]{0:T(1024)} %param.13) | copy-start | bytes 9220
  0.7 25.1 %copy-start.8 = (f32[768]{0:T(1024)S(1)}, f32[768]{0:T(1024)}, u32[]{:S(2)}) copy-start(f32[768]{0:T(1024)} %param.17) | copy-start | bytes 9220
  0.7 25.1 %copy-start.1 = (bf16[32,8,768]{2,1,0:T(8,128)(2,1)S(1)}, bf16[32,8,768]{2,1,0:T(8,128)(2,1)}, u32[]{:S(2)}) copy-start(bf16[32,8,768]{2,1,0:T(8,128)(2,1)} %param.11) | copy-start | bytes 1179652
  1.7 13.2 %collective-permute-start.1 = (bf16[2,48,384]{2,1,0:T(8,128)(2,1)S(1)}, bf16[2,48,384]{2,1,0:T(8,128)(2,1)S(1)}, u32[]{:S(2)}, u32[]{:S(2)}) collective-permute-start(bf16[2,48,384]{2,1,0:T(8,128)(2,1)S(1)} %get-tuple-element.70), channel_id=1, source_target_pairs={{0,4},{2,6},{4,0},{6,2},{8,12},{10,14},{12,8},{14,10},{16,20},{18,... | collective-permute-start | bytes 221192 | tf_op jit(solution)/shard_map/ppermute | solution.py:28
  4.8 10.2 %collective-permute-start = (bf16[2,48,384]{2,1,0:T(8,128)(2,1)S(1)}, bf16[2,48,384]{2,1,0:T(8,128)(2,1)S(1)}, u32[]{:S(2)}, u32[]{:S(2)}) collective-permute-start(bf16[2,48,384]{2,1,0:T(8,128)(2,1)S(1)} %get-tuple-element.69), channel_id=1, source_target_pairs={{0,6},{2,4},{4,2},{6,0},{8,14},{10,12},{12,10},{14,8},{16,22},{18,... | collective-permute-start | bytes 221192 | tf_op jit(solution)/shard_map/ppermute | solution.py:28
  6.2 8.8 %collective-permute-start.2 = (bf16[2,48,384]{2,1,0:T(8,128)(2,1)S(1)}, bf16[2,48,384]{2,1,0:T(8,128)(2,1)S(1)}, u32[]{:S(2)}, u32[]{:S(2)}) collective-permute-start(bf16[2,48,384]{2,1,0:T(8,128)(2,1)S(1)} %get-tuple-element.68), channel_id=1, source_target_pairs={{0,2},{2,0},{4,6},{6,4},{8,10},{10,8},{12,14},{14,12},{16,18},{18,... | collective-permute-start | bytes 221192 | tf_op jit(solution)/shard_map/ppermute | solution.py:28
  9.0 6.9 %collective-permute-start.3 = (bf16[32,768]{1,0:T(8,128)(2,1)S(1)}, bf16[32,768]{1,0:T(8,128)(2,1)S(1)}, u32[]{:S(2)}, u32[]{:S(2)}) collective-permute-start(bf16[32,768]{1,0:T(8,128)(2,1)S(1)} %constant_dynamic-slice_fusion), channel_id=1, source_target_pairs={{0,2},{2,4},{4,6},{6,8},{8,10},{10,12},{12,14},{14,16},{16,18},{18... | collective-permute-start | bytes 147464 | tf_op jit(solution)/shard_map/ppermute | solution.py:35
  13.6 6.0 %collective-permute-start.4 = (bf16[32,768]{1,0:T(8,128)(2,1)S(1)}, bf16[32,768]{1,0:T(8,128)(2,1)S(1)}, u32[]{:S(2)}, u32[]{:S(2)}) collective-permute-start(bf16[32,768]{1,0:T(8,128)(2,1)S(1)} %slice_bitcast_fusion.14), channel_id=1, source_target_pairs={{2,0},{4,2},{6,4},{8,6},{10,8},{12,10},{14,12},{16,14},{18,16},{20... | collective-permute-start | bytes 147464 | tf_op jit(solution)/shard_map/ppermute | solution.py:35
  19.6 14.5 %collective-permute-start.9 = (bf16[1,2,192,384]{3,2,1,0:T(8,128)(2,1)S(1)}, bf16[1,2,192,384]{3,2,1,0:T(8,128)(2,1)S(1)}, u32[]{:S(2)}, u32[]{:S(2)}) collective-permute-start(bf16[1,2,192,384]{3,2,1,0:T(8,128)(2,1)S(1)} %bitcast.89), channel_id=1, source_target_pairs={{0,16},{2,18},{4,20},{6,22},{8,24},{10,26},{12,28},{14,30},{16,0},... | collective-permute-start | bytes 884744 | tf_op jit(solution)/shard_map/ppermute | solution.py:28
  28.7 9.9 %collective-permute-start.5 = (bf16[2,128,768]{2,1,0:T(8,128)(2,1)S(1)}, bf16[2,128,768]{2,1,0:T(8,128)(2,1)S(1)}, u32[]{:S(2)}, u32[]{:S(2)}) collective-permute-start(bf16[2,128,768]{2,1,0:T(8,128)(2,1)S(1)} %get-tuple-element.30), channel_id=1, source_target_pairs={{0,2},{2,0},{4,6},{6,4},{8,10},{10,8},{12,14},{14,12},{16,18},{18,... | collective-permute-start | bytes 1179656 | tf_op jit(solution)/shard_map/ppermute | solution.py:28
  28.8 16.2 %collective-permute-start.6 = (bf16[2,128,768]{2,1,0:T(8,128)(2,1)S(1)}, bf16[2,128,768]{2,1,0:T(8,128)(2,1)S(1)}, u32[]{:S(2)}, u32[]{:S(2)}) collective-permute-start(bf16[2,128,768]{2,1,0:T(8,128)(2,1)S(1)} %get-tuple-element.30), channel_id=1, source_target_pairs={{0,4},{2,6},{4,0},{6,2},{8,12},{10,14},{12,8},{14,10},{16,20},{18,... | collective-permute-start | bytes 1179656 | tf_op jit(solution)/shard_map/ppermute | solution.py:28
  30.7 14.2 %collective-permute-start.7 = (bf16[2,128,768]{2,1,0:T(8,128)(2,1)S(1)}, bf16[2,128,768]{2,1,0:T(8,128)(2,1)S(1)}, u32[]{:S(2)}, u32[]{:S(2)}) collective-permute-start(bf16[2,128,768]{2,1,0:T(8,128)(2,1)S(1)} %get-tuple-element.30), channel_id=1, source_target_pairs={{0,6},{2,4},{4,2},{6,0},{8,14},{10,12},{12,10},{14,8},{16,22},{18,... | collective-permute-start | bytes 1179656 | tf_op jit(solution)/shard_map/ppermute | solution.py:28
  35.0 14.1 %collective-permute-start.10 = (bf16[2,2,192,384]{3,2,1,0:T(8,128)(2,1)}, bf16[2,2,192,384]{3,2,1,0:T(8,128)(2,1)}, u32[]{:S(2)}, u32[]{:S(2)}) collective-permute-start(bf16[2,2,192,384]{3,2,1,0:T(8,128)(2,1)} %pad_maximum_fusion.4), channel_id=1, source_target_pairs={{0,8},{2,10},{4,12},{6,14},{8,0},{10,2},{12,4},{14,6},{16,24},{18,... | collective-permute-start | bytes 1769480 | tf_op jit(solution)/shard_map/ppermute | solution.py:28
  44.9 1.3 copy-start.4
  46.3 4.1 %collective-permute-start.8 = (bf16[2,512,768]{2,1,0:T(8,128)(2,1)}, bf16[2,512,768]{2,1,0:T(8,128)(2,1)}, u32[]{:S(2)}, u32[]{:S(2)}) collective-permute-start(bf16[2,512,768]{2,1,0:T(8,128)(2,1)} %pad_maximum_fusion.1), channel_id=1, source_target_pairs={{0,1},{1,0},{2,3},{3,2},{4,5},{5,4},{6,7},{7,6},{8,9},{9,8},{10,11... | collective-permute-start | bytes 4718600 | tf_op jit(solution)/shard_map/ppermute | solution.py:28
  46.3 1.0 copy-start.5
  57.0 4.1 %copy-start.2 = (f32[1024,768]{1,0:T(8,128)}, f32[1024,768]{1,0:T(8,128)S(1)}, u32[]{:S(2)}) copy-start(f32[1024,768]{1,0:T(8,128)S(1)} %fusion.27) | copy-start | bytes 9437188
  58.0 1.7 %copy-start.3 = (f32[1024,768]{1,0:T(8,128)}, f32[1024,768]{1,0:T(8,128)S(1)}, u32[]{:S(2)}) copy-start(f32[1024,768]{1,0:T(8,128)S(1)} %fusion.28) | copy-start | bytes 9437188
  61.1 18.2 %collective-permute-start.11 = (bf16[2,4,128,768]{3,2,0,1:T(8,128)(2,1)}, bf16[2,4,128,768]{3,2,0,1:T(8,128)(2,1)}, u32[]{:S(2)}, u32[]{:S(2)}) collective-permute-start(bf16[2,4,128,768]{3,2,0,1:T(8,128)(2,1)} %fusion.11), channel_id=1, source_target_pairs={{0,1},{1,0},{2,3},{3,2},{4,5},{5,4},{6,7},{7,6},{8,9},{9,8},{10,11... | collective-permute-start | bytes 4718600 | tf_op jit(solution)/shard_map/ppermute | solution.py:28
  62.0 16.1 %collective-permute-start.15 = (bf16[2,192,768]{2,1,0:T(8,128)(2,1)}, bf16[2,192,768]{2,1,0:T(8,128)(2,1)}, u32[]{:S(2)}, u32[]{:S(2)}) collective-permute-start(bf16[2,192,768]{2,1,0:T(8,128)(2,1)} %dynamic-slice_bitcast_fusion), channel_id=1, source_target_pairs={{0,8},{2,10},{4,12},{6,14},{8,0},{10,2},{12,4},{14,6},{16,24},{18,... | collective-permute-start | bytes 1769480 | tf_op jit(solution)/shard_map/ppermute | solution.py:28
  82.1 12.1 %collective-permute-start.12 = (bf16[2,128,768]{2,1,0:T(8,128)(2,1)S(1)}, bf16[2,128,768]{2,1,0:T(8,128)(2,1)S(1)}, u32[]{:S(2)}, u32[]{:S(2)}) collective-permute-start(bf16[2,128,768]{2,1,0:T(8,128)(2,1)S(1)} %get-tuple-element.56), channel_id=1, source_target_pairs={{0,2},{2,0},{4,6},{6,4},{8,10},{10,8},{12,14},{14,12},{16,18},{18,... | collective-permute-start | bytes 1179656 | tf_op jit(solution)/shard_map/ppermute | solution.py:28
  84.2 17.6 %collective-permute-start.13 = (bf16[2,128,768]{2,1,0:T(8,128)(2,1)S(1)}, bf16[2,128,768]{2,1,0:T(8,128)(2,1)S(1)}, u32[]{:S(2)}, u32[]{:S(2)}) collective-permute-start(bf16[2,128,768]{2,1,0:T(8,128)(2,1)S(1)} %get-tuple-element.55), channel_id=1, source_target_pairs={{0,4},{2,6},{4,0},{6,2},{8,12},{10,14},{12,8},{14,10},{16,20},{18,... | collective-permute-start | bytes 1179656 | tf_op jit(solution)/shard_map/ppermute | solution.py:28
  85.3 17.8 %collective-permute-start.14 = (bf16[2,128,768]{2,1,0:T(8,128)(2,1)S(1)}, bf16[2,128,768]{2,1,0:T(8,128)(2,1)S(1)}, u32[]{:S(2)}, u32[]{:S(2)}) collective-permute-start(bf16[2,128,768]{2,1,0:T(8,128)(2,1)S(1)} %get-tuple-element.54), channel_id=1, source_target_pairs={{0,6},{2,4},{4,2},{6,0},{8,14},{10,12},{12,10},{14,8},{16,22},{18,... | collective-permute-start | bytes 1179656 | tf_op jit(solution)/shard_map/ppermute | solution.py:28
  86.0 18.9 %collective-permute-start.16 = (bf16[1,192,768]{2,1,0:T(8,128)(2,1)S(1)}, bf16[1,192,768]{2,1,0:T(8,128)(2,1)S(1)}, u32[]{:S(2)}, u32[]{:S(2)}) collective-permute-start(bf16[1,192,768]{2,1,0:T(8,128)(2,1)S(1)} %dynamic-slice_convert_fusion), channel_id=1, source_target_pairs={{0,16},{2,18},{4,20},{6,22},{8,24},{10,26},{12,28},{14,30},{16,0},... | collective-permute-start | bytes 884744 | tf_op jit(solution)/shard_map/ppermute | solution.py:28
  105.0 4.7 %collective-permute-start.17 = (bf16[1,64,768]{2,1,0:T(8,128)(2,1)S(1)}, bf16[1,64,768]{2,1,0:T(8,128)(2,1)S(1)}, u32[]{:S(2)}, u32[]{:S(2)}) collective-permute-start(bf16[1,64,768]{2,1,0:T(8,128)(2,1)S(1)} %get-tuple-element.64), channel_id=1, source_target_pairs={{0,2},{2,0},{4,6},{6,4},{8,10},{10,8},{12,14},{14,12},{16,18},{18,... | collective-permute-start | bytes 294920 | tf_op jit(solution)/shard_map/ppermute | solution.py:28
  105.9 5.0 %collective-permute-start.20 = (bf16[1,64,768]{2,1,0:T(8,128)(2,1)S(1)}, bf16[1,64,768]{2,1,0:T(8,128)(2,1)S(1)}, u32[]{:S(2)}, u32[]{:S(2)}) collective-permute-start(bf16[1,64,768]{2,1,0:T(8,128)(2,1)S(1)} %get-tuple-element.63), channel_id=1, source_target_pairs={{0,4},{2,6},{4,0},{6,2},{8,12},{10,14},{12,8},{14,10},{16,20},{18,... | collective-permute-start | bytes 294920 | tf_op jit(solution)/shard_map/ppermute | solution.py:28
  107.4 5.1 %collective-permute-start.23 = (bf16[1,64,768]{2,1,0:T(8,128)(2,1)S(1)}, bf16[1,64,768]{2,1,0:T(8,128)(2,1)S(1)}, u32[]{:S(2)}, u32[]{:S(2)}) collective-permute-start(bf16[1,64,768]{2,1,0:T(8,128)(2,1)S(1)} %get-tuple-element.62), channel_id=1, source_target_pairs={{0,8},{2,10},{4,12},{6,14},{8,0},{10,2},{12,4},{14,6},{16,24},{18,... | collective-permute-start | bytes 294920 | tf_op jit(solution)/shard_map/ppermute | solution.py:28
  108.9 11.5 %collective-permute-start.26 = (bf16[128,768]{1,0:T(8,128)(2,1)S(1)}, bf16[128,768]{1,0:T(8,128)(2,1)S(1)}, u32[]{:S(2)}, u32[]{:S(2)}) collective-permute-start(bf16[128,768]{1,0:T(8,128)(2,1)S(1)} %get-tuple-element.42.rest_0_), channel_id=1, source_target_pairs={{0,1},{1,0},{2,3},{3,2},{4,5},{5,4},{6,7},{7,6},{8,9},{9,8},{10,11... | collective-permute-start | bytes 589832 | tf_op jit(solution)/shard_map/ppermute | solution.py:28
  109.7 6.6 %collective-permute-start.18 = (bf16[2,64,768]{2,1,0:T(8,128)(2,1)S(1)}, bf16[2,64,768]{2,1,0:T(8,128)(2,1)S(1)}, u32[]{:S(2)}, u32[]{:S(2)}) collective-permute-start(bf16[2,64,768]{2,1,0:T(8,128)(2,1)S(1)} %pad_maximum_fusion.9), channel_id=1, source_target_pairs={{0,4},{2,6},{4,0},{6,2},{8,12},{10,14},{12,8},{14,10},{16,20},{18,... | collective-permute-start | bytes 589832 | tf_op jit(solution)/shard_map/ppermute | solution.py:28
  110.9 6.1 %collective-permute-start.21 = (bf16[2,64,768]{2,1,0:T(8,128)(2,1)S(1)}, bf16[2,64,768]{2,1,0:T(8,128)(2,1)S(1)}, u32[]{:S(2)}, u32[]{:S(2)}) collective-permute-start(bf16[2,64,768]{2,1,0:T(8,128)(2,1)S(1)} %pad_maximum_fusion.10), channel_id=1, source_target_pairs={{0,8},{2,10},{4,12},{6,14},{8,0},{10,2},{12,4},{14,6},{16,24},{18,... | collective-permute-start | bytes 589832 | tf_op jit(solution)/shard_map/ppermute | solution.py:28
  112.5 6.0 %collective-permute-start.24 = (bf16[2,64,768]{2,1,0:T(8,128)(2,1)S(1)}, bf16[2,64,768]{2,1,0:T(8,128)(2,1)S(1)}, u32[]{:S(2)}, u32[]{:S(2)}) collective-permute-start(bf16[2,64,768]{2,1,0:T(8,128)(2,1)S(1)} %pad_maximum_fusion.11), channel_id=1, source_target_pairs={{0,2},{2,0},{4,6},{6,4},{8,10},{10,8},{12,14},{14,12},{16,18},{18,... | collective-permute-start | bytes 589832 | tf_op jit(solution)/shard_map/ppermute | solution.py:28
  116.3 15.9 %collective-permute-start.19 = (bf16[4,64,768]{2,1,0:T(8,128)(2,1)S(1)}, bf16[4,64,768]{2,1,0:T(8,128)(2,1)S(1)}, u32[]{:S(2)}, u32[]{:S(2)}) collective-permute-start(bf16[4,64,768]{2,1,0:T(8,128)(2,1)S(1)} %pad_maximum_fusion.5.refs_0_), channel_id=1, source_target_pairs={{0,8},{2,10},{4,12},{6,14},{8,0},{10,2},{12,4},{14,6},{16,24},{18,... | collective-permute-start | bytes 1179656 | tf_op jit(solution)/shard_map/ppermute | solution.py:28
  117.1 15.2 %collective-permute-start.22 = (bf16[4,64,768]{2,1,0:T(8,128)(2,1)S(1)}, bf16[4,64,768]{2,1,0:T(8,128)(2,1)S(1)}, u32[]{:S(2)}, u32[]{:S(2)}) collective-permute-start(bf16[4,64,768]{2,1,0:T(8,128)(2,1)S(1)} %pad_maximum_fusion.6.refs_2_), channel_id=1, source_target_pairs={{0,2},{2,0},{4,6},{6,4},{8,10},{10,8},{12,14},{14,12},{16,18},{18,... | collective-permute-start | bytes 1179656 | tf_op jit(solution)/shard_map/ppermute | solution.py:28
  118.5 13.7 %collective-permute-start.25 = (bf16[4,64,768]{2,1,0:T(8,128)(2,1)S(1)}, bf16[4,64,768]{2,1,0:T(8,128)(2,1)S(1)}, u32[]{:S(2)}, u32[]{:S(2)}) collective-permute-start(bf16[4,64,768]{2,1,0:T(8,128)(2,1)S(1)} %pad_maximum_fusion.7.refs_4_), channel_id=1, source_target_pairs={{0,4},{2,6},{4,0},{6,2},{8,12},{10,14},{12,8},{14,10},{16,20},{18,... | collective-permute-start | bytes 1179656 | tf_op jit(solution)/shard_map/ppermute | solution.py:28
  120.4 6.6 %collective-permute-start.27 = (bf16[32,768]{1,0:T(8,128)(2,1)S(1)}, bf16[32,768]{1,0:T(8,128)(2,1)S(1)}, u32[]{:S(2)}, u32[]{:S(2)}) collective-permute-start(bf16[32,768]{1,0:T(8,128)(2,1)S(1)} %get-tuple-element.61), channel_id=1, source_target_pairs={{0,2},{2,4},{4,6},{6,8},{8,10},{10,12},{12,14},{14,16},{16,18},{18... | collective-permute-start | bytes 147464 | tf_op jit(solution)/shard_map/ppermute | solution.py:35
  123.0 6.0 %collective-permute-start.28 = (bf16[32,768]{1,0:T(8,128)(2,1)S(1)}, bf16[32,768]{1,0:T(8,128)(2,1)S(1)}, u32[]{:S(2)}, u32[]{:S(2)}) collective-permute-start(bf16[32,768]{1,0:T(8,128)(2,1)S(1)} %get-tuple-element.60), channel_id=1, source_target_pairs={{2,0},{4,2},{6,4},{8,6},{10,8},{12,10},{14,12},{16,14},{18,16},{20... | collective-permute-start | bytes 147464 | tf_op jit(solution)/shard_map/ppermute | solution.py:35
  141.3 9.0 %collective-permute-start.29 = (bf16[48,1536]{1,0:T(8,128)(2,1)S(1)}, bf16[48,1536]{1,0:T(8,128)(2,1)S(1)}, u32[]{:S(2)}, u32[]{:S(2)}) collective-permute-start(bf16[48,1536]{1,0:T(8,128)(2,1)S(1)} %get-tuple-element.51), channel_id=1, source_target_pairs={{0,16},{2,18},{4,20},{6,22},{8,24},{10,26},{12,28},{14,30},{16,0},... | collective-permute-start | bytes 442376 | tf_op jit(solution)/shard_map/ppermute | solution.py:28

commit v5 on v4

--- a/solution.py
+++ b/solution.py
@@ -1,3 +1,5 @@
+import functools
+
 import jax
 import jax.numpy as jnp
 from jax import lax
@@ -166,14 +168,100 @@
     grad_mixed[...] = jnp.where(live, value, 0.0).astype(BF16)
 
 
-def weights_kernel(scalars, held, up, down_t):
-    lines, _, rows, _ = held.shape
+def join_kernel(*refs):
+    *blocks, out = refs
+    start = 0
+    for ref in blocks:
+        out[:, start : start + ref.shape[1], :] = ref[...]
+        start += ref.shape[1]
+
+
+def double_kernel(*refs):
+    count = len(refs) // 3
+    for held, came, out in zip(refs[:count], refs[count : 2 * count], refs[2 * count :]):
+        out[: held.shape[0]] = held[...]
+        out[held.shape[0] :] = came[...]
+
+
+def piece_kernel(scalars, *refs):
+    *blocks, out = refs
+    rows = blocks[0].shape[1]
+    for s, block in enumerate(blocks):
+        start = pl.multiple_of((scalars[0] ^ s) * rows, rows)
+        out[:, pl.ds(start, rows), :] = block[...]
+
+
+def weights_kernel(scalars, early, late, up, down_t):
+    lines, rows = 2 * early.shape[0], early.shape[2]
     bits = lines.bit_length() - 1
     for e in range(lines):
         apart = sum(lines >> (i + 1) for i in range(bits) if e >> i & 1)
         start = pl.multiple_of((scalars[0] ^ apart) * rows, rows)
-        up[pl.ds(start, rows), :] = held[e, 0]
-        down_t[pl.ds(start, rows), :] = held[e, 1]
+        later, entry = divmod(e, lines // 2)
+        piece = (early, late)[later]
+        up[pl.ds(start, rows), :] = piece[entry, 0]
+        down_t[pl.ds(start, rows), :] = piece[entry, 1]
+
+
+def mlp_kernel(scalars, up, down_t, bias, *refs, owners):
+    tokens_of = refs[:owners]
+    kept, sent, act_out, grad_out, parts = refs[owners:]
+    lines = 2 * kept.shape[0]
+    plain, over_tokens = ((1,), (0,)), ((0,), (0,))
+    count = tokens_of[0].shape[1]
+    step = min(256, count)
+    for index, ref in enumerate(tokens_of):
+        for start in range(0, count, step):
+            hidden = dot(ref[0, start : start + step, :], up[...], plain) + bias[...]
+            cdf = 0.5 * (1.0 + lax.erf(hidden * INV_ROOT_TWO))
+            slope = cdf + hidden * jnp.exp(-0.5 * hidden * hidden) * INV_ROOT_TAU
+            grad_act = dot(ref[1, start : start + step, :], down_t[...], plain)
+            rows_out = pl.ds(index * count + start, step)
+            act_out[rows_out, :] = (hidden * cdf).astype(BF16)
+            grad_out[rows_out, :] = (grad_act * slope).astype(BF16)
+
+    units = act_out.shape[1]
+    for half, (hidden_side, which) in enumerate(((grad_out, 0), (act_out, 1))):
+        total = jnp.zeros((units, parts.shape[1]), F32)
+        for index, ref in enumerate(tokens_of):
+            rows_in = slice(index * count, (index + 1) * count)
+            total = total + dot(hidden_side[rows_in, :], ref[which], over_tokens)
+        parts[half * units : (half + 1) * units, :] = total
+    width = kept.shape[1]
+    for q in range(lines):
+        block = parts[q * width : (q + 1) * width, :].astype(BF16)
+        same = scalars[0] == q % 2
+
+        @pl.when(same)
+        def _():
+            kept[q // 2] = block
+
+        @pl.when(jnp.logical_not(same))
+        def _():
+            sent[q // 2] = block
+
+
+def partial_kernel(act, grad_hidden, up, down_t, mine, *others):
+    across = ((1,), (1,))
+    count = mine.shape[1]
+    step = min(256, count)
+    for index, ref in enumerate((mine,) + others):
+        for start in range(0, count, step):
+            rows_in = slice(index * count + start, index * count + start + step)
+            rows_out = slice(start, start + step)
+            ref[0, rows_out, :] = dot(grad_hidden[rows_in, :], up[...], across).astype(ref.dtype)
+            ref[1, rows_out, :] = dot(act[rows_in, :], down_t[...], across).astype(ref.dtype)
+
+
+def add_kernel(mine, *refs):
+    others, outs = refs[:-PLANE], refs[-PLANE:]
+    tokens = outs[0].shape[1]
+    for strip, out in enumerate(outs):
+        rows_in = slice(strip * tokens, (strip + 1) * tokens)
+        total = mine[:, rows_in, :]
+        for other in others:
+            total = total + other[:, rows_in, :].astype(F32)
+        out[...] = total.astype(BF16)
 
 
 def backward_kernel(scalars, cotangent, before, after, taps, *rest):
@@ -315,27 +403,27 @@
     wide = pltpu.VMEM((share, columns, channels), F32)
     rim = RIM * columns
 
+    height = channels // tiles
     units = weight_up.shape[1] // PLANE
     both_weights = jnp.stack([weight_up, weight_down.T])
     pieces = []
     for s in range(PLANE):
         piece = lax.dynamic_slice_in_dim(both_weights, (place ^ s) * units, units, 2)
         pieces.append(swap(piece, "tile", s) if s else piece)
-    piece = jnp.concatenate(in_order(pieces, place), 1)
+    if height % 16:
+        piece = jnp.concatenate(in_order(pieces, place), 1)
+    else:
+        (piece,) = call(
+            piece_kernel,
+            [jax.ShapeDtypeStruct((2, PLANE * height, units), BF16)],
+            [],
+            10**6,
+            place[None], *pieces,
+        )
 
     tail = lax.dynamic_slice_in_dim(strip, (live_rows - RIM) * columns, rim, 0)
     before, after = neighbours(strip[:rim], tail)
     piece, before, after = lax.optimization_barrier((piece, before, after))
-    held = piece[None]
-    for bit in line_bits[::-1]:
-        held = jnp.concatenate([held, swap(held, "tile", PLANE * bit)], 0)
-    up, down_t = call(
-        weights_kernel,
-        [jax.ShapeDtypeStruct((channels, units), BF16)] * 2,
-        [],
-        10 * 10**9,
-        line[None], held,
-    )
     bias = lax.dynamic_slice_in_dim(bias_up, place * units, units, 0)
 
     sent, centred, inverse = call(
@@ -349,50 +437,81 @@
         10**6,
         scalars, strip, cotangent.reshape(strip.shape), before, after, taps, gain, scale,
     )
-    mine = jnp.concatenate([sent] + [swap(sent, "tile", s) for s in range(1, PLANE)], 1)
-    both = jnp.concatenate([mine] + [swap(mine, "own", s) for s in range(1, owners)], 1)
-    normed, grad_branch = both[0], both[1]
-
-    plain, across, over_tokens = ((1,), (0,)), ((1,), (1,)), ((0,), (0,))
-    hidden = dot(normed, up, plain) + bias
-    cdf = 0.5 * (1.0 + lax.erf(hidden * INV_ROOT_TWO))
-    act = (hidden * cdf).astype(BF16)
-    slope = cdf + hidden * jnp.exp(-0.5 * hidden * hidden) * INV_ROOT_TAU
-    grad_hidden = (dot(grad_branch, down_t, plain) * slope).astype(BF16)
-
-    parts = jnp.concatenate(
-        [dot(grad_hidden, normed, over_tokens), dot(act, grad_branch, over_tokens)], 0
-    ).astype(BF16)
-    parts, grad_hidden, act = lax.optimization_barrier((parts, grad_hidden, act))
+    held = piece[None]
+    for bit in line_bits[:0:-1]:
+        shape = jax.ShapeDtypeStruct((2 * held.shape[0],) + held.shape[1:], BF16)
+        came = swap(held, "tile", PLANE * bit)
+        (held,) = call(double_kernel, [shape], [], 10**6, held, came, scalars=0)
+    late = swap(held, "tile", PLANE)
+    (mine,) = call(
+        join_kernel,
+        [jax.ShapeDtypeStruct((2, PLANE * tokens, channels), BF16)],
+        [],
+        10**6,
+        sent, *[swap(sent, "tile", s) for s in range(1, PLANE)],
+        scalars=0,
+    )
+    shares = [mine] + [swap(mine, "own", s) for s in range(1, owners)]
+
     kept = 2 * units // lines
-    reduced = parts.reshape(lines, kept, channels)
+    total_tokens = owners * PLANE * tokens
+    half_parts = jax.ShapeDtypeStruct((lines // 2, kept, channels), BF16)
+    hidden_shape = jax.ShapeDtypeStruct((total_tokens, units), BF16)
+    weight_shape = jax.ShapeDtypeStruct((channels, units), BF16)
+    up, down_t = call(
+        weights_kernel, [weight_shape, weight_shape], [], 13 * 10**9, line[None], held, late
+    )
+    reduced, other, act, grad_hidden = call(
+        functools.partial(mlp_kernel, owners=owners),
+        [half_parts, half_parts, hidden_shape, hidden_shape],
+        [pltpu.VMEM((2 * units, channels), F32)],
+        5 * 10**9,
+        (line & 1)[None], up, down_t, bias[None], *shares,
+    )
 
     def split(blocks, bit):
         blocks = blocks.reshape(-1, 2, kept, channels)
         which = jnp.where((line & bit) != 0, 1, 0)
         mine = lax.dynamic_slice_in_dim(blocks, which, 1, 1)
         other = lax.dynamic_slice_in_dim(blocks, 1 - which, 1, 1)
-        return mine[:, 0].astype(F32), other[:, 0].astype(BF16)
-
-    for bit in line_bits[:-1]:
+        return mine[:, 0], other[:, 0].astype(BF16)
+
+    arrived = swap(other, "tile", PLANE)
+
+    part_shape = (2, PLANE * tokens, channels)
+    mine, *others = call(
+        partial_kernel,
+        [jax.ShapeDtypeStruct(part_shape, F32)]
+        + [jax.ShapeDtypeStruct(part_shape, BF16)] * (owners - 1),
+        [],
+        10**9,
+        act, grad_hidden, up, down_t,
+        scalars=0,
+    )
+    others = [swap(value, "own", s + 1) for s, value in enumerate(others)]
+    total, *moved = call(
+        add_kernel,
+        [jax.ShapeDtypeStruct((2, tokens, channels), BF16)] * PLANE,
+        [],
+        10**6,
+        mine, *others,
+        scalars=0,
+    )
+    moved = [swap(value, "tile", s + 1) for s, value in enumerate(moved)]
+    arrived, moved[0] = lax.optimization_barrier((arrived, moved[0]))
+    reduced = reduced.astype(F32) + arrived.astype(F32)
+    for bit in line_bits[1:-1]:
         reduced, other = split(reduced, bit)
         reduced = reduced + swap(other, "tile", PLANE * bit).astype(F32)
     reduced, other = split(reduced, line_bits[-1])
     arrived = swap(other, "tile", PLANE * line_bits[-1])
 
-    partial = jnp.stack([dot(grad_hidden, up, across), dot(act, down_t, across)])
-    partial = partial.reshape(2, owners, PLANE, tokens, channels)
-    total = partial[:, 0]
-    for s in range(1, owners):
-        total = total + swap(partial[:, s].astype(BF16), "own", s).astype(F32)
-    total = total.astype(BF16)
-    moved = [swap(total[:, s], "tile", s) for s in range(1, PLANE)]
     grad_mixed, block_out = call(
         middle_kernel,
         [jax.ShapeDtypeStruct((tokens, channels), BF16)] * 2,
         [],
         10**6,
-        scalars, strip, total[:, 0], *moved, centred, inverse, gain, scale,
+        scalars, strip, total, *moved, centred, inverse, gain, scale,
     )
 
     arrived, grad_mixed = lax.optimization_barrier((arrived, grad_mixed))
@@ -400,13 +519,14 @@
     group = PLANE * half_lines
     bits = [1 << i for i in range(group.bit_length() - 1)]
     third = kept // 3
-    thirds = []
-    for turn in range(3):
-        held = grad_t[turn * third : (turn + 1) * third][None]
-        order = bits[turn:] + bits[:turn]
-        for bit in order[:-1]:
-            held = jnp.concatenate([held, swap(held, "tile", bit)], 0)
-        thirds += [held, swap(held, "tile", order[-1])]
+    helds = [grad_t[turn * third : (turn + 1) * third][None] for turn in range(3)]
+    orders = [bits[turn:] + bits[:turn] for turn in range(3)]
+    for stage in range(len(bits)):
+        came = [swap(held, "tile", order[stage]) for held, order in zip(helds, orders)]
+        if stage + 1 < len(bits):
+            shape = jax.ShapeDtypeStruct((2 << stage, third, channels), BF16)
+            helds = call(double_kernel, [shape] * 3, [], 10**6, *helds, *came, scalars=0)
+    thirds = [half for pair in zip(helds, came) for half in pair]
 
     halves = [grad_mixed] + [swap(grad_mixed, "own", s) for s in range(1, owners)]
     stacked = jnp.stack(halves)
@@ -424,7 +544,6 @@
         scalars, cotangent.reshape(strip.shape), before, after, taps, *halves,
     )
 
-    height = channels // tiles
     other = tile ^ (PLANE * half_lines)
     square = pltpu.VMEM((channels, channels), F32)
     thirds, grad_features = lax.optimization_barrier((thirds, grad_features))

time: 152 us -> 141 us (0.928)
  Pallas kernels: 17.1 us -> 27.4 us
  other arithmetic: 12 us -> 3.43 us
  matrix products: 6 us -> 0 us
  starting transfers between devices: 49.5 us -> 45.3 us
  local copies, waits for them, and re-layouts: 8.16 us -> 5.15 us
    pallas_call x5 -> x13, Pallas kernels: 17.1 us -> 27.4 us  [call(): pl.pallas_call(kernel, out_shape=out_shape, in_specs=[smem] * scalars + [...]
    dot_general x6 -> x0, matrix products: 6 us -> none  [dot(): lax.dot_general(left, right, (contract, ((), ())), precision=precision, p...]
    ppermute x26, starting transfers between devices: 40.4 us -> 35.4 us  [swap(): lax.ppermute(value, axis, [(i, i ^ bit) for i in range(lax.axis_size(axis...]
    convert_element_type x2 -> x0, other arithmetic: 4.11 us -> none  [the longest x1 2.71 us: shards(): total = total.astype(BF16)]
    concatenate x11 -> x0, other arithmetic: 3.68 us -> none  [the longest x2 2.09 us: shards(): held = jnp.concatenate([held, swap(held, 'tile', PLANE * bit)], 0)]
  transfers between devices with their start and end apart: 30 -> 30, of which waited for: 15 -> 19; matrix products, arithmetic and copies ran while one was open for 7% -> 4% of each run, Pallas kernels for 5% -> 7%
where the time goes in v5:
time: 141 us; the launch traced here: 140 us
  waiting for transfers between devices  57.6 us (41%)
  starting transfers between devices  45.3 us (32%)
  Pallas kernels  27.4 us (19%)
  local copies, waits for them, and re-layouts  5.15 us (4%)
  other arithmetic  3.43 us (2%)
  between operations  1.61 us (1%)
    ppermute x26, waiting for transfers between devices, swap(): lax.ppermute(value, axis, [(i, i ^ bit) for i in range(lax.axis_size(axis...  48.5 us
    ppermute x26, starting transfers between devices, swap(): lax.ppermute(value, axis, [(i, i ^ bit) for i in range(lax.axis_size(axis...  35.4 us
    pallas_call x13, Pallas kernels, call(): pl.pallas_call(kernel, out_shape=out_shape, in_specs=[smem] * scalars + [...  27.4 us
    ppermute x4, starting transfers between devices, neighbours(): return (lax.ppermute(last, 'tile', up), lax.ppermute(first, 'tile', down))  9.91 us
    ppermute x4, waiting for transfers between devices, neighbours(): return (lax.ppermute(last, 'tile', up), lax.ppermute(first, 'tile', down))  9.03 us
  transfers between devices with their start and end apart: 30, of which 19 were waited for; matrix products, arithmetic and copies ran while one was open for 4% of the time, Pallas kernels for 7%

profile of v5, /device:TPU:0, one launch (start us, length us, event | category | flops | bytes accessed | tf_op | source)
XLA Modules:
  0.0 140.4 jit_solution(222013885664933145)
XLA Ops:
  0.7 1.1 fusion.1
  1.8 3.0 %collective-permute-start = (bf16[2,48,384]{2,1,0:T(8,128)(2,1)S(1)}, bf16[2,48,384]{2,1,0:T(8,128)(2,1)S(1)}, u32[]{:S(2)}, u32[]{:S(2)}) collective-permute-start(bf16[2,48,384]{2,1,0:T(8,128)(2,1)S(1)} %get-tuple-element.91), channel_id=1, source_target_pairs={{0,2},{2,0},{4,6},{6,4},{8,10},{10,8},{12,14},{14,12},{16,18},{18,... | collective-permute-start | bytes 221192 | tf_op jit(solution)/shard_map/ppermute | solution.py:30
  4.8 1.5 %collective-permute-start.1 = (bf16[2,48,384]{2,1,0:T(8,128)(2,1)S(1)}, bf16[2,48,384]{2,1,0:T(8,128)(2,1)S(1)}, u32[]{:S(2)}, u32[]{:S(2)}) collective-permute-start(bf16[2,48,384]{2,1,0:T(8,128)(2,1)S(1)} %get-tuple-element.92), channel_id=1, source_target_pairs={{0,4},{2,6},{4,0},{6,2},{8,12},{10,14},{12,8},{14,10},{16,20},{18,... | collective-permute-start | bytes 221192 | tf_op jit(solution)/shard_map/ppermute | solution.py:30
  6.3 1.2 dynamic_slice.29
  9.0 3.8 %collective-permute-start.3 = (bf16[32,768]{1,0:T(8,128)(2,1)S(1)}, bf16[32,768]{1,0:T(8,128)(2,1)S(1)}, u32[]{:S(2)}, u32[]{:S(2)}) collective-permute-start(bf16[32,768]{1,0:T(8,128)(2,1)S(1)} %constant_dynamic-slice_fusion), channel_id=1, source_target_pairs={{0,2},{2,4},{4,6},{6,8},{8,10},{10,12},{12,14},{14,16},{16,18},{18... | collective-permute-start | bytes 147464 | tf_op jit(solution)/shard_map/ppermute | solution.py:37
  13.7 1.3 collective-permute-start.4
  15.1 4.6 %collective-permute-done.4.after = bf16[32,768]{1,0:T(8,128)(2,1)S(1)} collective-permute-done((bf16[32,768]{1,0:T(8,128)(2,1)S(1)}, bf16[32,768]{1,0:T(8,128)(2,1)S(1)}, u32[]{:S(2)}, u32[]{:S(2)}) %collective-permute-start.4) | collective-permute-done | bytes 49184 | tf_op jit(solution)/shard_map/ppermute | solution.py:37
  19.7 6.0 %collective-permute-start.5 = (bf16[1,2,192,384]{3,2,1,0:T(8,128)(2,1)S(1)}, bf16[1,2,192,384]{3,2,1,0:T(8,128)(2,1)S(1)}, u32[]{:S(2)}, u32[]{:S(2)}) collective-permute-start(bf16[1,2,192,384]{3,2,1,0:T(8,128)(2,1)S(1)} %bitcast.35), channel_id=1, source_target_pairs={{0,16},{2,18},{4,20},{6,22},{8,24},{10,26},{12,28},{14,30},{16,0},... | collective-permute-start | bytes 884744 | tf_op jit(solution)/shard_map/ppermute | solution.py:30
  25.8 2.9 %shard_map.132 = (bf16[2,128,768]{2,1,0:T(8,128)(2,1)S(1)}, f32[128,768]{1,0:T(8,128)S(1)}, f32[128,128]{1,0:T(8,128)S(1)}) custom-call(s32[6]{0:T(128)S(1)} %pad_add_fusion.scalars, bf16[256,768]{1,0:T(8,128)(2,1)S(1)} %bitcast.31, bf16[256,768]{1,0:T(8,128)(2,1)S(1)} %bitcast.33, bf16[32,768]{1,0:T(8,128)(2,1)S(1)} %collective-permute-done.3.before, ...), custom_call_target="tpu_custom_call" | custom-call | flops 1000000 | bytes 1048576 | tf_op jit(solution)/shard_map/pallas_call | solution.py:52
  29.4 1.9 %collective-permute-start.8 = (bf16[2,128,768]{2,1,0:T(8,128)(2,1)S(1)}, bf16[2,128,768]{2,1,0:T(8,128)(2,1)S(1)}, u32[]{:S(2)}, u32[]{:S(2)}) collective-permute-start(bf16[2,128,768]{2,1,0:T(8,128)(2,1)S(1)} %get-tuple-element.48.refs_0_), channel_id=1, source_target_pairs={{0,4},{2,6},{4,0},{6,2},{8,12},{10,14},{12,8},{14,10},{16,20},{18,... | collective-permute-start | bytes 1179656 | tf_op jit(solution)/shard_map/ppermute | solution.py:30
  31.3 1.5 %collective-permute-start.9 = (bf16[2,128,768]{2,1,0:T(8,128)(2,1)S(1)}, bf16[2,128,768]{2,1,0:T(8,128)(2,1)S(1)}, u32[]{:S(2)}, u32[]{:S(2)}) collective-permute-start(bf16[2,128,768]{2,1,0:T(8,128)(2,1)S(1)} %get-tuple-element.48.refs_0_), channel_id=1, source_target_pairs={{0,6},{2,4},{4,2},{6,0},{8,14},{10,12},{12,10},{14,8},{16,22},{18,... | collective-permute-start | bytes 1179656 | tf_op jit(solution)/shard_map/ppermute | solution.py:30
  32.9 1.3 collective-permute-done.5.refs_1_
  34.2 2.6 %collective-permute-start.6 = (bf16[2,2,192,384]{3,2,1,0:T(8,128)(2,1)S(1)}, bf16[2,2,192,384]{3,2,1,0:T(8,128)(2,1)}, u32[]{:S(2)}, u32[]{:S(2)}) collective-permute-start(bf16[2,2,192,384]{3,2,1,0:T(8,128)(2,1)S(1)} %shard_map.130.early), channel_id=1, source_target_pairs={{0,8},{2,10},{4,12},{6,14},{8,0},{10,2},{12,4},{14,6},{16,24},{18,... | collective-permute-start | bytes 1769480 | tf_op jit(solution)/shard_map/ppermute | solution.py:30
  36.8 2.4 %collective-permute-done.7.refs_1_ = bf16[2,128,768]{2,1,0:T(8,128)(2,1)S(1)} collective-permute-done((bf16[2,128,768]{2,1,0:T(8,128)(2,1)S(1)}, bf16[2,128,768]{2,1,0:T(8,128)(2,1)S(1)}, u32[]{:S(2)}, u32[]{:S(2)}) %collective-permute-start.7) | collective-permute-done | bytes 393248 | tf_op jit(solution)/shard_map/ppermute | solution.py:30
  39.2 6.3 %collective-permute-done.8.refs_2_ = bf16[2,128,768]{2,1,0:T(8,128)(2,1)S(1)} collective-permute-done((bf16[2,128,768]{2,1,0:T(8,128)(2,1)S(1)}, bf16[2,128,768]{2,1,0:T(8,128)(2,1)S(1)}, u32[]{:S(2)}, u32[]{:S(2)}) %collective-permute-start.8) | collective-permute-done | bytes 393248 | tf_op jit(solution)/shard_map/ppermute | solution.py:30
  46.5 1.6 %collective-permute-done.6.late = bf16[2,2,192,384]{3,2,1,0:T(8,128)(2,1)} collective-permute-done((bf16[2,2,192,384]{3,2,1,0:T(8,128)(2,1)S(1)}, bf16[2,2,192,384]{3,2,1,0:T(8,128)(2,1)}, u32[]{:S(2)}, u32[]{:S(2)}) %collective-permute-start.6) | collective-permute-done | bytes 589856 | tf_op jit(solution)/shard_map/ppermute | solution.py:30
  48.1 1.2 shard_map.131
  49.3 5.7 %shard_map.134 = (bf16[2,192,768]{2,1,0:T(8,128)(2,1)S(1)}, bf16[2,192,768]{2,1,0:T(8,128)(2,1)}, bf16[1024,384]{1,0:T(8,128)(2,1)S(1)}, bf16[1024,384]{1,0:T(8,128)(2,1)S(1)}) custom-call(s32[1]{0:T(128)} %bitcast.3.scalars, bf16[768,384]{1,0:T(8,128)(2,1)S(1)} %get-tuple-element.44.up, bf16[768,384]{1,0:T(8,128)(2,1)S(1)} %get-tuple-element.45.down_t, ...), custom_call_target="tpu_custom_call" | custom-call | flops 5000000000 | bytes 1048576 | tf_op jit(solution)/shard_map/pallas_call | solution.py:52
  55.0 1.9 %shard_map.135 = (f32[2,512,768]{2,1,0:T(8,128)S(1)}, bf16[2,512,768]{2,1,0:T(8,128)(2,1)S(1)}) custom-call(bf16[1024,384]{1,0:T(8,128)(2,1)S(1)} %get-tuple-element.49.act, bf16[1024,384]{1,0:T(8,128)(2,1)S(1)} %get-tuple-element.50.grad_hidden, bf16[768,384]{1,0:T(8,128)(2,1)S(1)} %get-tuple-element.44.up, bf16[768,384]{1,0:T(8,128)(2,1)S(1)} %get-tuple-element.45.down_t), custom_call_target="tpu_custom_call" | custom-call | flops 1000000000 | bytes 1048576 | tf_op jit(solution)/shard_map/pallas_call | solution.py:52
  57.0 2.0 %collective-permute-start.12 = (bf16[2,192,768]{2,1,0:T(8,128)(2,1)}, bf16[2,192,768]{2,1,0:T(8,128)(2,1)}, u32[]{:S(2)}, u32[]{:S(2)}) collective-permute-start(bf16[2,192,768]{2,1,0:T(8,128)(2,1)} %get-tuple-element.54), channel_id=1, source_target_pairs={{0,8},{2,10},{4,12},{6,14},{8,0},{10,2},{12,4},{14,6},{16,24},{18,... | collective-permute-start | bytes 1769480 | tf_op jit(solution)/shard_map/ppermute | solution.py:30
  59.0 1.3 collective-permute-done.11.refs_0_
  60.3 0.9 shard_map.136
  62.0 2.0 %collective-permute-start.13 = (bf16[2,128,768]{2,1,0:T(8,128)(2,1)}, bf16[2,128,768]{2,1,0:T(8,128)(2,1)S(1)}, u32[]{:S(2)}, u32[]{:S(2)}) collective-permute-start(bf16[2,128,768]{2,1,0:T(8,128)(2,1)} %get-tuple-element.55), channel_id=1, source_target_pairs={{0,2},{2,0},{4,6},{6,4},{8,10},{10,8},{12,14},{14,12},{16,18},{18,... | collective-permute-start | bytes 1179656 | tf_op jit(solution)/shard_map/ppermute | solution.py:30
  64.1 1.3 collective-permute-start.14
  65.5 7.6 %collective-permute-done.12 = bf16[2,192,768]{2,1,0:T(8,128)(2,1)} collective-permute-done((bf16[2,192,768]{2,1,0:T(8,128)(2,1)}, bf16[2,192,768]{2,1,0:T(8,128)(2,1)}, u32[]{:S(2)}, u32[]{:S(2)}) %collective-permute-start.12) | collective-permute-done | bytes 589856 | tf_op jit(solution)/shard_map/ppermute | solution.py:30
  73.2 1.0 collective-permute-done.13.one
  74.2 1.2 convert_add_fusion
  75.5 3.3 %collective-permute-start.16 = (bf16[1,192,768]{2,1,0:T(8,128)(2,1)S(1)}, bf16[1,192,768]{2,1,0:T(8,128)(2,1)S(1)}, u32[]{:S(2)}, u32[]{:S(2)}) collective-permute-start(bf16[1,192,768]{2,1,0:T(8,128)(2,1)S(1)} %dynamic-slice_convert_fusion), channel_id=1, source_target_pairs={{0,16},{2,18},{4,20},{6,22},{8,24},{10,26},{12,28},{14,30},{16,0},... | collective-permute-start | bytes 884744 | tf_op jit(solution)/shard_map/ppermute | solution.py:30
  78.8 4.8 %collective-permute-done.14.two = bf16[2,128,768]{2,1,0:T(8,128)(2,1)S(1)} collective-permute-done((bf16[2,128,768]{2,1,0:T(8,128)(2,1)}, bf16[2,128,768]{2,1,0:T(8,128)(2,1)S(1)}, u32[]{:S(2)}, u32[]{:S(2)}) %collective-permute-start.14) | collective-permute-done | bytes 393248 | tf_op jit(solution)/shard_map/ppermute | solution.py:30
  83.6 1.7 %shard_map.137 = (bf16[128,768]{1,0:T(8,128)(2,1)S(1)}, bf16[128,768]{1,0:T(8,128)(2,1)}) custom-call(s32[6]{0:T(128)S(1)} %pad_add_fusion.scalars, bf16[256,768]{1,0:T(8,128)(2,1)S(1)} %bitcast.32, bf16[2,128,768]{2,1,0:T(8,128)(2,1)S(1)} %get-tuple-element.53.total, bf16[2,128,768]{2,1,0:T(8,128)(2,1)S(1)} %collective-permute-done.13.one, ...), custom_call_target="tpu_custom_call" | custom-call | flops 1000000 | bytes 1048576 | tf_op jit(solution)/shard_map/pallas_call | solution.py:52
  85.3 6.1 %collective-permute-done.16 = bf16[1,192,768]{2,1,0:T(8,128)(2,1)S(1)} collective-permute-done((bf16[1,192,768]{2,1,0:T(8,128)(2,1)S(1)}, bf16[1,192,768]{2,1,0:T(8,128)(2,1)S(1)}, u32[]{:S(2)}, u32[]{:S(2)}) %collective-permute-start.16) | collective-permute-done | bytes 294944 | tf_op jit(solution)/shard_map/ppermute | solution.py:30
  91.5 1.6 %collective-permute-start.17 = (bf16[1,64,768]{2,1,0:T(8,128)(2,1)S(1)}, bf16[1,64,768]{2,1,0:T(8,128)(2,1)S(1)}, u32[]{:S(2)}, u32[]{:S(2)}) collective-permute-start(bf16[1,64,768]{2,1,0:T(8,128)(2,1)S(1)} %get-tuple-element.88.refs_0_), channel_id=1, source_target_pairs={{0,2},{2,0},{4,6},{6,4},{8,10},{10,8},{12,14},{14,12},{16,18},{18,... | collective-permute-start | bytes 294920 | tf_op jit(solution)/shard_map/ppermute | solution.py:30
  93.1 1.0 collective-permute-start.18
  94.1 2.1 %collective-permute-done.17.refs_3_ = bf16[1,64,768]{2,1,0:T(8,128)(2,1)S(1)} collective-permute-done((bf16[1,64,768]{2,1,0:T(8,128)(2,1)S(1)}, bf16[1,64,768]{2,1,0:T(8,128)(2,1)S(1)}, u32[]{:S(2)}, u32[]{:S(2)}) %collective-permute-start.17) | collective-permute-done | bytes 98336 | tf_op jit(solution)/shard_map/ppermute | solution.py:30
  96.2 1.5 %collective-permute-done.18.refs_4_ = bf16[1,64,768]{2,1,0:T(8,128)(2,1)S(1)} collective-permute-done((bf16[1,64,768]{2,1,0:T(8,128)(2,1)S(1)}, bf16[1,64,768]{2,1,0:T(8,128)(2,1)S(1)}, u32[]{:S(2)}, u32[]{:S(2)}) %collective-permute-start.18) | collective-permute-done | bytes 98336 | tf_op jit(solution)/shard_map/ppermute | solution.py:30
  97.7 1.0 collective-permute-done.19.refs_5_
  98.8 1.1 collective-permute-start.20
  101.1 3.4 %collective-permute-done.20.refs_3_ = bf16[2,64,768]{2,1,0:T(8,128)(2,1)S(1)} collective-permute-done((bf16[2,64,768]{2,1,0:T(8,128)(2,1)S(1)}, bf16[2,64,768]{2,1,0:T(8,128)(2,1)S(1)}, u32[]{:S(2)}, u32[]{:S(2)}) %collective-permute-start.20) | collective-permute-done | bytes 196640 | tf_op jit(solution)/shard_map/ppermute | solution.py:30
  104.5 1.0 collective-permute-done.21.refs_4_
  106.3 1.4 collective-permute-start.23
  108.2 1.9 %collective-permute-start.25 = (bf16[4,64,768]{2,1,0:T(8,128)(2,1)S(1)}, bf16[4,64,768]{2,1,0:T(8,128)(2,1)}, u32[]{:S(2)}, u32[]{:S(2)}) collective-permute-start(bf16[4,64,768]{2,1,0:T(8,128)(2,1)S(1)} %get-tuple-element.78.refs_4_), channel_id=1, source_target_pairs={{0,4},{2,6},{4,0},{6,2},{8,12},{10,14},{12,8},{14,10},{16,20},{18,... | collective-permute-start | bytes 1179656 | tf_op jit(solution)/shard_map/ppermute | solution.py:30
  110.2 3.3 %collective-permute-start.27 = (bf16[32,768]{1,0:T(8,128)(2,1)S(1)}, bf16[32,768]{1,0:T(8,128)(2,1)S(1)}, u32[]{:S(2)}, u32[]{:S(2)}) collective-permute-start(bf16[32,768]{1,0:T(8,128)(2,1)S(1)} %get-tuple-element.85), channel_id=1, source_target_pairs={{0,2},{2,4},{4,6},{6,8},{8,10},{10,12},{12,14},{14,16},{16,18},{18... | collective-permute-start | bytes 147464 | tf_op jit(solution)/shard_map/ppermute | solution.py:37
  113.5 1.5 %collective-permute-start.28 = (bf16[32,768]{1,0:T(8,128)(2,1)S(1)}, bf16[32,768]{1,0:T(8,128)(2,1)S(1)}, u32[]{:S(2)}, u32[]{:S(2)}) collective-permute-start(bf16[32,768]{1,0:T(8,128)(2,1)S(1)} %get-tuple-element.84), channel_id=1, source_target_pairs={{2,0},{4,2},{6,4},{8,6},{10,8},{12,10},{14,12},{16,14},{18,16},{20... | collective-permute-start | bytes 147464 | tf_op jit(solution)/shard_map/ppermute | solution.py:37
  115.3 4.3 %collective-permute-done.28.after = bf16[32,768]{1,0:T(8,128)(2,1)S(1)} collective-permute-done((bf16[32,768]{1,0:T(8,128)(2,1)S(1)}, bf16[32,768]{1,0:T(8,128)(2,1)S(1)}, u32[]{:S(2)}, u32[]{:S(2)}) %collective-permute-start.28) | collective-permute-done | bytes 49184 | tf_op jit(solution)/shard_map/ppermute | solution.py:37
  119.5 3.3 %shard_map.140 = bf16[128,768]{1,0:T(8,128)(2,1)} custom-call(s32[6]{0:T(128)S(1)} %pad_add_fusion.scalars, bf16[256,768]{1,0:T(8,128)(2,1)S(1)} %bitcast.34, bf16[32,768]{1,0:T(8,128)(2,1)S(1)} %collective-permute-done.27.before, bf16[32,768]{1,0:T(8,128)(2,1)S(1)} %collective-permute-done.28.after, f32[49,768]{1,0:T(8,128)S(1)} %reshape.53.taps, ...), custom_call_target="tpu_custom_call" | custom-call | flops 1000000 | bytes 1048576 | tf_op jit(solution)/shard_map/pallas_call | solution.py:52
  122.9 9.4 %shard_map.141 = (f32[48,1536]{1,0:T(8,128)S(1)}, bf16[48,1536]{1,0:T(8,128)(2,1)S(1)}) custom-call(s32[3]{0:T(128)S(1)} %pad_add_fusion.1.scalars, bf16[4,64,768]{2,1,0:T(8,128)(2,1)S(1)} %get-tuple-element.74.refs_0_, bf16[4,64,768]{2,1,0:T(8,128)(2,1)S(1)} %collective-permute-done.23.refs_1_, bf16[4,64,768]{2,1,0:T(8,128)(2,1)S(1)} %get-tuple-element.76.refs_2_, ...), custom_call_target="tpu_custom_call" | custom-call | flops 10000000000 | bytes 1048576 | tf_op jit(solution)/shard_map/pallas_call | solution.py:52
  132.3 1.0 collective-permute-start.29
  133.3 6.3 %collective-permute-done.29 = bf16[48,1536]{1,0:T(8,128)(2,1)S(1)} collective-permute-done((bf16[48,1536]{1,0:T(8,128)(2,1)S(1)}, bf16[48,1536]{1,0:T(8,128)(2,1)S(1)}, u32[]{:S(2)}, u32[]{:S(2)}) %collective-permute-start.29) | collective-permute-done | bytes 147488 | tf_op jit(solution)/shard_map/ppermute | solution.py:30
  (60 shorter events, 8.4 us)
Async XLA Ops:
  0.6 25.2 %copy-start = (bf16[32,8,768]{2,1,0:T(8,128)(2,1)S(1)}, bf16[32,8,768]{2,1,0:T(8,128)(2,1)}, u32[]{:S(2)}) copy-start(bf16[32,8,768]{2,1,0:T(8,128)(2,1)} %param.10) | copy-start | bytes 1179652
  0.6 25.0 %copy-start.5 = (f32[7,7,768]{2,1,0:T(8,128)S(1)}, f32[7,7,768]{2,1,0:T(8,128)}, u32[]{:S(2)}) copy-start(f32[7,7,768]{2,1,0:T(8,128)} %param.12) | copy-start | bytes 451588
  0.7 25.0 %copy-start.6 = (f32[768]{0:T(1024)S(1)}, f32[768]{0:T(1024)}, u32[]{:S(2)}) copy-start(f32[768]{0:T(1024)} %param.13) | copy-start | bytes 9220
  0.7 25.0 %copy-start.7 = (f32[768]{0:T(1024)S(1)}, f32[768]{0:T(1024)}, u32[]{:S(2)}) copy-start(f32[768]{0:T(1024)} %param.17) | copy-start | bytes 9220
  0.7 25.0 %copy-start.8 = (s32[4,1]{0,1:T(1,128)S(1)}, s32[4,1]{0,1:T(1,128)}, u32[]{:S(2)}) copy-start(s32[4,1]{0,1:T(1,128)} %param.18) | copy-start | bytes 52
  0.7 25.1 %copy-start.1 = (bf16[32,8,768]{2,1,0:T(8,128)(2,1)S(1)}, bf16[32,8,768]{2,1,0:T(8,128)(2,1)}, u32[]{:S(2)}) copy-start(bf16[32,8,768]{2,1,0:T(8,128)(2,1)} %param.11) | copy-start | bytes 1179652
  1.8 13.2 %collective-permute-start = (bf16[2,48,384]{2,1,0:T(8,128)(2,1)S(1)}, bf16[2,48,384]{2,1,0:T(8,128)(2,1)S(1)}, u32[]{:S(2)}, u32[]{:S(2)}) collective-permute-start(bf16[2,48,384]{2,1,0:T(8,128)(2,1)S(1)} %get-tuple-element.91), channel_id=1, source_target_pairs={{0,2},{2,0},{4,6},{6,4},{8,10},{10,8},{12,14},{14,12},{16,18},{18,... | collective-permute-start | bytes 221192 | tf_op jit(solution)/shard_map/ppermute | solution.py:30
  4.8 10.2 %collective-permute-start.1 = (bf16[2,48,384]{2,1,0:T(8,128)(2,1)S(1)}, bf16[2,48,384]{2,1,0:T(8,128)(2,1)S(1)}, u32[]{:S(2)}, u32[]{:S(2)}) collective-permute-start(bf16[2,48,384]{2,1,0:T(8,128)(2,1)S(1)} %get-tuple-element.92), channel_id=1, source_target_pairs={{0,4},{2,6},{4,0},{6,2},{8,12},{10,14},{12,8},{14,10},{16,20},{18,... | collective-permute-start | bytes 221192 | tf_op jit(solution)/shard_map/ppermute | solution.py:30
  6.3 8.7 %collective-permute-start.2 = (bf16[2,48,384]{2,1,0:T(8,128)(2,1)S(1)}, bf16[2,48,384]{2,1,0:T(8,128)(2,1)S(1)}, u32[]{:S(2)}, u32[]{:S(2)}) collective-permute-start(bf16[2,48,384]{2,1,0:T(8,128)(2,1)S(1)} %get-tuple-element.89), channel_id=1, source_target_pairs={{0,6},{2,4},{4,2},{6,0},{8,14},{10,12},{12,10},{14,8},{16,22},{18,... | collective-permute-start | bytes 221192 | tf_op jit(solution)/shard_map/ppermute | solution.py:30
  9.0 6.0 %collective-permute-start.3 = (bf16[32,768]{1,0:T(8,128)(2,1)S(1)}, bf16[32,768]{1,0:T(8,128)(2,1)S(1)}, u32[]{:S(2)}, u32[]{:S(2)}) collective-permute-start(bf16[32,768]{1,0:T(8,128)(2,1)S(1)} %constant_dynamic-slice_fusion), channel_id=1, source_target_pairs={{0,2},{2,4},{4,6},{6,8},{8,10},{10,12},{12,14},{14,16},{16,18},{18... | collective-permute-start | bytes 147464 | tf_op jit(solution)/shard_map/ppermute | solution.py:37
  13.7 6.0 %collective-permute-start.4 = (bf16[32,768]{1,0:T(8,128)(2,1)S(1)}, bf16[32,768]{1,0:T(8,128)(2,1)S(1)}, u32[]{:S(2)}, u32[]{:S(2)}) collective-permute-start(bf16[32,768]{1,0:T(8,128)(2,1)S(1)} %slice_bitcast_fusion), channel_id=1, source_target_pairs={{2,0},{4,2},{6,4},{8,6},{10,8},{12,10},{14,12},{16,14},{18,16},{20... | collective-permute-start | bytes 147464 | tf_op jit(solution)/shard_map/ppermute | solution.py:37
  19.7 14.5 %collective-permute-start.5 = (bf16[1,2,192,384]{3,2,1,0:T(8,128)(2,1)S(1)}, bf16[1,2,192,384]{3,2,1,0:T(8,128)(2,1)S(1)}, u32[]{:S(2)}, u32[]{:S(2)}) collective-permute-start(bf16[1,2,192,384]{3,2,1,0:T(8,128)(2,1)S(1)} %bitcast.35), channel_id=1, source_target_pairs={{0,16},{2,18},{4,20},{6,22},{8,24},{10,26},{12,28},{14,30},{16,0},... | collective-permute-start | bytes 884744 | tf_op jit(solution)/shard_map/ppermute | solution.py:30
  28.7 0.6 copy-start.2
  29.4 9.8 %collective-permute-start.7 = (bf16[2,128,768]{2,1,0:T(8,128)(2,1)S(1)}, bf16[2,128,768]{2,1,0:T(8,128)(2,1)S(1)}, u32[]{:S(2)}, u32[]{:S(2)}) collective-permute-start(bf16[2,128,768]{2,1,0:T(8,128)(2,1)S(1)} %get-tuple-element.48.refs_0_), channel_id=1, source_target_pairs={{0,2},{2,0},{4,6},{6,4},{8,10},{10,8},{12,14},{14,12},{16,18},{18,... | collective-permute-start | bytes 1179656 | tf_op jit(solution)/shard_map/ppermute | solution.py:30
  29.4 16.1 %collective-permute-start.8 = (bf16[2,128,768]{2,1,0:T(8,128)(2,1)S(1)}, bf16[2,128,768]{2,1,0:T(8,128)(2,1)S(1)}, u32[]{:S(2)}, u32[]{:S(2)}) collective-permute-start(bf16[2,128,768]{2,1,0:T(8,128)(2,1)S(1)} %get-tuple-element.48.refs_0_), channel_id=1, source_target_pairs={{0,4},{2,6},{4,0},{6,2},{8,12},{10,14},{12,8},{14,10},{16,20},{18,... | collective-permute-start | bytes 1179656 | tf_op jit(solution)/shard_map/ppermute | solution.py:30
  31.3 14.2 %collective-permute-start.9 = (bf16[2,128,768]{2,1,0:T(8,128)(2,1)S(1)}, bf16[2,128,768]{2,1,0:T(8,128)(2,1)S(1)}, u32[]{:S(2)}, u32[]{:S(2)}) collective-permute-start(bf16[2,128,768]{2,1,0:T(8,128)(2,1)S(1)} %get-tuple-element.48.refs_0_), channel_id=1, source_target_pairs={{0,6},{2,4},{4,2},{6,0},{8,14},{10,12},{12,10},{14,8},{16,22},{18,... | collective-permute-start | bytes 1179656 | tf_op jit(solution)/shard_map/ppermute | solution.py:30
  34.2 13.9 %collective-permute-start.6 = (bf16[2,2,192,384]{3,2,1,0:T(8,128)(2,1)S(1)}, bf16[2,2,192,384]{3,2,1,0:T(8,128)(2,1)}, u32[]{:S(2)}, u32[]{:S(2)}) collective-permute-start(bf16[2,2,192,384]{3,2,1,0:T(8,128)(2,1)S(1)} %shard_map.130.early), channel_id=1, source_target_pairs={{0,8},{2,10},{4,12},{6,14},{8,0},{10,2},{12,4},{14,6},{16,24},{18,... | collective-permute-start | bytes 1769480 | tf_op jit(solution)/shard_map/ppermute | solution.py:30
  45.6 3.7 %collective-permute-start.10 = (bf16[2,512,768]{2,1,0:T(8,128)(2,1)S(1)}, bf16[2,512,768]{2,1,0:T(8,128)(2,1)}, u32[]{:S(2)}, u32[]{:S(2)}) collective-permute-start(bf16[2,512,768]{2,1,0:T(8,128)(2,1)S(1)} %shard_map.133.refs_0_), channel_id=1, source_target_pairs={{0,1},{1,0},{2,3},{3,2},{4,5},{5,4},{6,7},{7,6},{8,9},{9,8},{10,11... | collective-permute-start | bytes 4718600 | tf_op jit(solution)/shard_map/ppermute | solution.py:30
  56.8 3.5 %collective-permute-start.11 = (bf16[2,512,768]{2,1,0:T(8,128)(2,1)S(1)}, bf16[2,512,768]{2,1,0:T(8,128)(2,1)S(1)}, u32[]{:S(2)}, u32[]{:S(2)}) collective-permute-start(bf16[2,512,768]{2,1,0:T(8,128)(2,1)S(1)} %get-tuple-element.52), channel_id=1, source_target_pairs={{0,1},{1,0},{2,3},{3,2},{4,5},{5,4},{6,7},{7,6},{8,9},{9,8},{10,11... | collective-permute-start | bytes 4718600 | tf_op jit(solution)/shard_map/ppermute | solution.py:30
  57.0 16.2 %collective-permute-start.12 = (bf16[2,192,768]{2,1,0:T(8,128)(2,1)}, bf16[2,192,768]{2,1,0:T(8,128)(2,1)}, u32[]{:S(2)}, u32[]{:S(2)}) collective-permute-start(bf16[2,192,768]{2,1,0:T(8,128)(2,1)} %get-tuple-element.54), channel_id=1, source_target_pairs={{0,8},{2,10},{4,12},{6,14},{8,0},{10,2},{12,4},{14,6},{16,24},{18,... | collective-permute-start | bytes 1769480 | tf_op jit(solution)/shard_map/ppermute | solution.py:30
  61.3 0.8 copy-start.4
  62.0 12.2 %collective-permute-start.13 = (bf16[2,128,768]{2,1,0:T(8,128)(2,1)}, bf16[2,128,768]{2,1,0:T(8,128)(2,1)S(1)}, u32[]{:S(2)}, u32[]{:S(2)}) collective-permute-start(bf16[2,128,768]{2,1,0:T(8,128)(2,1)} %get-tuple-element.55), channel_id=1, source_target_pairs={{0,2},{2,0},{4,6},{6,4},{8,10},{10,8},{12,14},{14,12},{16,18},{18,... | collective-permute-start | bytes 1179656 | tf_op jit(solution)/shard_map/ppermute | solution.py:30
  64.1 19.5 %collective-permute-start.14 = (bf16[2,128,768]{2,1,0:T(8,128)(2,1)}, bf16[2,128,768]{2,1,0:T(8,128)(2,1)S(1)}, u32[]{:S(2)}, u32[]{:S(2)}) collective-permute-start(bf16[2,128,768]{2,1,0:T(8,128)(2,1)} %copy-done.4), channel_id=1, source_target_pairs={{0,4},{2,6},{4,0},{6,2},{8,12},{10,14},{12,8},{14,10},{16,20},{18,... | collective-permute-start | bytes 1179656 | tf_op jit(solution)/shard_map/ppermute | solution.py:30
  65.4 18.2 %collective-permute-start.15 = (bf16[2,128,768]{2,1,0:T(8,128)(2,1)S(1)}, bf16[2,128,768]{2,1,0:T(8,128)(2,1)S(1)}, u32[]{:S(2)}, u32[]{:S(2)}) collective-permute-start(bf16[2,128,768]{2,1,0:T(8,128)(2,1)S(1)} %get-tuple-element.58), channel_id=1, source_target_pairs={{0,6},{2,4},{4,2},{6,0},{8,14},{10,12},{12,10},{14,8},{16,22},{18,... | collective-permute-start | bytes 1179656 | tf_op jit(solution)/shard_map/ppermute | solution.py:30
  74.2 9.4 %copy-start.3 = (f32[128,128]{1,0:T(8,128)S(1)}, f32[128,128]{1,0:T(8,128)}, u32[]{:S(2)}) copy-start(f32[128,128]{1,0:T(8,128)} %copy-done.2) | copy-start | bytes 196612
  75.5 15.9 %collective-permute-start.16 = (bf16[1,192,768]{2,1,0:T(8,128)(2,1)S(1)}, bf16[1,192,768]{2,1,0:T(8,128)(2,1)S(1)}, u32[]{:S(2)}, u32[]{:S(2)}) collective-permute-start(bf16[1,192,768]{2,1,0:T(8,128)(2,1)S(1)} %dynamic-slice_convert_fusion), channel_id=1, source_target_pairs={{0,16},{2,18},{4,20},{6,22},{8,24},{10,26},{12,28},{14,30},{16,0},... | collective-permute-start | bytes 884744 | tf_op jit(solution)/shard_map/ppermute | solution.py:30
  91.5 4.7 %collective-permute-start.17 = (bf16[1,64,768]{2,1,0:T(8,128)(2,1)S(1)}, bf16[1,64,768]{2,1,0:T(8,128)(2,1)S(1)}, u32[]{:S(2)}, u32[]{:S(2)}) collective-permute-start(bf16[1,64,768]{2,1,0:T(8,128)(2,1)S(1)} %get-tuple-element.88.refs_0_), channel_id=1, source_target_pairs={{0,2},{2,0},{4,6},{6,4},{8,10},{10,8},{12,14},{14,12},{16,18},{18,... | collective-permute-start | bytes 294920 | tf_op jit(solution)/shard_map/ppermute | solution.py:30
  93.1 4.6 %collective-permute-start.18 = (bf16[1,64,768]{2,1,0:T(8,128)(2,1)S(1)}, bf16[1,64,768]{2,1,0:T(8,128)(2,1)S(1)}, u32[]{:S(2)}, u32[]{:S(2)}) collective-permute-start(bf16[1,64,768]{2,1,0:T(8,128)(2,1)S(1)} %get-tuple-element.87.refs_1_), channel_id=1, source_target_pairs={{0,4},{2,6},{4,0},{6,2},{8,12},{10,14},{12,8},{14,10},{16,20},{18,... | collective-permute-start | bytes 294920 | tf_op jit(solution)/shard_map/ppermute | solution.py:30
  94.1 4.6 %collective-permute-start.19 = (bf16[1,64,768]{2,1,0:T(8,128)(2,1)S(1)}, bf16[1,64,768]{2,1,0:T(8,128)(2,1)S(1)}, u32[]{:S(2)}, u32[]{:S(2)}) collective-permute-start(bf16[1,64,768]{2,1,0:T(8,128)(2,1)S(1)} %get-tuple-element.86.refs_2_), channel_id=1, source_target_pairs={{0,8},{2,10},{4,12},{6,14},{8,0},{10,2},{12,4},{14,6},{16,24},{18,... | collective-permute-start | bytes 294920 | tf_op jit(solution)/shard_map/ppermute | solution.py:30
  98.8 5.7 %collective-permute-start.20 = (bf16[2,64,768]{2,1,0:T(8,128)(2,1)S(1)}, bf16[2,64,768]{2,1,0:T(8,128)(2,1)S(1)}, u32[]{:S(2)}, u32[]{:S(2)}) collective-permute-start(bf16[2,64,768]{2,1,0:T(8,128)(2,1)S(1)} %get-tuple-element.66.refs_0_), channel_id=1, source_target_pairs={{0,4},{2,6},{4,0},{6,2},{8,12},{10,14},{12,8},{14,10},{16,20},{18,... | collective-permute-start | bytes 589832 | tf_op jit(solution)/shard_map/ppermute | solution.py:30
  99.9 5.7 %collective-permute-start.21 = (bf16[2,64,768]{2,1,0:T(8,128)(2,1)S(1)}, bf16[2,64,768]{2,1,0:T(8,128)(2,1)S(1)}, u32[]{:S(2)}, u32[]{:S(2)}) collective-permute-start(bf16[2,64,768]{2,1,0:T(8,128)(2,1)S(1)} %get-tuple-element.67.refs_1_), channel_id=1, source_target_pairs={{0,8},{2,10},{4,12},{6,14},{8,0},{10,2},{12,4},{14,6},{16,24},{18,... | collective-permute-start | bytes 589832 | tf_op jit(solution)/shard_map/ppermute | solution.py:30
  100.6 5.7 %collective-permute-start.22 = (bf16[2,64,768]{2,1,0:T(8,128)(2,1)S(1)}, bf16[2,64,768]{2,1,0:T(8,128)(2,1)S(1)}, u32[]{:S(2)}, u32[]{:S(2)}) collective-permute-start(bf16[2,64,768]{2,1,0:T(8,128)(2,1)S(1)} %get-tuple-element.68.refs_2_), channel_id=1, source_target_pairs={{0,2},{2,0},{4,6},{6,4},{8,10},{10,8},{12,14},{14,12},{16,18},{18,... | collective-permute-start | bytes 589832 | tf_op jit(solution)/shard_map/ppermute | solution.py:30
  101.1 9.1 %collective-permute-start.26 = (bf16[128,768]{1,0:T(8,128)(2,1)S(1)}, bf16[128,768]{1,0:T(8,128)(2,1)S(1)}, u32[]{:S(2)}, u32[]{:S(2)}) collective-permute-start(bf16[128,768]{1,0:T(8,128)(2,1)S(1)} %get-tuple-element.72.rest_0_), channel_id=1, source_target_pairs={{0,1},{1,0},{2,3},{3,2},{4,5},{5,4},{6,7},{7,6},{8,9},{9,8},{10,11... | collective-permute-start | bytes 589832 | tf_op jit(solution)/shard_map/ppermute | solution.py:30
  106.3 16.5 %collective-permute-start.23 = (bf16[4,64,768]{2,1,0:T(8,128)(2,1)S(1)}, bf16[4,64,768]{2,1,0:T(8,128)(2,1)S(1)}, u32[]{:S(2)}, u32[]{:S(2)}) collective-permute-start(bf16[4,64,768]{2,1,0:T(8,128)(2,1)S(1)} %get-tuple-element.74.refs_0_), channel_id=1, source_target_pairs={{0,8},{2,10},{4,12},{6,14},{8,0},{10,2},{12,4},{14,6},{16,24},{18,... | collective-permute-start | bytes 1179656 | tf_op jit(solution)/shard_map/ppermute | solution.py:30
  107.7 15.1 %collective-permute-start.24 = (bf16[4,64,768]{2,1,0:T(8,128)(2,1)S(1)}, bf16[4,64,768]{2,1,0:T(8,128)(2,1)S(1)}, u32[]{:S(2)}, u32[]{:S(2)}) collective-permute-start(bf16[4,64,768]{2,1,0:T(8,128)(2,1)S(1)} %get-tuple-element.76.refs_2_), channel_id=1, source_target_pairs={{0,2},{2,0},{4,6},{6,4},{8,10},{10,8},{12,14},{14,12},{16,18},{18,... | collective-permute-start | bytes 1179656 | tf_op jit(solution)/shard_map/ppermute | solution.py:30
  108.2 14.6 %collective-permute-start.25 = (bf16[4,64,768]{2,1,0:T(8,128)(2,1)S(1)}, bf16[4,64,768]{2,1,0:T(8,128)(2,1)}, u32[]{:S(2)}, u32[]{:S(2)}) collective-permute-start(bf16[4,64,768]{2,1,0:T(8,128)(2,1)S(1)} %get-tuple-element.78.refs_4_), channel_id=1, source_target_pairs={{0,4},{2,6},{4,0},{6,2},{8,12},{10,14},{12,8},{14,10},{16,20},{18,... | collective-permute-start | bytes 1179656 | tf_op jit(solution)/shard_map/ppermute | solution.py:30
  110.2 5.1 %collective-permute-start.27 = (bf16[32,768]{1,0:T(8,128)(2,1)S(1)}, bf16[32,768]{1,0:T(8,128)(2,1)S(1)}, u32[]{:S(2)}, u32[]{:S(2)}) collective-permute-start(bf16[32,768]{1,0:T(8,128)(2,1)S(1)} %get-tuple-element.85), channel_id=1, source_target_pairs={{0,2},{2,4},{4,6},{6,8},{8,10},{10,12},{12,14},{14,16},{16,18},{18... | collective-permute-start | bytes 147464 | tf_op jit(solution)/shard_map/ppermute | solution.py:37
  113.5 6.0 %collective-permute-start.28 = (bf16[32,768]{1,0:T(8,128)(2,1)S(1)}, bf16[32,768]{1,0:T(8,128)(2,1)S(1)}, u32[]{:S(2)}, u32[]{:S(2)}) collective-permute-start(bf16[32,768]{1,0:T(8,128)(2,1)S(1)} %get-tuple-element.84), channel_id=1, source_target_pairs={{2,0},{4,2},{6,4},{8,6},{10,8},{12,10},{14,12},{16,14},{18,16},{20... | collective-permute-start | bytes 147464 | tf_op jit(solution)/shard_map/ppermute | solution.py:37
  132.3 7.3 %collective-permute-start.29 = (bf16[48,1536]{1,0:T(8,128)(2,1)S(1)}, bf16[48,1536]{1,0:T(8,128)(2,1)S(1)}, u32[]{:S(2)}, u32[]{:S(2)}) collective-permute-start(bf16[48,1536]{1,0:T(8,128)(2,1)S(1)} %get-tuple-element.81), channel_id=1, source_target_pairs={{0,16},{2,18},{4,20},{6,22},{8,24},{10,26},{12,28},{14,30},{16,0},... | collective-permute-start | bytes 442376 | tf_op jit(solution)/shard_map/ppermute | solution.py:30

commit v6 on v5

--- a/solution.py
+++ b/solution.py
@@ -104,17 +104,39 @@
     framed[pl.ds(live_rows + MARGIN, MARGIN)] = rows_of(after_ref)[:MARGIN]
 
 
-def kept_rows(scalars, tokens, patches):
-    row = scalars[1] + lax.broadcasted_iota(jnp.int32, (tokens, 1), 0) // COLS
+def live_rows(ids, lengths):
+    return PATCH * lengths[ids[0]]
+
+
+def kept_rows(ids, lengths, tissue, tokens):
+    row = ids[1] + lax.broadcasted_iota(jnp.int32, (tokens, 1), 0) // COLS
     keep = jnp.zeros((tokens, 1), F32)
-    for patch in range(patches):
-        keep = jnp.where(row // PATCH == patch, scalars[2 + patch].astype(F32), keep)
-    live = row < scalars[0]
+    for patch in range(tissue.shape[0]):
+        keep = jnp.where(row // PATCH == patch, tissue[patch].astype(F32), keep)
+    live = row < live_rows(ids, lengths)
     return live, jnp.where(live, keep, 0.0)
 
 
+def rims_kernel(ids, lengths, *refs):
+    *shares, head, tail = refs
+    tokens = shares[0].shape[0]
+    last = (live_rows(ids, lengths) - RIM) * COLS
+    for s, share in enumerate(shares):
+
+        @pl.when(ids[2] == s)
+        def _():
+            head[...] = share[: head.shape[0], :]
+
+        @pl.when((last // tokens) ^ ids[2] == s)
+        def _():
+            start = pl.multiple_of(lax.rem(last, tokens), RIM * COLS)
+            tail[...] = share[pl.ds(start, tail.shape[0]), :]
+
+
 def forward_kernel(
-    scalars,
+    ids,
+    lengths,
+    tissue,
     strip,
     cotangent,
     before,
@@ -128,8 +150,8 @@
     framed,
     mixed,
 ):
-    place_strip(framed, [(0, strip)], before, after, scalars[0])
-    convolve(framed, taps, scalars[1], mixed, False)
+    place_strip(framed, [(0, strip)], before, after, live_rows(ids, lengths))
+    convolve(framed, taps, ids[1], mixed, False)
     tokens, channels = centred_out.shape
     value = mixed[...].reshape(tokens, channels)
     shifted = value - jnp.sum(value, 1, keepdims=True) / channels
@@ -139,18 +161,31 @@
     centred_out[...] = centred
     inverse[...] = jnp.broadcast_to(inv_std, inverse.shape)
     sent[0] = (centred * gain[...]).astype(BF16)
-    _, keep = kept_rows(scalars, tokens, strip.shape[0] // (COLS * PATCH))
-    start = pl.multiple_of(scalars[1] * COLS, 16)
+    _, keep = kept_rows(ids, lengths, tissue, tokens)
+    start = pl.multiple_of(ids[1] * COLS, 16)
     grad_out = cotangent[pl.ds(start, tokens), :].astype(F32)
     sent[1] = (keep * layer_scale[...] * grad_out).astype(BF16)
 
 
 def middle_kernel(
-    scalars, strip, total, one, two, three, centred, inverse, gain, layer_scale, grad_mixed, block_out
+    ids,
+    lengths,
+    tissue,
+    strip,
+    total,
+    one,
+    two,
+    three,
+    centred,
+    inverse,
+    gain,
+    layer_scale,
+    grad_mixed,
+    block_out,
 ):
     tokens, channels = grad_mixed.shape
-    start = pl.multiple_of(scalars[1] * COLS, 16)
-    live, keep = kept_rows(scalars, tokens, strip.shape[0] // (COLS * PATCH))
+    start = pl.multiple_of(ids[1] * COLS, 16)
+    live, keep = kept_rows(ids, lengths, tissue, tokens)
 
     def summed(which):
         value = total[which].astype(F32)
@@ -264,18 +299,17 @@
         out[...] = total.astype(BF16)
 
 
-def backward_kernel(scalars, cotangent, before, after, taps, *rest):
+def backward_kernel(ids, lengths, cotangent, before, after, taps, *rest):
     *pieces, grad_features, framed, spread = rest
     tokens = grad_features.shape[0]
     share = spread.shape[0]
-    own = scalars[1] // share
-    placed = [((own ^ s) * share, piece) for s, piece in enumerate(pieces)]
-    place_strip(framed, placed, before, after, scalars[0])
-    convolve(framed, taps, scalars[1], spread, True)
-    start = pl.multiple_of(scalars[1] * COLS, 16)
+    placed = [((ids[2] ^ s) * share, piece) for s, piece in enumerate(pieces)]
+    place_strip(framed, placed, before, after, live_rows(ids, lengths))
+    convolve(framed, taps, ids[1], spread, True)
+    start = pl.multiple_of(ids[1] * COLS, 16)
     value = cotangent[pl.ds(start, tokens), :].astype(F32) + spread[...].reshape(grad_features.shape)
-    row = scalars[1] + lax.broadcasted_iota(jnp.int32, (tokens, 1), 0) // COLS
-    grad_features[...] = jnp.where(row < scalars[0], value, 0.0).astype(BF16)
+    row = ids[1] + lax.broadcasted_iota(jnp.int32, (tokens, 1), 0) // COLS
+    grad_features[...] = jnp.where(row < live_rows(ids, lengths), value, 0.0).astype(BF16)
 
 
 def dot(left, right, contract, precision=None):
@@ -340,31 +374,33 @@
     column = lax.broadcasted_iota(jnp.int32, (picked, channels), 1)
     wanted = jnp.where(row < height, scalars[0] + row, scalars[1] + row - height)
     chosen = (column == wanted) & (row < 2 * height)
-    pick = jnp.where(chosen, 1.0, 0.0).astype(BF16)
 
     def halves(matrix):
         top = matrix.astype(BF16)
         return top, (matrix - top.astype(F32)).astype(BF16)
 
-    def rows_of(matrix):
-        top, rest = halves(matrix)
+    def rows_of(ref):
+        if height % 8 == 0:
+            starts = [pl.multiple_of(scalars[i], 8) for i in range(2)]
+            return jnp.concatenate([ref[pl.ds(start, height), :] for start in starts], 0)
+        pick = jnp.where(chosen, 1.0, 0.0).astype(BF16)
+        top, rest = halves(ref[...])
         return dot(pick, top, plain) + dot(pick, rest, plain)
 
-    second_gram = gram[...]
-    gram_rows = rows_of(second_gram)
+    gram_rows = rows_of(gram)
     second = NS_B * gram_rows
-    second = second + NS_C * dot(gram_rows.astype(BF16), second_gram.astype(BF16), plain)
+    second = second + NS_C * dot(gram_rows.astype(BF16), gram[...].astype(BF16), plain)
     both = (
         jnp.where(chosen, NS_A * NS_A, 0.0)
-        + NS_A * (rows_of(first[...]) + second)
+        + NS_A * (rows_of(first) + second)
         + dot(second.astype(BF16), first_low, plain)
     ) * scale
-    top, rest = halves(both)
+    both = jnp.concatenate(halves(both), 0)
     across = ((1,), (1,))
     for start in range(0, value.shape[0], 256):
         step = min(256, value.shape[0] - start)
-        piece = value[start : start + step]
-        out = dot(top, piece, across) + dot(rest, piece, across)
+        out = dot(both, value[start : start + step], across)
+        out = out[:picked] + out[picked:]
         mine[:, start : start + step] = out[:height]
         theirs[:, start : start + step] = out[height : 2 * height].astype(BF16)
 
@@ -393,15 +429,14 @@
     share = tile_rows // owners
     offset = own * share
     tokens = share * columns
-    live_rows = PATCH * lengths[tile]
-    scalars = jnp.concatenate([jnp.stack([live_rows, offset]), tissue[:, 0]])
-    scalars = scalars.astype(jnp.int32)
+    ids = jnp.stack([tile, offset, own]).astype(jnp.int32)
+    flags = tissue.reshape(-1)
     strip = features.reshape(tile_rows * columns, channels)
     taps = depth_kernel.reshape(KERNEL * KERNEL, channels)
     gain, scale = ln_gain[None], layer_scale[None]
     frame = pltpu.VMEM((tile_rows + 2 * MARGIN, columns, channels), F32)
     wide = pltpu.VMEM((share, columns, channels), F32)
-    rim = RIM * columns
+    rims = [jax.ShapeDtypeStruct((RIM * columns, channels), BF16)] * 2
 
     height = channels // tiles
     units = weight_up.shape[1] // PLANE
@@ -421,8 +456,9 @@
             place[None], *pieces,
         )
 
-    tail = lax.dynamic_slice_in_dim(strip, (live_rows - RIM) * columns, rim, 0)
-    before, after = neighbours(strip[:rim], tail)
+    place_ids = jnp.stack([tile, 0 * tile, 0 * tile]).astype(jnp.int32)
+    head, tail = call(rims_kernel, rims, [], 10**6, place_ids, lengths, strip, scalars=2)
+    before, after = neighbours(head, tail)
     piece, before, after = lax.optimization_barrier((piece, before, after))
     bias = lax.dynamic_slice_in_dim(bias_up, place * units, units, 0)
 
@@ -435,7 +471,9 @@
         ],
         [frame, wide],
         10**6,
-        scalars, strip, cotangent.reshape(strip.shape), before, after, taps, gain, scale,
+        ids, lengths, flags, strip, cotangent.reshape(strip.shape),
+        before, after, taps, gain, scale,
+        scalars=3,
     )
     held = piece[None]
     for bit in line_bits[:0:-1]:
@@ -511,10 +549,14 @@
         [jax.ShapeDtypeStruct((tokens, channels), BF16)] * 2,
         [],
         10**6,
-        scalars, strip, total, *moved, centred, inverse, gain, scale,
-    )
-
-    arrived, grad_mixed = lax.optimization_barrier((arrived, grad_mixed))
+        ids, lengths, flags, strip, total, *moved, centred, inverse, gain, scale,
+        scalars=3,
+    )
+
+    halves = [grad_mixed] + [swap(grad_mixed, "own", s) for s in range(1, owners)]
+    arrived, halves = lax.optimization_barrier((arrived, halves))
+    head, tail = call(rims_kernel, rims, [], 10**6, ids, lengths, *halves, scalars=2)
+    before, after = neighbours(head, tail)
     grad_t = (reduced + arrived.astype(F32)).astype(BF16)[0]
     group = PLANE * half_lines
     bits = [1 << i for i in range(group.bit_length() - 1)]
@@ -523,25 +565,20 @@
     orders = [bits[turn:] + bits[:turn] for turn in range(3)]
     for stage in range(len(bits)):
         came = [swap(held, "tile", order[stage]) for held, order in zip(helds, orders)]
+        if stage + 2 == len(bits):
+            came, before, after = lax.optimization_barrier((came, before, after))
         if stage + 1 < len(bits):
             shape = jax.ShapeDtypeStruct((2 << stage, third, channels), BF16)
             helds = call(double_kernel, [shape] * 3, [], 10**6, *helds, *came, scalars=0)
     thirds = [half for pair in zip(helds, came) for half in pair]
 
-    halves = [grad_mixed] + [swap(grad_mixed, "own", s) for s in range(1, owners)]
-    stacked = jnp.stack(halves)
-    head = lax.dynamic_slice_in_dim(stacked, own, 1, 0)[0, :rim]
-    last = live_rows - RIM
-    tail = lax.dynamic_slice(
-        stacked, ((last >> (share.bit_length() - 1)) ^ own, (last & (share - 1)) * columns, 0), (1, rim, channels)
-    )[0]
-    before, after = neighbours(head, tail)
     (grad_features,) = call(
         backward_kernel,
         [jax.ShapeDtypeStruct((tokens, channels), BF16)],
         [frame, wide],
         10**6,
-        scalars, cotangent.reshape(strip.shape), before, after, taps, *halves,
+        ids, lengths, cotangent.reshape(strip.shape), before, after, taps, *halves,
+        scalars=2,
     )
 
     other = tile ^ (PLANE * half_lines)

time: 141 us -> 140 us (level)
    unnamed x18 -> x30, local copies, waits for them, and re-layouts: 1.42 us -> 4.55 us
    dynamic_slice x2 -> x0, local copies, waits for them, and re-layouts: 2.04 us -> none  [the longest x1 1.24 us: shards(): live_rows = PATCH * lengths[tile]]
    pallas_call x13 -> x15, Pallas kernels: 27.4 us -> 26.8 us  [call(): pl.pallas_call(kernel, out_shape=out_shape, in_specs=[smem] * scalars + [...]
  transfers between devices with their start and end apart: 30 -> 30, of which waited for: 19 -> 19; matrix products, arithmetic and copies ran while one was open for 4% -> 2% of each run, Pallas kernels for 7% -> 8%
where the time goes in v6:
time: 140 us
  waiting for transfers between devices  58.4 us (42%)
  starting transfers between devices  45.1 us (32%)
  Pallas kernels  26.8 us (19%)
  local copies, waits for them, and re-layouts  5.44 us (4%)
  other arithmetic  3.32 us (2%)
    ppermute x26, waiting for transfers between devices, swap(): lax.ppermute(value, axis, [(i, i ^ bit) for i in range(lax.axis_size(axis...  48.8 us
    ppermute x26, starting transfers between devices, swap(): lax.ppermute(value, axis, [(i, i ^ bit) for i in range(lax.axis_size(axis...  35 us
    pallas_call x15, Pallas kernels, call(): pl.pallas_call(kernel, out_shape=out_shape, in_specs=[smem] * scalars + [...  26.8 us
    ppermute x4, starting transfers between devices, neighbours(): return (lax.ppermute(last, 'tile', up), lax.ppermute(first, 'tile', down))  10.1 us
    ppermute x4, waiting for transfers between devices, neighbours(): return (lax.ppermute(last, 'tile', up), lax.ppermute(first, 'tile', down))  9.64 us
    unnamed x30, local copies, waits for them, and re-layouts  4.55 us
  transfers between devices with their start and end apart: 30, of which 19 were waited for; matrix products, arithmetic and copies ran while one was open for 2% of the time, Pallas kernels for 8%

profile of v6, /device:TPU:0, one launch (start us, length us, event | category | flops | bytes accessed | tf_op | source)
XLA Modules:
  0.0 140.1 jit_solution(561600391226840261)
XLA Ops:
  0.7 1.0 fusion.1
  1.8 3.0 %collective-permute-start = (bf16[2,48,384]{2,1,0:T(8,128)(2,1)S(1)}, bf16[2,48,384]{2,1,0:T(8,128)(2,1)S(1)}, u32[]{:S(2)}, u32[]{:S(2)}) collective-permute-start(bf16[2,48,384]{2,1,0:T(8,128)(2,1)S(1)} %get-tuple-element.109), channel_id=1, source_target_pairs={{0,2},{2,0},{4,6},{6,4},{8,10},{10,8},{12,14},{14,12},{16,18},{18,... | collective-permute-start | bytes 221192 | tf_op jit(solution)/shard_map/ppermute | solution.py:30
  4.8 1.5 %collective-permute-start.1 = (bf16[2,48,384]{2,1,0:T(8,128)(2,1)S(1)}, bf16[2,48,384]{2,1,0:T(8,128)(2,1)S(1)}, u32[]{:S(2)}, u32[]{:S(2)}) collective-permute-start(bf16[2,48,384]{2,1,0:T(8,128)(2,1)S(1)} %get-tuple-element.110), channel_id=1, source_target_pairs={{0,4},{2,6},{4,0},{6,2},{8,12},{10,14},{12,8},{14,10},{16,20},{18,... | collective-permute-start | bytes 221192 | tf_op jit(solution)/shard_map/ppermute | solution.py:30
  6.3 1.0 copy-done
  8.5 3.9 %collective-permute-start.3 = (bf16[32,768]{1,0:T(8,128)(2,1)S(1)}, bf16[32,768]{1,0:T(8,128)(2,1)S(1)}, u32[]{:S(2)}, u32[]{:S(2)}) collective-permute-start(bf16[32,768]{1,0:T(8,128)(2,1)S(1)} %get-tuple-element.53), channel_id=1, source_target_pairs={{0,2},{2,4},{4,6},{6,8},{8,10},{10,12},{12,14},{14,16},{16,18},{18... | collective-permute-start | bytes 147464 | tf_op jit(solution)/shard_map/ppermute | solution.py:37
  12.4 1.3 collective-permute-start.4
  14.1 4.3 %collective-permute-done.4.after = bf16[32,768]{1,0:T(8,128)(2,1)S(1)} collective-permute-done((bf16[32,768]{1,0:T(8,128)(2,1)S(1)}, bf16[32,768]{1,0:T(8,128)(2,1)S(1)}, u32[]{:S(2)}, u32[]{:S(2)}) %collective-permute-start.4) | collective-permute-done | bytes 49184 | tf_op jit(solution)/shard_map/ppermute | solution.py:37
  18.4 3.8 %collective-permute-start.5 = (bf16[1,2,192,384]{3,2,1,0:T(8,128)(2,1)S(1)}, bf16[1,2,192,384]{3,2,1,0:T(8,128)(2,1)S(1)}, u32[]{:S(2)}, u32[]{:S(2)}) collective-permute-start(bf16[1,2,192,384]{3,2,1,0:T(8,128)(2,1)S(1)} %bitcast.26), channel_id=1, source_target_pairs={{0,16},{2,18},{4,20},{6,22},{8,24},{10,26},{12,28},{14,30},{16,0},... | collective-permute-start | bytes 884744 | tf_op jit(solution)/shard_map/ppermute | solution.py:30
  22.3 2.9 %shard_map.133 = (bf16[2,128,768]{2,1,0:T(8,128)(2,1)S(1)}, f32[128,768]{1,0:T(8,128)S(1)}, f32[128,128]{1,0:T(8,128)S(1)}) custom-call(s32[3]{0:T(128)S(1)} %get-tuple-element.111.ids, s32[16]{0:T(128)S(1)} %copy-done.8, s32[4]{0:T(128)S(1)} %bitcast.28, bf16[256,768]{1,0:T(8,128)(2,1)S(1)} %bitcast.22, bf16[256,768]{1,0:T(8,128)(2,1)S(1)} %bitcast.24, ...), custom_call_target="tpu_custom_call" | custom-call | flops 1000000 | bytes 1048576 | tf_op jit(solution)/shard_map/pallas_call | solution.py:52
  25.9 1.2 collective-permute-start.7
  27.1 2.9 %collective-permute-start.8 = (bf16[2,128,768]{2,1,0:T(8,128)(2,1)S(1)}, bf16[2,128,768]{2,1,0:T(8,128)(2,1)S(1)}, u32[]{:S(2)}, u32[]{:S(2)}) collective-permute-start(bf16[2,128,768]{2,1,0:T(8,128)(2,1)S(1)} %get-tuple-element.60.refs_0_), channel_id=1, source_target_pairs={{0,4},{2,6},{4,0},{6,2},{8,12},{10,14},{12,8},{14,10},{16,20},{18,... | collective-permute-start | bytes 1179656 | tf_op jit(solution)/shard_map/ppermute | solution.py:30
  30.0 3.2 %collective-permute-done.5.refs_1_ = bf16[1,2,192,384]{3,2,1,0:T(8,128)(2,1)S(1)} collective-permute-done((bf16[1,2,192,384]{3,2,1,0:T(8,128)(2,1)S(1)}, bf16[1,2,192,384]{3,2,1,0:T(8,128)(2,1)S(1)}, u32[]{:S(2)}, u32[]{:S(2)}) %collective-permute-start.5) | collective-permute-done | bytes 294944 | tf_op jit(solution)/shard_map/ppermute | solution.py:30
  33.2 2.2 %collective-permute-start.6 = (bf16[2,2,192,384]{3,2,1,0:T(8,128)(2,1)S(1)}, bf16[2,2,192,384]{3,2,1,0:T(8,128)(2,1)}, u32[]{:S(2)}, u32[]{:S(2)}) collective-permute-start(bf16[2,2,192,384]{3,2,1,0:T(8,128)(2,1)S(1)} %shard_map.131.early), channel_id=1, source_target_pairs={{0,8},{2,10},{4,12},{6,14},{8,0},{10,2},{12,4},{14,6},{16,24},{18,... | collective-permute-start | bytes 1769480 | tf_op jit(solution)/shard_map/ppermute | solution.py:30
  35.5 2.4 %collective-permute-done.7.refs_1_ = bf16[2,128,768]{2,1,0:T(8,128)(2,1)S(1)} collective-permute-done((bf16[2,128,768]{2,1,0:T(8,128)(2,1)S(1)}, bf16[2,128,768]{2,1,0:T(8,128)(2,1)S(1)}, u32[]{:S(2)}, u32[]{:S(2)}) %collective-permute-start.7) | collective-permute-done | bytes 393248 | tf_op jit(solution)/shard_map/ppermute | solution.py:30
  37.9 6.4 %collective-permute-done.8.refs_2_ = bf16[2,128,768]{2,1,0:T(8,128)(2,1)S(1)} collective-permute-done((bf16[2,128,768]{2,1,0:T(8,128)(2,1)S(1)}, bf16[2,128,768]{2,1,0:T(8,128)(2,1)S(1)}, u32[]{:S(2)}, u32[]{:S(2)}) %collective-permute-start.8) | collective-permute-done | bytes 393248 | tf_op jit(solution)/shard_map/ppermute | solution.py:30
  45.2 2.3 %collective-permute-done.6.late = bf16[2,2,192,384]{3,2,1,0:T(8,128)(2,1)} collective-permute-done((bf16[2,2,192,384]{3,2,1,0:T(8,128)(2,1)S(1)}, bf16[2,2,192,384]{3,2,1,0:T(8,128)(2,1)}, u32[]{:S(2)}, u32[]{:S(2)}) %collective-permute-start.6) | collective-permute-done | bytes 589856 | tf_op jit(solution)/shard_map/ppermute | solution.py:30
  47.5 1.2 shard_map.132
  48.7 5.7 %shard_map.135 = (bf16[2,192,768]{2,1,0:T(8,128)(2,1)S(1)}, bf16[2,192,768]{2,1,0:T(8,128)(2,1)}, bf16[1024,384]{1,0:T(8,128)(2,1)S(1)}, bf16[1024,384]{1,0:T(8,128)(2,1)S(1)}) custom-call(s32[1]{0:T(128)} %bitcast.5.scalars, bf16[768,384]{1,0:T(8,128)(2,1)S(1)} %get-tuple-element.56.up, bf16[768,384]{1,0:T(8,128)(2,1)S(1)} %get-tuple-element.57.down_t, ...), custom_call_target="tpu_custom_call" | custom-call | flops 5000000000 | bytes 1048576 | tf_op jit(solution)/shard_map/pallas_call | solution.py:52
  54.4 1.9 %shard_map.136 = (f32[2,512,768]{2,1,0:T(8,128)S(1)}, bf16[2,512,768]{2,1,0:T(8,128)(2,1)S(1)}) custom-call(bf16[1024,384]{1,0:T(8,128)(2,1)S(1)} %get-tuple-element.61.act, bf16[1024,384]{1,0:T(8,128)(2,1)S(1)} %get-tuple-element.62.grad_hidden, bf16[768,384]{1,0:T(8,128)(2,1)S(1)} %get-tuple-element.56.up, bf16[768,384]{1,0:T(8,128)(2,1)S(1)} %get-tuple-element.57.down_t), custom_call_target="tpu_custom_call" | custom-call | flops 1000000000 | bytes 1048576 | tf_op jit(solution)/shard_map/pallas_call | solution.py:52
  56.4 1.4 %collective-permute-start.12 = (bf16[2,192,768]{2,1,0:T(8,128)(2,1)}, bf16[2,192,768]{2,1,0:T(8,128)(2,1)}, u32[]{:S(2)}, u32[]{:S(2)}) collective-permute-start(bf16[2,192,768]{2,1,0:T(8,128)(2,1)} %get-tuple-element.66), channel_id=1, source_target_pairs={{0,8},{2,10},{4,12},{6,14},{8,0},{10,2},{12,4},{14,6},{16,24},{18,... | collective-permute-start | bytes 1769480 | tf_op jit(solution)/shard_map/ppermute | solution.py:30
  57.8 2.0 %collective-permute-done.11.refs_0_ = bf16[2,512,768]{2,1,0:T(8,128)(2,1)S(1)} collective-permute-done((bf16[2,512,768]{2,1,0:T(8,128)(2,1)S(1)}, bf16[2,512,768]{2,1,0:T(8,128)(2,1)S(1)}, u32[]{:S(2)}, u32[]{:S(2)}) %collective-permute-start.11) | collective-permute-done | bytes 1572896 | tf_op jit(solution)/shard_map/ppermute | solution.py:30
  59.8 1.0 shard_map.137
  63.0 1.3 collective-permute-start.13
  64.3 1.2 collective-permute-start.14
  65.6 0.9 collective-permute-start.15
  66.5 6.0 %collective-permute-done.12 = bf16[2,192,768]{2,1,0:T(8,128)(2,1)} collective-permute-done((bf16[2,192,768]{2,1,0:T(8,128)(2,1)}, bf16[2,192,768]{2,1,0:T(8,128)(2,1)}, u32[]{:S(2)}, u32[]{:S(2)}) %collective-permute-start.12) | collective-permute-done | bytes 589856 | tf_op jit(solution)/shard_map/ppermute | solution.py:30
  72.5 2.7 %collective-permute-done.13.one = bf16[2,128,768]{2,1,0:T(8,128)(2,1)S(1)} collective-permute-done((bf16[2,128,768]{2,1,0:T(8,128)(2,1)}, bf16[2,128,768]{2,1,0:T(8,128)(2,1)S(1)}, u32[]{:S(2)}, u32[]{:S(2)}) %collective-permute-start.13) | collective-permute-done | bytes 393248 | tf_op jit(solution)/shard_map/ppermute | solution.py:30
  75.2 1.3 convert_add_fusion
  76.5 3.0 %collective-permute-start.16 = (bf16[1,192,768]{2,1,0:T(8,128)(2,1)S(1)}, bf16[1,192,768]{2,1,0:T(8,128)(2,1)S(1)}, u32[]{:S(2)}, u32[]{:S(2)}) collective-permute-start(bf16[1,192,768]{2,1,0:T(8,128)(2,1)S(1)} %dynamic-slice_convert_fusion), channel_id=1, source_target_pairs={{0,16},{2,18},{4,20},{6,22},{8,24},{10,26},{12,28},{14,30},{16,0},... | collective-permute-start | bytes 884744 | tf_op jit(solution)/shard_map/ppermute | solution.py:30
  79.5 4.3 %collective-permute-done.14.two = bf16[2,128,768]{2,1,0:T(8,128)(2,1)S(1)} collective-permute-done((bf16[2,128,768]{2,1,0:T(8,128)(2,1)}, bf16[2,128,768]{2,1,0:T(8,128)(2,1)S(1)}, u32[]{:S(2)}, u32[]{:S(2)}) %collective-permute-start.14) | collective-permute-done | bytes 393248 | tf_op jit(solution)/shard_map/ppermute | solution.py:30
  83.9 1.8 %shard_map.138 = (bf16[128,768]{1,0:T(8,128)(2,1)S(1)}, bf16[128,768]{1,0:T(8,128)(2,1)}) custom-call(s32[3]{0:T(128)S(1)} %get-tuple-element.111.ids, s32[16]{0:T(128)S(1)} %copy-done.8, s32[4]{0:T(128)S(1)} %bitcast.29, bf16[256,768]{1,0:T(8,128)(2,1)S(1)} %bitcast.23, bf16[2,128,768]{2,1,0:T(8,128)(2,1)S(1)} %copy-done.4, ...), custom_call_target="tpu_custom_call" | custom-call | flops 1000000 | bytes 1048576 | tf_op jit(solution)/shard_map/pallas_call | solution.py:52
  85.6 1.4 %collective-permute-done.17.refs_1_.rest_1_ = bf16[128,768]{1,0:T(8,128)(2,1)S(1)} collective-permute-done((bf16[128,768]{1,0:T(8,128)(2,1)S(1)}, bf16[128,768]{1,0:T(8,128)(2,1)S(1)}, u32[]{:S(2)}, u32[]{:S(2)}) %collective-permute-start.17) | collective-permute-done | bytes 196640 | tf_op jit(solution)/shard_map/ppermute | solution.py:30
  87.1 4.5 %collective-permute-done.16 = bf16[1,192,768]{2,1,0:T(8,128)(2,1)S(1)} collective-permute-done((bf16[1,192,768]{2,1,0:T(8,128)(2,1)S(1)}, bf16[1,192,768]{2,1,0:T(8,128)(2,1)S(1)}, u32[]{:S(2)}, u32[]{:S(2)}) %collective-permute-start.16) | collective-permute-done | bytes 294944 | tf_op jit(solution)/shard_map/ppermute | solution.py:30
  91.6 1.7 %collective-permute-start.18 = (bf16[1,64,768]{2,1,0:T(8,128)(2,1)S(1)}, bf16[1,64,768]{2,1,0:T(8,128)(2,1)S(1)}, u32[]{:S(2)}, u32[]{:S(2)}) collective-permute-start(bf16[1,64,768]{2,1,0:T(8,128)(2,1)S(1)} %get-tuple-element.106.refs_0_), channel_id=1, source_target_pairs={{0,2},{2,0},{4,6},{6,4},{8,10},{10,8},{12,14},{14,12},{16,18},{18,... | collective-permute-start | bytes 294920 | tf_op jit(solution)/shard_map/ppermute | solution.py:30
  94.0 2.2 %collective-permute-done.18.refs_3_ = bf16[1,64,768]{2,1,0:T(8,128)(2,1)S(1)} collective-permute-done((bf16[1,64,768]{2,1,0:T(8,128)(2,1)S(1)}, bf16[1,64,768]{2,1,0:T(8,128)(2,1)S(1)}, u32[]{:S(2)}, u32[]{:S(2)}) %collective-permute-start.18) | collective-permute-done | bytes 98336 | tf_op jit(solution)/shard_map/ppermute | solution.py:30
  96.3 1.6 %collective-permute-done.19.refs_4_ = bf16[1,64,768]{2,1,0:T(8,128)(2,1)S(1)} collective-permute-done((bf16[1,64,768]{2,1,0:T(8,128)(2,1)S(1)}, bf16[1,64,768]{2,1,0:T(8,128)(2,1)S(1)}, u32[]{:S(2)}, u32[]{:S(2)}) %collective-permute-start.19) | collective-permute-done | bytes 98336 | tf_op jit(solution)/shard_map/ppermute | solution.py:30
  98.6 1.5 %collective-permute-start.21 = (bf16[2,64,768]{2,1,0:T(8,128)(2,1)S(1)}, bf16[2,64,768]{2,1,0:T(8,128)(2,1)S(1)}, u32[]{:S(2)}, u32[]{:S(2)}) collective-permute-start(bf16[2,64,768]{2,1,0:T(8,128)(2,1)S(1)} %get-tuple-element.78.refs_0_), channel_id=1, source_target_pairs={{0,4},{2,6},{4,0},{6,2},{8,12},{10,14},{12,8},{14,10},{16,20},{18,... | collective-permute-start | bytes 589832 | tf_op jit(solution)/shard_map/ppermute | solution.py:30
  101.8 3.5 %collective-permute-start.24 = (bf16[32,768]{1,0:T(8,128)(2,1)S(1)}, bf16[32,768]{1,0:T(8,128)(2,1)S(1)}, u32[]{:S(2)}, u32[]{:S(2)}) collective-permute-start(bf16[32,768]{1,0:T(8,128)(2,1)S(1)} %get-tuple-element.83), channel_id=1, source_target_pairs={{0,2},{2,4},{4,6},{6,8},{8,10},{10,12},{12,14},{14,16},{16,18},{18... | collective-permute-start | bytes 147464 | tf_op jit(solution)/shard_map/ppermute | solution.py:37
  105.3 1.5 %collective-permute-start.25 = (bf16[32,768]{1,0:T(8,128)(2,1)S(1)}, bf16[32,768]{1,0:T(8,128)(2,1)S(1)}, u32[]{:S(2)}, u32[]{:S(2)}) collective-permute-start(bf16[32,768]{1,0:T(8,128)(2,1)S(1)} %get-tuple-element.84), channel_id=1, source_target_pairs={{2,0},{4,2},{6,4},{8,6},{10,8},{12,10},{14,12},{16,14},{18,16},{20... | collective-permute-start | bytes 147464 | tf_op jit(solution)/shard_map/ppermute | solution.py:37
  107.0 4.8 %collective-permute-done.25.after = bf16[32,768]{1,0:T(8,128)(2,1)S(1)} collective-permute-done((bf16[32,768]{1,0:T(8,128)(2,1)S(1)}, bf16[32,768]{1,0:T(8,128)(2,1)S(1)}, u32[]{:S(2)}, u32[]{:S(2)}) %collective-permute-start.25) | collective-permute-done | bytes 49184 | tf_op jit(solution)/shard_map/ppermute | solution.py:37
  111.9 1.2 collective-permute-start.26
  113.1 1.7 %collective-permute-start.27 = (bf16[4,64,768]{2,1,0:T(8,128)(2,1)S(1)}, bf16[4,64,768]{2,1,0:T(8,128)(2,1)S(1)}, u32[]{:S(2)}, u32[]{:S(2)}) collective-permute-start(bf16[4,64,768]{2,1,0:T(8,128)(2,1)S(1)} %get-tuple-element.96.refs_2_), channel_id=1, source_target_pairs={{0,2},{2,0},{4,6},{6,4},{8,10},{10,8},{12,14},{14,12},{16,18},{18,... | collective-permute-start | bytes 1179656 | tf_op jit(solution)/shard_map/ppermute | solution.py:30
  114.8 3.9 %collective-permute-start.28 = (bf16[4,64,768]{2,1,0:T(8,128)(2,1)S(1)}, bf16[4,64,768]{2,1,0:T(8,128)(2,1)S(1)}, u32[]{:S(2)}, u32[]{:S(2)}) collective-permute-start(bf16[4,64,768]{2,1,0:T(8,128)(2,1)S(1)} %get-tuple-element.98.refs_4_), channel_id=1, source_target_pairs={{0,4},{2,6},{4,0},{6,2},{8,12},{10,14},{12,8},{14,10},{16,20},{18,... | collective-permute-start | bytes 1179656 | tf_op jit(solution)/shard_map/ppermute | solution.py:30
  118.7 3.3 %shard_map.142 = bf16[128,768]{1,0:T(8,128)(2,1)} custom-call(s32[3]{0:T(128)S(1)} %get-tuple-element.111.ids, s32[16]{0:T(128)S(1)} %copy-done.8, bf16[256,768]{1,0:T(8,128)(2,1)S(1)} %bitcast.25, bf16[32,768]{1,0:T(8,128)(2,1)S(1)} %collective-permute-done.24.before, bf16[32,768]{1,0:T(8,128)(2,1)S(1)} %collective-permute-done.25.after, ...), custom_call_target="tpu_custom_call" | custom-call | flops 1000000 | bytes 1048576 | tf_op jit(solution)/shard_map/pallas_call | solution.py:52
  122.0 2.4 %collective-permute-done.28.refs_5_ = bf16[4,64,768]{2,1,0:T(8,128)(2,1)S(1)} collective-permute-done((bf16[4,64,768]{2,1,0:T(8,128)(2,1)S(1)}, bf16[4,64,768]{2,1,0:T(8,128)(2,1)S(1)}, u32[]{:S(2)}, u32[]{:S(2)}) %collective-permute-start.28) | collective-permute-done | bytes 393248 | tf_op jit(solution)/shard_map/ppermute | solution.py:30
  124.4 7.6 %shard_map.143 = (f32[48,1536]{1,0:T(8,128)S(1)}, bf16[48,1536]{1,0:T(8,128)(2,1)S(1)}) custom-call(s32[3]{0:T(128)S(1)} %get-tuple-element.112.scalars, bf16[4,64,768]{2,1,0:T(8,128)(2,1)S(1)} %get-tuple-element.94.refs_0_, bf16[4,64,768]{2,1,0:T(8,128)(2,1)S(1)} %collective-permute-done.26.refs_1_, bf16[4,64,768]{2,1,0:T(8,128)(2,1)S(1)} %get-tuple-element.96.refs_2_, ...), custom_call_target="tpu_custom_call" | custom-call | flops 10000000000 | bytes 1048576 | tf_op jit(solution)/shard_map/pallas_call | solution.py:52
  132.4 6.8 %collective-permute-done.29 = bf16[48,1536]{1,0:T(8,128)(2,1)S(1)} collective-permute-done((bf16[48,1536]{1,0:T(8,128)(2,1)S(1)}, bf16[48,1536]{1,0:T(8,128)(2,1)S(1)}, u32[]{:S(2)}, u32[]{:S(2)}) %collective-permute-start.29) | collective-permute-done | bytes 147488 | tf_op jit(solution)/shard_map/ppermute | solution.py:30
  139.2 0.9 fusion
  (70 shorter events, 9.8 us)
Async XLA Ops:
  0.6 21.7 %copy-start.1 = (bf16[32,8,768]{2,1,0:T(8,128)(2,1)S(1)}, bf16[32,8,768]{2,1,0:T(8,128)(2,1)}, u32[]{:S(2)}) copy-start(bf16[32,8,768]{2,1,0:T(8,128)(2,1)} %param.10) | copy-start | bytes 1179652
  0.6 21.7 %copy-start.8 = (s32[16]{0:T(128)S(1)}, s32[16]{0:T(128)}, u32[]{:S(2)}) copy-start(s32[16]{0:T(128)} %lengths.9) | copy-start | bytes 196
  0.7 21.5 %copy-start.12 = (f32[7,7,768]{2,1,0:T(8,128)S(1)}, f32[7,7,768]{2,1,0:T(8,128)}, u32[]{:S(2)}) copy-start(f32[7,7,768]{2,1,0:T(8,128)} %param.12) | copy-start | bytes 451588
  0.7 21.5 %copy-start.13 = (f32[768]{0:T(1024)S(1)}, f32[768]{0:T(1024)}, u32[]{:S(2)}) copy-start(f32[768]{0:T(1024)} %param.13) | copy-start | bytes 9220
  0.7 21.5 %copy-start.14 = (f32[768]{0:T(1024)S(1)}, f32[768]{0:T(1024)}, u32[]{:S(2)}) copy-start(f32[768]{0:T(1024)} %param.17) | copy-start | bytes 9220
  0.7 21.6 %copy-start.9 = (s32[4,1]{0,1:T(1,128)S(1)}, s32[4,1]{0,1:T(1,128)}, u32[]{:S(2)}) copy-start(s32[4,1]{0,1:T(1,128)} %param.18) | copy-start | bytes 52
  1.8 11.9 %collective-permute-start = (bf16[2,48,384]{2,1,0:T(8,128)(2,1)S(1)}, bf16[2,48,384]{2,1,0:T(8,128)(2,1)S(1)}, u32[]{:S(2)}, u32[]{:S(2)}) collective-permute-start(bf16[2,48,384]{2,1,0:T(8,128)(2,1)S(1)} %get-tuple-element.109), channel_id=1, source_target_pairs={{0,2},{2,0},{4,6},{6,4},{8,10},{10,8},{12,14},{14,12},{16,18},{18,... | collective-permute-start | bytes 221192 | tf_op jit(solution)/shard_map/ppermute | solution.py:30
  4.8 8.9 %collective-permute-start.1 = (bf16[2,48,384]{2,1,0:T(8,128)(2,1)S(1)}, bf16[2,48,384]{2,1,0:T(8,128)(2,1)S(1)}, u32[]{:S(2)}, u32[]{:S(2)}) collective-permute-start(bf16[2,48,384]{2,1,0:T(8,128)(2,1)S(1)} %get-tuple-element.110), channel_id=1, source_target_pairs={{0,4},{2,6},{4,0},{6,2},{8,12},{10,14},{12,8},{14,10},{16,20},{18,... | collective-permute-start | bytes 221192 | tf_op jit(solution)/shard_map/ppermute | solution.py:30
  6.3 7.4 %collective-permute-start.2 = (bf16[2,48,384]{2,1,0:T(8,128)(2,1)S(1)}, bf16[2,48,384]{2,1,0:T(8,128)(2,1)S(1)}, u32[]{:S(2)}, u32[]{:S(2)}) collective-permute-start(bf16[2,48,384]{2,1,0:T(8,128)(2,1)S(1)} %get-tuple-element.107), channel_id=1, source_target_pairs={{0,6},{2,4},{4,2},{6,0},{8,14},{10,12},{12,10},{14,8},{16,22},{18,... | collective-permute-start | bytes 221192 | tf_op jit(solution)/shard_map/ppermute | solution.py:30
  6.3 1.0 copy-start
  7.3 0.7 copy-start.7
  8.0 14.3 %copy-start.2 = (bf16[32,8,768]{2,1,0:T(8,128)(2,1)S(1)}, bf16[32,8,768]{2,1,0:T(8,128)(2,1)}, u32[]{:S(2)}) copy-start(bf16[32,8,768]{2,1,0:T(8,128)(2,1)} %param.11) | copy-start | bytes 1179652
  8.5 5.6 %collective-permute-start.3 = (bf16[32,768]{1,0:T(8,128)(2,1)S(1)}, bf16[32,768]{1,0:T(8,128)(2,1)S(1)}, u32[]{:S(2)}, u32[]{:S(2)}) collective-permute-start(bf16[32,768]{1,0:T(8,128)(2,1)S(1)} %get-tuple-element.53), channel_id=1, source_target_pairs={{0,2},{2,4},{4,6},{6,8},{8,10},{10,12},{12,14},{14,16},{16,18},{18... | collective-permute-start | bytes 147464 | tf_op jit(solution)/shard_map/ppermute | solution.py:37
  12.4 6.0 %collective-permute-start.4 = (bf16[32,768]{1,0:T(8,128)(2,1)S(1)}, bf16[32,768]{1,0:T(8,128)(2,1)S(1)}, u32[]{:S(2)}, u32[]{:S(2)}) collective-permute-start(bf16[32,768]{1,0:T(8,128)(2,1)S(1)} %get-tuple-element.54), channel_id=1, source_target_pairs={{2,0},{4,2},{6,4},{8,6},{10,8},{12,10},{14,12},{16,14},{18,16},{20... | collective-permute-start | bytes 147464 | tf_op jit(solution)/shard_map/ppermute | solution.py:37
  18.4 14.8 %collective-permute-start.5 = (bf16[1,2,192,384]{3,2,1,0:T(8,128)(2,1)S(1)}, bf16[1,2,192,384]{3,2,1,0:T(8,128)(2,1)S(1)}, u32[]{:S(2)}, u32[]{:S(2)}) collective-permute-start(bf16[1,2,192,384]{3,2,1,0:T(8,128)(2,1)S(1)} %bitcast.26), channel_id=1, source_target_pairs={{0,16},{2,18},{4,20},{6,22},{8,24},{10,26},{12,28},{14,30},{16,0},... | collective-permute-start | bytes 884744 | tf_op jit(solution)/shard_map/ppermute | solution.py:30
  25.3 0.6 copy-start.5
  25.9 12.0 %collective-permute-start.7 = (bf16[2,128,768]{2,1,0:T(8,128)(2,1)S(1)}, bf16[2,128,768]{2,1,0:T(8,128)(2,1)S(1)}, u32[]{:S(2)}, u32[]{:S(2)}) collective-permute-start(bf16[2,128,768]{2,1,0:T(8,128)(2,1)S(1)} %get-tuple-element.60.refs_0_), channel_id=1, source_target_pairs={{0,2},{2,0},{4,6},{6,4},{8,10},{10,8},{12,14},{14,12},{16,18},{18,... | collective-permute-start | bytes 1179656 | tf_op jit(solution)/shard_map/ppermute | solution.py:30
  27.1 17.1 %collective-permute-start.8 = (bf16[2,128,768]{2,1,0:T(8,128)(2,1)S(1)}, bf16[2,128,768]{2,1,0:T(8,128)(2,1)S(1)}, u32[]{:S(2)}, u32[]{:S(2)}) collective-permute-start(bf16[2,128,768]{2,1,0:T(8,128)(2,1)S(1)} %get-tuple-element.60.refs_0_), channel_id=1, source_target_pairs={{0,4},{2,6},{4,0},{6,2},{8,12},{10,14},{12,8},{14,10},{16,20},{18,... | collective-permute-start | bytes 1179656 | tf_op jit(solution)/shard_map/ppermute | solution.py:30
  30.0 14.2 %collective-permute-start.9 = (bf16[2,128,768]{2,1,0:T(8,128)(2,1)S(1)}, bf16[2,128,768]{2,1,0:T(8,128)(2,1)S(1)}, u32[]{:S(2)}, u32[]{:S(2)}) collective-permute-start(bf16[2,128,768]{2,1,0:T(8,128)(2,1)S(1)} %get-tuple-element.60.refs_0_), channel_id=1, source_target_pairs={{0,6},{2,4},{4,2},{6,0},{8,14},{10,12},{12,10},{14,8},{16,22},{18,... | collective-permute-start | bytes 1179656 | tf_op jit(solution)/shard_map/ppermute | solution.py:30
  33.2 14.3 %collective-permute-start.6 = (bf16[2,2,192,384]{3,2,1,0:T(8,128)(2,1)S(1)}, bf16[2,2,192,384]{3,2,1,0:T(8,128)(2,1)}, u32[]{:S(2)}, u32[]{:S(2)}) collective-permute-start(bf16[2,2,192,384]{3,2,1,0:T(8,128)(2,1)S(1)} %shard_map.131.early), channel_id=1, source_target_pairs={{0,8},{2,10},{4,12},{6,14},{8,0},{10,2},{12,4},{14,6},{16,24},{18,... | collective-permute-start | bytes 1769480 | tf_op jit(solution)/shard_map/ppermute | solution.py:30
  44.4 4.3 %collective-permute-start.10 = (bf16[2,512,768]{2,1,0:T(8,128)(2,1)S(1)}, bf16[2,512,768]{2,1,0:T(8,128)(2,1)}, u32[]{:S(2)}, u32[]{:S(2)}) collective-permute-start(bf16[2,512,768]{2,1,0:T(8,128)(2,1)S(1)} %shard_map.134.refs_0_), channel_id=1, source_target_pairs={{0,1},{1,0},{2,3},{3,2},{4,5},{5,4},{6,7},{7,6},{8,9},{9,8},{10,11... | collective-permute-start | bytes 4718600 | tf_op jit(solution)/shard_map/ppermute | solution.py:30
  56.3 3.5 %collective-permute-start.11 = (bf16[2,512,768]{2,1,0:T(8,128)(2,1)S(1)}, bf16[2,512,768]{2,1,0:T(8,128)(2,1)S(1)}, u32[]{:S(2)}, u32[]{:S(2)}) collective-permute-start(bf16[2,512,768]{2,1,0:T(8,128)(2,1)S(1)} %get-tuple-element.64), channel_id=1, source_target_pairs={{0,1},{1,0},{2,3},{3,2},{4,5},{5,4},{6,7},{7,6},{8,9},{9,8},{10,11... | collective-permute-start | bytes 4718600 | tf_op jit(solution)/shard_map/ppermute | solution.py:30
  56.4 16.1 %collective-permute-start.12 = (bf16[2,192,768]{2,1,0:T(8,128)(2,1)}, bf16[2,192,768]{2,1,0:T(8,128)(2,1)}, u32[]{:S(2)}, u32[]{:S(2)}) collective-permute-start(bf16[2,192,768]{2,1,0:T(8,128)(2,1)} %get-tuple-element.66), channel_id=1, source_target_pairs={{0,8},{2,10},{4,12},{6,14},{8,0},{10,2},{12,4},{14,6},{16,24},{18,... | collective-permute-start | bytes 1769480 | tf_op jit(solution)/shard_map/ppermute | solution.py:30
  60.7 0.8 copy-start.3
  61.5 0.7 copy-start.10
  62.2 0.7 copy-start.11
  63.0 12.2 %collective-permute-start.13 = (bf16[2,128,768]{2,1,0:T(8,128)(2,1)}, bf16[2,128,768]{2,1,0:T(8,128)(2,1)S(1)}, u32[]{:S(2)}, u32[]{:S(2)}) collective-permute-start(bf16[2,128,768]{2,1,0:T(8,128)(2,1)} %get-tuple-element.67), channel_id=1, source_target_pairs={{0,2},{2,0},{4,6},{6,4},{8,10},{10,8},{12,14},{14,12},{16,18},{18,... | collective-permute-start | bytes 1179656 | tf_op jit(solution)/shard_map/ppermute | solution.py:30
  64.3 19.5 %collective-permute-start.14 = (bf16[2,128,768]{2,1,0:T(8,128)(2,1)}, bf16[2,128,768]{2,1,0:T(8,128)(2,1)S(1)}, u32[]{:S(2)}, u32[]{:S(2)}) collective-permute-start(bf16[2,128,768]{2,1,0:T(8,128)(2,1)} %copy-done.11), channel_id=1, source_target_pairs={{0,4},{2,6},{4,0},{6,2},{8,12},{10,14},{12,8},{14,10},{16,20},{18,... | collective-permute-start | bytes 1179656 | tf_op jit(solution)/shard_map/ppermute | solution.py:30
  65.6 18.3 %collective-permute-start.15 = (bf16[2,128,768]{2,1,0:T(8,128)(2,1)}, bf16[2,128,768]{2,1,0:T(8,128)(2,1)S(1)}, u32[]{:S(2)}, u32[]{:S(2)}) collective-permute-start(bf16[2,128,768]{2,1,0:T(8,128)(2,1)} %copy-done.10), channel_id=1, source_target_pairs={{0,6},{2,4},{4,2},{6,0},{8,14},{10,12},{12,10},{14,8},{16,22},{18,... | collective-permute-start | bytes 1179656 | tf_op jit(solution)/shard_map/ppermute | solution.py:30
  75.2 8.7 %copy-start.4 = (bf16[2,128,768]{2,1,0:T(8,128)(2,1)S(1)}, bf16[2,128,768]{2,1,0:T(8,128)(2,1)}, u32[]{:S(2)}) copy-start(bf16[2,128,768]{2,1,0:T(8,128)(2,1)} %copy-done.3) | copy-start | bytes 1179652
  75.2 8.7 %copy-start.6 = (f32[128,128]{1,0:T(8,128)S(1)}, f32[128,128]{1,0:T(8,128)}, u32[]{:S(2)}) copy-start(f32[128,128]{1,0:T(8,128)} %copy-done.5) | copy-start | bytes 196612
  76.5 15.0 %collective-permute-start.16 = (bf16[1,192,768]{2,1,0:T(8,128)(2,1)S(1)}, bf16[1,192,768]{2,1,0:T(8,128)(2,1)S(1)}, u32[]{:S(2)}, u32[]{:S(2)}) collective-permute-start(bf16[1,192,768]{2,1,0:T(8,128)(2,1)S(1)} %dynamic-slice_convert_fusion), channel_id=1, source_target_pairs={{0,16},{2,18},{4,20},{6,22},{8,24},{10,26},{12,28},{14,30},{16,0},... | collective-permute-start | bytes 884744 | tf_op jit(solution)/shard_map/ppermute | solution.py:30
  85.6 1.4 %collective-permute-start.17 = (bf16[128,768]{1,0:T(8,128)(2,1)S(1)}, bf16[128,768]{1,0:T(8,128)(2,1)S(1)}, u32[]{:S(2)}, u32[]{:S(2)}) collective-permute-start(bf16[128,768]{1,0:T(8,128)(2,1)S(1)} %get-tuple-element.81.refs_0_.rest_0_), channel_id=1, source_target_pairs={{0,1},{1,0},{2,3},{3,2},{4,5},{5,4},{6,7},{7,6},{8,9},{9,8},{10,11... | collective-permute-start | bytes 589832 | tf_op jit(solution)/shard_map/ppermute | solution.py:30
  91.6 4.7 %collective-permute-start.18 = (bf16[1,64,768]{2,1,0:T(8,128)(2,1)S(1)}, bf16[1,64,768]{2,1,0:T(8,128)(2,1)S(1)}, u32[]{:S(2)}, u32[]{:S(2)}) collective-permute-start(bf16[1,64,768]{2,1,0:T(8,128)(2,1)S(1)} %get-tuple-element.106.refs_0_), channel_id=1, source_target_pairs={{0,2},{2,0},{4,6},{6,4},{8,10},{10,8},{12,14},{14,12},{16,18},{18,... | collective-permute-start | bytes 294920 | tf_op jit(solution)/shard_map/ppermute | solution.py:30
  93.3 4.6 %collective-permute-start.19 = (bf16[1,64,768]{2,1,0:T(8,128)(2,1)S(1)}, bf16[1,64,768]{2,1,0:T(8,128)(2,1)S(1)}, u32[]{:S(2)}, u32[]{:S(2)}) collective-permute-start(bf16[1,64,768]{2,1,0:T(8,128)(2,1)S(1)} %get-tuple-element.105.refs_1_), channel_id=1, source_target_pairs={{0,4},{2,6},{4,0},{6,2},{8,12},{10,14},{12,8},{14,10},{16,20},{18,... | collective-permute-start | bytes 294920 | tf_op jit(solution)/shard_map/ppermute | solution.py:30
  93.9 4.6 %collective-permute-start.20 = (bf16[1,64,768]{2,1,0:T(8,128)(2,1)S(1)}, bf16[1,64,768]{2,1,0:T(8,128)(2,1)S(1)}, u32[]{:S(2)}, u32[]{:S(2)}) collective-permute-start(bf16[1,64,768]{2,1,0:T(8,128)(2,1)S(1)} %get-tuple-element.104.refs_2_), channel_id=1, source_target_pairs={{0,8},{2,10},{4,12},{6,14},{8,0},{10,2},{12,4},{14,6},{16,24},{18,... | collective-permute-start | bytes 294920 | tf_op jit(solution)/shard_map/ppermute | solution.py:30
  98.6 13.2 %collective-permute-start.21 = (bf16[2,64,768]{2,1,0:T(8,128)(2,1)S(1)}, bf16[2,64,768]{2,1,0:T(8,128)(2,1)S(1)}, u32[]{:S(2)}, u32[]{:S(2)}) collective-permute-start(bf16[2,64,768]{2,1,0:T(8,128)(2,1)S(1)} %get-tuple-element.78.refs_0_), channel_id=1, source_target_pairs={{0,4},{2,6},{4,0},{6,2},{8,12},{10,14},{12,8},{14,10},{16,20},{18,... | collective-permute-start | bytes 589832 | tf_op jit(solution)/shard_map/ppermute | solution.py:30
  100.0 11.8 %collective-permute-start.22 = (bf16[2,64,768]{2,1,0:T(8,128)(2,1)S(1)}, bf16[2,64,768]{2,1,0:T(8,128)(2,1)S(1)}, u32[]{:S(2)}, u32[]{:S(2)}) collective-permute-start(bf16[2,64,768]{2,1,0:T(8,128)(2,1)S(1)} %get-tuple-element.79.refs_1_), channel_id=1, source_target_pairs={{0,8},{2,10},{4,12},{6,14},{8,0},{10,2},{12,4},{14,6},{16,24},{18,... | collective-permute-start | bytes 589832 | tf_op jit(solution)/shard_map/ppermute | solution.py:30
  100.8 11.0 %collective-permute-start.23 = (bf16[2,64,768]{2,1,0:T(8,128)(2,1)S(1)}, bf16[2,64,768]{2,1,0:T(8,128)(2,1)S(1)}, u32[]{:S(2)}, u32[]{:S(2)}) collective-permute-start(bf16[2,64,768]{2,1,0:T(8,128)(2,1)S(1)} %get-tuple-element.80.refs_2_), channel_id=1, source_target_pairs={{0,2},{2,0},{4,6},{6,4},{8,10},{10,8},{12,14},{14,12},{16,18},{18,... | collective-permute-start | bytes 589832 | tf_op jit(solution)/shard_map/ppermute | solution.py:30
  101.8 5.3 %collective-permute-start.24 = (bf16[32,768]{1,0:T(8,128)(2,1)S(1)}, bf16[32,768]{1,0:T(8,128)(2,1)S(1)}, u32[]{:S(2)}, u32[]{:S(2)}) collective-permute-start(bf16[32,768]{1,0:T(8,128)(2,1)S(1)} %get-tuple-element.83), channel_id=1, source_target_pairs={{0,2},{2,4},{4,6},{6,8},{8,10},{10,12},{12,14},{14,16},{16,18},{18... | collective-permute-start | bytes 147464 | tf_op jit(solution)/shard_map/ppermute | solution.py:37
  105.3 6.5 %collective-permute-start.25 = (bf16[32,768]{1,0:T(8,128)(2,1)S(1)}, bf16[32,768]{1,0:T(8,128)(2,1)S(1)}, u32[]{:S(2)}, u32[]{:S(2)}) collective-permute-start(bf16[32,768]{1,0:T(8,128)(2,1)S(1)} %get-tuple-element.84), channel_id=1, source_target_pairs={{2,0},{4,2},{6,4},{8,6},{10,8},{12,10},{14,12},{16,14},{18,16},{20... | collective-permute-start | bytes 147464 | tf_op jit(solution)/shard_map/ppermute | solution.py:37
  111.9 10.1 %collective-permute-start.26 = (bf16[4,64,768]{2,1,0:T(8,128)(2,1)S(1)}, bf16[4,64,768]{2,1,0:T(8,128)(2,1)S(1)}, u32[]{:S(2)}, u32[]{:S(2)}) collective-permute-start(bf16[4,64,768]{2,1,0:T(8,128)(2,1)S(1)} %get-tuple-element.94.refs_0_), channel_id=1, source_target_pairs={{0,8},{2,10},{4,12},{6,14},{8,0},{10,2},{12,4},{14,6},{16,24},{18,... | collective-permute-start | bytes 1179656 | tf_op jit(solution)/shard_map/ppermute | solution.py:30
  113.1 8.9 %collective-permute-start.27 = (bf16[4,64,768]{2,1,0:T(8,128)(2,1)S(1)}, bf16[4,64,768]{2,1,0:T(8,128)(2,1)S(1)}, u32[]{:S(2)}, u32[]{:S(2)}) collective-permute-start(bf16[4,64,768]{2,1,0:T(8,128)(2,1)S(1)} %get-tuple-element.96.refs_2_), channel_id=1, source_target_pairs={{0,2},{2,0},{4,6},{6,4},{8,10},{10,8},{12,14},{14,12},{16,18},{18,... | collective-permute-start | bytes 1179656 | tf_op jit(solution)/shard_map/ppermute | solution.py:30
  114.8 9.7 %collective-permute-start.28 = (bf16[4,64,768]{2,1,0:T(8,128)(2,1)S(1)}, bf16[4,64,768]{2,1,0:T(8,128)(2,1)S(1)}, u32[]{:S(2)}, u32[]{:S(2)}) collective-permute-start(bf16[4,64,768]{2,1,0:T(8,128)(2,1)S(1)} %get-tuple-element.98.refs_4_), channel_id=1, source_target_pairs={{0,4},{2,6},{4,0},{6,2},{8,12},{10,14},{12,8},{14,10},{16,20},{18,... | collective-permute-start | bytes 1179656 | tf_op jit(solution)/shard_map/ppermute | solution.py:30
  132.0 7.2 %collective-permute-start.29 = (bf16[48,1536]{1,0:T(8,128)(2,1)S(1)}, bf16[48,1536]{1,0:T(8,128)(2,1)S(1)}, u32[]{:S(2)}, u32[]{:S(2)}) collective-permute-start(bf16[48,1536]{1,0:T(8,128)(2,1)S(1)} %get-tuple-element.101), channel_id=1, source_target_pairs={{0,16},{2,18},{4,20},{6,22},{8,24},{10,26},{12,28},{14,30},{16,0},... | collective-permute-start | bytes 442376 | tf_op jit(solution)/shard_map/ppermute | solution.py:30

commit v7 on v6

--- a/solution.py
+++ b/solution.py
@@ -46,13 +46,15 @@
     return blocks
 
 
-def call(kernel, out_shape, scratch, flops, *operands, scalars=1):
+def call(kernel, out_shape, scratch, flops, *operands, scalars=1, apart=0):
     smem = pl.BlockSpec(memory_space=pltpu.SMEM)
     vmem = pl.BlockSpec(memory_space=pltpu.VMEM)
     return pl.pallas_call(
         kernel,
         out_shape=out_shape,
-        in_specs=[smem] * scalars + [vmem] * (len(operands) - scalars),
+        in_specs=[smem] * scalars
+        + [vmem] * (len(operands) - scalars - apart)
+        + [pl.BlockSpec(memory_space=pl.ANY)] * apart,
         out_specs=[vmem] * len(out_shape),
         scratch_shapes=scratch,
         compiler_params=pltpu.CompilerParams(vmem_limit_bytes=40 * 2**20),
@@ -131,6 +133,19 @@
         def _():
             start = pl.multiple_of(lax.rem(last, tokens), RIM * COLS)
             tail[...] = share[pl.ds(start, tail.shape[0]), :]
+
+
+def edges_kernel(ids, lengths, strip, head, tail, first_sem, last_sem):
+    rows = head.shape[0]
+    last = pl.multiple_of((live_rows(ids, lengths) - RIM) * COLS, RIM * COLS)
+    copies = [
+        pltpu.make_async_copy(strip.at[pl.ds(0, rows)], head, first_sem),
+        pltpu.make_async_copy(strip.at[pl.ds(last, rows)], tail, last_sem),
+    ]
+    for copy in copies:
+        copy.start()
+    for copy in copies:
+        copy.wait()
 
 
 def forward_kernel(
@@ -167,40 +182,32 @@
     sent[1] = (keep * layer_scale[...] * grad_out).astype(BF16)
 
 
-def middle_kernel(
-    ids,
-    lengths,
-    tissue,
-    strip,
-    total,
-    one,
-    two,
-    three,
-    centred,
-    inverse,
-    gain,
-    layer_scale,
-    grad_mixed,
-    block_out,
-):
+def summed(blocks):
+    value = blocks[0][...].astype(F32)
+    for ref in blocks[1:]:
+        value = value + ref[...].astype(F32)
+    return value
+
+
+def norm_back_kernel(ids, lengths, tissue, centred, inverse, gain, *refs):
+    *blocks, grad_mixed = refs
     tokens, channels = grad_mixed.shape
-    start = pl.multiple_of(ids[1] * COLS, 16)
-    live, keep = kept_rows(ids, lengths, tissue, tokens)
-
-    def summed(which):
-        value = total[which].astype(F32)
-        for ref in (one, two, three):
-            value = value + ref[which].astype(F32)
-        return value
-
-    inputs = strip[pl.ds(start, tokens), :].astype(F32)
-    block = inputs + keep * layer_scale[...] * summed(1)
-    block_out[...] = jnp.where(live, block, 0.0).astype(BF16)
-    scaled_grad = summed(0) * gain[...]
+    live, _ = kept_rows(ids, lengths, tissue, tokens)
+    scaled_grad = summed(blocks) * gain[...]
     first_mean = jnp.sum(scaled_grad, 1, keepdims=True) / channels
     second_mean = jnp.sum(scaled_grad * centred[...], 1, keepdims=True) / channels
     value = inverse[:, :1] * (scaled_grad - first_mean - centred[...] * second_mean)
     grad_mixed[...] = jnp.where(live, value, 0.0).astype(BF16)
+
+
+def output_kernel(ids, lengths, tissue, strip, layer_scale, *refs):
+    *blocks, block_out = refs
+    tokens = block_out.shape[0]
+    start = pl.multiple_of(ids[1] * COLS, 16)
+    live, keep = kept_rows(ids, lengths, tissue, tokens)
+    inputs = strip[pl.ds(start, tokens), :].astype(F32)
+    block = inputs + keep * layer_scale[...] * summed(blocks)
+    block_out[...] = jnp.where(live, block, 0.0).astype(BF16)
 
 
 def join_kernel(*refs):
@@ -245,9 +252,13 @@
     plain, over_tokens = ((1,), (0,)), ((0,), (0,))
     count = tokens_of[0].shape[1]
     step = min(256, count)
+    units = act_out.shape[1]
+    bias_row = bias[...]
+    if bias.shape[1] != units:
+        bias_row = bias[:, pl.ds(pl.multiple_of(scalars[1] * units, LANES), units)]
     for index, ref in enumerate(tokens_of):
         for start in range(0, count, step):
-            hidden = dot(ref[0, start : start + step, :], up[...], plain) + bias[...]
+            hidden = dot(ref[0, start : start + step, :], up[...], plain) + bias_row
             cdf = 0.5 * (1.0 + lax.erf(hidden * INV_ROOT_TWO))
             slope = cdf + hidden * jnp.exp(-0.5 * hidden * hidden) * INV_ROOT_TAU
             grad_act = dot(ref[1, start : start + step, :], down_t[...], plain)
@@ -255,7 +266,6 @@
             act_out[rows_out, :] = (hidden * cdf).astype(BF16)
             grad_out[rows_out, :] = (grad_act * slope).astype(BF16)
 
-    units = act_out.shape[1]
     for half, (hidden_side, which) in enumerate(((grad_out, 0), (act_out, 1))):
         total = jnp.zeros((units, parts.shape[1]), F32)
         for index, ref in enumerate(tokens_of):
@@ -289,13 +299,14 @@
 
 
 def add_kernel(mine, *refs):
-    others, outs = refs[:-PLANE], refs[-PLANE:]
-    tokens = outs[0].shape[1]
-    for strip, out in enumerate(outs):
+    others, outs = refs[: -2 * PLANE], refs[-2 * PLANE :]
+    tokens = outs[0].shape[0]
+    for index, out in enumerate(outs):
+        which, strip = divmod(index, PLANE)
         rows_in = slice(strip * tokens, (strip + 1) * tokens)
-        total = mine[:, rows_in, :]
+        total = mine[which, rows_in, :]
         for other in others:
-            total = total + other[:, rows_in, :].astype(F32)
+            total = total + other[which, rows_in, :].astype(F32)
         out[...] = total.astype(BF16)
 
 
@@ -456,11 +467,19 @@
             place[None], *pieces,
         )
 
-    place_ids = jnp.stack([tile, 0 * tile, 0 * tile]).astype(jnp.int32)
-    head, tail = call(rims_kernel, rims, [], 10**6, place_ids, lengths, strip, scalars=2)
+    head, tail = call(
+        edges_kernel,
+        rims,
+        [pltpu.SemaphoreType.DMA] * 2,
+        10**6,
+        tile[None], lengths, strip,
+        scalars=2, apart=1,
+    )
     before, after = neighbours(head, tail)
-    piece, before, after = lax.optimization_barrier((piece, before, after))
-    bias = lax.dynamic_slice_in_dim(bias_up, place * units, units, 0)
+    _, before, after = lax.optimization_barrier((piece, before, after))
+    bias = bias_up[None]
+    if units % LANES:
+        bias = lax.dynamic_slice_in_dim(bias, place * units, units, 1)
 
     sent, centred, inverse = call(
         forward_kernel,
@@ -504,7 +523,7 @@
         [half_parts, half_parts, hidden_shape, hidden_shape],
         [pltpu.VMEM((2 * units, channels), F32)],
         5 * 10**9,
-        (line & 1)[None], up, down_t, bias[None], *shares,
+        jnp.stack([line & 1, place]), up, down_t, bias, *shares,
     )
 
     def split(blocks, bit):
@@ -527,16 +546,13 @@
         scalars=0,
     )
     others = [swap(value, "own", s + 1) for s, value in enumerate(others)]
-    total, *moved = call(
-        add_kernel,
-        [jax.ShapeDtypeStruct((2, tokens, channels), BF16)] * PLANE,
-        [],
-        10**6,
-        mine, *others,
-        scalars=0,
-    )
-    moved = [swap(value, "tile", s + 1) for s, value in enumerate(moved)]
-    arrived, moved[0] = lax.optimization_barrier((arrived, moved[0]))
+    flat = jax.ShapeDtypeStruct((tokens, channels), BF16)
+    blocks = call(add_kernel, [flat] * (2 * PLANE), [], 10**6, mine, *others, scalars=0)
+    blocks = [
+        swap(value, "tile", i % PLANE) if i % PLANE else value for i, value in enumerate(blocks)
+    ]
+    for_norm, for_output = blocks[:PLANE], blocks[PLANE:]
+    arrived, for_norm[1] = lax.optimization_barrier((arrived, for_norm[1]))
     reduced = reduced.astype(F32) + arrived.astype(F32)
     for bit in line_bits[1:-1]:
         reduced, other = split(reduced, bit)
@@ -544,19 +560,28 @@
     reduced, other = split(reduced, line_bits[-1])
     arrived = swap(other, "tile", PLANE * line_bits[-1])
 
-    grad_mixed, block_out = call(
-        middle_kernel,
-        [jax.ShapeDtypeStruct((tokens, channels), BF16)] * 2,
+    (grad_mixed,) = call(
+        norm_back_kernel,
+        [flat],
         [],
         10**6,
-        ids, lengths, flags, strip, total, *moved, centred, inverse, gain, scale,
+        ids, lengths, flags, centred, inverse, gain, *for_norm,
         scalars=3,
     )
-
+    (block_out,) = call(
+        output_kernel,
+        [flat],
+        [],
+        10**6,
+        ids, lengths, flags, strip, scale, *for_output,
+        scalars=3,
+    )
     halves = [grad_mixed] + [swap(grad_mixed, "own", s) for s in range(1, owners)]
-    arrived, halves = lax.optimization_barrier((arrived, halves))
     head, tail = call(rims_kernel, rims, [], 10**6, ids, lengths, *halves, scalars=2)
     before, after = neighbours(head, tail)
+    arrived, before, after, block_out = lax.optimization_barrier(
+        (arrived, before, after, block_out)
+    )
     grad_t = (reduced + arrived.astype(F32)).astype(BF16)[0]
     group = PLANE * half_lines
     bits = [1 << i for i in range(group.bit_length() - 1)]
@@ -565,8 +590,6 @@
     orders = [bits[turn:] + bits[:turn] for turn in range(3)]
     for stage in range(len(bits)):
         came = [swap(held, "tile", order[stage]) for held, order in zip(helds, orders)]
-        if stage + 2 == len(bits):
-            came, before, after = lax.optimization_barrier((came, before, after))
         if stage + 1 < len(bits):
             shape = jax.ShapeDtypeStruct((2 << stage, third, channels), BF16)
             helds = call(double_kernel, [shape] * 3, [], 10**6, *helds, *came, scalars=0)
@@ -574,7 +597,7 @@
 
     (grad_features,) = call(
         backward_kernel,
-        [jax.ShapeDtypeStruct((tokens, channels), BF16)],
+        [flat],
         [frame, wide],
         10**6,
         ids, lengths, cotangent.reshape(strip.shape), before, after, taps, *halves,

time: 140 us -> 144 us (1.029)
  starting transfers between devices: 45.1 us -> 47.9 us
    ppermute x4, waiting for transfers between devices: 9.64 us -> 4.53 us  [neighbours(): return (lax.ppermute(last, 'tile', up), lax.ppermute(first, 'tile', down))]
    ppermute x26 -> x29, starting transfers between devices: 35 us -> 39 us  [swap(): lax.ppermute(value, axis, [(i, i ^ bit) for i in range(lax.axis_size(axis...]
    ppermute x26 -> x29, waiting for transfers between devices: 48.8 us -> 52.7 us  [swap(): lax.ppermute(value, axis, [(i, i ^ bit) for i in range(lax.axis_size(axis...]
    unnamed x30 -> x48, local copies, waits for them, and re-layouts: 4.55 us -> 6.41 us
    pallas_call x15 -> x16, Pallas kernels: 26.8 us -> 27.8 us  [call(): pl.pallas_call(kernel, out_shape=out_shape, in_specs=[smem] * scalars + [...]
  transfers between devices with their start and end apart: 30 -> 33, of which waited for: 19 -> 21; matrix products, arithmetic and copies ran while one was open for 2% -> 1% of each run, Pallas kernels for 8% -> 8%
where the time goes in v7:
time: 144 us
  waiting for transfers between devices  57.3 us (40%)
  starting transfers between devices  47.9 us (33%)
  Pallas kernels  27.8 us (19%)
  local copies, waits for them, and re-layouts  6.51 us (5%)
  other arithmetic  3.45 us (2%)
    ppermute x29, waiting for transfers between devices, swap(): lax.ppermute(value, axis, [(i, i ^ bit) for i in range(lax.axis_size(axis...  52.7 us
    ppermute x29, starting transfers between devices, swap(): lax.ppermute(value, axis, [(i, i ^ bit) for i in range(lax.axis_size(axis...  39 us
    pallas_call x16, Pallas kernels, call(): pl.pallas_call(kernel, out_shape=out_shape, in_specs=[smem] * scalars + [...  27.8 us
    ppermute x4, starting transfers between devices, neighbours(): return (lax.ppermute(last, 'tile', up), lax.ppermute(first, 'tile', down))  8.86 us
    unnamed x48, local copies, waits for them, and re-layouts  6.41 us
    ppermute x4, waiting for transfers between devices, neighbours(): return (lax.ppermute(last, 'tile', up), lax.ppermute(first, 'tile', down))  4.53 us
  transfers between devices with their start and end apart: 33, of which 21 were waited for; matrix products, arithmetic and copies ran while one was open for 1% of the time, Pallas kernels for 8%

profile of v7, /device:TPU:0, one launch (start us, length us, event | category | flops | bytes accessed | tf_op | source)
XLA Modules:
  0.0 144.0 jit_solution(6114465494445783302)
XLA Ops:
  0.7 1.0 fusion.1
  1.8 3.0 %collective-permute-start = (bf16[2,48,384]{2,1,0:T(8,128)(2,1)S(1)}, bf16[2,48,384]{2,1,0:T(8,128)(2,1)S(1)}, u32[]{:S(2)}, u32[]{:S(2)}) collective-permute-start(bf16[2,48,384]{2,1,0:T(8,128)(2,1)S(1)} %get-tuple-element.103), channel_id=1, source_target_pairs={{0,2},{2,0},{4,6},{6,4},{8,10},{10,8},{12,14},{14,12},{16,18},{18,... | collective-permute-start | bytes 221192 | tf_op jit(solution)/shard_map/ppermute | solution.py:30
  4.8 1.5 %collective-permute-start.1 = (bf16[2,48,384]{2,1,0:T(8,128)(2,1)S(1)}, bf16[2,48,384]{2,1,0:T(8,128)(2,1)S(1)}, u32[]{:S(2)}, u32[]{:S(2)}) collective-permute-start(bf16[2,48,384]{2,1,0:T(8,128)(2,1)S(1)} %get-tuple-element.104), channel_id=1, source_target_pairs={{0,4},{2,6},{4,0},{6,2},{8,12},{10,14},{12,8},{14,10},{16,20},{18,... | collective-permute-start | bytes 221192 | tf_op jit(solution)/shard_map/ppermute | solution.py:30
  6.3 1.0 collective-permute-done.refs_1_
  7.3 1.8 %collective-permute-done.1.refs_2_ = bf16[2,48,384]{2,1,0:T(8,128)(2,1)S(1)} collective-permute-done((bf16[2,48,384]{2,1,0:T(8,128)(2,1)S(1)}, bf16[2,48,384]{2,1,0:T(8,128)(2,1)S(1)}, u32[]{:S(2)}, u32[]{:S(2)}) %collective-permute-start.1) | collective-permute-done | bytes 73760 | tf_op jit(solution)/shard_map/ppermute | solution.py:30
  9.1 2.4 %collective-permute-done.2.refs_3_ = bf16[2,48,384]{2,1,0:T(8,128)(2,1)S(1)} collective-permute-done((bf16[2,48,384]{2,1,0:T(8,128)(2,1)S(1)}, bf16[2,48,384]{2,1,0:T(8,128)(2,1)S(1)}, u32[]{:S(2)}, u32[]{:S(2)}) %collective-permute-start.2) | collective-permute-done | bytes 73760 | tf_op jit(solution)/shard_map/ppermute | solution.py:30
  11.6 2.7 %collective-permute-start.3 = (bf16[1,2,192,384]{3,2,1,0:T(8,128)(2,1)S(1)}, bf16[1,2,192,384]{3,2,1,0:T(8,128)(2,1)S(1)}, u32[]{:S(2)}, u32[]{:S(2)}) collective-permute-start(bf16[1,2,192,384]{3,2,1,0:T(8,128)(2,1)S(1)} %bitcast.26), channel_id=1, source_target_pairs={{0,16},{2,18},{4,20},{6,22},{8,24},{10,26},{12,28},{14,30},{16,0},... | collective-permute-start | bytes 884744 | tf_op jit(solution)/shard_map/ppermute | solution.py:30
  14.9 2.4 %collective-permute-start.5 = (bf16[32,768]{1,0:T(8,128)(2,1)S(1)}, bf16[32,768]{1,0:T(8,128)(2,1)S(1)}, u32[]{:S(2)}, u32[]{:S(2)}) collective-permute-start(bf16[32,768]{1,0:T(8,128)(2,1)S(1)} %get-tuple-element.52), channel_id=1, source_target_pairs={{0,2},{2,4},{4,6},{6,8},{8,10},{10,12},{12,14},{14,16},{16,18},{18... | collective-permute-start | bytes 147464 | tf_op jit(solution)/shard_map/ppermute | solution.py:37
  17.4 1.3 collective-permute-start.6
  19.1 4.3 %collective-permute-done.6.after = bf16[32,768]{1,0:T(8,128)(2,1)S(1)} collective-permute-done((bf16[32,768]{1,0:T(8,128)(2,1)S(1)}, bf16[32,768]{1,0:T(8,128)(2,1)S(1)}, u32[]{:S(2)}, u32[]{:S(2)}) %collective-permute-start.6) | collective-permute-done | bytes 49184 | tf_op jit(solution)/shard_map/ppermute | solution.py:37
  23.4 2.9 %shard_map.133 = (bf16[2,128,768]{2,1,0:T(8,128)(2,1)S(1)}, f32[128,768]{1,0:T(8,128)S(1)}, f32[128,128]{1,0:T(8,128)S(1)}) custom-call(s32[3]{0:T(128)S(1)} %pad_add_fusion.1.ids, s32[16]{0:T(128)S(1)} %copy-done.8, s32[4]{0:T(128)S(1)} %bitcast.28, bf16[256,768]{1,0:T(8,128)(2,1)S(1)} %bitcast.22, bf16[256,768]{1,0:T(8,128)(2,1)S(1)} %bitcast.24, ...), custom_call_target="tpu_custom_call" | custom-call | flops 1000000 | bytes 1048576 | tf_op jit(solution)/shard_map/pallas_call | solution.py:52
  26.9 2.3 %collective-permute-start.7 = (bf16[2,128,768]{2,1,0:T(8,128)(2,1)S(1)}, bf16[2,128,768]{2,1,0:T(8,128)(2,1)S(1)}, u32[]{:S(2)}, u32[]{:S(2)}) collective-permute-start(bf16[2,128,768]{2,1,0:T(8,128)(2,1)S(1)} %get-tuple-element.56.refs_0_), channel_id=1, source_target_pairs={{0,2},{2,0},{4,6},{6,4},{8,10},{10,8},{12,14},{14,12},{16,18},{18,... | collective-permute-start | bytes 1179656 | tf_op jit(solution)/shard_map/ppermute | solution.py:30
  29.3 4.2 %collective-permute-start.8 = (bf16[2,128,768]{2,1,0:T(8,128)(2,1)S(1)}, bf16[2,128,768]{2,1,0:T(8,128)(2,1)S(1)}, u32[]{:S(2)}, u32[]{:S(2)}) collective-permute-start(bf16[2,128,768]{2,1,0:T(8,128)(2,1)S(1)} %get-tuple-element.56.refs_0_), channel_id=1, source_target_pairs={{0,4},{2,6},{4,0},{6,2},{8,12},{10,14},{12,8},{14,10},{16,20},{18,... | collective-permute-start | bytes 1179656 | tf_op jit(solution)/shard_map/ppermute | solution.py:30
  34.3 2.9 %collective-permute-done.7.refs_1_ = bf16[2,128,768]{2,1,0:T(8,128)(2,1)S(1)} collective-permute-done((bf16[2,128,768]{2,1,0:T(8,128)(2,1)S(1)}, bf16[2,128,768]{2,1,0:T(8,128)(2,1)S(1)}, u32[]{:S(2)}, u32[]{:S(2)}) %collective-permute-start.7) | collective-permute-done | bytes 393248 | tf_op jit(solution)/shard_map/ppermute | solution.py:30
  37.1 12.4 %collective-permute-done.8.refs_2_ = bf16[2,128,768]{2,1,0:T(8,128)(2,1)S(1)} collective-permute-done((bf16[2,128,768]{2,1,0:T(8,128)(2,1)S(1)}, bf16[2,128,768]{2,1,0:T(8,128)(2,1)S(1)}, u32[]{:S(2)}, u32[]{:S(2)}) %collective-permute-start.8) | collective-permute-done | bytes 393248 | tf_op jit(solution)/shard_map/ppermute | solution.py:30
  49.8 1.2 shard_map.131
  51.0 2.2 %collective-permute-done.10.refs_1_ = bf16[2,512,768]{2,1,0:T(8,128)(2,1)} collective-permute-done((bf16[2,512,768]{2,1,0:T(8,128)(2,1)S(1)}, bf16[2,512,768]{2,1,0:T(8,128)(2,1)}, u32[]{:S(2)}, u32[]{:S(2)}) %collective-permute-start.10) | collective-permute-done | bytes 1572896 | tf_op jit(solution)/shard_map/ppermute | solution.py:30
  53.2 5.7 %shard_map.135 = (bf16[2,192,768]{2,1,0:T(8,128)(2,1)S(1)}, bf16[2,192,768]{2,1,0:T(8,128)(2,1)}, bf16[1024,384]{1,0:T(8,128)(2,1)S(1)}, bf16[1024,384]{1,0:T(8,128)(2,1)S(1)}) custom-call(s32[2]{0:T(128)S(1)} %pad_add_fusion.scalars, bf16[768,384]{1,0:T(8,128)(2,1)S(1)} %get-tuple-element.50.up, bf16[768,384]{1,0:T(8,128)(2,1)S(1)} %get-tuple-element.51.down_t, ...), custom_call_target="tpu_custom_call" | custom-call | flops 5000000000 | bytes 1048576 | tf_op jit(solution)/shard_map/pallas_call | solution.py:52
  59.0 1.9 %shard_map.136 = (f32[2,512,768]{2,1,0:T(8,128)S(1)}, bf16[2,512,768]{2,1,0:T(8,128)(2,1)S(1)}) custom-call(bf16[1024,384]{1,0:T(8,128)(2,1)S(1)} %get-tuple-element.59.act, bf16[1024,384]{1,0:T(8,128)(2,1)S(1)} %get-tuple-element.60.grad_hidden, bf16[768,384]{1,0:T(8,128)(2,1)S(1)} %get-tuple-element.50.up, bf16[768,384]{1,0:T(8,128)(2,1)S(1)} %get-tuple-element.51.down_t), custom_call_target="tpu_custom_call" | custom-call | flops 1000000000 | bytes 1048576 | tf_op jit(solution)/shard_map/pallas_call | solution.py:52
  61.8 2.5 %collective-permute-done.12.refs_0_ = bf16[2,512,768]{2,1,0:T(8,128)(2,1)S(1)} collective-permute-done((bf16[2,512,768]{2,1,0:T(8,128)(2,1)S(1)}, bf16[2,512,768]{2,1,0:T(8,128)(2,1)S(1)}, u32[]{:S(2)}, u32[]{:S(2)}) %collective-permute-start.12) | collective-permute-done | bytes 1572896 | tf_op jit(solution)/shard_map/ppermute | solution.py:30
  64.3 0.9 shard_map.137
  69.9 1.5 %collective-permute-start.13 = (bf16[128,768]{1,0:T(8,128)(2,1)}, bf16[128,768]{1,0:T(8,128)(2,1)S(1)}, u32[]{:S(2)}, u32[]{:S(2)}) collective-permute-start(bf16[128,768]{1,0:T(8,128)(2,1)} %get-tuple-element.63), channel_id=1, source_target_pairs={{0,2},{2,0},{4,6},{6,4},{8,10},{10,8},{12,14},{14,12},{16,18},{18,... | collective-permute-start | bytes 589832 | tf_op jit(solution)/shard_map/ppermute | solution.py:30
  72.0 1.5 %collective-permute-start.16 = (bf16[128,768]{1,0:T(8,128)(2,1)}, bf16[128,768]{1,0:T(8,128)(2,1)S(1)}, u32[]{:S(2)}, u32[]{:S(2)}) collective-permute-start(bf16[128,768]{1,0:T(8,128)(2,1)} %copy-done.18), channel_id=1, source_target_pairs={{0,6},{2,4},{4,2},{6,0},{8,14},{10,12},{12,10},{14,8},{16,22},{18,... | collective-permute-start | bytes 589832 | tf_op jit(solution)/shard_map/ppermute | solution.py:30
  73.4 3.5 %collective-permute-done.11 = bf16[2,192,768]{2,1,0:T(8,128)(2,1)} collective-permute-done((bf16[2,192,768]{2,1,0:T(8,128)(2,1)}, bf16[2,192,768]{2,1,0:T(8,128)(2,1)}, u32[]{:S(2)}, u32[]{:S(2)}) %collective-permute-start.11) | collective-permute-done | bytes 589856 | tf_op jit(solution)/shard_map/ppermute | solution.py:30
  76.9 0.9 collective-permute-done.13.refs_1_
  77.9 1.3 convert_add_fusion
  79.2 3.6 %collective-permute-start.14 = (bf16[1,192,768]{2,1,0:T(8,128)(2,1)S(1)}, bf16[1,192,768]{2,1,0:T(8,128)(2,1)S(1)}, u32[]{:S(2)}, u32[]{:S(2)}) collective-permute-start(bf16[1,192,768]{2,1,0:T(8,128)(2,1)S(1)} %dynamic-slice_convert_fusion), channel_id=1, source_target_pairs={{0,16},{2,18},{4,20},{6,22},{8,24},{10,26},{12,28},{14,30},{16,0},... | collective-permute-start | bytes 884744 | tf_op jit(solution)/shard_map/ppermute | solution.py:30
  83.8 1.8 %collective-permute-start.20 = (bf16[128,768]{1,0:T(8,128)(2,1)S(1)}, bf16[128,768]{1,0:T(8,128)(2,1)S(1)}, u32[]{:S(2)}, u32[]{:S(2)}) collective-permute-start(bf16[128,768]{1,0:T(8,128)(2,1)S(1)} %copy-done.17), channel_id=1, source_target_pairs={{0,2},{2,0},{4,6},{6,4},{8,10},{10,8},{12,14},{14,12},{16,18},{18,... | collective-permute-start | bytes 589832 | tf_op jit(solution)/shard_map/ppermute | solution.py:30
  86.0 1.5 %collective-permute-start.22 = (bf16[128,768]{1,0:T(8,128)(2,1)S(1)}, bf16[128,768]{1,0:T(8,128)(2,1)S(1)}, u32[]{:S(2)}, u32[]{:S(2)}) collective-permute-start(bf16[128,768]{1,0:T(8,128)(2,1)S(1)} %copy-done.13), channel_id=1, source_target_pairs={{0,6},{2,4},{4,2},{6,0},{8,14},{10,12},{12,10},{14,8},{16,22},{18,... | collective-permute-start | bytes 589832 | tf_op jit(solution)/shard_map/ppermute | solution.py:30
  88.0 3.7 %collective-permute-start.18 = (bf16[32,768]{1,0:T(8,128)(2,1)S(1)}, bf16[32,768]{1,0:T(8,128)(2,1)S(1)}, u32[]{:S(2)}, u32[]{:S(2)}) collective-permute-start(bf16[32,768]{1,0:T(8,128)(2,1)S(1)} %get-tuple-element.71), channel_id=1, source_target_pairs={{0,2},{2,4},{4,6},{6,8},{8,10},{10,12},{12,14},{14,16},{16,18},{18... | collective-permute-start | bytes 147464 | tf_op jit(solution)/shard_map/ppermute | solution.py:37
  91.7 1.5 %collective-permute-start.19 = (bf16[32,768]{1,0:T(8,128)(2,1)S(1)}, bf16[32,768]{1,0:T(8,128)(2,1)S(1)}, u32[]{:S(2)}, u32[]{:S(2)}) collective-permute-start(bf16[32,768]{1,0:T(8,128)(2,1)S(1)} %get-tuple-element.72), channel_id=1, source_target_pairs={{2,0},{4,2},{6,4},{8,6},{10,8},{12,10},{14,12},{16,14},{18,16},{20... | collective-permute-start | bytes 147464 | tf_op jit(solution)/shard_map/ppermute | solution.py:37
  93.2 3.7 %collective-permute-done.21.refs_2_ = bf16[128,768]{1,0:T(8,128)(2,1)S(1)} collective-permute-done((bf16[128,768]{1,0:T(8,128)(2,1)S(1)}, bf16[128,768]{1,0:T(8,128)(2,1)S(1)}, u32[]{:S(2)}, u32[]{:S(2)}) %collective-permute-start.21) | collective-permute-done | bytes 196640 | tf_op jit(solution)/shard_map/ppermute | solution.py:30
  96.9 1.5 %shard_map.140 = bf16[128,768]{1,0:T(8,128)(2,1)} custom-call(s32[3]{0:T(128)S(1)} %pad_add_fusion.1.ids, s32[16]{0:T(128)S(1)} %copy-done.8, s32[4]{0:T(128)S(1)} %bitcast.30, bf16[256,768]{1,0:T(8,128)(2,1)S(1)} %bitcast.23, f32[1,768]{1,0:T(1,128)S(1)} %broadcast_in_dim.24.layer_scale, bf16[128,768]{1,0:T(8,128)(2,1)S(1)} %copy-done.3, ...), custom_call_target="tpu_custom_call" | custom-call | flops 1000000 | bytes 1048576 | tf_op jit(solution)/shard_map/pallas_call | solution.py:52
  98.4 2.0 %collective-permute-start.23 = (bf16[1,64,768]{2,1,0:T(8,128)(2,1)S(1)}, bf16[1,64,768]{2,1,0:T(8,128)(2,1)S(1)}, u32[]{:S(2)}, u32[]{:S(2)}) collective-permute-start(bf16[1,64,768]{2,1,0:T(8,128)(2,1)S(1)} %get-tuple-element.100.refs_0_), channel_id=1, source_target_pairs={{0,2},{2,0},{4,6},{6,4},{8,10},{10,8},{12,14},{14,12},{16,18},{18,... | collective-permute-start | bytes 294920 | tf_op jit(solution)/shard_map/ppermute | solution.py:30
  100.4 1.2 collective-permute-start.24
  101.6 3.3 %collective-permute-start.25 = (bf16[1,64,768]{2,1,0:T(8,128)(2,1)S(1)}, bf16[1,64,768]{2,1,0:T(8,128)(2,1)S(1)}, u32[]{:S(2)}, u32[]{:S(2)}) collective-permute-start(bf16[1,64,768]{2,1,0:T(8,128)(2,1)S(1)} %get-tuple-element.98.refs_2_), channel_id=1, source_target_pairs={{0,8},{2,10},{4,12},{6,14},{8,0},{10,2},{12,4},{14,6},{16,24},{18,... | collective-permute-start | bytes 294920 | tf_op jit(solution)/shard_map/ppermute | solution.py:30
  105.0 2.8 %collective-permute-done.25.refs_5_ = bf16[1,64,768]{2,1,0:T(8,128)(2,1)S(1)} collective-permute-done((bf16[1,64,768]{2,1,0:T(8,128)(2,1)S(1)}, bf16[1,64,768]{2,1,0:T(8,128)(2,1)S(1)}, u32[]{:S(2)}, u32[]{:S(2)}) %collective-permute-start.25) | collective-permute-done | bytes 98336 | tf_op jit(solution)/shard_map/ppermute | solution.py:30
  107.9 2.5 %collective-permute-start.27 = (bf16[2,64,768]{2,1,0:T(8,128)(2,1)S(1)}, bf16[2,64,768]{2,1,0:T(8,128)(2,1)S(1)}, u32[]{:S(2)}, u32[]{:S(2)}) collective-permute-start(bf16[2,64,768]{2,1,0:T(8,128)(2,1)S(1)} %get-tuple-element.80.refs_1_), channel_id=1, source_target_pairs={{0,8},{2,10},{4,12},{6,14},{8,0},{10,2},{12,4},{14,6},{16,24},{18,... | collective-permute-start | bytes 589832 | tf_op jit(solution)/shard_map/ppermute | solution.py:30
  110.5 3.1 %collective-permute-done.26.refs_3_ = bf16[2,64,768]{2,1,0:T(8,128)(2,1)S(1)} collective-permute-done((bf16[2,64,768]{2,1,0:T(8,128)(2,1)S(1)}, bf16[2,64,768]{2,1,0:T(8,128)(2,1)S(1)}, u32[]{:S(2)}, u32[]{:S(2)}) %collective-permute-start.26) | collective-permute-done | bytes 196640 | tf_op jit(solution)/shard_map/ppermute | solution.py:30
  113.6 2.1 %collective-permute-done.27.refs_4_ = bf16[2,64,768]{2,1,0:T(8,128)(2,1)S(1)} collective-permute-done((bf16[2,64,768]{2,1,0:T(8,128)(2,1)S(1)}, bf16[2,64,768]{2,1,0:T(8,128)(2,1)S(1)}, u32[]{:S(2)}, u32[]{:S(2)}) %collective-permute-start.27) | collective-permute-done | bytes 196640 | tf_op jit(solution)/shard_map/ppermute | solution.py:30
  115.6 2.6 %collective-permute-done.28.refs_5_ = bf16[2,64,768]{2,1,0:T(8,128)(2,1)S(1)} collective-permute-done((bf16[2,64,768]{2,1,0:T(8,128)(2,1)S(1)}, bf16[2,64,768]{2,1,0:T(8,128)(2,1)S(1)}, u32[]{:S(2)}, u32[]{:S(2)}) %collective-permute-start.28) | collective-permute-done | bytes 196640 | tf_op jit(solution)/shard_map/ppermute | solution.py:30
  118.5 2.0 %collective-permute-start.31 = (bf16[4,64,768]{2,1,0:T(8,128)(2,1)S(1)}, bf16[4,64,768]{2,1,0:T(8,128)(2,1)}, u32[]{:S(2)}, u32[]{:S(2)}) collective-permute-start(bf16[4,64,768]{2,1,0:T(8,128)(2,1)S(1)} %get-tuple-element.92.refs_4_), channel_id=1, source_target_pairs={{0,4},{2,6},{4,0},{6,2},{8,12},{10,14},{12,8},{14,10},{16,20},{18,... | collective-permute-start | bytes 1179656 | tf_op jit(solution)/shard_map/ppermute | solution.py:30
  120.6 3.3 %shard_map.143 = bf16[128,768]{1,0:T(8,128)(2,1)} custom-call(s32[3]{0:T(128)S(1)} %pad_add_fusion.1.ids, s32[16]{0:T(128)S(1)} %copy-done.8, bf16[256,768]{1,0:T(8,128)(2,1)S(1)} %bitcast.25, bf16[32,768]{1,0:T(8,128)(2,1)S(1)} %collective-permute-done.18.before, bf16[32,768]{1,0:T(8,128)(2,1)S(1)} %collective-permute-done.19.after, ...), custom_call_target="tpu_custom_call" | custom-call | flops 1000000 | bytes 1048576 | tf_op jit(solution)/shard_map/pallas_call | solution.py:52
  123.9 2.3 %collective-permute-done.29.refs_1_ = bf16[4,64,768]{2,1,0:T(8,128)(2,1)S(1)} collective-permute-done((bf16[4,64,768]{2,1,0:T(8,128)(2,1)S(1)}, bf16[4,64,768]{2,1,0:T(8,128)(2,1)S(1)}, u32[]{:S(2)}, u32[]{:S(2)}) %collective-permute-start.29) | collective-permute-done | bytes 393248 | tf_op jit(solution)/shard_map/ppermute | solution.py:30
  126.4 1.0 copy-done.11
  127.4 8.0 %shard_map.144 = (f32[48,1536]{1,0:T(8,128)S(1)}, bf16[48,1536]{1,0:T(8,128)(2,1)S(1)}) custom-call(s32[3]{0:T(128)S(1)} %pad_add_fusion.2.scalars, bf16[4,64,768]{2,1,0:T(8,128)(2,1)S(1)} %get-tuple-element.88.refs_0_, bf16[4,64,768]{2,1,0:T(8,128)(2,1)S(1)} %collective-permute-done.29.refs_1_, bf16[4,64,768]{2,1,0:T(8,128)(2,1)S(1)} %get-tuple-element.90.refs_2_, ...), custom_call_target="tpu_custom_call" | custom-call | flops 10000000000 | bytes 1048576 | tf_op jit(solution)/shard_map/pallas_call | solution.py:52
  135.5 1.6 %collective-permute-start.32 = (bf16[48,1536]{1,0:T(8,128)(2,1)S(1)}, bf16[48,1536]{1,0:T(8,128)(2,1)S(1)}, u32[]{:S(2)}, u32[]{:S(2)}) collective-permute-start(bf16[48,1536]{1,0:T(8,128)(2,1)S(1)} %get-tuple-element.95), channel_id=1, source_target_pairs={{0,16},{2,18},{4,20},{6,22},{8,24},{10,26},{12,28},{14,30},{16,0},... | collective-permute-start | bytes 442376 | tf_op jit(solution)/shard_map/ppermute | solution.py:30
  137.1 6.1 %collective-permute-done.32 = bf16[48,1536]{1,0:T(8,128)(2,1)S(1)} collective-permute-done((bf16[48,1536]{1,0:T(8,128)(2,1)S(1)}, bf16[48,1536]{1,0:T(8,128)(2,1)S(1)}, u32[]{:S(2)}, u32[]{:S(2)}) %collective-permute-start.32) | collective-permute-done | bytes 147488 | tf_op jit(solution)/shard_map/ppermute | solution.py:30
  (95 shorter events, 12.7 us)
Async XLA Ops:
  0.6 13.6 %copy-start = (bf16[32,8,768]{2,1,0:T(8,128)(2,1)S(1)}, bf16[32,8,768]{2,1,0:T(8,128)(2,1)}, u32[]{:S(2)}) copy-start(bf16[32,8,768]{2,1,0:T(8,128)(2,1)} %param.10) | copy-start | bytes 1179652
  0.6 13.6 %copy-start.8 = (s32[16]{0:T(128)S(1)}, s32[16]{0:T(128)}, u32[]{:S(2)}) copy-start(s32[16]{0:T(128)} %lengths.11) | copy-start | bytes 196
  0.7 18.1 %copy-start.20 = (f32[7,7,768]{2,1,0:T(8,128)S(1)}, f32[7,7,768]{2,1,0:T(8,128)}, u32[]{:S(2)}) copy-start(f32[7,7,768]{2,1,0:T(8,128)} %param.12) | copy-start | bytes 451588
  0.7 18.1 %copy-start.22 = (f32[768]{0:T(1024)S(1)}, f32[768]{0:T(1024)}, u32[]{:S(2)}) copy-start(f32[768]{0:T(1024)} %param.13) | copy-start | bytes 9220
  0.7 18.2 %copy-start.23 = (f32[768]{0:T(1024)S(1)}, f32[768]{0:T(1024)}, u32[]{:S(2)}) copy-start(f32[768]{0:T(1024)} %param.17) | copy-start | bytes 9220
  0.7 22.7 %copy-start.9 = (s32[4,1]{0,1:T(1,128)S(1)}, s32[4,1]{0,1:T(1,128)}, u32[]{:S(2)}) copy-start(s32[4,1]{0,1:T(1,128)} %param.18) | copy-start | bytes 52
  0.7 22.7 %copy-start.1 = (bf16[32,8,768]{2,1,0:T(8,128)(2,1)S(1)}, bf16[32,8,768]{2,1,0:T(8,128)(2,1)}, u32[]{:S(2)}) copy-start(bf16[32,8,768]{2,1,0:T(8,128)(2,1)} %param.11) | copy-start | bytes 1179652
  1.8 5.5 %collective-permute-start = (bf16[2,48,384]{2,1,0:T(8,128)(2,1)S(1)}, bf16[2,48,384]{2,1,0:T(8,128)(2,1)S(1)}, u32[]{:S(2)}, u32[]{:S(2)}) collective-permute-start(bf16[2,48,384]{2,1,0:T(8,128)(2,1)S(1)} %get-tuple-element.103), channel_id=1, source_target_pairs={{0,2},{2,0},{4,6},{6,4},{8,10},{10,8},{12,14},{14,12},{16,18},{18,... | collective-permute-start | bytes 221192 | tf_op jit(solution)/shard_map/ppermute | solution.py:30
  4.8 4.4 %collective-permute-start.1 = (bf16[2,48,384]{2,1,0:T(8,128)(2,1)S(1)}, bf16[2,48,384]{2,1,0:T(8,128)(2,1)S(1)}, u32[]{:S(2)}, u32[]{:S(2)}) collective-permute-start(bf16[2,48,384]{2,1,0:T(8,128)(2,1)S(1)} %get-tuple-element.104), channel_id=1, source_target_pairs={{0,4},{2,6},{4,0},{6,2},{8,12},{10,14},{12,8},{14,10},{16,20},{18,... | collective-permute-start | bytes 221192 | tf_op jit(solution)/shard_map/ppermute | solution.py:30
  6.3 5.3 %collective-permute-start.2 = (bf16[2,48,384]{2,1,0:T(8,128)(2,1)S(1)}, bf16[2,48,384]{2,1,0:T(8,128)(2,1)S(1)}, u32[]{:S(2)}, u32[]{:S(2)}) collective-permute-start(bf16[2,48,384]{2,1,0:T(8,128)(2,1)S(1)} %get-tuple-element.101), channel_id=1, source_target_pairs={{0,6},{2,4},{4,2},{6,0},{8,14},{10,12},{12,10},{14,8},{16,22},{18,... | collective-permute-start | bytes 221192 | tf_op jit(solution)/shard_map/ppermute | solution.py:30
  11.6 21.9 %collective-permute-start.3 = (bf16[1,2,192,384]{3,2,1,0:T(8,128)(2,1)S(1)}, bf16[1,2,192,384]{3,2,1,0:T(8,128)(2,1)S(1)}, u32[]{:S(2)}, u32[]{:S(2)}) collective-permute-start(bf16[1,2,192,384]{3,2,1,0:T(8,128)(2,1)S(1)} %bitcast.26), channel_id=1, source_target_pairs={{0,16},{2,18},{4,20},{6,22},{8,24},{10,26},{12,28},{14,30},{16,0},... | collective-permute-start | bytes 884744 | tf_op jit(solution)/shard_map/ppermute | solution.py:30
  14.9 4.2 %collective-permute-start.5 = (bf16[32,768]{1,0:T(8,128)(2,1)S(1)}, bf16[32,768]{1,0:T(8,128)(2,1)S(1)}, u32[]{:S(2)}, u32[]{:S(2)}) collective-permute-start(bf16[32,768]{1,0:T(8,128)(2,1)S(1)} %get-tuple-element.52), channel_id=1, source_target_pairs={{0,2},{2,4},{4,6},{6,8},{8,10},{10,12},{12,14},{14,16},{16,18},{18... | collective-permute-start | bytes 147464 | tf_op jit(solution)/shard_map/ppermute | solution.py:37
  17.4 6.0 %collective-permute-start.6 = (bf16[32,768]{1,0:T(8,128)(2,1)S(1)}, bf16[32,768]{1,0:T(8,128)(2,1)S(1)}, u32[]{:S(2)}, u32[]{:S(2)}) collective-permute-start(bf16[32,768]{1,0:T(8,128)(2,1)S(1)} %get-tuple-element.53), channel_id=1, source_target_pairs={{2,0},{4,2},{6,4},{8,6},{10,8},{12,10},{14,12},{16,14},{18,16},{20... | collective-permute-start | bytes 147464 | tf_op jit(solution)/shard_map/ppermute | solution.py:37
  26.9 10.2 %collective-permute-start.7 = (bf16[2,128,768]{2,1,0:T(8,128)(2,1)S(1)}, bf16[2,128,768]{2,1,0:T(8,128)(2,1)S(1)}, u32[]{:S(2)}, u32[]{:S(2)}) collective-permute-start(bf16[2,128,768]{2,1,0:T(8,128)(2,1)S(1)} %get-tuple-element.56.refs_0_), channel_id=1, source_target_pairs={{0,2},{2,0},{4,6},{6,4},{8,10},{10,8},{12,14},{14,12},{16,18},{18,... | collective-permute-start | bytes 1179656 | tf_op jit(solution)/shard_map/ppermute | solution.py:30
  29.3 20.3 %collective-permute-start.8 = (bf16[2,128,768]{2,1,0:T(8,128)(2,1)S(1)}, bf16[2,128,768]{2,1,0:T(8,128)(2,1)S(1)}, u32[]{:S(2)}, u32[]{:S(2)}) collective-permute-start(bf16[2,128,768]{2,1,0:T(8,128)(2,1)S(1)} %get-tuple-element.56.refs_0_), channel_id=1, source_target_pairs={{0,4},{2,6},{4,0},{6,2},{8,12},{10,14},{12,8},{14,10},{16,20},{18,... | collective-permute-start | bytes 1179656 | tf_op jit(solution)/shard_map/ppermute | solution.py:30
  33.5 16.0 %collective-permute-start.9 = (bf16[2,128,768]{2,1,0:T(8,128)(2,1)S(1)}, bf16[2,128,768]{2,1,0:T(8,128)(2,1)S(1)}, u32[]{:S(2)}, u32[]{:S(2)}) collective-permute-start(bf16[2,128,768]{2,1,0:T(8,128)(2,1)S(1)} %get-tuple-element.56.refs_0_), channel_id=1, source_target_pairs={{0,6},{2,4},{4,2},{6,0},{8,14},{10,12},{12,10},{14,8},{16,22},{18,... | collective-permute-start | bytes 1179656 | tf_op jit(solution)/shard_map/ppermute | solution.py:30
  33.6 16.2 %copy-start.21 = (f32[1536]{0:T(1024)S(1)}, f32[1536]{0:T(1024)}, u32[]{:S(2)}) copy-start(f32[1536]{0:T(1024)} %param.15) | copy-start | bytes 18436
  33.6 16.2 %collective-permute-start.4 = (bf16[2,2,192,384]{3,2,1,0:T(8,128)(2,1)S(1)}, bf16[2,2,192,384]{3,2,1,0:T(8,128)(2,1)}, u32[]{:S(2)}, u32[]{:S(2)}) collective-permute-start(bf16[2,2,192,384]{3,2,1,0:T(8,128)(2,1)S(1)} %shard_map.130.early), channel_id=1, source_target_pairs={{0,8},{2,10},{4,12},{6,14},{8,0},{10,2},{12,4},{14,6},{16,24},{18,... | collective-permute-start | bytes 1769480 | tf_op jit(solution)/shard_map/ppermute | solution.py:30
  49.6 3.6 %collective-permute-start.10 = (bf16[2,512,768]{2,1,0:T(8,128)(2,1)S(1)}, bf16[2,512,768]{2,1,0:T(8,128)(2,1)}, u32[]{:S(2)}, u32[]{:S(2)}) collective-permute-start(bf16[2,512,768]{2,1,0:T(8,128)(2,1)S(1)} %shard_map.134.refs_0_), channel_id=1, source_target_pairs={{0,1},{1,0},{2,3},{3,2},{4,5},{5,4},{6,7},{7,6},{8,9},{9,8},{10,11... | collective-permute-start | bytes 4718600 | tf_op jit(solution)/shard_map/ppermute | solution.py:30
  60.8 3.5 %collective-permute-start.12 = (bf16[2,512,768]{2,1,0:T(8,128)(2,1)S(1)}, bf16[2,512,768]{2,1,0:T(8,128)(2,1)S(1)}, u32[]{:S(2)}, u32[]{:S(2)}) collective-permute-start(bf16[2,512,768]{2,1,0:T(8,128)(2,1)S(1)} %get-tuple-element.62), channel_id=1, source_target_pairs={{0,1},{1,0},{2,3},{3,2},{4,5},{5,4},{6,7},{7,6},{8,9},{9,8},{10,11... | collective-permute-start | bytes 4718600 | tf_op jit(solution)/shard_map/ppermute | solution.py:30
  61.0 15.9 %collective-permute-start.11 = (bf16[2,192,768]{2,1,0:T(8,128)(2,1)}, bf16[2,192,768]{2,1,0:T(8,128)(2,1)}, u32[]{:S(2)}, u32[]{:S(2)}) collective-permute-start(bf16[2,192,768]{2,1,0:T(8,128)(2,1)} %get-tuple-element.58), channel_id=1, source_target_pairs={{0,8},{2,10},{4,12},{6,14},{8,0},{10,2},{12,4},{14,6},{16,24},{18,... | collective-permute-start | bytes 1769480 | tf_op jit(solution)/shard_map/ppermute | solution.py:30
  69.9 8.0 %collective-permute-start.13 = (bf16[128,768]{1,0:T(8,128)(2,1)}, bf16[128,768]{1,0:T(8,128)(2,1)S(1)}, u32[]{:S(2)}, u32[]{:S(2)}) collective-permute-start(bf16[128,768]{1,0:T(8,128)(2,1)} %get-tuple-element.63), channel_id=1, source_target_pairs={{0,2},{2,0},{4,6},{6,4},{8,10},{10,8},{12,14},{14,12},{16,18},{18,... | collective-permute-start | bytes 589832 | tf_op jit(solution)/shard_map/ppermute | solution.py:30
  71.4 11.5 %collective-permute-start.15 = (bf16[128,768]{1,0:T(8,128)(2,1)}, bf16[128,768]{1,0:T(8,128)(2,1)S(1)}, u32[]{:S(2)}, u32[]{:S(2)}) collective-permute-start(bf16[128,768]{1,0:T(8,128)(2,1)} %copy-done.19), channel_id=1, source_target_pairs={{0,4},{2,6},{4,0},{6,2},{8,12},{10,14},{12,8},{14,10},{16,20},{18,... | collective-permute-start | bytes 589832 | tf_op jit(solution)/shard_map/ppermute | solution.py:30
  72.0 10.9 %collective-permute-start.16 = (bf16[128,768]{1,0:T(8,128)(2,1)}, bf16[128,768]{1,0:T(8,128)(2,1)S(1)}, u32[]{:S(2)}, u32[]{:S(2)}) collective-permute-start(bf16[128,768]{1,0:T(8,128)(2,1)} %copy-done.18), channel_id=1, source_target_pairs={{0,6},{2,4},{4,2},{6,0},{8,14},{10,12},{12,10},{14,8},{16,22},{18,... | collective-permute-start | bytes 589832 | tf_op jit(solution)/shard_map/ppermute | solution.py:30
  77.9 5.0 %copy-start.5 = (bf16[128,768]{1,0:T(8,128)(2,1)S(1)}, bf16[128,768]{1,0:T(8,128)(2,1)}, u32[]{:S(2)}) copy-start(bf16[128,768]{1,0:T(8,128)(2,1)} %copy-done.4) | copy-start | bytes 589828
  77.9 5.0 %copy-start.7 = (f32[128,128]{1,0:T(8,128)S(1)}, f32[128,128]{1,0:T(8,128)}, u32[]{:S(2)}) copy-start(f32[128,128]{1,0:T(8,128)} %copy-done.6) | copy-start | bytes 196612
  79.1 4.7 %copy-start.17 = (bf16[128,768]{1,0:T(8,128)(2,1)S(1)}, bf16[128,768]{1,0:T(8,128)(2,1)}, u32[]{:S(2)}) copy-start(bf16[128,768]{1,0:T(8,128)(2,1)} %copy-done.16) | copy-start | bytes 589828
  79.2 6.5 %copy-start.15 = (bf16[128,768]{1,0:T(8,128)(2,1)S(1)}, bf16[128,768]{1,0:T(8,128)(2,1)}, u32[]{:S(2)}) copy-start(bf16[128,768]{1,0:T(8,128)(2,1)} %copy-done.14) | copy-start | bytes 589828
  79.2 6.8 %copy-start.13 = (bf16[128,768]{1,0:T(8,128)(2,1)S(1)}, bf16[128,768]{1,0:T(8,128)(2,1)}, u32[]{:S(2)}) copy-start(bf16[128,768]{1,0:T(8,128)(2,1)} %copy-done.12) | copy-start | bytes 589828
  79.2 17.7 %copy-start.3 = (bf16[128,768]{1,0:T(8,128)(2,1)S(1)}, bf16[128,768]{1,0:T(8,128)(2,1)}, u32[]{:S(2)}) copy-start(bf16[128,768]{1,0:T(8,128)(2,1)} %copy-done.2) | copy-start | bytes 589828
  79.2 19.1 %collective-permute-start.14 = (bf16[1,192,768]{2,1,0:T(8,128)(2,1)S(1)}, bf16[1,192,768]{2,1,0:T(8,128)(2,1)S(1)}, u32[]{:S(2)}, u32[]{:S(2)}) collective-permute-start(bf16[1,192,768]{2,1,0:T(8,128)(2,1)S(1)} %dynamic-slice_convert_fusion), channel_id=1, source_target_pairs={{0,16},{2,18},{4,20},{6,22},{8,24},{10,26},{12,28},{14,30},{16,0},... | collective-permute-start | bytes 884744 | tf_op jit(solution)/shard_map/ppermute | solution.py:30
  83.8 3.7 %collective-permute-start.17 = (bf16[128,768]{1,0:T(8,128)(2,1)S(1)}, bf16[128,768]{1,0:T(8,128)(2,1)S(1)}, u32[]{:S(2)}, u32[]{:S(2)}) collective-permute-start(bf16[128,768]{1,0:T(8,128)(2,1)S(1)} %shard_map.138.refs_0_.rest_0_), channel_id=1, source_target_pairs={{0,1},{1,0},{2,3},{3,2},{4,5},{5,4},{6,7},{7,6},{8,9},{9,8},{10,11... | collective-permute-start | bytes 589832 | tf_op jit(solution)/shard_map/ppermute | solution.py:30
  83.8 7.8 %collective-permute-start.20 = (bf16[128,768]{1,0:T(8,128)(2,1)S(1)}, bf16[128,768]{1,0:T(8,128)(2,1)S(1)}, u32[]{:S(2)}, u32[]{:S(2)}) collective-permute-start(bf16[128,768]{1,0:T(8,128)(2,1)S(1)} %copy-done.17), channel_id=1, source_target_pairs={{0,2},{2,0},{4,6},{6,4},{8,10},{10,8},{12,14},{14,12},{16,18},{18,... | collective-permute-start | bytes 589832 | tf_op jit(solution)/shard_map/ppermute | solution.py:30
  85.7 11.2 %collective-permute-start.21 = (bf16[128,768]{1,0:T(8,128)(2,1)S(1)}, bf16[128,768]{1,0:T(8,128)(2,1)S(1)}, u32[]{:S(2)}, u32[]{:S(2)}) collective-permute-start(bf16[128,768]{1,0:T(8,128)(2,1)S(1)} %copy-done.15), channel_id=1, source_target_pairs={{0,4},{2,6},{4,0},{6,2},{8,12},{10,14},{12,8},{14,10},{16,20},{18,... | collective-permute-start | bytes 589832 | tf_op jit(solution)/shard_map/ppermute | solution.py:30
  86.0 10.9 %collective-permute-start.22 = (bf16[128,768]{1,0:T(8,128)(2,1)S(1)}, bf16[128,768]{1,0:T(8,128)(2,1)S(1)}, u32[]{:S(2)}, u32[]{:S(2)}) collective-permute-start(bf16[128,768]{1,0:T(8,128)(2,1)S(1)} %copy-done.13), channel_id=1, source_target_pairs={{0,6},{2,4},{4,2},{6,0},{8,14},{10,12},{12,10},{14,8},{16,22},{18,... | collective-permute-start | bytes 589832 | tf_op jit(solution)/shard_map/ppermute | solution.py:30
  88.0 10.3 %collective-permute-start.18 = (bf16[32,768]{1,0:T(8,128)(2,1)S(1)}, bf16[32,768]{1,0:T(8,128)(2,1)S(1)}, u32[]{:S(2)}, u32[]{:S(2)}) collective-permute-start(bf16[32,768]{1,0:T(8,128)(2,1)S(1)} %get-tuple-element.71), channel_id=1, source_target_pairs={{0,2},{2,4},{4,6},{6,8},{8,10},{10,12},{12,14},{14,16},{16,18},{18... | collective-permute-start | bytes 147464 | tf_op jit(solution)/shard_map/ppermute | solution.py:37
  91.7 6.6 %collective-permute-start.19 = (bf16[32,768]{1,0:T(8,128)(2,1)S(1)}, bf16[32,768]{1,0:T(8,128)(2,1)S(1)}, u32[]{:S(2)}, u32[]{:S(2)}) collective-permute-start(bf16[32,768]{1,0:T(8,128)(2,1)S(1)} %get-tuple-element.72), channel_id=1, source_target_pairs={{2,0},{4,2},{6,4},{8,6},{10,8},{12,10},{14,12},{16,14},{18,16},{20... | collective-permute-start | bytes 147464 | tf_op jit(solution)/shard_map/ppermute | solution.py:37
  98.4 6.4 %collective-permute-start.23 = (bf16[1,64,768]{2,1,0:T(8,128)(2,1)S(1)}, bf16[1,64,768]{2,1,0:T(8,128)(2,1)S(1)}, u32[]{:S(2)}, u32[]{:S(2)}) collective-permute-start(bf16[1,64,768]{2,1,0:T(8,128)(2,1)S(1)} %get-tuple-element.100.refs_0_), channel_id=1, source_target_pairs={{0,2},{2,0},{4,6},{6,4},{8,10},{10,8},{12,14},{14,12},{16,18},{18,... | collective-permute-start | bytes 294920 | tf_op jit(solution)/shard_map/ppermute | solution.py:30
  100.4 4.6 %collective-permute-start.24 = (bf16[1,64,768]{2,1,0:T(8,128)(2,1)S(1)}, bf16[1,64,768]{2,1,0:T(8,128)(2,1)S(1)}, u32[]{:S(2)}, u32[]{:S(2)}) collective-permute-start(bf16[1,64,768]{2,1,0:T(8,128)(2,1)S(1)} %get-tuple-element.99.refs_1_), channel_id=1, source_target_pairs={{0,4},{2,6},{4,0},{6,2},{8,12},{10,14},{12,8},{14,10},{16,20},{18,... | collective-permute-start | bytes 294920 | tf_op jit(solution)/shard_map/ppermute | solution.py:30
  101.6 6.2 %collective-permute-start.25 = (bf16[1,64,768]{2,1,0:T(8,128)(2,1)S(1)}, bf16[1,64,768]{2,1,0:T(8,128)(2,1)S(1)}, u32[]{:S(2)}, u32[]{:S(2)}) collective-permute-start(bf16[1,64,768]{2,1,0:T(8,128)(2,1)S(1)} %get-tuple-element.98.refs_2_), channel_id=1, source_target_pairs={{0,8},{2,10},{4,12},{6,14},{8,0},{10,2},{12,4},{14,6},{16,24},{18,... | collective-permute-start | bytes 294920 | tf_op jit(solution)/shard_map/ppermute | solution.py:30
  107.8 5.7 %collective-permute-start.26 = (bf16[2,64,768]{2,1,0:T(8,128)(2,1)S(1)}, bf16[2,64,768]{2,1,0:T(8,128)(2,1)S(1)}, u32[]{:S(2)}, u32[]{:S(2)}) collective-permute-start(bf16[2,64,768]{2,1,0:T(8,128)(2,1)S(1)} %get-tuple-element.79.refs_0_), channel_id=1, source_target_pairs={{0,4},{2,6},{4,0},{6,2},{8,12},{10,14},{12,8},{14,10},{16,20},{18,... | collective-permute-start | bytes 589832 | tf_op jit(solution)/shard_map/ppermute | solution.py:30
  107.9 7.7 %collective-permute-start.27 = (bf16[2,64,768]{2,1,0:T(8,128)(2,1)S(1)}, bf16[2,64,768]{2,1,0:T(8,128)(2,1)S(1)}, u32[]{:S(2)}, u32[]{:S(2)}) collective-permute-start(bf16[2,64,768]{2,1,0:T(8,128)(2,1)S(1)} %get-tuple-element.80.refs_1_), channel_id=1, source_target_pairs={{0,8},{2,10},{4,12},{6,14},{8,0},{10,2},{12,4},{14,6},{16,24},{18,... | collective-permute-start | bytes 589832 | tf_op jit(solution)/shard_map/ppermute | solution.py:30
  110.5 7.8 %collective-permute-start.28 = (bf16[2,64,768]{2,1,0:T(8,128)(2,1)S(1)}, bf16[2,64,768]{2,1,0:T(8,128)(2,1)S(1)}, u32[]{:S(2)}, u32[]{:S(2)}) collective-permute-start(bf16[2,64,768]{2,1,0:T(8,128)(2,1)S(1)} %get-tuple-element.81.refs_2_), channel_id=1, source_target_pairs={{0,2},{2,0},{4,6},{6,4},{8,10},{10,8},{12,14},{14,12},{16,18},{18,... | collective-permute-start | bytes 589832 | tf_op jit(solution)/shard_map/ppermute | solution.py:30
  118.3 7.9 %copy-start.10 = (bf16[4,64,768]{2,1,0:T(8,128)(2,1)}, bf16[4,64,768]{2,1,0:T(8,128)(2,1)S(1)}, u32[]{:S(2)}) copy-start(bf16[4,64,768]{2,1,0:T(8,128)(2,1)S(1)} %get-tuple-element.92.refs_4_) | copy-start | bytes 1179652
  118.3 7.8 %collective-permute-start.29 = (bf16[4,64,768]{2,1,0:T(8,128)(2,1)S(1)}, bf16[4,64,768]{2,1,0:T(8,128)(2,1)S(1)}, u32[]{:S(2)}, u32[]{:S(2)}) collective-permute-start(bf16[4,64,768]{2,1,0:T(8,128)(2,1)S(1)} %get-tuple-element.88.refs_0_), channel_id=1, source_target_pairs={{0,8},{2,10},{4,12},{6,14},{8,0},{10,2},{12,4},{14,6},{16,24},{18,... | collective-permute-start | bytes 1179656 | tf_op jit(solution)/shard_map/ppermute | solution.py:30
  118.4 7.8 %collective-permute-start.30 = (bf16[4,64,768]{2,1,0:T(8,128)(2,1)S(1)}, bf16[4,64,768]{2,1,0:T(8,128)(2,1)S(1)}, u32[]{:S(2)}, u32[]{:S(2)}) collective-permute-start(bf16[4,64,768]{2,1,0:T(8,128)(2,1)S(1)} %get-tuple-element.90.refs_2_), channel_id=1, source_target_pairs={{0,2},{2,0},{4,6},{6,4},{8,10},{10,8},{12,14},{14,12},{16,18},{18,... | collective-permute-start | bytes 1179656 | tf_op jit(solution)/shard_map/ppermute | solution.py:30
  118.5 7.9 %collective-permute-start.31 = (bf16[4,64,768]{2,1,0:T(8,128)(2,1)S(1)}, bf16[4,64,768]{2,1,0:T(8,128)(2,1)}, u32[]{:S(2)}, u32[]{:S(2)}) collective-permute-start(bf16[4,64,768]{2,1,0:T(8,128)(2,1)S(1)} %get-tuple-element.92.refs_4_), channel_id=1, source_target_pairs={{0,4},{2,6},{4,0},{6,2},{8,12},{10,14},{12,8},{14,10},{16,20},{18,... | collective-permute-start | bytes 1179656 | tf_op jit(solution)/shard_map/ppermute | solution.py:30
  135.5 7.7 %collective-permute-start.32 = (bf16[48,1536]{1,0:T(8,128)(2,1)S(1)}, bf16[48,1536]{1,0:T(8,128)(2,1)S(1)}, u32[]{:S(2)}, u32[]{:S(2)}) collective-permute-start(bf16[48,1536]{1,0:T(8,128)(2,1)S(1)} %get-tuple-element.95), channel_id=1, source_target_pairs={{0,16},{2,18},{4,20},{6,22},{8,24},{10,26},{12,28},{14,30},{16,0},... | collective-permute-start | bytes 442376 | tf_op jit(solution)/shard_map/ppermute | solution.py:30
  (9 other events, 6.4 us)

commit v8 on v7

--- a/solution.py
+++ b/solution.py
@@ -46,7 +46,9 @@
     return blocks
 
 
-def call(kernel, out_shape, scratch, flops, *operands, scalars=1, apart=0):
+def call(
+    kernel, out_shape, scratch, flops, *operands, scalars=1, apart=0, out_space=pltpu.VMEM
+):
     smem = pl.BlockSpec(memory_space=pltpu.SMEM)
     vmem = pl.BlockSpec(memory_space=pltpu.VMEM)
     return pl.pallas_call(
@@ -55,7 +57,7 @@
         in_specs=[smem] * scalars
         + [vmem] * (len(operands) - scalars - apart)
         + [pl.BlockSpec(memory_space=pl.ANY)] * apart,
-        out_specs=[vmem] * len(out_shape),
+        out_specs=[pl.BlockSpec(memory_space=out_space)] * len(out_shape),
         scratch_shapes=scratch,
         compiler_params=pltpu.CompilerParams(vmem_limit_bytes=40 * 2**20),
         cost_estimate=pl.CostEstimate(flops=flops, bytes_accessed=2**20, transcendentals=0),
@@ -299,15 +301,21 @@
 
 
 def add_kernel(mine, *refs):
+    *refs, staged, sems = refs
     others, outs = refs[: -2 * PLANE], refs[-2 * PLANE :]
     tokens = outs[0].shape[0]
+    copies = []
     for index, out in enumerate(outs):
         which, strip = divmod(index, PLANE)
         rows_in = slice(strip * tokens, (strip + 1) * tokens)
         total = mine[which, rows_in, :]
         for other in others:
             total = total + other[which, rows_in, :].astype(F32)
-        out[...] = total.astype(BF16)
+        staged[index] = total.astype(BF16)
+        copies.append(pltpu.make_async_copy(staged.at[index], out, sems.at[index]))
+        copies[-1].start()
+    for copy in copies:
+        copy.wait()
 
 
 def backward_kernel(ids, lengths, cotangent, before, after, taps, *rest):
@@ -329,11 +337,6 @@
     )
 
 
-def member_bits(entry, turn, group):
-    bits = group.bit_length() - 1
-    return sum(1 << ((i + turn) % bits) for i in range(bits) if entry >> i & 1)
-
-
 def hidden_block(member, group):
     return (member & (PLANE - 1)) * (group // PLANE) + (member >> (PLANE.bit_length() - 1))
 
@@ -344,14 +347,10 @@
     if len(gathered) == 1:
         whole[...] = gathered[0][...]
     else:
-        group, third, _ = gathered[0].shape
-        group *= 2
-        for turn in range(3):
-            for e in range(group):
-                block = hidden_block(scalars[2] ^ member_bits(e, turn, group), group)
-                start = pl.multiple_of((block * 3 + turn) * third, third)
-                later, entry = divmod(e, group // 2)
-                whole[pl.ds(start, third), :] = gathered[2 * turn + later][entry]
+        rows = gathered[0].shape[0]
+        for e, ref in enumerate(gathered):
+            block = hidden_block(scalars[2] ^ e, len(gathered))
+            whole[pl.ds(pl.multiple_of(block * rows, rows), rows), :] = ref[...]
 
     plain = ((1,), (0,))
     steps = [pl.ds(i, 256) for i in range(0, channels, 256)]
@@ -476,7 +475,7 @@
         scalars=2, apart=1,
     )
     before, after = neighbours(head, tail)
-    _, before, after = lax.optimization_barrier((piece, before, after))
+    piece, before, after = lax.optimization_barrier((piece, before, after))
     bias = bias_up[None]
     if units % LANES:
         bias = lax.dynamic_slice_in_dim(bias, place * units, units, 1)
@@ -547,7 +546,17 @@
     )
     others = [swap(value, "own", s + 1) for s, value in enumerate(others)]
     flat = jax.ShapeDtypeStruct((tokens, channels), BF16)
-    blocks = call(add_kernel, [flat] * (2 * PLANE), [], 10**6, mine, *others, scalars=0)
+    blocks = call(
+        add_kernel,
+        [flat] * (2 * PLANE),
+        [
+            pltpu.VMEM((2 * PLANE, tokens, channels), BF16),
+            pltpu.SemaphoreType.DMA((2 * PLANE,)),
+        ],
+        10**6,
+        mine, *others,
+        scalars=0, out_space=pltpu.HBM,
+    )
     blocks = [
         swap(value, "tile", i % PLANE) if i % PLANE else value for i, value in enumerate(blocks)
     ]
@@ -584,16 +593,13 @@
     )
     grad_t = (reduced + arrived.astype(F32)).astype(BF16)[0]
     group = PLANE * half_lines
-    bits = [1 << i for i in range(group.bit_length() - 1)]
-    third = kept // 3
-    helds = [grad_t[turn * third : (turn + 1) * third][None] for turn in range(3)]
-    orders = [bits[turn:] + bits[:turn] for turn in range(3)]
-    for stage in range(len(bits)):
-        came = [swap(held, "tile", order[stage]) for held, order in zip(helds, orders)]
-        if stage + 1 < len(bits):
-            shape = jax.ShapeDtypeStruct((2 << stage, third, channels), BF16)
-            helds = call(double_kernel, [shape] * 3, [], 10**6, *helds, *came, scalars=0)
-    thirds = [half for pair in zip(helds, came) for half in pair]
+    if group == 8:
+        near = [swap(grad_t, "tile", bit) for bit in (1, 2, 4)]
+        corner = swap(grad_t, "tile", 7)
+        far = [swap(near[1], "tile", 1), swap(near[0], "tile", 4), swap(near[2], "tile", 2)]
+        gathered = [grad_t, near[0], near[1], far[0], near[2], far[1], far[2], corner]
+    else:
+        gathered = [swap(grad_t, "tile", e) if e else grad_t for e in range(group)]
 
     (grad_features,) = call(
         backward_kernel,
@@ -606,16 +612,12 @@
 
     other = tile ^ (PLANE * half_lines)
     square = pltpu.VMEM((channels, channels), F32)
-    thirds, grad_features = lax.optimization_barrier((thirds, grad_features))
-    if third % 16:
-        entries = [(e, turn) for turn in range(3) for e in range(group)]
-        slots = [
-            hidden_block((tile & (group - 1)) ^ member_bits(e, turn, group), group) * 3 + turn
-            for e, turn in entries
-        ]
-        ordered = jnp.zeros((3 * group, third, channels), BF16)
-        ordered = ordered.at[jnp.stack(slots)].set(jnp.concatenate(thirds, 0))
-        thirds = [ordered.reshape(-1, channels)]
+    gathered, grad_features = lax.optimization_barrier((gathered, grad_features))
+    if kept % 16:
+        slots = [hidden_block((tile & (group - 1)) ^ e, group) for e in range(group)]
+        ordered = jnp.zeros((group, kept, channels), BF16)
+        ordered = ordered.at[jnp.stack(slots)].set(jnp.stack(gathered))
+        gathered = [ordered.reshape(-1, channels)]
     mine, theirs = call(
         ortho_kernel,
         [
@@ -624,7 +626,7 @@
         ],
         [pltpu.VMEM((weight_up.shape[1], channels), BF16), square, square, square],
         10 * 10**9,
-        jnp.stack([tile * height, other * height, tile & (group - 1)]), *thirds,
+        jnp.stack([tile * height, other * height, tile & (group - 1)]), *gathered,
     )
     theirs = swap(theirs, "tile", PLANE * half_lines)
     theirs = theirs.astype(F32)

time: 144 us -> 137 us (0.951)
  waiting for transfers between devices: 57.3 us -> 43.7 us
  starting transfers between devices: 47.9 us -> 50.6 us
  local copies, waits for them, and re-layouts: 6.51 us -> 8.86 us
    ppermute x29 -> x27, waiting for transfers between devices: 52.7 us -> 39.1 us  [swap(): lax.ppermute(value, axis, [(i, i ^ bit) for i in range(lax.axis_size(axis...]
    unnamed x48 -> x52, local copies, waits for them, and re-layouts: 6.41 us -> 8.78 us
    ppermute x29 -> x27, starting transfers between devices: 39 us -> 40.6 us  [swap(): lax.ppermute(value, axis, [(i, i ^ bit) for i in range(lax.axis_size(axis...]
    pallas_call x16 -> x14, Pallas kernels: 27.8 us -> 29 us  [call(): pl.pallas_call(kernel, out_shape=out_shape, in_specs=[smem] * scalars + [...]
  transfers between devices with their start and end apart: 33 -> 31, of which waited for: 21 -> 18; matrix products, arithmetic and copies ran while one was open for 1% -> 1% of each run, Pallas kernels for 8% -> 10%
where the time goes in v8:
time: 137 us
  starting transfers between devices  50.6 us (37%)
  waiting for transfers between devices  43.7 us (32%)
  Pallas kernels  29 us (21%)
  local copies, waits for them, and re-layouts  8.86 us (6%)
  other arithmetic  3.46 us (3%)
    ppermute x27, starting transfers between devices, swap(): lax.ppermute(value, axis, [(i, i ^ bit) for i in range(lax.axis_size(axis...  40.6 us
    ppermute x27, waiting for transfers between devices, swap(): lax.ppermute(value, axis, [(i, i ^ bit) for i in range(lax.axis_size(axis...  39.1 us
    pallas_call x14, Pallas kernels, call(): pl.pallas_call(kernel, out_shape=out_shape, in_specs=[smem] * scalars + [...  29 us
    ppermute x4, starting transfers between devices, neighbours(): return (lax.ppermute(last, 'tile', up), lax.ppermute(first, 'tile', down))  10.1 us
    unnamed x52, local copies, waits for them, and re-layouts  8.78 us
    ppermute x4, waiting for transfers between devices, neighbours(): return (lax.ppermute(last, 'tile', up), lax.ppermute(first, 'tile', down))  4.62 us
  transfers between devices with their start and end apart: 31, of which 18 were waited for; matrix products, arithmetic and copies ran while one was open for 1% of the time, Pallas kernels for 10%

profile of v8, /device:TPU:0, one launch (start us, length us, event | category | flops | bytes accessed | tf_op | source)
XLA Modules:
  0.0 136.7 jit_solution(3319648979934897120)
XLA Ops:
  0.7 1.0 fusion.2
  1.8 3.0 %collective-permute-start = (bf16[2,48,384]{2,1,0:T(8,128)(2,1)S(1)}, bf16[2,48,384]{2,1,0:T(8,128)(2,1)S(1)}, u32[]{:S(2)}, u32[]{:S(2)}) collective-permute-start(bf16[2,48,384]{2,1,0:T(8,128)(2,1)S(1)} %get-tuple-element.94), channel_id=1, source_target_pairs={{0,2},{2,0},{4,6},{6,4},{8,10},{10,8},{12,14},{14,12},{16,18},{18,... | collective-permute-start | bytes 221192 | tf_op jit(solution)/shard_map/ppermute | solution.py:30
  4.8 1.5 %collective-permute-start.1 = (bf16[2,48,384]{2,1,0:T(8,128)(2,1)S(1)}, bf16[2,48,384]{2,1,0:T(8,128)(2,1)S(1)}, u32[]{:S(2)}, u32[]{:S(2)}) collective-permute-start(bf16[2,48,384]{2,1,0:T(8,128)(2,1)S(1)} %get-tuple-element.95), channel_id=1, source_target_pairs={{0,4},{2,6},{4,0},{6,2},{8,12},{10,14},{12,8},{14,10},{16,20},{18,... | collective-permute-start | bytes 221192 | tf_op jit(solution)/shard_map/ppermute | solution.py:30
  6.3 1.0 copy-done
  8.7 3.9 %collective-permute-start.3 = (bf16[32,768]{1,0:T(8,128)(2,1)S(1)}, bf16[32,768]{1,0:T(8,128)(2,1)S(1)}, u32[]{:S(2)}, u32[]{:S(2)}) collective-permute-start(bf16[32,768]{1,0:T(8,128)(2,1)S(1)} %get-tuple-element.47), channel_id=1, source_target_pairs={{0,2},{2,4},{4,6},{6,8},{8,10},{10,12},{12,14},{14,16},{16,18},{18... | collective-permute-start | bytes 147464 | tf_op jit(solution)/shard_map/ppermute | solution.py:37
  12.5 1.3 collective-permute-start.4
  14.3 4.3 %collective-permute-done.4.after = bf16[32,768]{1,0:T(8,128)(2,1)S(1)} collective-permute-done((bf16[32,768]{1,0:T(8,128)(2,1)S(1)}, bf16[32,768]{1,0:T(8,128)(2,1)S(1)}, u32[]{:S(2)}, u32[]{:S(2)}) %collective-permute-start.4) | collective-permute-done | bytes 49184 | tf_op jit(solution)/shard_map/ppermute | solution.py:37
  18.5 3.8 %collective-permute-start.5 = (bf16[1,2,192,384]{3,2,1,0:T(8,128)(2,1)S(1)}, bf16[1,2,192,384]{3,2,1,0:T(8,128)(2,1)S(1)}, u32[]{:S(2)}, u32[]{:S(2)}) collective-permute-start(bf16[1,2,192,384]{3,2,1,0:T(8,128)(2,1)S(1)} %bitcast.28), channel_id=1, source_target_pairs={{0,16},{2,18},{4,20},{6,22},{8,24},{10,26},{12,28},{14,30},{16,0},... | collective-permute-start | bytes 884744 | tf_op jit(solution)/shard_map/ppermute | solution.py:30
  22.4 2.9 %shard_map.133 = (bf16[2,128,768]{2,1,0:T(8,128)(2,1)S(1)}, f32[128,768]{1,0:T(8,128)S(1)}, f32[128,128]{1,0:T(8,128)S(1)}) custom-call(s32[3]{0:T(128)S(1)} %pad_add_fusion.1.ids, s32[16]{0:T(128)S(1)} %copy-done.10, s32[4]{0:T(128)S(1)} %bitcast.30, bf16[256,768]{1,0:T(8,128)(2,1)S(1)} %bitcast.24, bf16[256,768]{1,0:T(8,128)(2,1)S(1)} %bitcast.26, ...), custom_call_target="tpu_custom_call" | custom-call | flops 1000000 | bytes 1048576 | tf_op jit(solution)/shard_map/pallas_call | solution.py:54
  26.0 1.2 collective-permute-start.7
  27.2 2.9 %collective-permute-start.8 = (bf16[2,128,768]{2,1,0:T(8,128)(2,1)S(1)}, bf16[2,128,768]{2,1,0:T(8,128)(2,1)S(1)}, u32[]{:S(2)}, u32[]{:S(2)}) collective-permute-start(bf16[2,128,768]{2,1,0:T(8,128)(2,1)S(1)} %get-tuple-element.54.refs_0_), channel_id=1, source_target_pairs={{0,4},{2,6},{4,0},{6,2},{8,12},{10,14},{12,8},{14,10},{16,20},{18,... | collective-permute-start | bytes 1179656 | tf_op jit(solution)/shard_map/ppermute | solution.py:30
  30.1 3.2 %collective-permute-done.5.refs_1_ = bf16[1,2,192,384]{3,2,1,0:T(8,128)(2,1)S(1)} collective-permute-done((bf16[1,2,192,384]{3,2,1,0:T(8,128)(2,1)S(1)}, bf16[1,2,192,384]{3,2,1,0:T(8,128)(2,1)S(1)}, u32[]{:S(2)}, u32[]{:S(2)}) %collective-permute-start.5) | collective-permute-done | bytes 294944 | tf_op jit(solution)/shard_map/ppermute | solution.py:30
  33.4 2.2 %collective-permute-start.6 = (bf16[2,2,192,384]{3,2,1,0:T(8,128)(2,1)S(1)}, bf16[2,2,192,384]{3,2,1,0:T(8,128)(2,1)}, u32[]{:S(2)}, u32[]{:S(2)}) collective-permute-start(bf16[2,2,192,384]{3,2,1,0:T(8,128)(2,1)S(1)} %shard_map.131.early), channel_id=1, source_target_pairs={{0,8},{2,10},{4,12},{6,14},{8,0},{10,2},{12,4},{14,6},{16,24},{18,... | collective-permute-start | bytes 1769480 | tf_op jit(solution)/shard_map/ppermute | solution.py:30
  35.6 2.4 %collective-permute-done.7.refs_1_ = bf16[2,128,768]{2,1,0:T(8,128)(2,1)S(1)} collective-permute-done((bf16[2,128,768]{2,1,0:T(8,128)(2,1)S(1)}, bf16[2,128,768]{2,1,0:T(8,128)(2,1)S(1)}, u32[]{:S(2)}, u32[]{:S(2)}) %collective-permute-start.7) | collective-permute-done | bytes 393248 | tf_op jit(solution)/shard_map/ppermute | solution.py:30
  38.0 6.4 %collective-permute-done.8.refs_2_ = bf16[2,128,768]{2,1,0:T(8,128)(2,1)S(1)} collective-permute-done((bf16[2,128,768]{2,1,0:T(8,128)(2,1)S(1)}, bf16[2,128,768]{2,1,0:T(8,128)(2,1)S(1)}, u32[]{:S(2)}, u32[]{:S(2)}) %collective-permute-start.8) | collective-permute-done | bytes 393248 | tf_op jit(solution)/shard_map/ppermute | solution.py:30
  44.7 3.0 %collective-permute-done.6.late = bf16[2,2,192,384]{3,2,1,0:T(8,128)(2,1)} collective-permute-done((bf16[2,2,192,384]{3,2,1,0:T(8,128)(2,1)S(1)}, bf16[2,2,192,384]{3,2,1,0:T(8,128)(2,1)}, u32[]{:S(2)}, u32[]{:S(2)}) %collective-permute-start.6) | collective-permute-done | bytes 589856 | tf_op jit(solution)/shard_map/ppermute | solution.py:30
  47.7 1.2 shard_map.132
  48.9 5.7 %shard_map.135 = (bf16[2,192,768]{2,1,0:T(8,128)(2,1)S(1)}, bf16[2,192,768]{2,1,0:T(8,128)(2,1)}, bf16[1024,384]{1,0:T(8,128)(2,1)S(1)}, bf16[1024,384]{1,0:T(8,128)(2,1)S(1)}) custom-call(s32[2]{0:T(128)S(1)} %pad_add_fusion.scalars, bf16[768,384]{1,0:T(8,128)(2,1)S(1)} %get-tuple-element.50.up, bf16[768,384]{1,0:T(8,128)(2,1)S(1)} %get-tuple-element.51.down_t, ...), custom_call_target="tpu_custom_call" | custom-call | flops 5000000000 | bytes 1048576 | tf_op jit(solution)/shard_map/pallas_call | solution.py:54
  54.6 1.9 %shard_map.136 = (f32[2,512,768]{2,1,0:T(8,128)S(1)}, bf16[2,512,768]{2,1,0:T(8,128)(2,1)S(1)}) custom-call(bf16[1024,384]{1,0:T(8,128)(2,1)S(1)} %get-tuple-element.57.act, bf16[1024,384]{1,0:T(8,128)(2,1)S(1)} %get-tuple-element.58.grad_hidden, bf16[768,384]{1,0:T(8,128)(2,1)S(1)} %get-tuple-element.50.up, bf16[768,384]{1,0:T(8,128)(2,1)S(1)} %get-tuple-element.51.down_t), custom_call_target="tpu_custom_call" | custom-call | flops 1000000000 | bytes 1048576 | tf_op jit(solution)/shard_map/pallas_call | solution.py:54
  56.5 1.4 %collective-permute-start.11 = (bf16[2,192,768]{2,1,0:T(8,128)(2,1)}, bf16[2,192,768]{2,1,0:T(8,128)(2,1)}, u32[]{:S(2)}, u32[]{:S(2)}) collective-permute-start(bf16[2,192,768]{2,1,0:T(8,128)(2,1)} %get-tuple-element.56), channel_id=1, source_target_pairs={{0,8},{2,10},{4,12},{6,14},{8,0},{10,2},{12,4},{14,6},{16,24},{18,... | collective-permute-start | bytes 1769480 | tf_op jit(solution)/shard_map/ppermute | solution.py:30
  57.9 2.0 %collective-permute-done.12.refs_0_ = bf16[2,512,768]{2,1,0:T(8,128)(2,1)S(1)} collective-permute-done((bf16[2,512,768]{2,1,0:T(8,128)(2,1)S(1)}, bf16[2,512,768]{2,1,0:T(8,128)(2,1)S(1)}, u32[]{:S(2)}, u32[]{:S(2)}) %collective-permute-start.12) | collective-permute-done | bytes 1572896 | tf_op jit(solution)/shard_map/ppermute | solution.py:30
  59.9 2.1 %shard_map.137 = (bf16[128,768]{1,0:T(8,128)(2,1)S(1)}, bf16[128,768]{1,0:T(8,128)(2,1)}, bf16[128,768]{1,0:T(8,128)(2,1)S(1)}, bf16[128,768]{1,0:T(8,128)(2,1)S...) custom-call(f32[2,512,768]{2,1,0:T(8,128)S(1)} %get-tuple-element.59, ...), custom_call_target="tpu_custom_call" | custom-call | flops 1000000 | bytes 1048576 | tf_op jit(solution)/shard_map/pallas_call | solution.py:54
  66.8 1.3 collective-permute-start.13
  68.2 1.3 collective-permute-start.15
  70.3 2.3 %collective-permute-done.11 = bf16[2,192,768]{2,1,0:T(8,128)(2,1)} collective-permute-done((bf16[2,192,768]{2,1,0:T(8,128)(2,1)}, bf16[2,192,768]{2,1,0:T(8,128)(2,1)}, u32[]{:S(2)}, u32[]{:S(2)}) %collective-permute-start.11) | collective-permute-done | bytes 589856 | tf_op jit(solution)/shard_map/ppermute | solution.py:30
  72.6 2.2 %collective-permute-done.13.refs_1_ = bf16[128,768]{1,0:T(8,128)(2,1)S(1)} collective-permute-done((bf16[128,768]{1,0:T(8,128)(2,1)}, bf16[128,768]{1,0:T(8,128)(2,1)S(1)}, u32[]{:S(2)}, u32[]{:S(2)}) %collective-permute-start.13) | collective-permute-done | bytes 196640 | tf_op jit(solution)/shard_map/ppermute | solution.py:30
  74.8 1.3 convert_add_fusion
  76.1 3.0 %collective-permute-start.14 = (bf16[1,192,768]{2,1,0:T(8,128)(2,1)S(1)}, bf16[1,192,768]{2,1,0:T(8,128)(2,1)S(1)}, u32[]{:S(2)}, u32[]{:S(2)}) collective-permute-start(bf16[1,192,768]{2,1,0:T(8,128)(2,1)S(1)} %dynamic-slice_convert_fusion), channel_id=1, source_target_pairs={{0,16},{2,18},{4,20},{6,22},{8,24},{10,26},{12,28},{14,30},{16,0},... | collective-permute-start | bytes 884744 | tf_op jit(solution)/shard_map/ppermute | solution.py:30
  80.2 1.6 %collective-permute-start.20 = (bf16[128,768]{1,0:T(8,128)(2,1)S(1)}, bf16[128,768]{1,0:T(8,128)(2,1)S(1)}, u32[]{:S(2)}, u32[]{:S(2)}) collective-permute-start(bf16[128,768]{1,0:T(8,128)(2,1)S(1)} %copy-done.19), channel_id=1, source_target_pairs={{0,2},{2,0},{4,6},{6,4},{8,10},{10,8},{12,14},{14,12},{16,18},{18,... | collective-permute-start | bytes 589832 | tf_op jit(solution)/shard_map/ppermute | solution.py:30
  82.0 1.8 %collective-permute-start.22 = (bf16[128,768]{1,0:T(8,128)(2,1)S(1)}, bf16[128,768]{1,0:T(8,128)(2,1)S(1)}, u32[]{:S(2)}, u32[]{:S(2)}) collective-permute-start(bf16[128,768]{1,0:T(8,128)(2,1)S(1)} %copy-done.15), channel_id=1, source_target_pairs={{0,6},{2,4},{4,2},{6,0},{8,14},{10,12},{12,10},{14,8},{16,22},{18,... | collective-permute-start | bytes 589832 | tf_op jit(solution)/shard_map/ppermute | solution.py:30
  84.4 3.5 %collective-permute-start.18 = (bf16[32,768]{1,0:T(8,128)(2,1)S(1)}, bf16[32,768]{1,0:T(8,128)(2,1)S(1)}, u32[]{:S(2)}, u32[]{:S(2)}) collective-permute-start(bf16[32,768]{1,0:T(8,128)(2,1)S(1)} %get-tuple-element.69), channel_id=1, source_target_pairs={{0,2},{2,4},{4,6},{6,8},{8,10},{10,12},{12,14},{14,16},{16,18},{18... | collective-permute-start | bytes 147464 | tf_op jit(solution)/shard_map/ppermute | solution.py:37
  88.0 1.5 %collective-permute-start.19 = (bf16[32,768]{1,0:T(8,128)(2,1)S(1)}, bf16[32,768]{1,0:T(8,128)(2,1)S(1)}, u32[]{:S(2)}, u32[]{:S(2)}) collective-permute-start(bf16[32,768]{1,0:T(8,128)(2,1)S(1)} %get-tuple-element.70), channel_id=1, source_target_pairs={{2,0},{4,2},{6,4},{8,6},{10,8},{12,10},{14,12},{16,14},{18,16},{20... | collective-permute-start | bytes 147464 | tf_op jit(solution)/shard_map/ppermute | solution.py:37
  89.5 3.6 %collective-permute-done.21.refs_2_ = bf16[128,768]{1,0:T(8,128)(2,1)S(1)} collective-permute-done((bf16[128,768]{1,0:T(8,128)(2,1)S(1)}, bf16[128,768]{1,0:T(8,128)(2,1)S(1)}, u32[]{:S(2)}, u32[]{:S(2)}) %collective-permute-start.21) | collective-permute-done | bytes 196640 | tf_op jit(solution)/shard_map/ppermute | solution.py:30
  93.0 1.5 %shard_map.140 = bf16[128,768]{1,0:T(8,128)(2,1)} custom-call(s32[3]{0:T(128)S(1)} %pad_add_fusion.1.ids, s32[16]{0:T(128)S(1)} %copy-done.10, s32[4]{0:T(128)S(1)} %bitcast.32, bf16[256,768]{1,0:T(8,128)(2,1)S(1)} %bitcast.25, f32[1,768]{1,0:T(1,128)S(1)} %broadcast_in_dim.24.layer_scale, bf16[128,768]{1,0:T(8,128)(2,1)S(1)} %copy-done.4, ...), custom_call_target="tpu_custom_call" | custom-call | flops 1000000 | bytes 1048576 | tf_op jit(solution)/shard_map/pallas_call | solution.py:54
  95.4 3.8 %collective-permute-start.23 = (bf16[192,768]{1,0:T(8,128)(2,1)S(1)}, bf16[192,768]{1,0:T(8,128)(2,1)S(1)}, u32[]{:S(2)}, u32[]{:S(2)}) collective-permute-start(bf16[192,768]{1,0:T(8,128)(2,1)S(1)} %fusion.1.refs_0_), channel_id=1, source_target_pairs={{0,2},{2,0},{4,6},{6,4},{8,10},{10,8},{12,14},{14,12},{16,18},{18,... | collective-permute-start | bytes 884744 | tf_op jit(solution)/shard_map/ppermute | solution.py:30
  99.3 1.7 %collective-permute-start.26 = (bf16[192,768]{1,0:T(8,128)(2,1)S(1)}, bf16[192,768]{1,0:T(8,128)(2,1)S(1)}, u32[]{:S(2)}, u32[]{:S(2)}) collective-permute-start(bf16[192,768]{1,0:T(8,128)(2,1)S(1)} %fusion.1.refs_0_), channel_id=1, source_target_pairs={{0,8},{2,10},{4,12},{6,14},{8,0},{10,2},{12,4},{14,6},{16,24},{18,... | collective-permute-start | bytes 884744 | tf_op jit(solution)/shard_map/ppermute | solution.py:30
  101.0 1.8 %collective-permute-done.24.refs_2_ = bf16[192,768]{1,0:T(8,128)(2,1)S(1)} collective-permute-done((bf16[192,768]{1,0:T(8,128)(2,1)S(1)}, bf16[192,768]{1,0:T(8,128)(2,1)S(1)}, u32[]{:S(2)}, u32[]{:S(2)}) %collective-permute-start.24) | collective-permute-done | bytes 294944 | tf_op jit(solution)/shard_map/ppermute | solution.py:30
  102.7 2.6 %collective-permute-start.25 = (bf16[192,768]{1,0:T(8,128)(2,1)S(1)}, bf16[192,768]{1,0:T(8,128)(2,1)S(1)}, u32[]{:S(2)}, u32[]{:S(2)}) collective-permute-start(bf16[192,768]{1,0:T(8,128)(2,1)S(1)} %collective-permute-done.24.refs_2_), channel_id=1, source_target_pairs={{0,2},{2,0},{4,6},{6,4},{8,10},{10,8},{12,14},{14,12},{16,18},{18,... | collective-permute-start | bytes 884744 | tf_op jit(solution)/shard_map/ppermute | solution.py:30
  105.3 3.4 %collective-permute-done.23.refs_1_ = bf16[192,768]{1,0:T(8,128)(2,1)S(1)} collective-permute-done((bf16[192,768]{1,0:T(8,128)(2,1)S(1)}, bf16[192,768]{1,0:T(8,128)(2,1)S(1)}, u32[]{:S(2)}, u32[]{:S(2)}) %collective-permute-start.23) | collective-permute-done | bytes 294944 | tf_op jit(solution)/shard_map/ppermute | solution.py:30
  108.7 1.0 collective-permute-start.27
  109.8 1.3 collective-permute-start.28
  111.1 3.3 %shard_map.141 = bf16[128,768]{1,0:T(8,128)(2,1)} custom-call(s32[3]{0:T(128)S(1)} %pad_add_fusion.1.ids, s32[16]{0:T(128)S(1)} %copy-done.10, bf16[256,768]{1,0:T(8,128)(2,1)S(1)} %bitcast.27, bf16[32,768]{1,0:T(8,128)(2,1)S(1)} %collective-permute-done.18.before, bf16[32,768]{1,0:T(8,128)(2,1)S(1)} %collective-permute-done.19.after, ...), custom_call_target="tpu_custom_call" | custom-call | flops 1000000 | bytes 1048576 | tf_op jit(solution)/shard_map/pallas_call | solution.py:54
  115.0 2.0 %collective-permute-done.25.refs_3_ = bf16[192,768]{1,0:T(8,128)(2,1)S(1)} collective-permute-done((bf16[192,768]{1,0:T(8,128)(2,1)S(1)}, bf16[192,768]{1,0:T(8,128)(2,1)S(1)}, u32[]{:S(2)}, u32[]{:S(2)}) %collective-permute-start.25) | collective-permute-done | bytes 294944 | tf_op jit(solution)/shard_map/ppermute | solution.py:30
  117.0 1.5 %collective-permute-done.27.refs_5_ = bf16[192,768]{1,0:T(8,128)(2,1)S(1)} collective-permute-done((bf16[192,768]{1,0:T(8,128)(2,1)S(1)}, bf16[192,768]{1,0:T(8,128)(2,1)S(1)}, u32[]{:S(2)}, u32[]{:S(2)}) %collective-permute-start.27) | collective-permute-done | bytes 294944 | tf_op jit(solution)/shard_map/ppermute | solution.py:30
  119.1 1.0 copy-done.13
  120.1 8.0 %shard_map.142 = (f32[48,1536]{1,0:T(8,128)S(1)}, bf16[48,1536]{1,0:T(8,128)(2,1)S(1)}) custom-call(s32[3]{0:T(128)S(1)} %pad_add_fusion.2.scalars, bf16[192,768]{1,0:T(8,128)(2,1)S(1)} %fusion.1.refs_0_, bf16[192,768]{1,0:T(8,128)(2,1)S(1)} %collective-permute-done.23.refs_1_, bf16[192,768]{1,0:T(8,128)(2,1)S(1)} %collective-permute-done.24.refs_2_, ...), custom_call_target="tpu_custom_call" | custom-call | flops 10000000000 | bytes 1048576 | tf_op jit(solution)/shard_map/pallas_call | solution.py:54
  128.1 3.0 %collective-permute-start.30 = (bf16[48,1536]{1,0:T(8,128)(2,1)S(1)}, bf16[48,1536]{1,0:T(8,128)(2,1)S(1)}, u32[]{:S(2)}, u32[]{:S(2)}) collective-permute-start(bf16[48,1536]{1,0:T(8,128)(2,1)S(1)} %get-tuple-element.89), channel_id=1, source_target_pairs={{0,16},{2,18},{4,20},{6,22},{8,24},{10,26},{12,28},{14,30},{16,0},... | collective-permute-start | bytes 442376 | tf_op jit(solution)/shard_map/ppermute | solution.py:30
  131.1 4.7 %collective-permute-done.30 = bf16[48,1536]{1,0:T(8,128)(2,1)S(1)} collective-permute-done((bf16[48,1536]{1,0:T(8,128)(2,1)S(1)}, bf16[48,1536]{1,0:T(8,128)(2,1)S(1)}, u32[]{:S(2)}, u32[]{:S(2)}) %collective-permute-start.30) | collective-permute-done | bytes 147488 | tf_op jit(solution)/shard_map/ppermute | solution.py:30
  (92 shorter events, 13.7 us)
Async XLA Ops:
  0.6 21.8 %copy-start.1 = (bf16[32,8,768]{2,1,0:T(8,128)(2,1)S(1)}, bf16[32,8,768]{2,1,0:T(8,128)(2,1)}, u32[]{:S(2)}) copy-start(bf16[32,8,768]{2,1,0:T(8,128)(2,1)} %param.10) | copy-start | bytes 1179652
  0.6 21.8 %copy-start.10 = (s32[16]{0:T(128)S(1)}, s32[16]{0:T(128)}, u32[]{:S(2)}) copy-start(s32[16]{0:T(128)} %lengths.11) | copy-start | bytes 196
  0.7 21.6 %copy-start.22 = (f32[7,7,768]{2,1,0:T(8,128)S(1)}, f32[7,7,768]{2,1,0:T(8,128)}, u32[]{:S(2)}) copy-start(f32[7,7,768]{2,1,0:T(8,128)} %param.12) | copy-start | bytes 451588
  0.7 21.6 %copy-start.24 = (f32[768]{0:T(1024)S(1)}, f32[768]{0:T(1024)}, u32[]{:S(2)}) copy-start(f32[768]{0:T(1024)} %param.13) | copy-start | bytes 9220
  0.7 21.6 %copy-start.25 = (f32[768]{0:T(1024)S(1)}, f32[768]{0:T(1024)}, u32[]{:S(2)}) copy-start(f32[768]{0:T(1024)} %param.17) | copy-start | bytes 9220
  0.7 21.7 %copy-start.11 = (s32[4,1]{0,1:T(1,128)S(1)}, s32[4,1]{0,1:T(1,128)}, u32[]{:S(2)}) copy-start(s32[4,1]{0,1:T(1,128)} %param.18) | copy-start | bytes 52
  1.8 12.1 %collective-permute-start = (bf16[2,48,384]{2,1,0:T(8,128)(2,1)S(1)}, bf16[2,48,384]{2,1,0:T(8,128)(2,1)S(1)}, u32[]{:S(2)}, u32[]{:S(2)}) collective-permute-start(bf16[2,48,384]{2,1,0:T(8,128)(2,1)S(1)} %get-tuple-element.94), channel_id=1, source_target_pairs={{0,2},{2,0},{4,6},{6,4},{8,10},{10,8},{12,14},{14,12},{16,18},{18,... | collective-permute-start | bytes 221192 | tf_op jit(solution)/shard_map/ppermute | solution.py:30
  4.8 9.1 %collective-permute-start.1 = (bf16[2,48,384]{2,1,0:T(8,128)(2,1)S(1)}, bf16[2,48,384]{2,1,0:T(8,128)(2,1)S(1)}, u32[]{:S(2)}, u32[]{:S(2)}) collective-permute-start(bf16[2,48,384]{2,1,0:T(8,128)(2,1)S(1)} %get-tuple-element.95), channel_id=1, source_target_pairs={{0,4},{2,6},{4,0},{6,2},{8,12},{10,14},{12,8},{14,10},{16,20},{18,... | collective-permute-start | bytes 221192 | tf_op jit(solution)/shard_map/ppermute | solution.py:30
  6.3 7.6 %collective-permute-start.2 = (bf16[2,48,384]{2,1,0:T(8,128)(2,1)S(1)}, bf16[2,48,384]{2,1,0:T(8,128)(2,1)S(1)}, u32[]{:S(2)}, u32[]{:S(2)}) collective-permute-start(bf16[2,48,384]{2,1,0:T(8,128)(2,1)S(1)} %get-tuple-element.92), channel_id=1, source_target_pairs={{0,6},{2,4},{4,2},{6,0},{8,14},{10,12},{12,10},{14,8},{16,22},{18,... | collective-permute-start | bytes 221192 | tf_op jit(solution)/shard_map/ppermute | solution.py:30
  6.3 1.0 copy-start
  8.0 14.5 %copy-start.2 = (bf16[32,8,768]{2,1,0:T(8,128)(2,1)S(1)}, bf16[32,8,768]{2,1,0:T(8,128)(2,1)}, u32[]{:S(2)}) copy-start(bf16[32,8,768]{2,1,0:T(8,128)(2,1)} %param.11) | copy-start | bytes 1179652
  8.7 5.6 %collective-permute-start.3 = (bf16[32,768]{1,0:T(8,128)(2,1)S(1)}, bf16[32,768]{1,0:T(8,128)(2,1)S(1)}, u32[]{:S(2)}, u32[]{:S(2)}) collective-permute-start(bf16[32,768]{1,0:T(8,128)(2,1)S(1)} %get-tuple-element.47), channel_id=1, source_target_pairs={{0,2},{2,4},{4,6},{6,8},{8,10},{10,12},{12,14},{14,16},{16,18},{18... | collective-permute-start | bytes 147464 | tf_op jit(solution)/shard_map/ppermute | solution.py:37
  12.5 6.0 %collective-permute-start.4 = (bf16[32,768]{1,0:T(8,128)(2,1)S(1)}, bf16[32,768]{1,0:T(8,128)(2,1)S(1)}, u32[]{:S(2)}, u32[]{:S(2)}) collective-permute-start(bf16[32,768]{1,0:T(8,128)(2,1)S(1)} %get-tuple-element.48), channel_id=1, source_target_pairs={{2,0},{4,2},{6,4},{8,6},{10,8},{12,10},{14,12},{16,14},{18,16},{20... | collective-permute-start | bytes 147464 | tf_op jit(solution)/shard_map/ppermute | solution.py:37
  18.5 14.8 %collective-permute-start.5 = (bf16[1,2,192,384]{3,2,1,0:T(8,128)(2,1)S(1)}, bf16[1,2,192,384]{3,2,1,0:T(8,128)(2,1)S(1)}, u32[]{:S(2)}, u32[]{:S(2)}) collective-permute-start(bf16[1,2,192,384]{3,2,1,0:T(8,128)(2,1)S(1)} %bitcast.28), channel_id=1, source_target_pairs={{0,16},{2,18},{4,20},{6,22},{8,24},{10,26},{12,28},{14,30},{16,0},... | collective-permute-start | bytes 884744 | tf_op jit(solution)/shard_map/ppermute | solution.py:30
  26.0 12.0 %collective-permute-start.7 = (bf16[2,128,768]{2,1,0:T(8,128)(2,1)S(1)}, bf16[2,128,768]{2,1,0:T(8,128)(2,1)S(1)}, u32[]{:S(2)}, u32[]{:S(2)}) collective-permute-start(bf16[2,128,768]{2,1,0:T(8,128)(2,1)S(1)} %get-tuple-element.54.refs_0_), channel_id=1, source_target_pairs={{0,2},{2,0},{4,6},{6,4},{8,10},{10,8},{12,14},{14,12},{16,18},{18,... | collective-permute-start | bytes 1179656 | tf_op jit(solution)/shard_map/ppermute | solution.py:30
  27.2 17.1 %collective-permute-start.8 = (bf16[2,128,768]{2,1,0:T(8,128)(2,1)S(1)}, bf16[2,128,768]{2,1,0:T(8,128)(2,1)S(1)}, u32[]{:S(2)}, u32[]{:S(2)}) collective-permute-start(bf16[2,128,768]{2,1,0:T(8,128)(2,1)S(1)} %get-tuple-element.54.refs_0_), channel_id=1, source_target_pairs={{0,4},{2,6},{4,0},{6,2},{8,12},{10,14},{12,8},{14,10},{16,20},{18,... | collective-permute-start | bytes 1179656 | tf_op jit(solution)/shard_map/ppermute | solution.py:30
  30.1 14.2 %collective-permute-start.9 = (bf16[2,128,768]{2,1,0:T(8,128)(2,1)S(1)}, bf16[2,128,768]{2,1,0:T(8,128)(2,1)S(1)}, u32[]{:S(2)}, u32[]{:S(2)}) collective-permute-start(bf16[2,128,768]{2,1,0:T(8,128)(2,1)S(1)} %get-tuple-element.54.refs_0_), channel_id=1, source_target_pairs={{0,6},{2,4},{4,2},{6,0},{8,14},{10,12},{12,10},{14,8},{16,22},{18,... | collective-permute-start | bytes 1179656 | tf_op jit(solution)/shard_map/ppermute | solution.py:30
  33.4 11.2 %copy-start.23 = (f32[1536]{0:T(1024)S(1)}, f32[1536]{0:T(1024)}, u32[]{:S(2)}) copy-start(f32[1536]{0:T(1024)} %param.15) | copy-start | bytes 18436
  33.4 14.3 %collective-permute-start.6 = (bf16[2,2,192,384]{3,2,1,0:T(8,128)(2,1)S(1)}, bf16[2,2,192,384]{3,2,1,0:T(8,128)(2,1)}, u32[]{:S(2)}, u32[]{:S(2)}) collective-permute-start(bf16[2,2,192,384]{3,2,1,0:T(8,128)(2,1)S(1)} %shard_map.131.early), channel_id=1, source_target_pairs={{0,8},{2,10},{4,12},{6,14},{8,0},{10,2},{12,4},{14,6},{16,24},{18,... | collective-permute-start | bytes 1769480 | tf_op jit(solution)/shard_map/ppermute | solution.py:30
  44.5 4.4 %collective-permute-start.10 = (bf16[2,512,768]{2,1,0:T(8,128)(2,1)S(1)}, bf16[2,512,768]{2,1,0:T(8,128)(2,1)}, u32[]{:S(2)}, u32[]{:S(2)}) collective-permute-start(bf16[2,512,768]{2,1,0:T(8,128)(2,1)S(1)} %shard_map.134.refs_0_), channel_id=1, source_target_pairs={{0,1},{1,0},{2,3},{3,2},{4,5},{5,4},{6,7},{7,6},{8,9},{9,8},{10,11... | collective-permute-start | bytes 4718600 | tf_op jit(solution)/shard_map/ppermute | solution.py:30
  56.4 3.5 %collective-permute-start.12 = (bf16[2,512,768]{2,1,0:T(8,128)(2,1)S(1)}, bf16[2,512,768]{2,1,0:T(8,128)(2,1)S(1)}, u32[]{:S(2)}, u32[]{:S(2)}) collective-permute-start(bf16[2,512,768]{2,1,0:T(8,128)(2,1)S(1)} %get-tuple-element.60), channel_id=1, source_target_pairs={{0,1},{1,0},{2,3},{3,2},{4,5},{5,4},{6,7},{7,6},{8,9},{9,8},{10,11... | collective-permute-start | bytes 4718600 | tf_op jit(solution)/shard_map/ppermute | solution.py:30
  56.5 16.1 %collective-permute-start.11 = (bf16[2,192,768]{2,1,0:T(8,128)(2,1)}, bf16[2,192,768]{2,1,0:T(8,128)(2,1)}, u32[]{:S(2)}, u32[]{:S(2)}) collective-permute-start(bf16[2,192,768]{2,1,0:T(8,128)(2,1)} %get-tuple-element.56), channel_id=1, source_target_pairs={{0,8},{2,10},{4,12},{6,14},{8,0},{10,2},{12,4},{14,6},{16,24},{18,... | collective-permute-start | bytes 1769480 | tf_op jit(solution)/shard_map/ppermute | solution.py:30
  66.8 8.0 %collective-permute-start.13 = (bf16[128,768]{1,0:T(8,128)(2,1)}, bf16[128,768]{1,0:T(8,128)(2,1)S(1)}, u32[]{:S(2)}, u32[]{:S(2)}) collective-permute-start(bf16[128,768]{1,0:T(8,128)(2,1)} %get-tuple-element.61), channel_id=1, source_target_pairs={{0,2},{2,0},{4,6},{6,4},{8,10},{10,8},{12,14},{14,12},{16,18},{18,... | collective-permute-start | bytes 589832 | tf_op jit(solution)/shard_map/ppermute | solution.py:30
  68.2 11.1 %collective-permute-start.15 = (bf16[128,768]{1,0:T(8,128)(2,1)}, bf16[128,768]{1,0:T(8,128)(2,1)S(1)}, u32[]{:S(2)}, u32[]{:S(2)}) collective-permute-start(bf16[128,768]{1,0:T(8,128)(2,1)} %copy-done.21), channel_id=1, source_target_pairs={{0,4},{2,6},{4,0},{6,2},{8,12},{10,14},{12,8},{14,10},{16,20},{18,... | collective-permute-start | bytes 589832 | tf_op jit(solution)/shard_map/ppermute | solution.py:30
  69.5 9.8 %collective-permute-start.16 = (bf16[128,768]{1,0:T(8,128)(2,1)}, bf16[128,768]{1,0:T(8,128)(2,1)S(1)}, u32[]{:S(2)}, u32[]{:S(2)}) collective-permute-start(bf16[128,768]{1,0:T(8,128)(2,1)} %copy-done.20), channel_id=1, source_target_pairs={{0,6},{2,4},{4,2},{6,0},{8,14},{10,12},{12,10},{14,8},{16,22},{18,... | collective-permute-start | bytes 589832 | tf_op jit(solution)/shard_map/ppermute | solution.py:30
  74.8 4.5 %copy-start.6 = (bf16[128,768]{1,0:T(8,128)(2,1)S(1)}, bf16[128,768]{1,0:T(8,128)(2,1)}, u32[]{:S(2)}) copy-start(bf16[128,768]{1,0:T(8,128)(2,1)} %copy-done.5) | copy-start | bytes 589828
  74.8 4.5 %copy-start.8 = (f32[128,128]{1,0:T(8,128)S(1)}, f32[128,128]{1,0:T(8,128)}, u32[]{:S(2)}) copy-start(f32[128,128]{1,0:T(8,128)} %copy-done.7) | copy-start | bytes 196612
  76.1 4.2 %copy-start.19 = (bf16[128,768]{1,0:T(8,128)(2,1)S(1)}, bf16[128,768]{1,0:T(8,128)(2,1)}, u32[]{:S(2)}) copy-start(bf16[128,768]{1,0:T(8,128)(2,1)} %copy-done.18) | copy-start | bytes 589828
  76.1 5.8 %copy-start.17 = (bf16[128,768]{1,0:T(8,128)(2,1)S(1)}, bf16[128,768]{1,0:T(8,128)(2,1)}, u32[]{:S(2)}) copy-start(bf16[128,768]{1,0:T(8,128)(2,1)} %copy-done.16) | copy-start | bytes 589828
  76.1 6.0 %copy-start.15 = (bf16[128,768]{1,0:T(8,128)(2,1)S(1)}, bf16[128,768]{1,0:T(8,128)(2,1)}, u32[]{:S(2)}) copy-start(bf16[128,768]{1,0:T(8,128)(2,1)} %copy-done.14) | copy-start | bytes 589828
  76.1 17.0 %copy-start.4 = (bf16[128,768]{1,0:T(8,128)(2,1)S(1)}, bf16[128,768]{1,0:T(8,128)(2,1)}, u32[]{:S(2)}) copy-start(bf16[128,768]{1,0:T(8,128)(2,1)} %copy-done.3) | copy-start | bytes 589828
  76.1 18.4 %collective-permute-start.14 = (bf16[1,192,768]{2,1,0:T(8,128)(2,1)S(1)}, bf16[1,192,768]{2,1,0:T(8,128)(2,1)S(1)}, u32[]{:S(2)}, u32[]{:S(2)}) collective-permute-start(bf16[1,192,768]{2,1,0:T(8,128)(2,1)S(1)} %dynamic-slice_convert_fusion), channel_id=1, source_target_pairs={{0,16},{2,18},{4,20},{6,22},{8,24},{10,26},{12,28},{14,30},{16,0},... | collective-permute-start | bytes 884744 | tf_op jit(solution)/shard_map/ppermute | solution.py:30
  80.2 3.7 %collective-permute-start.17 = (bf16[128,768]{1,0:T(8,128)(2,1)S(1)}, bf16[128,768]{1,0:T(8,128)(2,1)S(1)}, u32[]{:S(2)}, u32[]{:S(2)}) collective-permute-start(bf16[128,768]{1,0:T(8,128)(2,1)S(1)} %shard_map.138.refs_0_.rest_0_), channel_id=1, source_target_pairs={{0,1},{1,0},{2,3},{3,2},{4,5},{5,4},{6,7},{7,6},{8,9},{9,8},{10,11... | collective-permute-start | bytes 589832 | tf_op jit(solution)/shard_map/ppermute | solution.py:30
  80.2 7.8 %collective-permute-start.20 = (bf16[128,768]{1,0:T(8,128)(2,1)S(1)}, bf16[128,768]{1,0:T(8,128)(2,1)S(1)}, u32[]{:S(2)}, u32[]{:S(2)}) collective-permute-start(bf16[128,768]{1,0:T(8,128)(2,1)S(1)} %copy-done.19), channel_id=1, source_target_pairs={{0,2},{2,0},{4,6},{6,4},{8,10},{10,8},{12,14},{14,12},{16,18},{18,... | collective-permute-start | bytes 589832 | tf_op jit(solution)/shard_map/ppermute | solution.py:30
  81.9 11.2 %collective-permute-start.21 = (bf16[128,768]{1,0:T(8,128)(2,1)S(1)}, bf16[128,768]{1,0:T(8,128)(2,1)S(1)}, u32[]{:S(2)}, u32[]{:S(2)}) collective-permute-start(bf16[128,768]{1,0:T(8,128)(2,1)S(1)} %copy-done.17), channel_id=1, source_target_pairs={{0,4},{2,6},{4,0},{6,2},{8,12},{10,14},{12,8},{14,10},{16,20},{18,... | collective-permute-start | bytes 589832 | tf_op jit(solution)/shard_map/ppermute | solution.py:30
  82.0 11.0 %collective-permute-start.22 = (bf16[128,768]{1,0:T(8,128)(2,1)S(1)}, bf16[128,768]{1,0:T(8,128)(2,1)S(1)}, u32[]{:S(2)}, u32[]{:S(2)}) collective-permute-start(bf16[128,768]{1,0:T(8,128)(2,1)S(1)} %copy-done.15), channel_id=1, source_target_pairs={{0,6},{2,4},{4,2},{6,0},{8,14},{10,12},{12,10},{14,8},{16,22},{18,... | collective-permute-start | bytes 589832 | tf_op jit(solution)/shard_map/ppermute | solution.py:30
  84.4 10.1 %collective-permute-start.18 = (bf16[32,768]{1,0:T(8,128)(2,1)S(1)}, bf16[32,768]{1,0:T(8,128)(2,1)S(1)}, u32[]{:S(2)}, u32[]{:S(2)}) collective-permute-start(bf16[32,768]{1,0:T(8,128)(2,1)S(1)} %get-tuple-element.69), channel_id=1, source_target_pairs={{0,2},{2,4},{4,6},{6,8},{8,10},{10,12},{12,14},{14,16},{16,18},{18... | collective-permute-start | bytes 147464 | tf_op jit(solution)/shard_map/ppermute | solution.py:37
  88.0 6.5 %collective-permute-start.19 = (bf16[32,768]{1,0:T(8,128)(2,1)S(1)}, bf16[32,768]{1,0:T(8,128)(2,1)S(1)}, u32[]{:S(2)}, u32[]{:S(2)}) collective-permute-start(bf16[32,768]{1,0:T(8,128)(2,1)S(1)} %get-tuple-element.70), channel_id=1, source_target_pairs={{2,0},{4,2},{6,4},{8,6},{10,8},{12,10},{14,12},{16,14},{18,16},{20... | collective-permute-start | bytes 147464 | tf_op jit(solution)/shard_map/ppermute | solution.py:37
  94.6 8.2 %collective-permute-start.24 = (bf16[192,768]{1,0:T(8,128)(2,1)S(1)}, bf16[192,768]{1,0:T(8,128)(2,1)S(1)}, u32[]{:S(2)}, u32[]{:S(2)}) collective-permute-start(bf16[192,768]{1,0:T(8,128)(2,1)S(1)} %fusion.1.refs_0_), channel_id=1, source_target_pairs={{0,4},{2,6},{4,0},{6,2},{8,12},{10,14},{12,8},{14,10},{16,20},{18,... | collective-permute-start | bytes 884744 | tf_op jit(solution)/shard_map/ppermute | solution.py:30
  95.4 13.3 %collective-permute-start.23 = (bf16[192,768]{1,0:T(8,128)(2,1)S(1)}, bf16[192,768]{1,0:T(8,128)(2,1)S(1)}, u32[]{:S(2)}, u32[]{:S(2)}) collective-permute-start(bf16[192,768]{1,0:T(8,128)(2,1)S(1)} %fusion.1.refs_0_), channel_id=1, source_target_pairs={{0,2},{2,0},{4,6},{6,4},{8,10},{10,8},{12,14},{14,12},{16,18},{18,... | collective-permute-start | bytes 884744 | tf_op jit(solution)/shard_map/ppermute | solution.py:30
  99.3 10.5 %collective-permute-start.26 = (bf16[192,768]{1,0:T(8,128)(2,1)S(1)}, bf16[192,768]{1,0:T(8,128)(2,1)S(1)}, u32[]{:S(2)}, u32[]{:S(2)}) collective-permute-start(bf16[192,768]{1,0:T(8,128)(2,1)S(1)} %fusion.1.refs_0_), channel_id=1, source_target_pairs={{0,8},{2,10},{4,12},{6,14},{8,0},{10,2},{12,4},{14,6},{16,24},{18,... | collective-permute-start | bytes 884744 | tf_op jit(solution)/shard_map/ppermute | solution.py:30
  101.0 14.0 %collective-permute-start.29 = (bf16[192,768]{1,0:T(8,128)(2,1)S(1)}, bf16[192,768]{1,0:T(8,128)(2,1)S(1)}, u32[]{:S(2)}, u32[]{:S(2)}) collective-permute-start(bf16[192,768]{1,0:T(8,128)(2,1)S(1)} %fusion.1.refs_0_), channel_id=1, source_target_pairs={{0,14},{2,12},{4,10},{6,8},{8,6},{10,4},{12,2},{14,0},{16,30},{18,... | collective-permute-start | bytes 884744 | tf_op jit(solution)/shard_map/ppermute | solution.py:30
  102.7 14.2 %collective-permute-start.25 = (bf16[192,768]{1,0:T(8,128)(2,1)S(1)}, bf16[192,768]{1,0:T(8,128)(2,1)S(1)}, u32[]{:S(2)}, u32[]{:S(2)}) collective-permute-start(bf16[192,768]{1,0:T(8,128)(2,1)S(1)} %collective-permute-done.24.refs_2_), channel_id=1, source_target_pairs={{0,2},{2,0},{4,6},{6,4},{8,10},{10,8},{12,14},{14,12},{16,18},{18,... | collective-permute-start | bytes 884744 | tf_op jit(solution)/shard_map/ppermute | solution.py:30
  108.7 9.7 %collective-permute-start.27 = (bf16[192,768]{1,0:T(8,128)(2,1)S(1)}, bf16[192,768]{1,0:T(8,128)(2,1)S(1)}, u32[]{:S(2)}, u32[]{:S(2)}) collective-permute-start(bf16[192,768]{1,0:T(8,128)(2,1)S(1)} %collective-permute-done.23.refs_1_), channel_id=1, source_target_pairs={{0,8},{2,10},{4,12},{6,14},{8,0},{10,2},{12,4},{14,6},{16,24},{18,... | collective-permute-start | bytes 884744 | tf_op jit(solution)/shard_map/ppermute | solution.py:30
  109.8 9.4 %collective-permute-start.28 = (bf16[192,768]{1,0:T(8,128)(2,1)S(1)}, bf16[192,768]{1,0:T(8,128)(2,1)}, u32[]{:S(2)}, u32[]{:S(2)}) collective-permute-start(bf16[192,768]{1,0:T(8,128)(2,1)S(1)} %collective-permute-done.26.refs_4_), channel_id=1, source_target_pairs={{0,4},{2,6},{4,0},{6,2},{8,12},{10,14},{12,8},{14,10},{16,20},{18,... | collective-permute-start | bytes 884744 | tf_op jit(solution)/shard_map/ppermute | solution.py:30
  118.4 0.7 copy-start.12
  119.1 1.0 copy-start.13
  128.1 7.7 %collective-permute-start.30 = (bf16[48,1536]{1,0:T(8,128)(2,1)S(1)}, bf16[48,1536]{1,0:T(8,128)(2,1)S(1)}, u32[]{:S(2)}, u32[]{:S(2)}) collective-permute-start(bf16[48,1536]{1,0:T(8,128)(2,1)S(1)} %get-tuple-element.89), channel_id=1, source_target_pairs={{0,16},{2,18},{4,20},{6,22},{8,24},{10,26},{12,28},{14,30},{16,0},... | collective-permute-start | bytes 442376 | tf_op jit(solution)/shard_map/ppermute | solution.py:30
  (9 other events, 6.1 us)

commit v9 on v8

--- a/solution.py
+++ b/solution.py
@@ -1,4 +1,5 @@
 import functools
+import math
 
 import jax
 import jax.numpy as jnp
@@ -15,6 +16,7 @@
 PLANE = 4
 LANES = 128
 CHUNK = 8
+SLACK = 4 * 2**20
 
 INV_ROOT_TWO = 0.7071067811865476
 INV_ROOT_TAU = 0.3989422804014327
@@ -46,9 +48,9 @@
     return blocks
 
 
-def call(
-    kernel, out_shape, scratch, flops, *operands, scalars=1, apart=0, out_space=pltpu.VMEM
-):
+def call(kernel, out_shape, scratch, flops, *operands, scalars=1, apart=0):
+    held = sum(a.size * a.dtype.itemsize for a in operands + tuple(out_shape))
+    room = sum(math.prod(a.shape) * 4 for a in scratch if hasattr(a, "shape"))
     smem = pl.BlockSpec(memory_space=pltpu.SMEM)
     vmem = pl.BlockSpec(memory_space=pltpu.VMEM)
     return pl.pallas_call(
@@ -56,10 +58,10 @@
         out_shape=out_shape,
         in_specs=[smem] * scalars
         + [vmem] * (len(operands) - scalars - apart)
-        + [pl.BlockSpec(memory_space=pl.ANY)] * apart,
-        out_specs=[pl.BlockSpec(memory_space=out_space)] * len(out_shape),
+        + [pl.BlockSpec(memory_space=pltpu.HBM)] * apart,
+        out_specs=[vmem] * len(out_shape),
         scratch_shapes=scratch,
-        compiler_params=pltpu.CompilerParams(vmem_limit_bytes=40 * 2**20),
+        compiler_params=pltpu.CompilerParams(vmem_limit_bytes=2 * held + room + SLACK),
         cost_estimate=pl.CostEstimate(flops=flops, bytes_accessed=2**20, transcendentals=0),
     )(*operands)
 
@@ -301,21 +303,15 @@
 
 
 def add_kernel(mine, *refs):
-    *refs, staged, sems = refs
     others, outs = refs[: -2 * PLANE], refs[-2 * PLANE :]
     tokens = outs[0].shape[0]
-    copies = []
     for index, out in enumerate(outs):
         which, strip = divmod(index, PLANE)
         rows_in = slice(strip * tokens, (strip + 1) * tokens)
         total = mine[which, rows_in, :]
         for other in others:
             total = total + other[which, rows_in, :].astype(F32)
-        staged[index] = total.astype(BF16)
-        copies.append(pltpu.make_async_copy(staged.at[index], out, sems.at[index]))
-        copies[-1].start()
-    for copy in copies:
-        copy.wait()
+        out[...] = total.astype(BF16)
 
 
 def backward_kernel(ids, lengths, cotangent, before, after, taps, *rest):
@@ -549,13 +545,10 @@
     blocks = call(
         add_kernel,
         [flat] * (2 * PLANE),
-        [
-            pltpu.VMEM((2 * PLANE, tokens, channels), BF16),
-            pltpu.SemaphoreType.DMA((2 * PLANE,)),
-        ],
+        [],
         10**6,
         mine, *others,
-        scalars=0, out_space=pltpu.HBM,
+        scalars=0,
     )
     blocks = [
         swap(value, "tile", i % PLANE) if i % PLANE else value for i, value in enumerate(blocks)

time: 137 us -> 136 us (level)
  Pallas kernels: 29 us -> 27.6 us
    pallas_call x14, Pallas kernels: 29 us -> 27.6 us  [call(): pl.pallas_call(kernel, out_shape=out_shape, in_specs=[smem] * scalars + [...]
  transfers between devices with their start and end apart: 31 -> 31, of which waited for: 18 -> 18; matrix products, arithmetic and copies ran while one was open for 1% -> 1% of each run, Pallas kernels for 10% -> 9%
where the time goes in v9:
time: 136 us; the launch traced here: 135 us
  starting transfers between devices  50.2 us (37%)
  waiting for transfers between devices  44.8 us (33%)
  Pallas kernels  27.6 us (20%)
  local copies, waits for them, and re-layouts  8.25 us (6%)
  other arithmetic  3.46 us (3%)
    ppermute x27, waiting for transfers between devices, swap(): lax.ppermute(value, axis, [(i, i ^ bit) for i in range(lax.axis_size(axis...  40.1 us
    ppermute x27, starting transfers between devices, swap(): lax.ppermute(value, axis, [(i, i ^ bit) for i in range(lax.axis_size(axis...  40.1 us
    pallas_call x14, Pallas kernels, call(): pl.pallas_call(kernel, out_shape=out_shape, in_specs=[smem] * scalars + [...  27.6 us
    ppermute x4, starting transfers between devices, neighbours(): return (lax.ppermute(last, 'tile', up), lax.ppermute(first, 'tile', down))  10.1 us
    unnamed x52, local copies, waits for them, and re-layouts  8.17 us
    ppermute x4, waiting for transfers between devices, neighbours(): return (lax.ppermute(last, 'tile', up), lax.ppermute(first, 'tile', down))  4.62 us
  transfers between devices with their start and end apart: 31, of which 18 were waited for; matrix products, arithmetic and copies ran while one was open for 1% of the time, Pallas kernels for 9%

profile of v9, /device:TPU:0, one launch (start us, length us, event | category | flops | bytes accessed | tf_op | source)
XLA Modules:
  0.0 135.3 jit_solution(12678497021940176274)
XLA Ops:
  0.7 1.0 fusion.2
  1.8 3.0 %collective-permute-start = (bf16[2,48,384]{2,1,0:T(8,128)(2,1)S(1)}, bf16[2,48,384]{2,1,0:T(8,128)(2,1)S(1)}, u32[]{:S(2)}, u32[]{:S(2)}) collective-permute-start(bf16[2,48,384]{2,1,0:T(8,128)(2,1)S(1)} %get-tuple-element.94), channel_id=1, source_target_pairs={{0,2},{2,0},{4,6},{6,4},{8,10},{10,8},{12,14},{14,12},{16,18},{18,... | collective-permute-start | bytes 221192 | tf_op jit(solution)/shard_map/ppermute | solution.py:32
  4.8 1.5 %collective-permute-start.1 = (bf16[2,48,384]{2,1,0:T(8,128)(2,1)S(1)}, bf16[2,48,384]{2,1,0:T(8,128)(2,1)S(1)}, u32[]{:S(2)}, u32[]{:S(2)}) collective-permute-start(bf16[2,48,384]{2,1,0:T(8,128)(2,1)S(1)} %get-tuple-element.95), channel_id=1, source_target_pairs={{0,4},{2,6},{4,0},{6,2},{8,12},{10,14},{12,8},{14,10},{16,20},{18,... | collective-permute-start | bytes 221192 | tf_op jit(solution)/shard_map/ppermute | solution.py:32
  6.3 1.0 copy-done
  8.7 3.9 %collective-permute-start.3 = (bf16[32,768]{1,0:T(8,128)(2,1)S(1)}, bf16[32,768]{1,0:T(8,128)(2,1)S(1)}, u32[]{:S(2)}, u32[]{:S(2)}) collective-permute-start(bf16[32,768]{1,0:T(8,128)(2,1)S(1)} %get-tuple-element.47), channel_id=1, source_target_pairs={{0,2},{2,4},{4,6},{6,8},{8,10},{10,12},{12,14},{14,16},{16,18},{18... | collective-permute-start | bytes 147464 | tf_op jit(solution)/shard_map/ppermute | solution.py:39
  12.5 1.3 collective-permute-start.4
  14.3 4.3 %collective-permute-done.4.after = bf16[32,768]{1,0:T(8,128)(2,1)S(1)} collective-permute-done((bf16[32,768]{1,0:T(8,128)(2,1)S(1)}, bf16[32,768]{1,0:T(8,128)(2,1)S(1)}, u32[]{:S(2)}, u32[]{:S(2)}) %collective-permute-start.4) | collective-permute-done | bytes 49184 | tf_op jit(solution)/shard_map/ppermute | solution.py:39
  18.5 3.8 %collective-permute-start.5 = (bf16[1,2,192,384]{3,2,1,0:T(8,128)(2,1)S(1)}, bf16[1,2,192,384]{3,2,1,0:T(8,128)(2,1)S(1)}, u32[]{:S(2)}, u32[]{:S(2)}) collective-permute-start(bf16[1,2,192,384]{3,2,1,0:T(8,128)(2,1)S(1)} %bitcast.28), channel_id=1, source_target_pairs={{0,16},{2,18},{4,20},{6,22},{8,24},{10,26},{12,28},{14,30},{16,0},... | collective-permute-start | bytes 884744 | tf_op jit(solution)/shard_map/ppermute | solution.py:32
  22.4 2.9 %shard_map.133 = (bf16[2,128,768]{2,1,0:T(8,128)(2,1)S(1)}, f32[128,768]{1,0:T(8,128)S(1)}, f32[128,128]{1,0:T(8,128)S(1)}) custom-call(s32[3]{0:T(128)S(1)} %pad_add_fusion.1.ids, s32[16]{0:T(128)S(1)} %copy-done.10, s32[4]{0:T(128)S(1)} %bitcast.30, bf16[256,768]{1,0:T(8,128)(2,1)S(1)} %bitcast.24, bf16[256,768]{1,0:T(8,128)(2,1)S(1)} %bitcast.26, ...), custom_call_target="tpu_custom_call" | custom-call | flops 1000000 | bytes 1048576 | tf_op jit(solution)/shard_map/pallas_call | solution.py:56
  25.4 1.3 collective-permute-start.7
  26.7 2.9 %collective-permute-start.8 = (bf16[2,128,768]{2,1,0:T(8,128)(2,1)S(1)}, bf16[2,128,768]{2,1,0:T(8,128)(2,1)S(1)}, u32[]{:S(2)}, u32[]{:S(2)}) collective-permute-start(bf16[2,128,768]{2,1,0:T(8,128)(2,1)S(1)} %get-tuple-element.54.refs_0_), channel_id=1, source_target_pairs={{0,4},{2,6},{4,0},{6,2},{8,12},{10,14},{12,8},{14,10},{16,20},{18,... | collective-permute-start | bytes 1179656 | tf_op jit(solution)/shard_map/ppermute | solution.py:32
  29.6 3.7 %collective-permute-done.5.refs_1_ = bf16[1,2,192,384]{3,2,1,0:T(8,128)(2,1)S(1)} collective-permute-done((bf16[1,2,192,384]{3,2,1,0:T(8,128)(2,1)S(1)}, bf16[1,2,192,384]{3,2,1,0:T(8,128)(2,1)S(1)}, u32[]{:S(2)}, u32[]{:S(2)}) %collective-permute-start.5) | collective-permute-done | bytes 294944 | tf_op jit(solution)/shard_map/ppermute | solution.py:32
  33.4 1.7 %collective-permute-start.6 = (bf16[2,2,192,384]{3,2,1,0:T(8,128)(2,1)S(1)}, bf16[2,2,192,384]{3,2,1,0:T(8,128)(2,1)}, u32[]{:S(2)}, u32[]{:S(2)}) collective-permute-start(bf16[2,2,192,384]{3,2,1,0:T(8,128)(2,1)S(1)} %shard_map.131.early), channel_id=1, source_target_pairs={{0,8},{2,10},{4,12},{6,14},{8,0},{10,2},{12,4},{14,6},{16,24},{18,... | collective-permute-start | bytes 1769480 | tf_op jit(solution)/shard_map/ppermute | solution.py:32
  35.1 2.4 %collective-permute-done.7.refs_1_ = bf16[2,128,768]{2,1,0:T(8,128)(2,1)S(1)} collective-permute-done((bf16[2,128,768]{2,1,0:T(8,128)(2,1)S(1)}, bf16[2,128,768]{2,1,0:T(8,128)(2,1)S(1)}, u32[]{:S(2)}, u32[]{:S(2)}) %collective-permute-start.7) | collective-permute-done | bytes 393248 | tf_op jit(solution)/shard_map/ppermute | solution.py:32
  37.5 6.3 %collective-permute-done.8.refs_2_ = bf16[2,128,768]{2,1,0:T(8,128)(2,1)S(1)} collective-permute-done((bf16[2,128,768]{2,1,0:T(8,128)(2,1)S(1)}, bf16[2,128,768]{2,1,0:T(8,128)(2,1)S(1)}, u32[]{:S(2)}, u32[]{:S(2)}) %collective-permute-start.8) | collective-permute-done | bytes 393248 | tf_op jit(solution)/shard_map/ppermute | solution.py:32
  44.1 3.6 %collective-permute-done.6.late = bf16[2,2,192,384]{3,2,1,0:T(8,128)(2,1)} collective-permute-done((bf16[2,2,192,384]{3,2,1,0:T(8,128)(2,1)S(1)}, bf16[2,2,192,384]{3,2,1,0:T(8,128)(2,1)}, u32[]{:S(2)}, u32[]{:S(2)}) %collective-permute-start.6) | collective-permute-done | bytes 589856 | tf_op jit(solution)/shard_map/ppermute | solution.py:32
  47.7 1.2 shard_map.132
  48.9 5.6 %shard_map.135 = (bf16[2,192,768]{2,1,0:T(8,128)(2,1)S(1)}, bf16[2,192,768]{2,1,0:T(8,128)(2,1)}, bf16[1024,384]{1,0:T(8,128)(2,1)S(1)}, bf16[1024,384]{1,0:T(8,128)(2,1)S(1)}) custom-call(s32[2]{0:T(128)S(1)} %pad_add_fusion.scalars, bf16[768,384]{1,0:T(8,128)(2,1)S(1)} %get-tuple-element.50.up, bf16[768,384]{1,0:T(8,128)(2,1)S(1)} %get-tuple-element.51.down_t, ...), custom_call_target="tpu_custom_call" | custom-call | flops 5000000000 | bytes 1048576 | tf_op jit(solution)/shard_map/pallas_call | solution.py:56
  54.5 1.8 %shard_map.136 = (f32[2,512,768]{2,1,0:T(8,128)S(1)}, bf16[2,512,768]{2,1,0:T(8,128)(2,1)S(1)}) custom-call(bf16[1024,384]{1,0:T(8,128)(2,1)S(1)} %get-tuple-element.57.act, bf16[1024,384]{1,0:T(8,128)(2,1)S(1)} %get-tuple-element.58.grad_hidden, bf16[768,384]{1,0:T(8,128)(2,1)S(1)} %get-tuple-element.50.up, bf16[768,384]{1,0:T(8,128)(2,1)S(1)} %get-tuple-element.51.down_t), custom_call_target="tpu_custom_call" | custom-call | flops 1000000000 | bytes 1048576 | tf_op jit(solution)/shard_map/pallas_call | solution.py:56
  56.4 1.4 %collective-permute-start.11 = (bf16[2,192,768]{2,1,0:T(8,128)(2,1)}, bf16[2,192,768]{2,1,0:T(8,128)(2,1)}, u32[]{:S(2)}, u32[]{:S(2)}) collective-permute-start(bf16[2,192,768]{2,1,0:T(8,128)(2,1)} %get-tuple-element.56), channel_id=1, source_target_pairs={{0,8},{2,10},{4,12},{6,14},{8,0},{10,2},{12,4},{14,6},{16,24},{18,... | collective-permute-start | bytes 1769480 | tf_op jit(solution)/shard_map/ppermute | solution.py:32
  57.8 2.0 %collective-permute-done.12.refs_0_ = bf16[2,512,768]{2,1,0:T(8,128)(2,1)S(1)} collective-permute-done((bf16[2,512,768]{2,1,0:T(8,128)(2,1)S(1)}, bf16[2,512,768]{2,1,0:T(8,128)(2,1)S(1)}, u32[]{:S(2)}, u32[]{:S(2)}) %collective-permute-start.12) | collective-permute-done | bytes 1572896 | tf_op jit(solution)/shard_map/ppermute | solution.py:32
  59.8 0.9 shard_map.137
  65.5 1.3 collective-permute-start.13
  66.8 1.3 collective-permute-start.15
  68.9 3.5 %collective-permute-done.11 = bf16[2,192,768]{2,1,0:T(8,128)(2,1)} collective-permute-done((bf16[2,192,768]{2,1,0:T(8,128)(2,1)}, bf16[2,192,768]{2,1,0:T(8,128)(2,1)}, u32[]{:S(2)}, u32[]{:S(2)}) %collective-permute-start.11) | collective-permute-done | bytes 589856 | tf_op jit(solution)/shard_map/ppermute | solution.py:32
  72.5 1.0 collective-permute-done.13.refs_1_
  73.4 1.3 convert_add_fusion
  74.8 3.0 %collective-permute-start.14 = (bf16[1,192,768]{2,1,0:T(8,128)(2,1)S(1)}, bf16[1,192,768]{2,1,0:T(8,128)(2,1)S(1)}, u32[]{:S(2)}, u32[]{:S(2)}) collective-permute-start(bf16[1,192,768]{2,1,0:T(8,128)(2,1)S(1)} %dynamic-slice_convert_fusion), channel_id=1, source_target_pairs={{0,16},{2,18},{4,20},{6,22},{8,24},{10,26},{12,28},{14,30},{16,0},... | collective-permute-start | bytes 884744 | tf_op jit(solution)/shard_map/ppermute | solution.py:32
  78.9 1.6 %collective-permute-start.20 = (bf16[128,768]{1,0:T(8,128)(2,1)S(1)}, bf16[128,768]{1,0:T(8,128)(2,1)S(1)}, u32[]{:S(2)}, u32[]{:S(2)}) collective-permute-start(bf16[128,768]{1,0:T(8,128)(2,1)S(1)} %copy-done.19), channel_id=1, source_target_pairs={{0,2},{2,0},{4,6},{6,4},{8,10},{10,8},{12,14},{14,12},{16,18},{18,... | collective-permute-start | bytes 589832 | tf_op jit(solution)/shard_map/ppermute | solution.py:32
  80.7 1.8 %collective-permute-start.22 = (bf16[128,768]{1,0:T(8,128)(2,1)S(1)}, bf16[128,768]{1,0:T(8,128)(2,1)S(1)}, u32[]{:S(2)}, u32[]{:S(2)}) collective-permute-start(bf16[128,768]{1,0:T(8,128)(2,1)S(1)} %copy-done.15), channel_id=1, source_target_pairs={{0,6},{2,4},{4,2},{6,0},{8,14},{10,12},{12,10},{14,8},{16,22},{18,... | collective-permute-start | bytes 589832 | tf_op jit(solution)/shard_map/ppermute | solution.py:32
  83.0 3.5 %collective-permute-start.18 = (bf16[32,768]{1,0:T(8,128)(2,1)S(1)}, bf16[32,768]{1,0:T(8,128)(2,1)S(1)}, u32[]{:S(2)}, u32[]{:S(2)}) collective-permute-start(bf16[32,768]{1,0:T(8,128)(2,1)S(1)} %get-tuple-element.69), channel_id=1, source_target_pairs={{0,2},{2,4},{4,6},{6,8},{8,10},{10,12},{12,14},{14,16},{16,18},{18... | collective-permute-start | bytes 147464 | tf_op jit(solution)/shard_map/ppermute | solution.py:39
  86.6 1.5 %collective-permute-start.19 = (bf16[32,768]{1,0:T(8,128)(2,1)S(1)}, bf16[32,768]{1,0:T(8,128)(2,1)S(1)}, u32[]{:S(2)}, u32[]{:S(2)}) collective-permute-start(bf16[32,768]{1,0:T(8,128)(2,1)S(1)} %get-tuple-element.70), channel_id=1, source_target_pairs={{2,0},{4,2},{6,4},{8,6},{10,8},{12,10},{14,12},{16,14},{18,16},{20... | collective-permute-start | bytes 147464 | tf_op jit(solution)/shard_map/ppermute | solution.py:39
  88.1 3.6 %collective-permute-done.21.refs_2_ = bf16[128,768]{1,0:T(8,128)(2,1)S(1)} collective-permute-done((bf16[128,768]{1,0:T(8,128)(2,1)S(1)}, bf16[128,768]{1,0:T(8,128)(2,1)S(1)}, u32[]{:S(2)}, u32[]{:S(2)}) %collective-permute-start.21) | collective-permute-done | bytes 196640 | tf_op jit(solution)/shard_map/ppermute | solution.py:32
  91.7 1.5 %shard_map.140 = bf16[128,768]{1,0:T(8,128)(2,1)} custom-call(s32[3]{0:T(128)S(1)} %pad_add_fusion.1.ids, s32[16]{0:T(128)S(1)} %copy-done.10, s32[4]{0:T(128)S(1)} %bitcast.32, bf16[256,768]{1,0:T(8,128)(2,1)S(1)} %bitcast.25, f32[1,768]{1,0:T(1,128)S(1)} %broadcast_in_dim.24.layer_scale, bf16[128,768]{1,0:T(8,128)(2,1)S(1)} %copy-done.4, ...), custom_call_target="tpu_custom_call" | custom-call | flops 1000000 | bytes 1048576 | tf_op jit(solution)/shard_map/pallas_call | solution.py:56
  94.1 3.4 %collective-permute-start.23 = (bf16[192,768]{1,0:T(8,128)(2,1)S(1)}, bf16[192,768]{1,0:T(8,128)(2,1)S(1)}, u32[]{:S(2)}, u32[]{:S(2)}) collective-permute-start(bf16[192,768]{1,0:T(8,128)(2,1)S(1)} %fusion.1.refs_0_), channel_id=1, source_target_pairs={{0,2},{2,0},{4,6},{6,4},{8,10},{10,8},{12,14},{14,12},{16,18},{18,... | collective-permute-start | bytes 884744 | tf_op jit(solution)/shard_map/ppermute | solution.py:32
  97.5 2.1 %collective-permute-start.26 = (bf16[192,768]{1,0:T(8,128)(2,1)S(1)}, bf16[192,768]{1,0:T(8,128)(2,1)S(1)}, u32[]{:S(2)}, u32[]{:S(2)}) collective-permute-start(bf16[192,768]{1,0:T(8,128)(2,1)S(1)} %fusion.1.refs_0_), channel_id=1, source_target_pairs={{0,8},{2,10},{4,12},{6,14},{8,0},{10,2},{12,4},{14,6},{16,24},{18,... | collective-permute-start | bytes 884744 | tf_op jit(solution)/shard_map/ppermute | solution.py:32
  99.6 1.8 %collective-permute-done.24.refs_2_ = bf16[192,768]{1,0:T(8,128)(2,1)S(1)} collective-permute-done((bf16[192,768]{1,0:T(8,128)(2,1)S(1)}, bf16[192,768]{1,0:T(8,128)(2,1)S(1)}, u32[]{:S(2)}, u32[]{:S(2)}) %collective-permute-start.24) | collective-permute-done | bytes 294944 | tf_op jit(solution)/shard_map/ppermute | solution.py:32
  101.4 1.5 %collective-permute-start.25 = (bf16[192,768]{1,0:T(8,128)(2,1)S(1)}, bf16[192,768]{1,0:T(8,128)(2,1)S(1)}, u32[]{:S(2)}, u32[]{:S(2)}) collective-permute-start(bf16[192,768]{1,0:T(8,128)(2,1)S(1)} %collective-permute-done.24.refs_2_), channel_id=1, source_target_pairs={{0,2},{2,0},{4,6},{6,4},{8,10},{10,8},{12,14},{14,12},{16,18},{18,... | collective-permute-start | bytes 884744 | tf_op jit(solution)/shard_map/ppermute | solution.py:32
  102.9 2.8 %collective-permute-done.23.refs_1_ = bf16[192,768]{1,0:T(8,128)(2,1)S(1)} collective-permute-done((bf16[192,768]{1,0:T(8,128)(2,1)S(1)}, bf16[192,768]{1,0:T(8,128)(2,1)S(1)}, u32[]{:S(2)}, u32[]{:S(2)}) %collective-permute-start.23) | collective-permute-done | bytes 294944 | tf_op jit(solution)/shard_map/ppermute | solution.py:32
  105.7 2.7 %collective-permute-start.27 = (bf16[192,768]{1,0:T(8,128)(2,1)S(1)}, bf16[192,768]{1,0:T(8,128)(2,1)S(1)}, u32[]{:S(2)}, u32[]{:S(2)}) collective-permute-start(bf16[192,768]{1,0:T(8,128)(2,1)S(1)} %collective-permute-done.23.refs_1_), channel_id=1, source_target_pairs={{0,8},{2,10},{4,12},{6,14},{8,0},{10,2},{12,4},{14,6},{16,24},{18,... | collective-permute-start | bytes 884744 | tf_op jit(solution)/shard_map/ppermute | solution.py:32
  109.1 3.3 %shard_map.141 = bf16[128,768]{1,0:T(8,128)(2,1)} custom-call(s32[3]{0:T(128)S(1)} %pad_add_fusion.1.ids, s32[16]{0:T(128)S(1)} %copy-done.10, bf16[256,768]{1,0:T(8,128)(2,1)S(1)} %bitcast.27, bf16[32,768]{1,0:T(8,128)(2,1)S(1)} %collective-permute-done.18.before, bf16[32,768]{1,0:T(8,128)(2,1)S(1)} %collective-permute-done.19.after, ...), custom_call_target="tpu_custom_call" | custom-call | flops 1000000 | bytes 1048576 | tf_op jit(solution)/shard_map/pallas_call | solution.py:56
  112.5 1.1 collective-permute-done.29.refs_7_
  113.6 1.6 %collective-permute-done.25.refs_3_ = bf16[192,768]{1,0:T(8,128)(2,1)S(1)} collective-permute-done((bf16[192,768]{1,0:T(8,128)(2,1)S(1)}, bf16[192,768]{1,0:T(8,128)(2,1)S(1)}, u32[]{:S(2)}, u32[]{:S(2)}) %collective-permute-start.25) | collective-permute-done | bytes 294944 | tf_op jit(solution)/shard_map/ppermute | solution.py:32
  115.2 1.8 %collective-permute-done.27.refs_5_ = bf16[192,768]{1,0:T(8,128)(2,1)S(1)} collective-permute-done((bf16[192,768]{1,0:T(8,128)(2,1)S(1)}, bf16[192,768]{1,0:T(8,128)(2,1)S(1)}, u32[]{:S(2)}, u32[]{:S(2)}) %collective-permute-start.27) | collective-permute-done | bytes 294944 | tf_op jit(solution)/shard_map/ppermute | solution.py:32
  117.7 1.0 copy-done.13
  118.7 8.0 %shard_map.142 = (f32[48,1536]{1,0:T(8,128)S(1)}, bf16[48,1536]{1,0:T(8,128)(2,1)S(1)}) custom-call(s32[3]{0:T(128)S(1)} %pad_add_fusion.2.scalars, bf16[192,768]{1,0:T(8,128)(2,1)S(1)} %fusion.1.refs_0_, bf16[192,768]{1,0:T(8,128)(2,1)S(1)} %collective-permute-done.23.refs_1_, bf16[192,768]{1,0:T(8,128)(2,1)S(1)} %collective-permute-done.24.refs_2_, ...), custom_call_target="tpu_custom_call" | custom-call | flops 10000000000 | bytes 1048576 | tf_op jit(solution)/shard_map/pallas_call | solution.py:56
  126.7 3.0 %collective-permute-start.30 = (bf16[48,1536]{1,0:T(8,128)(2,1)S(1)}, bf16[48,1536]{1,0:T(8,128)(2,1)S(1)}, u32[]{:S(2)}, u32[]{:S(2)}) collective-permute-start(bf16[48,1536]{1,0:T(8,128)(2,1)S(1)} %get-tuple-element.89), channel_id=1, source_target_pairs={{0,16},{2,18},{4,20},{6,22},{8,24},{10,26},{12,28},{14,30},{16,0},... | collective-permute-start | bytes 442376 | tf_op jit(solution)/shard_map/ppermute | solution.py:32
  129.7 4.7 %collective-permute-done.30 = bf16[48,1536]{1,0:T(8,128)(2,1)S(1)} collective-permute-done((bf16[48,1536]{1,0:T(8,128)(2,1)S(1)}, bf16[48,1536]{1,0:T(8,128)(2,1)S(1)}, u32[]{:S(2)}, u32[]{:S(2)}) %collective-permute-start.30) | collective-permute-done | bytes 147488 | tf_op jit(solution)/shard_map/ppermute | solution.py:32
  (92 shorter events, 13.2 us)
Async XLA Ops:
  0.6 21.8 %copy-start.1 = (bf16[32,8,768]{2,1,0:T(8,128)(2,1)S(1)}, bf16[32,8,768]{2,1,0:T(8,128)(2,1)}, u32[]{:S(2)}) copy-start(bf16[32,8,768]{2,1,0:T(8,128)(2,1)} %param.10) | copy-start | bytes 1179652
  0.6 21.8 %copy-start.10 = (s32[16]{0:T(128)S(1)}, s32[16]{0:T(128)}, u32[]{:S(2)}) copy-start(s32[16]{0:T(128)} %lengths.11) | copy-start | bytes 196
  0.7 21.6 %copy-start.22 = (f32[7,7,768]{2,1,0:T(8,128)S(1)}, f32[7,7,768]{2,1,0:T(8,128)}, u32[]{:S(2)}) copy-start(f32[7,7,768]{2,1,0:T(8,128)} %param.12) | copy-start | bytes 451588
  0.7 21.6 %copy-start.24 = (f32[768]{0:T(1024)S(1)}, f32[768]{0:T(1024)}, u32[]{:S(2)}) copy-start(f32[768]{0:T(1024)} %param.13) | copy-start | bytes 9220
  0.7 21.6 %copy-start.25 = (f32[768]{0:T(1024)S(1)}, f32[768]{0:T(1024)}, u32[]{:S(2)}) copy-start(f32[768]{0:T(1024)} %param.17) | copy-start | bytes 9220
  0.7 21.7 %copy-start.11 = (s32[4,1]{0,1:T(1,128)S(1)}, s32[4,1]{0,1:T(1,128)}, u32[]{:S(2)}) copy-start(s32[4,1]{0,1:T(1,128)} %param.18) | copy-start | bytes 52
  1.8 12.1 %collective-permute-start = (bf16[2,48,384]{2,1,0:T(8,128)(2,1)S(1)}, bf16[2,48,384]{2,1,0:T(8,128)(2,1)S(1)}, u32[]{:S(2)}, u32[]{:S(2)}) collective-permute-start(bf16[2,48,384]{2,1,0:T(8,128)(2,1)S(1)} %get-tuple-element.94), channel_id=1, source_target_pairs={{0,2},{2,0},{4,6},{6,4},{8,10},{10,8},{12,14},{14,12},{16,18},{18,... | collective-permute-start | bytes 221192 | tf_op jit(solution)/shard_map/ppermute | solution.py:32
  4.8 9.1 %collective-permute-start.1 = (bf16[2,48,384]{2,1,0:T(8,128)(2,1)S(1)}, bf16[2,48,384]{2,1,0:T(8,128)(2,1)S(1)}, u32[]{:S(2)}, u32[]{:S(2)}) collective-permute-start(bf16[2,48,384]{2,1,0:T(8,128)(2,1)S(1)} %get-tuple-element.95), channel_id=1, source_target_pairs={{0,4},{2,6},{4,0},{6,2},{8,12},{10,14},{12,8},{14,10},{16,20},{18,... | collective-permute-start | bytes 221192 | tf_op jit(solution)/shard_map/ppermute | solution.py:32
  6.3 7.6 %collective-permute-start.2 = (bf16[2,48,384]{2,1,0:T(8,128)(2,1)S(1)}, bf16[2,48,384]{2,1,0:T(8,128)(2,1)S(1)}, u32[]{:S(2)}, u32[]{:S(2)}) collective-permute-start(bf16[2,48,384]{2,1,0:T(8,128)(2,1)S(1)} %get-tuple-element.92), channel_id=1, source_target_pairs={{0,6},{2,4},{4,2},{6,0},{8,14},{10,12},{12,10},{14,8},{16,22},{18,... | collective-permute-start | bytes 221192 | tf_op jit(solution)/shard_map/ppermute | solution.py:32
  6.3 1.0 copy-start
  8.0 14.5 %copy-start.2 = (bf16[32,8,768]{2,1,0:T(8,128)(2,1)S(1)}, bf16[32,8,768]{2,1,0:T(8,128)(2,1)}, u32[]{:S(2)}) copy-start(bf16[32,8,768]{2,1,0:T(8,128)(2,1)} %param.11) | copy-start | bytes 1179652
  8.7 5.6 %collective-permute-start.3 = (bf16[32,768]{1,0:T(8,128)(2,1)S(1)}, bf16[32,768]{1,0:T(8,128)(2,1)S(1)}, u32[]{:S(2)}, u32[]{:S(2)}) collective-permute-start(bf16[32,768]{1,0:T(8,128)(2,1)S(1)} %get-tuple-element.47), channel_id=1, source_target_pairs={{0,2},{2,4},{4,6},{6,8},{8,10},{10,12},{12,14},{14,16},{16,18},{18... | collective-permute-start | bytes 147464 | tf_op jit(solution)/shard_map/ppermute | solution.py:39
  12.5 6.0 %collective-permute-start.4 = (bf16[32,768]{1,0:T(8,128)(2,1)S(1)}, bf16[32,768]{1,0:T(8,128)(2,1)S(1)}, u32[]{:S(2)}, u32[]{:S(2)}) collective-permute-start(bf16[32,768]{1,0:T(8,128)(2,1)S(1)} %get-tuple-element.48), channel_id=1, source_target_pairs={{2,0},{4,2},{6,4},{8,6},{10,8},{12,10},{14,12},{16,14},{18,16},{20... | collective-permute-start | bytes 147464 | tf_op jit(solution)/shard_map/ppermute | solution.py:39
  18.5 14.8 %collective-permute-start.5 = (bf16[1,2,192,384]{3,2,1,0:T(8,128)(2,1)S(1)}, bf16[1,2,192,384]{3,2,1,0:T(8,128)(2,1)S(1)}, u32[]{:S(2)}, u32[]{:S(2)}) collective-permute-start(bf16[1,2,192,384]{3,2,1,0:T(8,128)(2,1)S(1)} %bitcast.28), channel_id=1, source_target_pairs={{0,16},{2,18},{4,20},{6,22},{8,24},{10,26},{12,28},{14,30},{16,0},... | collective-permute-start | bytes 884744 | tf_op jit(solution)/shard_map/ppermute | solution.py:32
  25.4 18.4 %copy-start.7 = (f32[128,128]{1,0:T(8,128)}, f32[128,128]{1,0:T(8,128)S(1)}, u32[]{:S(2)}) copy-start(f32[128,128]{1,0:T(8,128)S(1)} %get-tuple-element.64.inverse) | copy-start | bytes 196612
  25.4 12.1 %collective-permute-start.7 = (bf16[2,128,768]{2,1,0:T(8,128)(2,1)S(1)}, bf16[2,128,768]{2,1,0:T(8,128)(2,1)S(1)}, u32[]{:S(2)}, u32[]{:S(2)}) collective-permute-start(bf16[2,128,768]{2,1,0:T(8,128)(2,1)S(1)} %get-tuple-element.54.refs_0_), channel_id=1, source_target_pairs={{0,2},{2,0},{4,6},{6,4},{8,10},{10,8},{12,14},{14,12},{16,18},{18,... | collective-permute-start | bytes 1179656 | tf_op jit(solution)/shard_map/ppermute | solution.py:32
  26.7 17.1 %collective-permute-start.8 = (bf16[2,128,768]{2,1,0:T(8,128)(2,1)S(1)}, bf16[2,128,768]{2,1,0:T(8,128)(2,1)S(1)}, u32[]{:S(2)}, u32[]{:S(2)}) collective-permute-start(bf16[2,128,768]{2,1,0:T(8,128)(2,1)S(1)} %get-tuple-element.54.refs_0_), channel_id=1, source_target_pairs={{0,4},{2,6},{4,0},{6,2},{8,12},{10,14},{12,8},{14,10},{16,20},{18,... | collective-permute-start | bytes 1179656 | tf_op jit(solution)/shard_map/ppermute | solution.py:32
  29.6 14.2 %collective-permute-start.9 = (bf16[2,128,768]{2,1,0:T(8,128)(2,1)S(1)}, bf16[2,128,768]{2,1,0:T(8,128)(2,1)S(1)}, u32[]{:S(2)}, u32[]{:S(2)}) collective-permute-start(bf16[2,128,768]{2,1,0:T(8,128)(2,1)S(1)} %get-tuple-element.54.refs_0_), channel_id=1, source_target_pairs={{0,6},{2,4},{4,2},{6,0},{8,14},{10,12},{12,10},{14,8},{16,22},{18,... | collective-permute-start | bytes 1179656 | tf_op jit(solution)/shard_map/ppermute | solution.py:32
  33.4 10.6 %copy-start.23 = (f32[1536]{0:T(1024)S(1)}, f32[1536]{0:T(1024)}, u32[]{:S(2)}) copy-start(f32[1536]{0:T(1024)} %param.15) | copy-start | bytes 18436
  33.4 14.3 %collective-permute-start.6 = (bf16[2,2,192,384]{3,2,1,0:T(8,128)(2,1)S(1)}, bf16[2,2,192,384]{3,2,1,0:T(8,128)(2,1)}, u32[]{:S(2)}, u32[]{:S(2)}) collective-permute-start(bf16[2,2,192,384]{3,2,1,0:T(8,128)(2,1)S(1)} %shard_map.131.early), channel_id=1, source_target_pairs={{0,8},{2,10},{4,12},{6,14},{8,0},{10,2},{12,4},{14,6},{16,24},{18,... | collective-permute-start | bytes 1769480 | tf_op jit(solution)/shard_map/ppermute | solution.py:32
  43.9 4.9 %collective-permute-start.10 = (bf16[2,512,768]{2,1,0:T(8,128)(2,1)S(1)}, bf16[2,512,768]{2,1,0:T(8,128)(2,1)}, u32[]{:S(2)}, u32[]{:S(2)}) collective-permute-start(bf16[2,512,768]{2,1,0:T(8,128)(2,1)S(1)} %shard_map.134.refs_0_), channel_id=1, source_target_pairs={{0,1},{1,0},{2,3},{3,2},{4,5},{5,4},{6,7},{7,6},{8,9},{9,8},{10,11... | collective-permute-start | bytes 4718600 | tf_op jit(solution)/shard_map/ppermute | solution.py:32
  56.3 3.5 %collective-permute-start.12 = (bf16[2,512,768]{2,1,0:T(8,128)(2,1)S(1)}, bf16[2,512,768]{2,1,0:T(8,128)(2,1)S(1)}, u32[]{:S(2)}, u32[]{:S(2)}) collective-permute-start(bf16[2,512,768]{2,1,0:T(8,128)(2,1)S(1)} %get-tuple-element.60), channel_id=1, source_target_pairs={{0,1},{1,0},{2,3},{3,2},{4,5},{5,4},{6,7},{7,6},{8,9},{9,8},{10,11... | collective-permute-start | bytes 4718600 | tf_op jit(solution)/shard_map/ppermute | solution.py:32
  56.4 16.1 %collective-permute-start.11 = (bf16[2,192,768]{2,1,0:T(8,128)(2,1)}, bf16[2,192,768]{2,1,0:T(8,128)(2,1)}, u32[]{:S(2)}, u32[]{:S(2)}) collective-permute-start(bf16[2,192,768]{2,1,0:T(8,128)(2,1)} %get-tuple-element.56), channel_id=1, source_target_pairs={{0,8},{2,10},{4,12},{6,14},{8,0},{10,2},{12,4},{14,6},{16,24},{18,... | collective-permute-start | bytes 1769480 | tf_op jit(solution)/shard_map/ppermute | solution.py:32
  65.5 8.0 %collective-permute-start.13 = (bf16[128,768]{1,0:T(8,128)(2,1)}, bf16[128,768]{1,0:T(8,128)(2,1)S(1)}, u32[]{:S(2)}, u32[]{:S(2)}) collective-permute-start(bf16[128,768]{1,0:T(8,128)(2,1)} %get-tuple-element.61), channel_id=1, source_target_pairs={{0,2},{2,0},{4,6},{6,4},{8,10},{10,8},{12,14},{14,12},{16,18},{18,... | collective-permute-start | bytes 589832 | tf_op jit(solution)/shard_map/ppermute | solution.py:32
  66.8 11.1 %collective-permute-start.15 = (bf16[128,768]{1,0:T(8,128)(2,1)}, bf16[128,768]{1,0:T(8,128)(2,1)S(1)}, u32[]{:S(2)}, u32[]{:S(2)}) collective-permute-start(bf16[128,768]{1,0:T(8,128)(2,1)} %copy-done.21), channel_id=1, source_target_pairs={{0,4},{2,6},{4,0},{6,2},{8,12},{10,14},{12,8},{14,10},{16,20},{18,... | collective-permute-start | bytes 589832 | tf_op jit(solution)/shard_map/ppermute | solution.py:32
  68.1 9.8 %collective-permute-start.16 = (bf16[128,768]{1,0:T(8,128)(2,1)}, bf16[128,768]{1,0:T(8,128)(2,1)S(1)}, u32[]{:S(2)}, u32[]{:S(2)}) collective-permute-start(bf16[128,768]{1,0:T(8,128)(2,1)} %copy-done.20), channel_id=1, source_target_pairs={{0,6},{2,4},{4,2},{6,0},{8,14},{10,12},{12,10},{14,8},{16,22},{18,... | collective-permute-start | bytes 589832 | tf_op jit(solution)/shard_map/ppermute | solution.py:32
  73.4 4.5 %copy-start.6 = (bf16[128,768]{1,0:T(8,128)(2,1)S(1)}, bf16[128,768]{1,0:T(8,128)(2,1)}, u32[]{:S(2)}) copy-start(bf16[128,768]{1,0:T(8,128)(2,1)} %copy-done.5) | copy-start | bytes 589828
  73.4 4.5 %copy-start.8 = (f32[128,128]{1,0:T(8,128)S(1)}, f32[128,128]{1,0:T(8,128)}, u32[]{:S(2)}) copy-start(f32[128,128]{1,0:T(8,128)} %copy-done.7) | copy-start | bytes 196612
  74.7 4.2 %copy-start.19 = (bf16[128,768]{1,0:T(8,128)(2,1)S(1)}, bf16[128,768]{1,0:T(8,128)(2,1)}, u32[]{:S(2)}) copy-start(bf16[128,768]{1,0:T(8,128)(2,1)} %copy-done.18) | copy-start | bytes 589828
  74.7 5.8 %copy-start.17 = (bf16[128,768]{1,0:T(8,128)(2,1)S(1)}, bf16[128,768]{1,0:T(8,128)(2,1)}, u32[]{:S(2)}) copy-start(bf16[128,768]{1,0:T(8,128)(2,1)} %copy-done.16) | copy-start | bytes 589828
  74.7 6.0 %copy-start.15 = (bf16[128,768]{1,0:T(8,128)(2,1)S(1)}, bf16[128,768]{1,0:T(8,128)(2,1)}, u32[]{:S(2)}) copy-start(bf16[128,768]{1,0:T(8,128)(2,1)} %copy-done.14) | copy-start | bytes 589828
  74.7 17.0 %copy-start.4 = (bf16[128,768]{1,0:T(8,128)(2,1)S(1)}, bf16[128,768]{1,0:T(8,128)(2,1)}, u32[]{:S(2)}) copy-start(bf16[128,768]{1,0:T(8,128)(2,1)} %copy-done.3) | copy-start | bytes 589828
  74.8 18.4 %collective-permute-start.14 = (bf16[1,192,768]{2,1,0:T(8,128)(2,1)S(1)}, bf16[1,192,768]{2,1,0:T(8,128)(2,1)S(1)}, u32[]{:S(2)}, u32[]{:S(2)}) collective-permute-start(bf16[1,192,768]{2,1,0:T(8,128)(2,1)S(1)} %dynamic-slice_convert_fusion), channel_id=1, source_target_pairs={{0,16},{2,18},{4,20},{6,22},{8,24},{10,26},{12,28},{14,30},{16,0},... | collective-permute-start | bytes 884744 | tf_op jit(solution)/shard_map/ppermute | solution.py:32
  78.8 3.7 %collective-permute-start.17 = (bf16[128,768]{1,0:T(8,128)(2,1)S(1)}, bf16[128,768]{1,0:T(8,128)(2,1)S(1)}, u32[]{:S(2)}, u32[]{:S(2)}) collective-permute-start(bf16[128,768]{1,0:T(8,128)(2,1)S(1)} %shard_map.138.refs_0_.rest_0_), channel_id=1, source_target_pairs={{0,1},{1,0},{2,3},{3,2},{4,5},{5,4},{6,7},{7,6},{8,9},{9,8},{10,11... | collective-permute-start | bytes 589832 | tf_op jit(solution)/shard_map/ppermute | solution.py:32
  78.9 7.8 %collective-permute-start.20 = (bf16[128,768]{1,0:T(8,128)(2,1)S(1)}, bf16[128,768]{1,0:T(8,128)(2,1)S(1)}, u32[]{:S(2)}, u32[]{:S(2)}) collective-permute-start(bf16[128,768]{1,0:T(8,128)(2,1)S(1)} %copy-done.19), channel_id=1, source_target_pairs={{0,2},{2,0},{4,6},{6,4},{8,10},{10,8},{12,14},{14,12},{16,18},{18,... | collective-permute-start | bytes 589832 | tf_op jit(solution)/shard_map/ppermute | solution.py:32
  80.5 11.2 %collective-permute-start.21 = (bf16[128,768]{1,0:T(8,128)(2,1)S(1)}, bf16[128,768]{1,0:T(8,128)(2,1)S(1)}, u32[]{:S(2)}, u32[]{:S(2)}) collective-permute-start(bf16[128,768]{1,0:T(8,128)(2,1)S(1)} %copy-done.17), channel_id=1, source_target_pairs={{0,4},{2,6},{4,0},{6,2},{8,12},{10,14},{12,8},{14,10},{16,20},{18,... | collective-permute-start | bytes 589832 | tf_op jit(solution)/shard_map/ppermute | solution.py:32
  80.7 11.0 %collective-permute-start.22 = (bf16[128,768]{1,0:T(8,128)(2,1)S(1)}, bf16[128,768]{1,0:T(8,128)(2,1)S(1)}, u32[]{:S(2)}, u32[]{:S(2)}) collective-permute-start(bf16[128,768]{1,0:T(8,128)(2,1)S(1)} %copy-done.15), channel_id=1, source_target_pairs={{0,6},{2,4},{4,2},{6,0},{8,14},{10,12},{12,10},{14,8},{16,22},{18,... | collective-permute-start | bytes 589832 | tf_op jit(solution)/shard_map/ppermute | solution.py:32
  83.0 10.1 %collective-permute-start.18 = (bf16[32,768]{1,0:T(8,128)(2,1)S(1)}, bf16[32,768]{1,0:T(8,128)(2,1)S(1)}, u32[]{:S(2)}, u32[]{:S(2)}) collective-permute-start(bf16[32,768]{1,0:T(8,128)(2,1)S(1)} %get-tuple-element.69), channel_id=1, source_target_pairs={{0,2},{2,4},{4,6},{6,8},{8,10},{10,12},{12,14},{14,16},{16,18},{18... | collective-permute-start | bytes 147464 | tf_op jit(solution)/shard_map/ppermute | solution.py:39
  86.6 6.5 %collective-permute-start.19 = (bf16[32,768]{1,0:T(8,128)(2,1)S(1)}, bf16[32,768]{1,0:T(8,128)(2,1)S(1)}, u32[]{:S(2)}, u32[]{:S(2)}) collective-permute-start(bf16[32,768]{1,0:T(8,128)(2,1)S(1)} %get-tuple-element.70), channel_id=1, source_target_pairs={{2,0},{4,2},{6,4},{8,6},{10,8},{12,10},{14,12},{16,14},{18,16},{20... | collective-permute-start | bytes 147464 | tf_op jit(solution)/shard_map/ppermute | solution.py:39
  93.2 8.2 %collective-permute-start.24 = (bf16[192,768]{1,0:T(8,128)(2,1)S(1)}, bf16[192,768]{1,0:T(8,128)(2,1)S(1)}, u32[]{:S(2)}, u32[]{:S(2)}) collective-permute-start(bf16[192,768]{1,0:T(8,128)(2,1)S(1)} %fusion.1.refs_0_), channel_id=1, source_target_pairs={{0,4},{2,6},{4,0},{6,2},{8,12},{10,14},{12,8},{14,10},{16,20},{18,... | collective-permute-start | bytes 884744 | tf_op jit(solution)/shard_map/ppermute | solution.py:32
  94.1 11.6 %collective-permute-start.23 = (bf16[192,768]{1,0:T(8,128)(2,1)S(1)}, bf16[192,768]{1,0:T(8,128)(2,1)S(1)}, u32[]{:S(2)}, u32[]{:S(2)}) collective-permute-start(bf16[192,768]{1,0:T(8,128)(2,1)S(1)} %fusion.1.refs_0_), channel_id=1, source_target_pairs={{0,2},{2,0},{4,6},{6,4},{8,10},{10,8},{12,14},{14,12},{16,18},{18,... | collective-permute-start | bytes 884744 | tf_op jit(solution)/shard_map/ppermute | solution.py:32
  97.5 10.9 %collective-permute-start.26 = (bf16[192,768]{1,0:T(8,128)(2,1)S(1)}, bf16[192,768]{1,0:T(8,128)(2,1)S(1)}, u32[]{:S(2)}, u32[]{:S(2)}) collective-permute-start(bf16[192,768]{1,0:T(8,128)(2,1)S(1)} %fusion.1.refs_0_), channel_id=1, source_target_pairs={{0,8},{2,10},{4,12},{6,14},{8,0},{10,2},{12,4},{14,6},{16,24},{18,... | collective-permute-start | bytes 884744 | tf_op jit(solution)/shard_map/ppermute | solution.py:32
  99.6 14.0 %collective-permute-start.29 = (bf16[192,768]{1,0:T(8,128)(2,1)S(1)}, bf16[192,768]{1,0:T(8,128)(2,1)S(1)}, u32[]{:S(2)}, u32[]{:S(2)}) collective-permute-start(bf16[192,768]{1,0:T(8,128)(2,1)S(1)} %fusion.1.refs_0_), channel_id=1, source_target_pairs={{0,14},{2,12},{4,10},{6,8},{8,6},{10,4},{12,2},{14,0},{16,30},{18,... | collective-permute-start | bytes 884744 | tf_op jit(solution)/shard_map/ppermute | solution.py:32
  101.4 13.8 %collective-permute-start.25 = (bf16[192,768]{1,0:T(8,128)(2,1)S(1)}, bf16[192,768]{1,0:T(8,128)(2,1)S(1)}, u32[]{:S(2)}, u32[]{:S(2)}) collective-permute-start(bf16[192,768]{1,0:T(8,128)(2,1)S(1)} %collective-permute-done.24.refs_2_), channel_id=1, source_target_pairs={{0,2},{2,0},{4,6},{6,4},{8,10},{10,8},{12,14},{14,12},{16,18},{18,... | collective-permute-start | bytes 884744 | tf_op jit(solution)/shard_map/ppermute | solution.py:32
  105.7 11.3 %collective-permute-start.27 = (bf16[192,768]{1,0:T(8,128)(2,1)S(1)}, bf16[192,768]{1,0:T(8,128)(2,1)S(1)}, u32[]{:S(2)}, u32[]{:S(2)}) collective-permute-start(bf16[192,768]{1,0:T(8,128)(2,1)S(1)} %collective-permute-done.23.refs_1_), channel_id=1, source_target_pairs={{0,8},{2,10},{4,12},{6,14},{8,0},{10,2},{12,4},{14,6},{16,24},{18,... | collective-permute-start | bytes 884744 | tf_op jit(solution)/shard_map/ppermute | solution.py:32
  108.4 9.3 %collective-permute-start.28 = (bf16[192,768]{1,0:T(8,128)(2,1)S(1)}, bf16[192,768]{1,0:T(8,128)(2,1)}, u32[]{:S(2)}, u32[]{:S(2)}) collective-permute-start(bf16[192,768]{1,0:T(8,128)(2,1)S(1)} %collective-permute-done.26.refs_4_), channel_id=1, source_target_pairs={{0,4},{2,6},{4,0},{6,2},{8,12},{10,14},{12,8},{14,10},{16,20},{18,... | collective-permute-start | bytes 884744 | tf_op jit(solution)/shard_map/ppermute | solution.py:32
  117.7 1.0 copy-start.13
  126.7 7.7 %collective-permute-start.30 = (bf16[48,1536]{1,0:T(8,128)(2,1)S(1)}, bf16[48,1536]{1,0:T(8,128)(2,1)S(1)}, u32[]{:S(2)}, u32[]{:S(2)}) collective-permute-start(bf16[48,1536]{1,0:T(8,128)(2,1)S(1)} %get-tuple-element.89), channel_id=1, source_target_pairs={{0,16},{2,18},{4,20},{6,22},{8,24},{10,26},{12,28},{14,30},{16,0},... | collective-permute-start | bytes 442376 | tf_op jit(solution)/shard_map/ppermute | solution.py:32
  (9 other events, 6.1 us)

commit v10 on v9

--- a/solution.py
+++ b/solution.py
@@ -570,19 +570,11 @@
         ids, lengths, flags, centred, inverse, gain, *for_norm,
         scalars=3,
     )
-    (block_out,) = call(
-        output_kernel,
-        [flat],
-        [],
-        10**6,
-        ids, lengths, flags, strip, scale, *for_output,
-        scalars=3,
-    )
     halves = [grad_mixed] + [swap(grad_mixed, "own", s) for s in range(1, owners)]
     head, tail = call(rims_kernel, rims, [], 10**6, ids, lengths, *halves, scalars=2)
     before, after = neighbours(head, tail)
-    arrived, before, after, block_out = lax.optimization_barrier(
-        (arrived, before, after, block_out)
+    arrived, before, after, for_output = lax.optimization_barrier(
+        (arrived, before, after, for_output)
     )
     grad_t = (reduced + arrived.astype(F32)).astype(BF16)[0]
     group = PLANE * half_lines
@@ -605,7 +597,17 @@
 
     other = tile ^ (PLANE * half_lines)
     square = pltpu.VMEM((channels, channels), F32)
-    gathered, grad_features = lax.optimization_barrier((gathered, grad_features))
+    (block_out,) = call(
+        output_kernel,
+        [flat],
+        [],
+        10**6,
+        ids, lengths, flags, strip, scale, *for_output,
+        scalars=3,
+    )
+    gathered, grad_features, block_out = lax.optimization_barrier(
+        (gathered, grad_features, block_out)
+    )
     if kept % 16:
         slots = [hidden_block((tile & (group - 1)) ^ e, group) for e in range(group)]
         ordered = jnp.zeros((group, kept, channels), BF16)

time: 136 us -> 134 us (0.985)
  local copies, waits for them, and re-layouts: 8.25 us -> 6.57 us
    ppermute x27, waiting for transfers between devices: 40.1 us -> 38.2 us  [swap(): lax.ppermute(value, axis, [(i, i ^ bit) for i in range(lax.axis_size(axis...]
    unnamed x52 -> x48, local copies, waits for them, and re-layouts: 8.17 us -> 6.49 us
where the time goes in v10:
time: 134 us
  starting transfers between devices  51.3 us (38%)
  waiting for transfers between devices  43.7 us (33%)
  Pallas kernels  27.9 us (21%)
  local copies, waits for them, and re-layouts  6.57 us (5%)
  other arithmetic  3.45 us (3%)
    ppermute x27, starting transfers between devices, swap(): lax.ppermute(value, axis, [(i, i ^ bit) for i in range(lax.axis_size(axis...  41.3 us
    ppermute x27, waiting for transfers between devices, swap(): lax.ppermute(value, axis, [(i, i ^ bit) for i in range(lax.axis_size(axis...  38.2 us
    pallas_call x14, Pallas kernels, call(): pl.pallas_call(kernel, out_shape=out_shape, in_specs=[smem] * scalars + [...  27.9 us
    ppermute x4, starting transfers between devices, neighbours(): return (lax.ppermute(last, 'tile', up), lax.ppermute(first, 'tile', down))  10.1 us
    unnamed x48, local copies, waits for them, and re-layouts  6.49 us
    ppermute x4, waiting for transfers between devices, neighbours(): return (lax.ppermute(last, 'tile', up), lax.ppermute(first, 'tile', down))  5.56 us
  transfers between devices with their start and end apart: 31, of which 18 were waited for; matrix products, arithmetic and copies ran while one was open for 1% of the time, Pallas kernels for 9%

profile of v10, /device:TPU:0, one launch (start us, length us, event | category | flops | bytes accessed | tf_op | source)
XLA Modules:
  0.0 134.1 jit_solution(14180447620922538640)
XLA Ops:
  0.7 1.0 fusion.2
  1.8 3.0 %collective-permute-start = (bf16[2,48,384]{2,1,0:T(8,128)(2,1)S(1)}, bf16[2,48,384]{2,1,0:T(8,128)(2,1)S(1)}, u32[]{:S(2)}, u32[]{:S(2)}) collective-permute-start(bf16[2,48,384]{2,1,0:T(8,128)(2,1)S(1)} %get-tuple-element.102), channel_id=1, source_target_pairs={{0,2},{2,0},{4,6},{6,4},{8,10},{10,8},{12,14},{14,12},{16,18},{18,... | collective-permute-start | bytes 221192 | tf_op jit(solution)/shard_map/ppermute | solution.py:32
  4.8 1.5 %collective-permute-start.1 = (bf16[2,48,384]{2,1,0:T(8,128)(2,1)S(1)}, bf16[2,48,384]{2,1,0:T(8,128)(2,1)S(1)}, u32[]{:S(2)}, u32[]{:S(2)}) collective-permute-start(bf16[2,48,384]{2,1,0:T(8,128)(2,1)S(1)} %get-tuple-element.103), channel_id=1, source_target_pairs={{0,4},{2,6},{4,0},{6,2},{8,12},{10,14},{12,8},{14,10},{16,20},{18,... | collective-permute-start | bytes 221192 | tf_op jit(solution)/shard_map/ppermute | solution.py:32
  6.3 1.0 copy-done
  8.7 3.9 %collective-permute-start.3 = (bf16[32,768]{1,0:T(8,128)(2,1)S(1)}, bf16[32,768]{1,0:T(8,128)(2,1)S(1)}, u32[]{:S(2)}, u32[]{:S(2)}) collective-permute-start(bf16[32,768]{1,0:T(8,128)(2,1)S(1)} %get-tuple-element.51), channel_id=1, source_target_pairs={{0,2},{2,4},{4,6},{6,8},{8,10},{10,12},{12,14},{14,16},{16,18},{18... | collective-permute-start | bytes 147464 | tf_op jit(solution)/shard_map/ppermute | solution.py:39
  12.5 1.3 collective-permute-start.4
  14.3 4.3 %collective-permute-done.4.after = bf16[32,768]{1,0:T(8,128)(2,1)S(1)} collective-permute-done((bf16[32,768]{1,0:T(8,128)(2,1)S(1)}, bf16[32,768]{1,0:T(8,128)(2,1)S(1)}, u32[]{:S(2)}, u32[]{:S(2)}) %collective-permute-start.4) | collective-permute-done | bytes 49184 | tf_op jit(solution)/shard_map/ppermute | solution.py:39
  18.5 3.8 %collective-permute-start.5 = (bf16[1,2,192,384]{3,2,1,0:T(8,128)(2,1)S(1)}, bf16[1,2,192,384]{3,2,1,0:T(8,128)(2,1)S(1)}, u32[]{:S(2)}, u32[]{:S(2)}) collective-permute-start(bf16[1,2,192,384]{3,2,1,0:T(8,128)(2,1)S(1)} %bitcast.28), channel_id=1, source_target_pairs={{0,16},{2,18},{4,20},{6,22},{8,24},{10,26},{12,28},{14,30},{16,0},... | collective-permute-start | bytes 884744 | tf_op jit(solution)/shard_map/ppermute | solution.py:32
  22.4 2.9 %shard_map.133 = (bf16[2,128,768]{2,1,0:T(8,128)(2,1)S(1)}, f32[128,768]{1,0:T(8,128)S(1)}, f32[128,128]{1,0:T(8,128)S(1)}) custom-call(s32[3]{0:T(128)S(1)} %pad_add_fusion.1.ids, s32[16]{0:T(128)S(1)} %copy-done.10, s32[4]{0:T(128)S(1)} %bitcast.30, bf16[256,768]{1,0:T(8,128)(2,1)S(1)} %bitcast.24, bf16[256,768]{1,0:T(8,128)(2,1)S(1)} %bitcast.26, ...), custom_call_target="tpu_custom_call" | custom-call | flops 1000000 | bytes 1048576 | tf_op jit(solution)/shard_map/pallas_call | solution.py:56
  25.4 1.3 collective-permute-start.7
  26.7 2.9 %collective-permute-start.8 = (bf16[2,128,768]{2,1,0:T(8,128)(2,1)S(1)}, bf16[2,128,768]{2,1,0:T(8,128)(2,1)S(1)}, u32[]{:S(2)}, u32[]{:S(2)}) collective-permute-start(bf16[2,128,768]{2,1,0:T(8,128)(2,1)S(1)} %get-tuple-element.58.refs_0_), channel_id=1, source_target_pairs={{0,4},{2,6},{4,0},{6,2},{8,12},{10,14},{12,8},{14,10},{16,20},{18,... | collective-permute-start | bytes 1179656 | tf_op jit(solution)/shard_map/ppermute | solution.py:32
  29.6 3.7 %collective-permute-done.5.refs_1_ = bf16[1,2,192,384]{3,2,1,0:T(8,128)(2,1)S(1)} collective-permute-done((bf16[1,2,192,384]{3,2,1,0:T(8,128)(2,1)S(1)}, bf16[1,2,192,384]{3,2,1,0:T(8,128)(2,1)S(1)}, u32[]{:S(2)}, u32[]{:S(2)}) %collective-permute-start.5) | collective-permute-done | bytes 294944 | tf_op jit(solution)/shard_map/ppermute | solution.py:32
  33.4 1.7 %collective-permute-start.6 = (bf16[2,2,192,384]{3,2,1,0:T(8,128)(2,1)S(1)}, bf16[2,2,192,384]{3,2,1,0:T(8,128)(2,1)}, u32[]{:S(2)}, u32[]{:S(2)}) collective-permute-start(bf16[2,2,192,384]{3,2,1,0:T(8,128)(2,1)S(1)} %shard_map.131.early), channel_id=1, source_target_pairs={{0,8},{2,10},{4,12},{6,14},{8,0},{10,2},{12,4},{14,6},{16,24},{18,... | collective-permute-start | bytes 1769480 | tf_op jit(solution)/shard_map/ppermute | solution.py:32
  35.1 2.4 %collective-permute-done.7.refs_1_ = bf16[2,128,768]{2,1,0:T(8,128)(2,1)S(1)} collective-permute-done((bf16[2,128,768]{2,1,0:T(8,128)(2,1)S(1)}, bf16[2,128,768]{2,1,0:T(8,128)(2,1)S(1)}, u32[]{:S(2)}, u32[]{:S(2)}) %collective-permute-start.7) | collective-permute-done | bytes 393248 | tf_op jit(solution)/shard_map/ppermute | solution.py:32
  37.5 6.3 %collective-permute-done.8.refs_2_ = bf16[2,128,768]{2,1,0:T(8,128)(2,1)S(1)} collective-permute-done((bf16[2,128,768]{2,1,0:T(8,128)(2,1)S(1)}, bf16[2,128,768]{2,1,0:T(8,128)(2,1)S(1)}, u32[]{:S(2)}, u32[]{:S(2)}) %collective-permute-start.8) | collective-permute-done | bytes 393248 | tf_op jit(solution)/shard_map/ppermute | solution.py:32
  44.1 3.6 %collective-permute-done.6.late = bf16[2,2,192,384]{3,2,1,0:T(8,128)(2,1)} collective-permute-done((bf16[2,2,192,384]{3,2,1,0:T(8,128)(2,1)S(1)}, bf16[2,2,192,384]{3,2,1,0:T(8,128)(2,1)}, u32[]{:S(2)}, u32[]{:S(2)}) %collective-permute-start.6) | collective-permute-done | bytes 589856 | tf_op jit(solution)/shard_map/ppermute | solution.py:32
  47.7 1.2 shard_map.132
  48.9 5.6 %shard_map.135 = (bf16[2,192,768]{2,1,0:T(8,128)(2,1)S(1)}, bf16[2,192,768]{2,1,0:T(8,128)(2,1)}, bf16[1024,384]{1,0:T(8,128)(2,1)S(1)}, bf16[1024,384]{1,0:T(8,128)(2,1)S(1)}) custom-call(s32[2]{0:T(128)S(1)} %pad_add_fusion.scalars, bf16[768,384]{1,0:T(8,128)(2,1)S(1)} %get-tuple-element.54.up, bf16[768,384]{1,0:T(8,128)(2,1)S(1)} %get-tuple-element.55.down_t, ...), custom_call_target="tpu_custom_call" | custom-call | flops 5000000000 | bytes 1048576 | tf_op jit(solution)/shard_map/pallas_call | solution.py:56
  54.5 1.8 %shard_map.136 = (f32[2,512,768]{2,1,0:T(8,128)S(1)}, bf16[2,512,768]{2,1,0:T(8,128)(2,1)S(1)}) custom-call(bf16[1024,384]{1,0:T(8,128)(2,1)S(1)} %get-tuple-element.61.act, bf16[1024,384]{1,0:T(8,128)(2,1)S(1)} %get-tuple-element.62.grad_hidden, bf16[768,384]{1,0:T(8,128)(2,1)S(1)} %get-tuple-element.54.up, bf16[768,384]{1,0:T(8,128)(2,1)S(1)} %get-tuple-element.55.down_t), custom_call_target="tpu_custom_call" | custom-call | flops 1000000000 | bytes 1048576 | tf_op jit(solution)/shard_map/pallas_call | solution.py:56
  56.4 1.4 %collective-permute-start.11 = (bf16[2,192,768]{2,1,0:T(8,128)(2,1)}, bf16[2,192,768]{2,1,0:T(8,128)(2,1)}, u32[]{:S(2)}, u32[]{:S(2)}) collective-permute-start(bf16[2,192,768]{2,1,0:T(8,128)(2,1)} %get-tuple-element.60), channel_id=1, source_target_pairs={{0,8},{2,10},{4,12},{6,14},{8,0},{10,2},{12,4},{14,6},{16,24},{18,... | collective-permute-start | bytes 1769480 | tf_op jit(solution)/shard_map/ppermute | solution.py:32
  57.8 2.0 %collective-permute-done.12.refs_0_ = bf16[2,512,768]{2,1,0:T(8,128)(2,1)S(1)} collective-permute-done((bf16[2,512,768]{2,1,0:T(8,128)(2,1)S(1)}, bf16[2,512,768]{2,1,0:T(8,128)(2,1)S(1)}, u32[]{:S(2)}, u32[]{:S(2)}) %collective-permute-start.12) | collective-permute-done | bytes 1572896 | tf_op jit(solution)/shard_map/ppermute | solution.py:32
  59.8 0.9 shard_map.137
  65.4 1.3 collective-permute-start.13
  66.8 1.3 collective-permute-start.15
  68.9 3.5 %collective-permute-done.11 = bf16[2,192,768]{2,1,0:T(8,128)(2,1)} collective-permute-done((bf16[2,192,768]{2,1,0:T(8,128)(2,1)}, bf16[2,192,768]{2,1,0:T(8,128)(2,1)}, u32[]{:S(2)}, u32[]{:S(2)}) %collective-permute-start.11) | collective-permute-done | bytes 589856 | tf_op jit(solution)/shard_map/ppermute | solution.py:32
  72.4 0.9 collective-permute-done.13.refs_1_
  73.4 1.3 convert_add_fusion
  74.7 3.0 %collective-permute-start.14 = (bf16[1,192,768]{2,1,0:T(8,128)(2,1)S(1)}, bf16[1,192,768]{2,1,0:T(8,128)(2,1)S(1)}, u32[]{:S(2)}, u32[]{:S(2)}) collective-permute-start(bf16[1,192,768]{2,1,0:T(8,128)(2,1)S(1)} %dynamic-slice_convert_fusion), channel_id=1, source_target_pairs={{0,16},{2,18},{4,20},{6,22},{8,24},{10,26},{12,28},{14,30},{16,0},... | collective-permute-start | bytes 884744 | tf_op jit(solution)/shard_map/ppermute | solution.py:32
  78.9 1.6 %collective-permute-start.20 = (bf16[128,768]{1,0:T(8,128)(2,1)S(1)}, bf16[128,768]{1,0:T(8,128)(2,1)S(1)}, u32[]{:S(2)}, u32[]{:S(2)}) collective-permute-start(bf16[128,768]{1,0:T(8,128)(2,1)S(1)} %copy-done.17), channel_id=1, source_target_pairs={{0,2},{2,0},{4,6},{6,4},{8,10},{10,8},{12,14},{14,12},{16,18},{18,... | collective-permute-start | bytes 589832 | tf_op jit(solution)/shard_map/ppermute | solution.py:32
  80.7 1.8 %collective-permute-start.22 = (bf16[128,768]{1,0:T(8,128)(2,1)S(1)}, bf16[128,768]{1,0:T(8,128)(2,1)S(1)}, u32[]{:S(2)}, u32[]{:S(2)}) collective-permute-start(bf16[128,768]{1,0:T(8,128)(2,1)S(1)} %copy-done.13), channel_id=1, source_target_pairs={{0,6},{2,4},{4,2},{6,0},{8,14},{10,12},{12,10},{14,8},{16,22},{18,... | collective-permute-start | bytes 589832 | tf_op jit(solution)/shard_map/ppermute | solution.py:32
  83.0 3.4 %collective-permute-start.18 = (bf16[32,768]{1,0:T(8,128)(2,1)S(1)}, bf16[32,768]{1,0:T(8,128)(2,1)S(1)}, u32[]{:S(2)}, u32[]{:S(2)}) collective-permute-start(bf16[32,768]{1,0:T(8,128)(2,1)S(1)} %get-tuple-element.73), channel_id=1, source_target_pairs={{0,2},{2,4},{4,6},{6,8},{8,10},{10,12},{12,14},{14,16},{16,18},{18... | collective-permute-start | bytes 147464 | tf_op jit(solution)/shard_map/ppermute | solution.py:39
  86.6 1.5 %collective-permute-start.19 = (bf16[32,768]{1,0:T(8,128)(2,1)S(1)}, bf16[32,768]{1,0:T(8,128)(2,1)S(1)}, u32[]{:S(2)}, u32[]{:S(2)}) collective-permute-start(bf16[32,768]{1,0:T(8,128)(2,1)S(1)} %get-tuple-element.74), channel_id=1, source_target_pairs={{2,0},{4,2},{6,4},{8,6},{10,8},{12,10},{14,12},{16,14},{18,16},{20... | collective-permute-start | bytes 147464 | tf_op jit(solution)/shard_map/ppermute | solution.py:39
  88.1 3.5 %collective-permute-done.21.refs_2_ = bf16[128,768]{1,0:T(8,128)(2,1)S(1)} collective-permute-done((bf16[128,768]{1,0:T(8,128)(2,1)S(1)}, bf16[128,768]{1,0:T(8,128)(2,1)S(1)}, u32[]{:S(2)}, u32[]{:S(2)}) %collective-permute-start.21) | collective-permute-done | bytes 196640 | tf_op jit(solution)/shard_map/ppermute | solution.py:32
  91.7 1.0 collective-permute-done.19.after
  92.7 1.4 %collective-permute-start.24 = (bf16[192,768]{1,0:T(8,128)(2,1)S(1)}, bf16[192,768]{1,0:T(8,128)(2,1)S(1)}, u32[]{:S(2)}, u32[]{:S(2)}) collective-permute-start(bf16[192,768]{1,0:T(8,128)(2,1)S(1)} %fusion.1.refs_0_), channel_id=1, source_target_pairs={{0,4},{2,6},{4,0},{6,2},{8,12},{10,14},{12,8},{14,10},{16,20},{18,... | collective-permute-start | bytes 884744 | tf_op jit(solution)/shard_map/ppermute | solution.py:32
  94.1 3.4 %collective-permute-start.23 = (bf16[192,768]{1,0:T(8,128)(2,1)S(1)}, bf16[192,768]{1,0:T(8,128)(2,1)S(1)}, u32[]{:S(2)}, u32[]{:S(2)}) collective-permute-start(bf16[192,768]{1,0:T(8,128)(2,1)S(1)} %fusion.1.refs_0_), channel_id=1, source_target_pairs={{0,2},{2,0},{4,6},{6,4},{8,10},{10,8},{12,14},{14,12},{16,18},{18,... | collective-permute-start | bytes 884744 | tf_op jit(solution)/shard_map/ppermute | solution.py:32
  97.5 2.1 %collective-permute-start.26 = (bf16[192,768]{1,0:T(8,128)(2,1)S(1)}, bf16[192,768]{1,0:T(8,128)(2,1)}, u32[]{:S(2)}, u32[]{:S(2)}) collective-permute-start(bf16[192,768]{1,0:T(8,128)(2,1)S(1)} %fusion.1.refs_0_), channel_id=1, source_target_pairs={{0,8},{2,10},{4,12},{6,14},{8,0},{10,2},{12,4},{14,6},{16,24},{18,... | collective-permute-start | bytes 884744 | tf_op jit(solution)/shard_map/ppermute | solution.py:32
  99.6 1.3 collective-permute-done.24.refs_2_
  100.9 2.0 %collective-permute-start.25 = (bf16[192,768]{1,0:T(8,128)(2,1)S(1)}, bf16[192,768]{1,0:T(8,128)(2,1)}, u32[]{:S(2)}, u32[]{:S(2)}) collective-permute-start(bf16[192,768]{1,0:T(8,128)(2,1)S(1)} %collective-permute-done.24.refs_2_), channel_id=1, source_target_pairs={{0,2},{2,0},{4,6},{6,4},{8,10},{10,8},{12,14},{14,12},{16,18},{18,... | collective-permute-start | bytes 884744 | tf_op jit(solution)/shard_map/ppermute | solution.py:32
  102.9 2.9 %collective-permute-done.23.refs_1_ = bf16[192,768]{1,0:T(8,128)(2,1)S(1)} collective-permute-done((bf16[192,768]{1,0:T(8,128)(2,1)S(1)}, bf16[192,768]{1,0:T(8,128)(2,1)S(1)}, u32[]{:S(2)}, u32[]{:S(2)}) %collective-permute-start.23) | collective-permute-done | bytes 294944 | tf_op jit(solution)/shard_map/ppermute | solution.py:32
  105.8 3.4 %collective-permute-start.27 = (bf16[192,768]{1,0:T(8,128)(2,1)S(1)}, bf16[192,768]{1,0:T(8,128)(2,1)}, u32[]{:S(2)}, u32[]{:S(2)}) collective-permute-start(bf16[192,768]{1,0:T(8,128)(2,1)S(1)} %collective-permute-done.23.refs_1_), channel_id=1, source_target_pairs={{0,8},{2,10},{4,12},{6,14},{8,0},{10,2},{12,4},{14,6},{16,24},{18,... | collective-permute-start | bytes 884744 | tf_op jit(solution)/shard_map/ppermute | solution.py:32
  109.3 1.5 %shard_map.141 = bf16[128,768]{1,0:T(8,128)(2,1)} custom-call(s32[3]{0:T(128)S(1)} %pad_add_fusion.1.ids, s32[16]{0:T(128)S(1)} %copy-done.10, s32[4]{0:T(128)S(1)} %bitcast.32, bf16[256,768]{1,0:T(8,128)(2,1)S(1)} %bitcast.25, f32[1,768]{1,0:T(1,128)S(1)} %broadcast_in_dim.24.layer_scale, bf16[128,768]{1,0:T(8,128)(2,1)S(1)} %copy-done.4, ...), custom_call_target="tpu_custom_call" | custom-call | flops 1000000 | bytes 1048576 | tf_op jit(solution)/shard_map/pallas_call | solution.py:56
  110.8 3.3 %shard_map.140 = bf16[128,768]{1,0:T(8,128)(2,1)} custom-call(s32[3]{0:T(128)S(1)} %pad_add_fusion.1.ids, s32[16]{0:T(128)S(1)} %copy-done.10, bf16[256,768]{1,0:T(8,128)(2,1)S(1)} %bitcast.27, bf16[32,768]{1,0:T(8,128)(2,1)S(1)} %collective-permute-done.18.before, bf16[32,768]{1,0:T(8,128)(2,1)S(1)} %collective-permute-done.19.after, ...), custom_call_target="tpu_custom_call" | custom-call | flops 1000000 | bytes 1048576 | tf_op jit(solution)/shard_map/pallas_call | solution.py:56
  114.2 1.1 collective-permute-done.25.refs_3_
  115.3 1.8 %collective-permute-done.27.refs_5_ = bf16[192,768]{1,0:T(8,128)(2,1)} collective-permute-done((bf16[192,768]{1,0:T(8,128)(2,1)S(1)}, bf16[192,768]{1,0:T(8,128)(2,1)}, u32[]{:S(2)}, u32[]{:S(2)}) %collective-permute-start.27) | collective-permute-done | bytes 294944 | tf_op jit(solution)/shard_map/ppermute | solution.py:32
  117.1 8.4 %shard_map.142 = (f32[48,1536]{1,0:T(8,128)S(1)}, bf16[48,1536]{1,0:T(8,128)(2,1)S(1)}) custom-call(s32[3]{0:T(128)S(1)} %pad_add_fusion.2.scalars, bf16[192,768]{1,0:T(8,128)(2,1)S(1)} %fusion.1.refs_0_, bf16[192,768]{1,0:T(8,128)(2,1)S(1)} %collective-permute-done.23.refs_1_, bf16[192,768]{1,0:T(8,128)(2,1)S(1)} %collective-permute-done.24.refs_2_, ...), custom_call_target="tpu_custom_call" | custom-call | flops 10000000000 | bytes 1048576 | tf_op jit(solution)/shard_map/pallas_call | solution.py:56
  125.5 3.0 %collective-permute-start.30 = (bf16[48,1536]{1,0:T(8,128)(2,1)S(1)}, bf16[48,1536]{1,0:T(8,128)(2,1)S(1)}, u32[]{:S(2)}, u32[]{:S(2)}) collective-permute-start(bf16[48,1536]{1,0:T(8,128)(2,1)S(1)} %get-tuple-element.97), channel_id=1, source_target_pairs={{0,16},{2,18},{4,20},{6,22},{8,24},{10,26},{12,28},{14,30},{16,0},... | collective-permute-start | bytes 442376 | tf_op jit(solution)/shard_map/ppermute | solution.py:32
  128.5 4.7 %collective-permute-done.30 = bf16[48,1536]{1,0:T(8,128)(2,1)S(1)} collective-permute-done((bf16[48,1536]{1,0:T(8,128)(2,1)S(1)}, bf16[48,1536]{1,0:T(8,128)(2,1)S(1)}, u32[]{:S(2)}, u32[]{:S(2)}) %collective-permute-start.30) | collective-permute-done | bytes 147488 | tf_op jit(solution)/shard_map/ppermute | solution.py:32
  (88 shorter events, 11.0 us)
Async XLA Ops:
  0.6 21.8 %copy-start.1 = (bf16[32,8,768]{2,1,0:T(8,128)(2,1)S(1)}, bf16[32,8,768]{2,1,0:T(8,128)(2,1)}, u32[]{:S(2)}) copy-start(bf16[32,8,768]{2,1,0:T(8,128)(2,1)} %param.10) | copy-start | bytes 1179652
  0.6 21.8 %copy-start.10 = (s32[16]{0:T(128)S(1)}, s32[16]{0:T(128)}, u32[]{:S(2)}) copy-start(s32[16]{0:T(128)} %lengths.11) | copy-start | bytes 196
  0.7 21.6 %copy-start.20 = (f32[7,7,768]{2,1,0:T(8,128)S(1)}, f32[7,7,768]{2,1,0:T(8,128)}, u32[]{:S(2)}) copy-start(f32[7,7,768]{2,1,0:T(8,128)} %param.12) | copy-start | bytes 451588
  0.7 21.6 %copy-start.22 = (f32[768]{0:T(1024)S(1)}, f32[768]{0:T(1024)}, u32[]{:S(2)}) copy-start(f32[768]{0:T(1024)} %param.13) | copy-start | bytes 9220
  0.7 21.6 %copy-start.23 = (f32[768]{0:T(1024)S(1)}, f32[768]{0:T(1024)}, u32[]{:S(2)}) copy-start(f32[768]{0:T(1024)} %param.17) | copy-start | bytes 9220
  0.7 21.7 %copy-start.11 = (s32[4,1]{0,1:T(1,128)S(1)}, s32[4,1]{0,1:T(1,128)}, u32[]{:S(2)}) copy-start(s32[4,1]{0,1:T(1,128)} %param.18) | copy-start | bytes 52
  1.8 12.1 %collective-permute-start = (bf16[2,48,384]{2,1,0:T(8,128)(2,1)S(1)}, bf16[2,48,384]{2,1,0:T(8,128)(2,1)S(1)}, u32[]{:S(2)}, u32[]{:S(2)}) collective-permute-start(bf16[2,48,384]{2,1,0:T(8,128)(2,1)S(1)} %get-tuple-element.102), channel_id=1, source_target_pairs={{0,2},{2,0},{4,6},{6,4},{8,10},{10,8},{12,14},{14,12},{16,18},{18,... | collective-permute-start | bytes 221192 | tf_op jit(solution)/shard_map/ppermute | solution.py:32
  4.8 9.1 %collective-permute-start.1 = (bf16[2,48,384]{2,1,0:T(8,128)(2,1)S(1)}, bf16[2,48,384]{2,1,0:T(8,128)(2,1)S(1)}, u32[]{:S(2)}, u32[]{:S(2)}) collective-permute-start(bf16[2,48,384]{2,1,0:T(8,128)(2,1)S(1)} %get-tuple-element.103), channel_id=1, source_target_pairs={{0,4},{2,6},{4,0},{6,2},{8,12},{10,14},{12,8},{14,10},{16,20},{18,... | collective-permute-start | bytes 221192 | tf_op jit(solution)/shard_map/ppermute | solution.py:32
  6.3 7.6 %collective-permute-start.2 = (bf16[2,48,384]{2,1,0:T(8,128)(2,1)S(1)}, bf16[2,48,384]{2,1,0:T(8,128)(2,1)S(1)}, u32[]{:S(2)}, u32[]{:S(2)}) collective-permute-start(bf16[2,48,384]{2,1,0:T(8,128)(2,1)S(1)} %get-tuple-element.100), channel_id=1, source_target_pairs={{0,6},{2,4},{4,2},{6,0},{8,14},{10,12},{12,10},{14,8},{16,22},{18,... | collective-permute-start | bytes 221192 | tf_op jit(solution)/shard_map/ppermute | solution.py:32
  6.3 1.0 copy-start
  8.0 14.5 %copy-start.2 = (bf16[32,8,768]{2,1,0:T(8,128)(2,1)S(1)}, bf16[32,8,768]{2,1,0:T(8,128)(2,1)}, u32[]{:S(2)}) copy-start(bf16[32,8,768]{2,1,0:T(8,128)(2,1)} %param.11) | copy-start | bytes 1179652
  8.7 5.6 %collective-permute-start.3 = (bf16[32,768]{1,0:T(8,128)(2,1)S(1)}, bf16[32,768]{1,0:T(8,128)(2,1)S(1)}, u32[]{:S(2)}, u32[]{:S(2)}) collective-permute-start(bf16[32,768]{1,0:T(8,128)(2,1)S(1)} %get-tuple-element.51), channel_id=1, source_target_pairs={{0,2},{2,4},{4,6},{6,8},{8,10},{10,12},{12,14},{14,16},{16,18},{18... | collective-permute-start | bytes 147464 | tf_op jit(solution)/shard_map/ppermute | solution.py:39
  12.5 6.0 %collective-permute-start.4 = (bf16[32,768]{1,0:T(8,128)(2,1)S(1)}, bf16[32,768]{1,0:T(8,128)(2,1)S(1)}, u32[]{:S(2)}, u32[]{:S(2)}) collective-permute-start(bf16[32,768]{1,0:T(8,128)(2,1)S(1)} %get-tuple-element.52), channel_id=1, source_target_pairs={{2,0},{4,2},{6,4},{8,6},{10,8},{12,10},{14,12},{16,14},{18,16},{20... | collective-permute-start | bytes 147464 | tf_op jit(solution)/shard_map/ppermute | solution.py:39
  18.5 14.8 %collective-permute-start.5 = (bf16[1,2,192,384]{3,2,1,0:T(8,128)(2,1)S(1)}, bf16[1,2,192,384]{3,2,1,0:T(8,128)(2,1)S(1)}, u32[]{:S(2)}, u32[]{:S(2)}) collective-permute-start(bf16[1,2,192,384]{3,2,1,0:T(8,128)(2,1)S(1)} %bitcast.28), channel_id=1, source_target_pairs={{0,16},{2,18},{4,20},{6,22},{8,24},{10,26},{12,28},{14,30},{16,0},... | collective-permute-start | bytes 884744 | tf_op jit(solution)/shard_map/ppermute | solution.py:32
  25.4 18.4 %copy-start.7 = (f32[128,128]{1,0:T(8,128)}, f32[128,128]{1,0:T(8,128)S(1)}, u32[]{:S(2)}) copy-start(f32[128,128]{1,0:T(8,128)S(1)} %get-tuple-element.68.inverse) | copy-start | bytes 196612
  25.4 12.1 %collective-permute-start.7 = (bf16[2,128,768]{2,1,0:T(8,128)(2,1)S(1)}, bf16[2,128,768]{2,1,0:T(8,128)(2,1)S(1)}, u32[]{:S(2)}, u32[]{:S(2)}) collective-permute-start(bf16[2,128,768]{2,1,0:T(8,128)(2,1)S(1)} %get-tuple-element.58.refs_0_), channel_id=1, source_target_pairs={{0,2},{2,0},{4,6},{6,4},{8,10},{10,8},{12,14},{14,12},{16,18},{18,... | collective-permute-start | bytes 1179656 | tf_op jit(solution)/shard_map/ppermute | solution.py:32
  26.7 17.1 %collective-permute-start.8 = (bf16[2,128,768]{2,1,0:T(8,128)(2,1)S(1)}, bf16[2,128,768]{2,1,0:T(8,128)(2,1)S(1)}, u32[]{:S(2)}, u32[]{:S(2)}) collective-permute-start(bf16[2,128,768]{2,1,0:T(8,128)(2,1)S(1)} %get-tuple-element.58.refs_0_), channel_id=1, source_target_pairs={{0,4},{2,6},{4,0},{6,2},{8,12},{10,14},{12,8},{14,10},{16,20},{18,... | collective-permute-start | bytes 1179656 | tf_op jit(solution)/shard_map/ppermute | solution.py:32
  29.6 14.2 %collective-permute-start.9 = (bf16[2,128,768]{2,1,0:T(8,128)(2,1)S(1)}, bf16[2,128,768]{2,1,0:T(8,128)(2,1)S(1)}, u32[]{:S(2)}, u32[]{:S(2)}) collective-permute-start(bf16[2,128,768]{2,1,0:T(8,128)(2,1)S(1)} %get-tuple-element.58.refs_0_), channel_id=1, source_target_pairs={{0,6},{2,4},{4,2},{6,0},{8,14},{10,12},{12,10},{14,8},{16,22},{18,... | collective-permute-start | bytes 1179656 | tf_op jit(solution)/shard_map/ppermute | solution.py:32
  33.4 10.6 %copy-start.21 = (f32[1536]{0:T(1024)S(1)}, f32[1536]{0:T(1024)}, u32[]{:S(2)}) copy-start(f32[1536]{0:T(1024)} %param.15) | copy-start | bytes 18436
  33.4 14.3 %collective-permute-start.6 = (bf16[2,2,192,384]{3,2,1,0:T(8,128)(2,1)S(1)}, bf16[2,2,192,384]{3,2,1,0:T(8,128)(2,1)}, u32[]{:S(2)}, u32[]{:S(2)}) collective-permute-start(bf16[2,2,192,384]{3,2,1,0:T(8,128)(2,1)S(1)} %shard_map.131.early), channel_id=1, source_target_pairs={{0,8},{2,10},{4,12},{6,14},{8,0},{10,2},{12,4},{14,6},{16,24},{18,... | collective-permute-start | bytes 1769480 | tf_op jit(solution)/shard_map/ppermute | solution.py:32
  43.9 4.9 %collective-permute-start.10 = (bf16[2,512,768]{2,1,0:T(8,128)(2,1)S(1)}, bf16[2,512,768]{2,1,0:T(8,128)(2,1)}, u32[]{:S(2)}, u32[]{:S(2)}) collective-permute-start(bf16[2,512,768]{2,1,0:T(8,128)(2,1)S(1)} %shard_map.134.refs_0_), channel_id=1, source_target_pairs={{0,1},{1,0},{2,3},{3,2},{4,5},{5,4},{6,7},{7,6},{8,9},{9,8},{10,11... | collective-permute-start | bytes 4718600 | tf_op jit(solution)/shard_map/ppermute | solution.py:32
  56.3 3.5 %collective-permute-start.12 = (bf16[2,512,768]{2,1,0:T(8,128)(2,1)S(1)}, bf16[2,512,768]{2,1,0:T(8,128)(2,1)S(1)}, u32[]{:S(2)}, u32[]{:S(2)}) collective-permute-start(bf16[2,512,768]{2,1,0:T(8,128)(2,1)S(1)} %get-tuple-element.64), channel_id=1, source_target_pairs={{0,1},{1,0},{2,3},{3,2},{4,5},{5,4},{6,7},{7,6},{8,9},{9,8},{10,11... | collective-permute-start | bytes 4718600 | tf_op jit(solution)/shard_map/ppermute | solution.py:32
  56.4 16.1 %collective-permute-start.11 = (bf16[2,192,768]{2,1,0:T(8,128)(2,1)}, bf16[2,192,768]{2,1,0:T(8,128)(2,1)}, u32[]{:S(2)}, u32[]{:S(2)}) collective-permute-start(bf16[2,192,768]{2,1,0:T(8,128)(2,1)} %get-tuple-element.60), channel_id=1, source_target_pairs={{0,8},{2,10},{4,12},{6,14},{8,0},{10,2},{12,4},{14,6},{16,24},{18,... | collective-permute-start | bytes 1769480 | tf_op jit(solution)/shard_map/ppermute | solution.py:32
  64.1 0.7 copy-start.18
  65.4 8.0 %collective-permute-start.13 = (bf16[128,768]{1,0:T(8,128)(2,1)}, bf16[128,768]{1,0:T(8,128)(2,1)S(1)}, u32[]{:S(2)}, u32[]{:S(2)}) collective-permute-start(bf16[128,768]{1,0:T(8,128)(2,1)} %get-tuple-element.65), channel_id=1, source_target_pairs={{0,2},{2,0},{4,6},{6,4},{8,10},{10,8},{12,14},{14,12},{16,18},{18,... | collective-permute-start | bytes 589832 | tf_op jit(solution)/shard_map/ppermute | solution.py:32
  66.8 11.1 %collective-permute-start.15 = (bf16[128,768]{1,0:T(8,128)(2,1)}, bf16[128,768]{1,0:T(8,128)(2,1)S(1)}, u32[]{:S(2)}, u32[]{:S(2)}) collective-permute-start(bf16[128,768]{1,0:T(8,128)(2,1)} %copy-done.19), channel_id=1, source_target_pairs={{0,4},{2,6},{4,0},{6,2},{8,12},{10,14},{12,8},{14,10},{16,20},{18,... | collective-permute-start | bytes 589832 | tf_op jit(solution)/shard_map/ppermute | solution.py:32
  68.1 9.8 %collective-permute-start.16 = (bf16[128,768]{1,0:T(8,128)(2,1)}, bf16[128,768]{1,0:T(8,128)(2,1)S(1)}, u32[]{:S(2)}, u32[]{:S(2)}) collective-permute-start(bf16[128,768]{1,0:T(8,128)(2,1)} %copy-done.18), channel_id=1, source_target_pairs={{0,6},{2,4},{4,2},{6,0},{8,14},{10,12},{12,10},{14,8},{16,22},{18,... | collective-permute-start | bytes 589832 | tf_op jit(solution)/shard_map/ppermute | solution.py:32
  73.4 4.5 %copy-start.6 = (bf16[128,768]{1,0:T(8,128)(2,1)S(1)}, bf16[128,768]{1,0:T(8,128)(2,1)}, u32[]{:S(2)}) copy-start(bf16[128,768]{1,0:T(8,128)(2,1)} %copy-done.5) | copy-start | bytes 589828
  73.4 4.5 %copy-start.8 = (f32[128,128]{1,0:T(8,128)S(1)}, f32[128,128]{1,0:T(8,128)}, u32[]{:S(2)}) copy-start(f32[128,128]{1,0:T(8,128)} %copy-done.7) | copy-start | bytes 196612
  74.7 4.2 %copy-start.17 = (bf16[128,768]{1,0:T(8,128)(2,1)S(1)}, bf16[128,768]{1,0:T(8,128)(2,1)}, u32[]{:S(2)}) copy-start(bf16[128,768]{1,0:T(8,128)(2,1)} %copy-done.16) | copy-start | bytes 589828
  74.7 5.8 %copy-start.15 = (bf16[128,768]{1,0:T(8,128)(2,1)S(1)}, bf16[128,768]{1,0:T(8,128)(2,1)}, u32[]{:S(2)}) copy-start(bf16[128,768]{1,0:T(8,128)(2,1)} %copy-done.14) | copy-start | bytes 589828
  74.7 6.0 %copy-start.13 = (bf16[128,768]{1,0:T(8,128)(2,1)S(1)}, bf16[128,768]{1,0:T(8,128)(2,1)}, u32[]{:S(2)}) copy-start(bf16[128,768]{1,0:T(8,128)(2,1)} %copy-done.12) | copy-start | bytes 589828
  74.7 17.9 %collective-permute-start.14 = (bf16[1,192,768]{2,1,0:T(8,128)(2,1)S(1)}, bf16[1,192,768]{2,1,0:T(8,128)(2,1)S(1)}, u32[]{:S(2)}, u32[]{:S(2)}) collective-permute-start(bf16[1,192,768]{2,1,0:T(8,128)(2,1)S(1)} %dynamic-slice_convert_fusion), channel_id=1, source_target_pairs={{0,16},{2,18},{4,20},{6,22},{8,24},{10,26},{12,28},{14,30},{16,0},... | collective-permute-start | bytes 884744 | tf_op jit(solution)/shard_map/ppermute | solution.py:32
  77.9 31.5 %copy-start.4 = (bf16[128,768]{1,0:T(8,128)(2,1)S(1)}, bf16[128,768]{1,0:T(8,128)(2,1)}, u32[]{:S(2)}) copy-start(bf16[128,768]{1,0:T(8,128)(2,1)} %copy-done.3) | copy-start | bytes 589828
  78.8 3.7 %collective-permute-start.17 = (bf16[128,768]{1,0:T(8,128)(2,1)S(1)}, bf16[128,768]{1,0:T(8,128)(2,1)S(1)}, u32[]{:S(2)}, u32[]{:S(2)}) collective-permute-start(bf16[128,768]{1,0:T(8,128)(2,1)S(1)} %shard_map.138.refs_0_.rest_0_), channel_id=1, source_target_pairs={{0,1},{1,0},{2,3},{3,2},{4,5},{5,4},{6,7},{7,6},{8,9},{9,8},{10,11... | collective-permute-start | bytes 589832 | tf_op jit(solution)/shard_map/ppermute | solution.py:32
  78.9 7.8 %collective-permute-start.20 = (bf16[128,768]{1,0:T(8,128)(2,1)S(1)}, bf16[128,768]{1,0:T(8,128)(2,1)S(1)}, u32[]{:S(2)}, u32[]{:S(2)}) collective-permute-start(bf16[128,768]{1,0:T(8,128)(2,1)S(1)} %copy-done.17), channel_id=1, source_target_pairs={{0,2},{2,0},{4,6},{6,4},{8,10},{10,8},{12,14},{14,12},{16,18},{18,... | collective-permute-start | bytes 589832 | tf_op jit(solution)/shard_map/ppermute | solution.py:32
  80.5 11.2 %collective-permute-start.21 = (bf16[128,768]{1,0:T(8,128)(2,1)S(1)}, bf16[128,768]{1,0:T(8,128)(2,1)S(1)}, u32[]{:S(2)}, u32[]{:S(2)}) collective-permute-start(bf16[128,768]{1,0:T(8,128)(2,1)S(1)} %copy-done.15), channel_id=1, source_target_pairs={{0,4},{2,6},{4,0},{6,2},{8,12},{10,14},{12,8},{14,10},{16,20},{18,... | collective-permute-start | bytes 589832 | tf_op jit(solution)/shard_map/ppermute | solution.py:32
  80.7 11.0 %collective-permute-start.22 = (bf16[128,768]{1,0:T(8,128)(2,1)S(1)}, bf16[128,768]{1,0:T(8,128)(2,1)S(1)}, u32[]{:S(2)}, u32[]{:S(2)}) collective-permute-start(bf16[128,768]{1,0:T(8,128)(2,1)S(1)} %copy-done.13), channel_id=1, source_target_pairs={{0,6},{2,4},{4,2},{6,0},{8,14},{10,12},{12,10},{14,8},{16,22},{18,... | collective-permute-start | bytes 589832 | tf_op jit(solution)/shard_map/ppermute | solution.py:32
  83.0 8.6 %collective-permute-start.18 = (bf16[32,768]{1,0:T(8,128)(2,1)S(1)}, bf16[32,768]{1,0:T(8,128)(2,1)S(1)}, u32[]{:S(2)}, u32[]{:S(2)}) collective-permute-start(bf16[32,768]{1,0:T(8,128)(2,1)S(1)} %get-tuple-element.73), channel_id=1, source_target_pairs={{0,2},{2,4},{4,6},{6,8},{8,10},{10,12},{12,14},{14,16},{16,18},{18... | collective-permute-start | bytes 147464 | tf_op jit(solution)/shard_map/ppermute | solution.py:39
  86.6 6.0 %collective-permute-start.19 = (bf16[32,768]{1,0:T(8,128)(2,1)S(1)}, bf16[32,768]{1,0:T(8,128)(2,1)S(1)}, u32[]{:S(2)}, u32[]{:S(2)}) collective-permute-start(bf16[32,768]{1,0:T(8,128)(2,1)S(1)} %get-tuple-element.74), channel_id=1, source_target_pairs={{2,0},{4,2},{6,4},{8,6},{10,8},{12,10},{14,12},{16,14},{18,16},{20... | collective-permute-start | bytes 147464 | tf_op jit(solution)/shard_map/ppermute | solution.py:39
  92.7 8.2 %collective-permute-start.24 = (bf16[192,768]{1,0:T(8,128)(2,1)S(1)}, bf16[192,768]{1,0:T(8,128)(2,1)S(1)}, u32[]{:S(2)}, u32[]{:S(2)}) collective-permute-start(bf16[192,768]{1,0:T(8,128)(2,1)S(1)} %fusion.1.refs_0_), channel_id=1, source_target_pairs={{0,4},{2,6},{4,0},{6,2},{8,12},{10,14},{12,8},{14,10},{16,20},{18,... | collective-permute-start | bytes 884744 | tf_op jit(solution)/shard_map/ppermute | solution.py:32
  94.1 11.7 %collective-permute-start.23 = (bf16[192,768]{1,0:T(8,128)(2,1)S(1)}, bf16[192,768]{1,0:T(8,128)(2,1)S(1)}, u32[]{:S(2)}, u32[]{:S(2)}) collective-permute-start(bf16[192,768]{1,0:T(8,128)(2,1)S(1)} %fusion.1.refs_0_), channel_id=1, source_target_pairs={{0,2},{2,0},{4,6},{6,4},{8,10},{10,8},{12,14},{14,12},{16,18},{18,... | collective-permute-start | bytes 884744 | tf_op jit(solution)/shard_map/ppermute | solution.py:32
  97.5 11.8 %collective-permute-start.26 = (bf16[192,768]{1,0:T(8,128)(2,1)S(1)}, bf16[192,768]{1,0:T(8,128)(2,1)}, u32[]{:S(2)}, u32[]{:S(2)}) collective-permute-start(bf16[192,768]{1,0:T(8,128)(2,1)S(1)} %fusion.1.refs_0_), channel_id=1, source_target_pairs={{0,8},{2,10},{4,12},{6,14},{8,0},{10,2},{12,4},{14,6},{16,24},{18,... | collective-permute-start | bytes 884744 | tf_op jit(solution)/shard_map/ppermute | solution.py:32
  99.6 14.6 %collective-permute-start.29 = (bf16[192,768]{1,0:T(8,128)(2,1)S(1)}, bf16[192,768]{1,0:T(8,128)(2,1)}, u32[]{:S(2)}, u32[]{:S(2)}) collective-permute-start(bf16[192,768]{1,0:T(8,128)(2,1)S(1)} %fusion.1.refs_0_), channel_id=1, source_target_pairs={{0,14},{2,12},{4,10},{6,8},{8,6},{10,4},{12,2},{14,0},{16,30},{18,... | collective-permute-start | bytes 884744 | tf_op jit(solution)/shard_map/ppermute | solution.py:32
  100.9 14.4 %collective-permute-start.25 = (bf16[192,768]{1,0:T(8,128)(2,1)S(1)}, bf16[192,768]{1,0:T(8,128)(2,1)}, u32[]{:S(2)}, u32[]{:S(2)}) collective-permute-start(bf16[192,768]{1,0:T(8,128)(2,1)S(1)} %collective-permute-done.24.refs_2_), channel_id=1, source_target_pairs={{0,2},{2,0},{4,6},{6,4},{8,10},{10,8},{12,14},{14,12},{16,18},{18,... | collective-permute-start | bytes 884744 | tf_op jit(solution)/shard_map/ppermute | solution.py:32
  105.8 11.3 %collective-permute-start.27 = (bf16[192,768]{1,0:T(8,128)(2,1)S(1)}, bf16[192,768]{1,0:T(8,128)(2,1)}, u32[]{:S(2)}, u32[]{:S(2)}) collective-permute-start(bf16[192,768]{1,0:T(8,128)(2,1)S(1)} %collective-permute-done.23.refs_1_), channel_id=1, source_target_pairs={{0,8},{2,10},{4,12},{6,14},{8,0},{10,2},{12,4},{14,6},{16,24},{18,... | collective-permute-start | bytes 884744 | tf_op jit(solution)/shard_map/ppermute | solution.py:32
  109.3 7.9 %collective-permute-start.28 = (bf16[192,768]{1,0:T(8,128)(2,1)}, bf16[192,768]{1,0:T(8,128)(2,1)}, u32[]{:S(2)}, u32[]{:S(2)}) collective-permute-start(bf16[192,768]{1,0:T(8,128)(2,1)} %collective-permute-done.26.refs_4_), channel_id=1, source_target_pairs={{0,4},{2,6},{4,0},{6,2},{8,12},{10,14},{12,8},{14,10},{16,20},{18,... | collective-permute-start | bytes 884744 | tf_op jit(solution)/shard_map/ppermute | solution.py:32
  125.5 7.7 %collective-permute-start.30 = (bf16[48,1536]{1,0:T(8,128)(2,1)S(1)}, bf16[48,1536]{1,0:T(8,128)(2,1)S(1)}, u32[]{:S(2)}, u32[]{:S(2)}) collective-permute-start(bf16[48,1536]{1,0:T(8,128)(2,1)S(1)} %get-tuple-element.97), channel_id=1, source_target_pairs={{0,16},{2,18},{4,20},{6,22},{8,24},{10,26},{12,28},{14,30},{16,0},... | collective-permute-start | bytes 442376 | tf_op jit(solution)/shard_map/ppermute | solution.py:32
  (7 other events, 4.7 us)

commit v11 on v10

--- a/solution.py
+++ b/solution.py
@@ -573,9 +573,7 @@
     halves = [grad_mixed] + [swap(grad_mixed, "own", s) for s in range(1, owners)]
     head, tail = call(rims_kernel, rims, [], 10**6, ids, lengths, *halves, scalars=2)
     before, after = neighbours(head, tail)
-    arrived, before, after, for_output = lax.optimization_barrier(
-        (arrived, before, after, for_output)
-    )
+    arrived, before, after = lax.optimization_barrier((arrived, before, after))
     grad_t = (reduced + arrived.astype(F32)).astype(BF16)[0]
     group = PLANE * half_lines
     if group == 8:

time: 134 us -> 149 us (1.11)
  waiting for transfers between devices: 43.7 us -> 59.7 us
  starting transfers between devices: 51.3 us -> 49.4 us
    ppermute x27, waiting for transfers between devices: 38.2 us -> 50.6 us  [swap(): lax.ppermute(value, axis, [(i, i ^ bit) for i in range(lax.axis_size(axis...]
    ppermute x4, waiting for transfers between devices: 5.56 us -> 9.11 us  [neighbours(): return (lax.ppermute(last, 'tile', up), lax.ppermute(first, 'tile', down))]
    ppermute x27, starting transfers between devices: 41.3 us -> 39.4 us  [swap(): lax.ppermute(value, axis, [(i, i ^ bit) for i in range(lax.axis_size(axis...]
  transfers between devices with their start and end apart: 31 -> 31, of which waited for: 18 -> 16; matrix products, arithmetic and copies ran while one was open for 1% -> 1% of each run, Pallas kernels for 9% -> 8%
where the time goes in v11:
time: 149 us; the launch traced here: 148 us
  waiting for transfers between devices  59.7 us (40%)
  starting transfers between devices  49.4 us (33%)
  Pallas kernels  27.9 us (19%)
  local copies, waits for them, and re-layouts  6.57 us (4%)
  other arithmetic  3.45 us (2%)
    ppermute x27, waiting for transfers between devices, swap(): lax.ppermute(value, axis, [(i, i ^ bit) for i in range(lax.axis_size(axis...  50.6 us
    ppermute x27, starting transfers between devices, swap(): lax.ppermute(value, axis, [(i, i ^ bit) for i in range(lax.axis_size(axis...  39.4 us
    pallas_call x14, Pallas kernels, call(): pl.pallas_call(kernel, out_shape=out_shape, in_specs=[smem] * scalars + [...  27.9 us
    ppermute x4, starting transfers between devices, neighbours(): return (lax.ppermute(last, 'tile', up), lax.ppermute(first, 'tile', down))  10 us
    ppermute x4, waiting for transfers between devices, neighbours(): return (lax.ppermute(last, 'tile', up), lax.ppermute(first, 'tile', down))  9.11 us
    unnamed x48, local copies, waits for them, and re-layouts  6.49 us
  transfers between devices with their start and end apart: 31, of which 16 were waited for; matrix products, arithmetic and copies ran while one was open for 1% of the time, Pallas kernels for 8%

profile of v11, /device:TPU:0, one launch (start us, length us, event | category | flops | bytes accessed | tf_op | source)
XLA Modules:
  0.0 148.1 jit_solution(7327018715932090641)
XLA Ops:
  0.7 1.0 fusion.2
  1.8 3.0 %collective-permute-start = (bf16[2,48,384]{2,1,0:T(8,128)(2,1)S(1)}, bf16[2,48,384]{2,1,0:T(8,128)(2,1)S(1)}, u32[]{:S(2)}, u32[]{:S(2)}) collective-permute-start(bf16[2,48,384]{2,1,0:T(8,128)(2,1)S(1)} %get-tuple-element.94), channel_id=1, source_target_pairs={{0,2},{2,0},{4,6},{6,4},{8,10},{10,8},{12,14},{14,12},{16,18},{18,... | collective-permute-start | bytes 221192 | tf_op jit(solution)/shard_map/ppermute | solution.py:32
  4.8 1.5 %collective-permute-start.1 = (bf16[2,48,384]{2,1,0:T(8,128)(2,1)S(1)}, bf16[2,48,384]{2,1,0:T(8,128)(2,1)S(1)}, u32[]{:S(2)}, u32[]{:S(2)}) collective-permute-start(bf16[2,48,384]{2,1,0:T(8,128)(2,1)S(1)} %get-tuple-element.95), channel_id=1, source_target_pairs={{0,4},{2,6},{4,0},{6,2},{8,12},{10,14},{12,8},{14,10},{16,20},{18,... | collective-permute-start | bytes 221192 | tf_op jit(solution)/shard_map/ppermute | solution.py:32
  6.3 1.0 copy-done
  8.7 3.9 %collective-permute-start.3 = (bf16[32,768]{1,0:T(8,128)(2,1)S(1)}, bf16[32,768]{1,0:T(8,128)(2,1)S(1)}, u32[]{:S(2)}, u32[]{:S(2)}) collective-permute-start(bf16[32,768]{1,0:T(8,128)(2,1)S(1)} %get-tuple-element.47), channel_id=1, source_target_pairs={{0,2},{2,4},{4,6},{6,8},{8,10},{10,12},{12,14},{14,16},{16,18},{18... | collective-permute-start | bytes 147464 | tf_op jit(solution)/shard_map/ppermute | solution.py:39
  12.5 1.3 collective-permute-start.4
  14.3 4.3 %collective-permute-done.4.after = bf16[32,768]{1,0:T(8,128)(2,1)S(1)} collective-permute-done((bf16[32,768]{1,0:T(8,128)(2,1)S(1)}, bf16[32,768]{1,0:T(8,128)(2,1)S(1)}, u32[]{:S(2)}, u32[]{:S(2)}) %collective-permute-start.4) | collective-permute-done | bytes 49184 | tf_op jit(solution)/shard_map/ppermute | solution.py:39
  18.5 3.8 %collective-permute-start.5 = (bf16[1,2,192,384]{3,2,1,0:T(8,128)(2,1)S(1)}, bf16[1,2,192,384]{3,2,1,0:T(8,128)(2,1)S(1)}, u32[]{:S(2)}, u32[]{:S(2)}) collective-permute-start(bf16[1,2,192,384]{3,2,1,0:T(8,128)(2,1)S(1)} %bitcast.28), channel_id=1, source_target_pairs={{0,16},{2,18},{4,20},{6,22},{8,24},{10,26},{12,28},{14,30},{16,0},... | collective-permute-start | bytes 884744 | tf_op jit(solution)/shard_map/ppermute | solution.py:32
  22.4 2.9 %shard_map.133 = (bf16[2,128,768]{2,1,0:T(8,128)(2,1)S(1)}, f32[128,768]{1,0:T(8,128)S(1)}, f32[128,128]{1,0:T(8,128)S(1)}) custom-call(s32[3]{0:T(128)S(1)} %pad_add_fusion.1.ids, s32[16]{0:T(128)S(1)} %copy-done.10, s32[4]{0:T(128)S(1)} %bitcast.30, bf16[256,768]{1,0:T(8,128)(2,1)S(1)} %bitcast.24, bf16[256,768]{1,0:T(8,128)(2,1)S(1)} %bitcast.26, ...), custom_call_target="tpu_custom_call" | custom-call | flops 1000000 | bytes 1048576 | tf_op jit(solution)/shard_map/pallas_call | solution.py:56
  25.4 1.3 collective-permute-start.7
  26.7 2.9 %collective-permute-start.8 = (bf16[2,128,768]{2,1,0:T(8,128)(2,1)S(1)}, bf16[2,128,768]{2,1,0:T(8,128)(2,1)S(1)}, u32[]{:S(2)}, u32[]{:S(2)}) collective-permute-start(bf16[2,128,768]{2,1,0:T(8,128)(2,1)S(1)} %get-tuple-element.54.refs_0_), channel_id=1, source_target_pairs={{0,4},{2,6},{4,0},{6,2},{8,12},{10,14},{12,8},{14,10},{16,20},{18,... | collective-permute-start | bytes 1179656 | tf_op jit(solution)/shard_map/ppermute | solution.py:32
  29.6 3.7 %collective-permute-done.5.refs_1_ = bf16[1,2,192,384]{3,2,1,0:T(8,128)(2,1)S(1)} collective-permute-done((bf16[1,2,192,384]{3,2,1,0:T(8,128)(2,1)S(1)}, bf16[1,2,192,384]{3,2,1,0:T(8,128)(2,1)S(1)}, u32[]{:S(2)}, u32[]{:S(2)}) %collective-permute-start.5) | collective-permute-done | bytes 294944 | tf_op jit(solution)/shard_map/ppermute | solution.py:32
  33.4 1.7 %collective-permute-start.6 = (bf16[2,2,192,384]{3,2,1,0:T(8,128)(2,1)S(1)}, bf16[2,2,192,384]{3,2,1,0:T(8,128)(2,1)}, u32[]{:S(2)}, u32[]{:S(2)}) collective-permute-start(bf16[2,2,192,384]{3,2,1,0:T(8,128)(2,1)S(1)} %shard_map.131.early), channel_id=1, source_target_pairs={{0,8},{2,10},{4,12},{6,14},{8,0},{10,2},{12,4},{14,6},{16,24},{18,... | collective-permute-start | bytes 1769480 | tf_op jit(solution)/shard_map/ppermute | solution.py:32
  35.1 2.4 %collective-permute-done.7.refs_1_ = bf16[2,128,768]{2,1,0:T(8,128)(2,1)S(1)} collective-permute-done((bf16[2,128,768]{2,1,0:T(8,128)(2,1)S(1)}, bf16[2,128,768]{2,1,0:T(8,128)(2,1)S(1)}, u32[]{:S(2)}, u32[]{:S(2)}) %collective-permute-start.7) | collective-permute-done | bytes 393248 | tf_op jit(solution)/shard_map/ppermute | solution.py:32
  37.5 6.3 %collective-permute-done.8.refs_2_ = bf16[2,128,768]{2,1,0:T(8,128)(2,1)S(1)} collective-permute-done((bf16[2,128,768]{2,1,0:T(8,128)(2,1)S(1)}, bf16[2,128,768]{2,1,0:T(8,128)(2,1)S(1)}, u32[]{:S(2)}, u32[]{:S(2)}) %collective-permute-start.8) | collective-permute-done | bytes 393248 | tf_op jit(solution)/shard_map/ppermute | solution.py:32
  44.1 3.6 %collective-permute-done.6.late = bf16[2,2,192,384]{3,2,1,0:T(8,128)(2,1)} collective-permute-done((bf16[2,2,192,384]{3,2,1,0:T(8,128)(2,1)S(1)}, bf16[2,2,192,384]{3,2,1,0:T(8,128)(2,1)}, u32[]{:S(2)}, u32[]{:S(2)}) %collective-permute-start.6) | collective-permute-done | bytes 589856 | tf_op jit(solution)/shard_map/ppermute | solution.py:32
  47.7 1.2 shard_map.132
  48.9 5.6 %shard_map.135 = (bf16[2,192,768]{2,1,0:T(8,128)(2,1)S(1)}, bf16[2,192,768]{2,1,0:T(8,128)(2,1)}, bf16[1024,384]{1,0:T(8,128)(2,1)S(1)}, bf16[1024,384]{1,0:T(8,128)(2,1)S(1)}) custom-call(s32[2]{0:T(128)S(1)} %pad_add_fusion.scalars, bf16[768,384]{1,0:T(8,128)(2,1)S(1)} %get-tuple-element.50.up, bf16[768,384]{1,0:T(8,128)(2,1)S(1)} %get-tuple-element.51.down_t, ...), custom_call_target="tpu_custom_call" | custom-call | flops 5000000000 | bytes 1048576 | tf_op jit(solution)/shard_map/pallas_call | solution.py:56
  54.5 1.8 %shard_map.136 = (f32[2,512,768]{2,1,0:T(8,128)S(1)}, bf16[2,512,768]{2,1,0:T(8,128)(2,1)S(1)}) custom-call(bf16[1024,384]{1,0:T(8,128)(2,1)S(1)} %get-tuple-element.57.act, bf16[1024,384]{1,0:T(8,128)(2,1)S(1)} %get-tuple-element.58.grad_hidden, bf16[768,384]{1,0:T(8,128)(2,1)S(1)} %get-tuple-element.50.up, bf16[768,384]{1,0:T(8,128)(2,1)S(1)} %get-tuple-element.51.down_t), custom_call_target="tpu_custom_call" | custom-call | flops 1000000000 | bytes 1048576 | tf_op jit(solution)/shard_map/pallas_call | solution.py:56
  56.4 1.4 collective-permute-start.11
  57.8 2.0 %collective-permute-done.12.refs_0_ = bf16[2,512,768]{2,1,0:T(8,128)(2,1)S(1)} collective-permute-done((bf16[2,512,768]{2,1,0:T(8,128)(2,1)S(1)}, bf16[2,512,768]{2,1,0:T(8,128)(2,1)S(1)}, u32[]{:S(2)}, u32[]{:S(2)}) %collective-permute-start.12) | collective-permute-done | bytes 1572896 | tf_op jit(solution)/shard_map/ppermute | solution.py:32
  59.8 0.9 shard_map.137
  65.4 1.3 collective-permute-start.13
  66.8 1.3 collective-permute-start.15
  68.1 0.8 collective-permute-start.16
  68.9 3.5 %collective-permute-done.11 = bf16[2,192,768]{2,1,0:T(8,128)(2,1)} collective-permute-done((bf16[2,192,768]{2,1,0:T(8,128)(2,1)}, bf16[2,192,768]{2,1,0:T(8,128)(2,1)}, u32[]{:S(2)}, u32[]{:S(2)}) %collective-permute-start.11) | collective-permute-done | bytes 589856 | tf_op jit(solution)/shard_map/ppermute | solution.py:32
  72.4 0.9 collective-permute-done.13.refs_1_
  73.4 1.3 convert_add_fusion
  74.7 3.0 %collective-permute-start.14 = (bf16[1,192,768]{2,1,0:T(8,128)(2,1)S(1)}, bf16[1,192,768]{2,1,0:T(8,128)(2,1)S(1)}, u32[]{:S(2)}, u32[]{:S(2)}) collective-permute-start(bf16[1,192,768]{2,1,0:T(8,128)(2,1)S(1)} %dynamic-slice_convert_fusion), channel_id=1, source_target_pairs={{0,16},{2,18},{4,20},{6,22},{8,24},{10,26},{12,28},{14,30},{16,0},... | collective-permute-start | bytes 884744 | tf_op jit(solution)/shard_map/ppermute | solution.py:32
  77.9 0.9 shard_map.138.refs_0_.rest_0_
  78.9 1.4 collective-permute-done.17.refs_1_.rest_1_
  80.9 3.4 %collective-permute-start.18 = (bf16[32,768]{1,0:T(8,128)(2,1)S(1)}, bf16[32,768]{1,0:T(8,128)(2,1)S(1)}, u32[]{:S(2)}, u32[]{:S(2)}) collective-permute-start(bf16[32,768]{1,0:T(8,128)(2,1)S(1)} %get-tuple-element.69), channel_id=1, source_target_pairs={{0,2},{2,4},{4,6},{6,8},{8,10},{10,12},{12,14},{14,16},{16,18},{18... | collective-permute-start | bytes 147464 | tf_op jit(solution)/shard_map/ppermute | solution.py:39
  84.3 1.5 collective-permute-start.19
  86.0 4.3 %collective-permute-done.19.after = bf16[32,768]{1,0:T(8,128)(2,1)S(1)} collective-permute-done((bf16[32,768]{1,0:T(8,128)(2,1)S(1)}, bf16[32,768]{1,0:T(8,128)(2,1)S(1)}, u32[]{:S(2)}, u32[]{:S(2)}) %collective-permute-start.19) | collective-permute-done | bytes 49184 | tf_op jit(solution)/shard_map/ppermute | solution.py:39
  90.4 1.1 collective-permute-start.21
  91.5 3.8 %collective-permute-start.20 = (bf16[192,768]{1,0:T(8,128)(2,1)S(1)}, bf16[192,768]{1,0:T(8,128)(2,1)S(1)}, u32[]{:S(2)}, u32[]{:S(2)}) collective-permute-start(bf16[192,768]{1,0:T(8,128)(2,1)S(1)} %fusion.1.refs_0_), channel_id=1, source_target_pairs={{0,2},{2,0},{4,6},{6,4},{8,10},{10,8},{12,14},{14,12},{16,18},{18,... | collective-permute-start | bytes 884744 | tf_op jit(solution)/shard_map/ppermute | solution.py:32
  95.3 2.2 %collective-permute-start.23 = (bf16[192,768]{1,0:T(8,128)(2,1)S(1)}, bf16[192,768]{1,0:T(8,128)(2,1)}, u32[]{:S(2)}, u32[]{:S(2)}) collective-permute-start(bf16[192,768]{1,0:T(8,128)(2,1)S(1)} %fusion.1.refs_0_), channel_id=1, source_target_pairs={{0,8},{2,10},{4,12},{6,14},{8,0},{10,2},{12,4},{14,6},{16,24},{18,... | collective-permute-start | bytes 884744 | tf_op jit(solution)/shard_map/ppermute | solution.py:32
  97.6 7.5 %collective-permute-done.27.refs_1_ = bf16[128,768]{1,0:T(8,128)(2,1)S(1)} collective-permute-done((bf16[128,768]{1,0:T(8,128)(2,1)S(1)}, bf16[128,768]{1,0:T(8,128)(2,1)S(1)}, u32[]{:S(2)}, u32[]{:S(2)}) %collective-permute-start.27) | collective-permute-done | bytes 196640 | tf_op jit(solution)/shard_map/ppermute | solution.py:32
  105.1 3.1 %collective-permute-start.26 = (bf16[192,768]{1,0:T(8,128)(2,1)S(1)}, bf16[192,768]{1,0:T(8,128)(2,1)}, u32[]{:S(2)}, u32[]{:S(2)}) collective-permute-start(bf16[192,768]{1,0:T(8,128)(2,1)S(1)} %fusion.1.refs_0_), channel_id=1, source_target_pairs={{0,14},{2,12},{4,10},{6,8},{8,6},{10,4},{12,2},{14,0},{16,30},{18,... | collective-permute-start | bytes 884744 | tf_op jit(solution)/shard_map/ppermute | solution.py:32
  109.0 1.2 collective-permute-start.25
  110.3 1.5 %collective-permute-start.29 = (bf16[128,768]{1,0:T(8,128)(2,1)S(1)}, bf16[128,768]{1,0:T(8,128)(2,1)S(1)}, u32[]{:S(2)}, u32[]{:S(2)}) collective-permute-start(bf16[128,768]{1,0:T(8,128)(2,1)S(1)} %copy-done.13), channel_id=1, source_target_pairs={{0,6},{2,4},{4,2},{6,0},{8,14},{10,12},{12,10},{14,8},{16,22},{18,... | collective-permute-start | bytes 589832 | tf_op jit(solution)/shard_map/ppermute | solution.py:32
  111.9 12.3 %collective-permute-done.29.refs_3_ = bf16[128,768]{1,0:T(8,128)(2,1)S(1)} collective-permute-done((bf16[128,768]{1,0:T(8,128)(2,1)S(1)}, bf16[128,768]{1,0:T(8,128)(2,1)S(1)}, u32[]{:S(2)}, u32[]{:S(2)}) %collective-permute-start.29) | collective-permute-done | bytes 196640 | tf_op jit(solution)/shard_map/ppermute | solution.py:32
  124.3 1.5 shard_map.141
  125.7 3.3 %shard_map.140 = bf16[128,768]{1,0:T(8,128)(2,1)} custom-call(s32[3]{0:T(128)S(1)} %pad_add_fusion.1.ids, s32[16]{0:T(128)S(1)} %copy-done.10, bf16[256,768]{1,0:T(8,128)(2,1)S(1)} %bitcast.27, bf16[32,768]{1,0:T(8,128)(2,1)S(1)} %collective-permute-done.18.before, bf16[32,768]{1,0:T(8,128)(2,1)S(1)} %collective-permute-done.19.after, ...), custom_call_target="tpu_custom_call" | custom-call | flops 1000000 | bytes 1048576 | tf_op jit(solution)/shard_map/pallas_call | solution.py:56
  129.1 8.4 %shard_map.142 = (f32[48,1536]{1,0:T(8,128)S(1)}, bf16[48,1536]{1,0:T(8,128)(2,1)S(1)}) custom-call(s32[3]{0:T(128)S(1)} %pad_add_fusion.2.scalars, bf16[192,768]{1,0:T(8,128)(2,1)S(1)} %fusion.1.refs_0_, bf16[192,768]{1,0:T(8,128)(2,1)S(1)} %collective-permute-done.20.refs_1_, bf16[192,768]{1,0:T(8,128)(2,1)S(1)} %collective-permute-done.21.refs_2_, ...), custom_call_target="tpu_custom_call" | custom-call | flops 10000000000 | bytes 1048576 | tf_op jit(solution)/shard_map/pallas_call | solution.py:56
  137.4 3.1 %collective-permute-start.30 = (bf16[48,1536]{1,0:T(8,128)(2,1)S(1)}, bf16[48,1536]{1,0:T(8,128)(2,1)S(1)}, u32[]{:S(2)}, u32[]{:S(2)}) collective-permute-start(bf16[48,1536]{1,0:T(8,128)(2,1)S(1)} %get-tuple-element.89), channel_id=1, source_target_pairs={{0,16},{2,18},{4,20},{6,22},{8,24},{10,26},{12,28},{14,30},{16,0},... | collective-permute-start | bytes 442376 | tf_op jit(solution)/shard_map/ppermute | solution.py:32
  140.5 6.7 %collective-permute-done.30 = bf16[48,1536]{1,0:T(8,128)(2,1)S(1)} collective-permute-done((bf16[48,1536]{1,0:T(8,128)(2,1)S(1)}, bf16[48,1536]{1,0:T(8,128)(2,1)S(1)}, u32[]{:S(2)}, u32[]{:S(2)}) %collective-permute-start.30) | collective-permute-done | bytes 147488 | tf_op jit(solution)/shard_map/ppermute | solution.py:32
  147.3 0.9 fusion
  (88 shorter events, 9.3 us)
Async XLA Ops:
  0.6 21.8 %copy-start.1 = (bf16[32,8,768]{2,1,0:T(8,128)(2,1)S(1)}, bf16[32,8,768]{2,1,0:T(8,128)(2,1)}, u32[]{:S(2)}) copy-start(bf16[32,8,768]{2,1,0:T(8,128)(2,1)} %param.10) | copy-start | bytes 1179652
  0.6 21.8 %copy-start.10 = (s32[16]{0:T(128)S(1)}, s32[16]{0:T(128)}, u32[]{:S(2)}) copy-start(s32[16]{0:T(128)} %lengths.11) | copy-start | bytes 196
  0.7 21.6 %copy-start.20 = (f32[7,7,768]{2,1,0:T(8,128)S(1)}, f32[7,7,768]{2,1,0:T(8,128)}, u32[]{:S(2)}) copy-start(f32[7,7,768]{2,1,0:T(8,128)} %param.12) | copy-start | bytes 451588
  0.7 21.6 %copy-start.22 = (f32[768]{0:T(1024)S(1)}, f32[768]{0:T(1024)}, u32[]{:S(2)}) copy-start(f32[768]{0:T(1024)} %param.13) | copy-start | bytes 9220
  0.7 21.6 %copy-start.23 = (f32[768]{0:T(1024)S(1)}, f32[768]{0:T(1024)}, u32[]{:S(2)}) copy-start(f32[768]{0:T(1024)} %param.17) | copy-start | bytes 9220
  0.7 21.7 %copy-start.11 = (s32[4,1]{0,1:T(1,128)S(1)}, s32[4,1]{0,1:T(1,128)}, u32[]{:S(2)}) copy-start(s32[4,1]{0,1:T(1,128)} %param.18) | copy-start | bytes 52
  1.8 12.1 %collective-permute-start = (bf16[2,48,384]{2,1,0:T(8,128)(2,1)S(1)}, bf16[2,48,384]{2,1,0:T(8,128)(2,1)S(1)}, u32[]{:S(2)}, u32[]{:S(2)}) collective-permute-start(bf16[2,48,384]{2,1,0:T(8,128)(2,1)S(1)} %get-tuple-element.94), channel_id=1, source_target_pairs={{0,2},{2,0},{4,6},{6,4},{8,10},{10,8},{12,14},{14,12},{16,18},{18,... | collective-permute-start | bytes 221192 | tf_op jit(solution)/shard_map/ppermute | solution.py:32
  4.8 9.1 %collective-permute-start.1 = (bf16[2,48,384]{2,1,0:T(8,128)(2,1)S(1)}, bf16[2,48,384]{2,1,0:T(8,128)(2,1)S(1)}, u32[]{:S(2)}, u32[]{:S(2)}) collective-permute-start(bf16[2,48,384]{2,1,0:T(8,128)(2,1)S(1)} %get-tuple-element.95), channel_id=1, source_target_pairs={{0,4},{2,6},{4,0},{6,2},{8,12},{10,14},{12,8},{14,10},{16,20},{18,... | collective-permute-start | bytes 221192 | tf_op jit(solution)/shard_map/ppermute | solution.py:32
  6.3 7.6 %collective-permute-start.2 = (bf16[2,48,384]{2,1,0:T(8,128)(2,1)S(1)}, bf16[2,48,384]{2,1,0:T(8,128)(2,1)S(1)}, u32[]{:S(2)}, u32[]{:S(2)}) collective-permute-start(bf16[2,48,384]{2,1,0:T(8,128)(2,1)S(1)} %get-tuple-element.92), channel_id=1, source_target_pairs={{0,6},{2,4},{4,2},{6,0},{8,14},{10,12},{12,10},{14,8},{16,22},{18,... | collective-permute-start | bytes 221192 | tf_op jit(solution)/shard_map/ppermute | solution.py:32
  6.3 1.0 copy-start
  8.0 14.5 %copy-start.2 = (bf16[32,8,768]{2,1,0:T(8,128)(2,1)S(1)}, bf16[32,8,768]{2,1,0:T(8,128)(2,1)}, u32[]{:S(2)}) copy-start(bf16[32,8,768]{2,1,0:T(8,128)(2,1)} %param.11) | copy-start | bytes 1179652
  8.7 5.6 %collective-permute-start.3 = (bf16[32,768]{1,0:T(8,128)(2,1)S(1)}, bf16[32,768]{1,0:T(8,128)(2,1)S(1)}, u32[]{:S(2)}, u32[]{:S(2)}) collective-permute-start(bf16[32,768]{1,0:T(8,128)(2,1)S(1)} %get-tuple-element.47), channel_id=1, source_target_pairs={{0,2},{2,4},{4,6},{6,8},{8,10},{10,12},{12,14},{14,16},{16,18},{18... | collective-permute-start | bytes 147464 | tf_op jit(solution)/shard_map/ppermute | solution.py:39
  12.5 6.0 %collective-permute-start.4 = (bf16[32,768]{1,0:T(8,128)(2,1)S(1)}, bf16[32,768]{1,0:T(8,128)(2,1)S(1)}, u32[]{:S(2)}, u32[]{:S(2)}) collective-permute-start(bf16[32,768]{1,0:T(8,128)(2,1)S(1)} %get-tuple-element.48), channel_id=1, source_target_pairs={{2,0},{4,2},{6,4},{8,6},{10,8},{12,10},{14,12},{16,14},{18,16},{20... | collective-permute-start | bytes 147464 | tf_op jit(solution)/shard_map/ppermute | solution.py:39
  18.5 14.8 %collective-permute-start.5 = (bf16[1,2,192,384]{3,2,1,0:T(8,128)(2,1)S(1)}, bf16[1,2,192,384]{3,2,1,0:T(8,128)(2,1)S(1)}, u32[]{:S(2)}, u32[]{:S(2)}) collective-permute-start(bf16[1,2,192,384]{3,2,1,0:T(8,128)(2,1)S(1)} %bitcast.28), channel_id=1, source_target_pairs={{0,16},{2,18},{4,20},{6,22},{8,24},{10,26},{12,28},{14,30},{16,0},... | collective-permute-start | bytes 884744 | tf_op jit(solution)/shard_map/ppermute | solution.py:32
  25.4 18.4 %copy-start.7 = (f32[128,128]{1,0:T(8,128)}, f32[128,128]{1,0:T(8,128)S(1)}, u32[]{:S(2)}) copy-start(f32[128,128]{1,0:T(8,128)S(1)} %get-tuple-element.64.inverse) | copy-start | bytes 196612
  25.4 12.1 %collective-permute-start.7 = (bf16[2,128,768]{2,1,0:T(8,128)(2,1)S(1)}, bf16[2,128,768]{2,1,0:T(8,128)(2,1)S(1)}, u32[]{:S(2)}, u32[]{:S(2)}) collective-permute-start(bf16[2,128,768]{2,1,0:T(8,128)(2,1)S(1)} %get-tuple-element.54.refs_0_), channel_id=1, source_target_pairs={{0,2},{2,0},{4,6},{6,4},{8,10},{10,8},{12,14},{14,12},{16,18},{18,... | collective-permute-start | bytes 1179656 | tf_op jit(solution)/shard_map/ppermute | solution.py:32
  26.7 17.1 %collective-permute-start.8 = (bf16[2,128,768]{2,1,0:T(8,128)(2,1)S(1)}, bf16[2,128,768]{2,1,0:T(8,128)(2,1)S(1)}, u32[]{:S(2)}, u32[]{:S(2)}) collective-permute-start(bf16[2,128,768]{2,1,0:T(8,128)(2,1)S(1)} %get-tuple-element.54.refs_0_), channel_id=1, source_target_pairs={{0,4},{2,6},{4,0},{6,2},{8,12},{10,14},{12,8},{14,10},{16,20},{18,... | collective-permute-start | bytes 1179656 | tf_op jit(solution)/shard_map/ppermute | solution.py:32
  29.6 14.2 %collective-permute-start.9 = (bf16[2,128,768]{2,1,0:T(8,128)(2,1)S(1)}, bf16[2,128,768]{2,1,0:T(8,128)(2,1)S(1)}, u32[]{:S(2)}, u32[]{:S(2)}) collective-permute-start(bf16[2,128,768]{2,1,0:T(8,128)(2,1)S(1)} %get-tuple-element.54.refs_0_), channel_id=1, source_target_pairs={{0,6},{2,4},{4,2},{6,0},{8,14},{10,12},{12,10},{14,8},{16,22},{18,... | collective-permute-start | bytes 1179656 | tf_op jit(solution)/shard_map/ppermute | solution.py:32
  33.4 10.6 %copy-start.21 = (f32[1536]{0:T(1024)S(1)}, f32[1536]{0:T(1024)}, u32[]{:S(2)}) copy-start(f32[1536]{0:T(1024)} %param.15) | copy-start | bytes 18436
  33.4 14.3 %collective-permute-start.6 = (bf16[2,2,192,384]{3,2,1,0:T(8,128)(2,1)S(1)}, bf16[2,2,192,384]{3,2,1,0:T(8,128)(2,1)}, u32[]{:S(2)}, u32[]{:S(2)}) collective-permute-start(bf16[2,2,192,384]{3,2,1,0:T(8,128)(2,1)S(1)} %shard_map.131.early), channel_id=1, source_target_pairs={{0,8},{2,10},{4,12},{6,14},{8,0},{10,2},{12,4},{14,6},{16,24},{18,... | collective-permute-start | bytes 1769480 | tf_op jit(solution)/shard_map/ppermute | solution.py:32
  43.9 4.9 %collective-permute-start.10 = (bf16[2,512,768]{2,1,0:T(8,128)(2,1)S(1)}, bf16[2,512,768]{2,1,0:T(8,128)(2,1)}, u32[]{:S(2)}, u32[]{:S(2)}) collective-permute-start(bf16[2,512,768]{2,1,0:T(8,128)(2,1)S(1)} %shard_map.134.refs_0_), channel_id=1, source_target_pairs={{0,1},{1,0},{2,3},{3,2},{4,5},{5,4},{6,7},{7,6},{8,9},{9,8},{10,11... | collective-permute-start | bytes 4718600 | tf_op jit(solution)/shard_map/ppermute | solution.py:32
  56.3 3.5 %collective-permute-start.12 = (bf16[2,512,768]{2,1,0:T(8,128)(2,1)S(1)}, bf16[2,512,768]{2,1,0:T(8,128)(2,1)S(1)}, u32[]{:S(2)}, u32[]{:S(2)}) collective-permute-start(bf16[2,512,768]{2,1,0:T(8,128)(2,1)S(1)} %get-tuple-element.60), channel_id=1, source_target_pairs={{0,1},{1,0},{2,3},{3,2},{4,5},{5,4},{6,7},{7,6},{8,9},{9,8},{10,11... | collective-permute-start | bytes 4718600 | tf_op jit(solution)/shard_map/ppermute | solution.py:32
  56.4 16.1 %collective-permute-start.11 = (bf16[2,192,768]{2,1,0:T(8,128)(2,1)}, bf16[2,192,768]{2,1,0:T(8,128)(2,1)}, u32[]{:S(2)}, u32[]{:S(2)}) collective-permute-start(bf16[2,192,768]{2,1,0:T(8,128)(2,1)} %get-tuple-element.56), channel_id=1, source_target_pairs={{0,8},{2,10},{4,12},{6,14},{8,0},{10,2},{12,4},{14,6},{16,24},{18,... | collective-permute-start | bytes 1769480 | tf_op jit(solution)/shard_map/ppermute | solution.py:32
  64.7 0.7 copy-start.19
  65.4 8.0 %collective-permute-start.13 = (bf16[128,768]{1,0:T(8,128)(2,1)}, bf16[128,768]{1,0:T(8,128)(2,1)S(1)}, u32[]{:S(2)}, u32[]{:S(2)}) collective-permute-start(bf16[128,768]{1,0:T(8,128)(2,1)} %get-tuple-element.61), channel_id=1, source_target_pairs={{0,2},{2,0},{4,6},{6,4},{8,10},{10,8},{12,14},{14,12},{16,18},{18,... | collective-permute-start | bytes 589832 | tf_op jit(solution)/shard_map/ppermute | solution.py:32
  66.8 11.1 %collective-permute-start.15 = (bf16[128,768]{1,0:T(8,128)(2,1)}, bf16[128,768]{1,0:T(8,128)(2,1)S(1)}, u32[]{:S(2)}, u32[]{:S(2)}) collective-permute-start(bf16[128,768]{1,0:T(8,128)(2,1)} %copy-done.19), channel_id=1, source_target_pairs={{0,4},{2,6},{4,0},{6,2},{8,12},{10,14},{12,8},{14,10},{16,20},{18,... | collective-permute-start | bytes 589832 | tf_op jit(solution)/shard_map/ppermute | solution.py:32
  68.1 9.8 %collective-permute-start.16 = (bf16[128,768]{1,0:T(8,128)(2,1)}, bf16[128,768]{1,0:T(8,128)(2,1)S(1)}, u32[]{:S(2)}, u32[]{:S(2)}) collective-permute-start(bf16[128,768]{1,0:T(8,128)(2,1)} %copy-done.18), channel_id=1, source_target_pairs={{0,6},{2,4},{4,2},{6,0},{8,14},{10,12},{12,10},{14,8},{16,22},{18,... | collective-permute-start | bytes 589832 | tf_op jit(solution)/shard_map/ppermute | solution.py:32
  73.4 4.5 %copy-start.6 = (bf16[128,768]{1,0:T(8,128)(2,1)S(1)}, bf16[128,768]{1,0:T(8,128)(2,1)}, u32[]{:S(2)}) copy-start(bf16[128,768]{1,0:T(8,128)(2,1)} %copy-done.5) | copy-start | bytes 589828
  73.4 4.5 %copy-start.8 = (f32[128,128]{1,0:T(8,128)S(1)}, f32[128,128]{1,0:T(8,128)}, u32[]{:S(2)}) copy-start(f32[128,128]{1,0:T(8,128)} %copy-done.7) | copy-start | bytes 196612
  74.7 15.6 %collective-permute-start.14 = (bf16[1,192,768]{2,1,0:T(8,128)(2,1)S(1)}, bf16[1,192,768]{2,1,0:T(8,128)(2,1)S(1)}, u32[]{:S(2)}, u32[]{:S(2)}) collective-permute-start(bf16[1,192,768]{2,1,0:T(8,128)(2,1)S(1)} %dynamic-slice_convert_fusion), channel_id=1, source_target_pairs={{0,16},{2,18},{4,20},{6,22},{8,24},{10,26},{12,28},{14,30},{16,0},... | collective-permute-start | bytes 884744 | tf_op jit(solution)/shard_map/ppermute | solution.py:32
  77.9 19.6 %copy-start.17 = (bf16[128,768]{1,0:T(8,128)(2,1)S(1)}, bf16[128,768]{1,0:T(8,128)(2,1)}, u32[]{:S(2)}) copy-start(bf16[128,768]{1,0:T(8,128)(2,1)} %copy-done.16) | copy-start | bytes 589828
  77.9 19.6 %copy-start.15 = (bf16[128,768]{1,0:T(8,128)(2,1)S(1)}, bf16[128,768]{1,0:T(8,128)(2,1)}, u32[]{:S(2)}) copy-start(bf16[128,768]{1,0:T(8,128)(2,1)} %copy-done.14) | copy-start | bytes 589828
  77.9 32.4 %copy-start.13 = (bf16[128,768]{1,0:T(8,128)(2,1)S(1)}, bf16[128,768]{1,0:T(8,128)(2,1)}, u32[]{:S(2)}) copy-start(bf16[128,768]{1,0:T(8,128)(2,1)} %copy-done.12) | copy-start | bytes 589828
  77.9 46.3 %copy-start.4 = (bf16[128,768]{1,0:T(8,128)(2,1)S(1)}, bf16[128,768]{1,0:T(8,128)(2,1)}, u32[]{:S(2)}) copy-start(bf16[128,768]{1,0:T(8,128)(2,1)} %copy-done.3) | copy-start | bytes 589828
  78.8 1.5 %collective-permute-start.17 = (bf16[128,768]{1,0:T(8,128)(2,1)S(1)}, bf16[128,768]{1,0:T(8,128)(2,1)S(1)}, u32[]{:S(2)}, u32[]{:S(2)}) collective-permute-start(bf16[128,768]{1,0:T(8,128)(2,1)S(1)} %shard_map.138.refs_0_.rest_0_), channel_id=1, source_target_pairs={{0,1},{1,0},{2,3},{3,2},{4,5},{5,4},{6,7},{7,6},{8,9},{9,8},{10,11... | collective-permute-start | bytes 589832 | tf_op jit(solution)/shard_map/ppermute | solution.py:32
  80.9 5.2 %collective-permute-start.18 = (bf16[32,768]{1,0:T(8,128)(2,1)S(1)}, bf16[32,768]{1,0:T(8,128)(2,1)S(1)}, u32[]{:S(2)}, u32[]{:S(2)}) collective-permute-start(bf16[32,768]{1,0:T(8,128)(2,1)S(1)} %get-tuple-element.69), channel_id=1, source_target_pairs={{0,2},{2,4},{4,6},{6,8},{8,10},{10,12},{12,14},{14,16},{16,18},{18... | collective-permute-start | bytes 147464 | tf_op jit(solution)/shard_map/ppermute | solution.py:39
  84.3 6.0 %collective-permute-start.19 = (bf16[32,768]{1,0:T(8,128)(2,1)S(1)}, bf16[32,768]{1,0:T(8,128)(2,1)S(1)}, u32[]{:S(2)}, u32[]{:S(2)}) collective-permute-start(bf16[32,768]{1,0:T(8,128)(2,1)S(1)} %get-tuple-element.70), channel_id=1, source_target_pairs={{2,0},{4,2},{6,4},{8,6},{10,8},{12,10},{14,12},{16,14},{18,16},{20... | collective-permute-start | bytes 147464 | tf_op jit(solution)/shard_map/ppermute | solution.py:39
  90.4 17.9 %collective-permute-start.21 = (bf16[192,768]{1,0:T(8,128)(2,1)S(1)}, bf16[192,768]{1,0:T(8,128)(2,1)S(1)}, u32[]{:S(2)}, u32[]{:S(2)}) collective-permute-start(bf16[192,768]{1,0:T(8,128)(2,1)S(1)} %fusion.1.refs_0_), channel_id=1, source_target_pairs={{0,4},{2,6},{4,0},{6,2},{8,12},{10,14},{12,8},{14,10},{16,20},{18,... | collective-permute-start | bytes 884744 | tf_op jit(solution)/shard_map/ppermute | solution.py:32
  91.5 17.1 %collective-permute-start.20 = (bf16[192,768]{1,0:T(8,128)(2,1)S(1)}, bf16[192,768]{1,0:T(8,128)(2,1)S(1)}, u32[]{:S(2)}, u32[]{:S(2)}) collective-permute-start(bf16[192,768]{1,0:T(8,128)(2,1)S(1)} %fusion.1.refs_0_), channel_id=1, source_target_pairs={{0,2},{2,0},{4,6},{6,4},{8,10},{10,8},{12,14},{14,12},{16,18},{18,... | collective-permute-start | bytes 884744 | tf_op jit(solution)/shard_map/ppermute | solution.py:32
  95.3 13.7 %collective-permute-start.23 = (bf16[192,768]{1,0:T(8,128)(2,1)S(1)}, bf16[192,768]{1,0:T(8,128)(2,1)}, u32[]{:S(2)}, u32[]{:S(2)}) collective-permute-start(bf16[192,768]{1,0:T(8,128)(2,1)S(1)} %fusion.1.refs_0_), channel_id=1, source_target_pairs={{0,8},{2,10},{4,12},{6,14},{8,0},{10,2},{12,4},{14,6},{16,24},{18,... | collective-permute-start | bytes 884744 | tf_op jit(solution)/shard_map/ppermute | solution.py:32
  97.5 7.6 %collective-permute-start.27 = (bf16[128,768]{1,0:T(8,128)(2,1)S(1)}, bf16[128,768]{1,0:T(8,128)(2,1)S(1)}, u32[]{:S(2)}, u32[]{:S(2)}) collective-permute-start(bf16[128,768]{1,0:T(8,128)(2,1)S(1)} %copy-done.17), channel_id=1, source_target_pairs={{0,2},{2,0},{4,6},{6,4},{8,10},{10,8},{12,14},{14,12},{16,18},{18,... | collective-permute-start | bytes 589832 | tf_op jit(solution)/shard_map/ppermute | solution.py:32
  97.5 12.8 %collective-permute-start.28 = (bf16[128,768]{1,0:T(8,128)(2,1)S(1)}, bf16[128,768]{1,0:T(8,128)(2,1)S(1)}, u32[]{:S(2)}, u32[]{:S(2)}) collective-permute-start(bf16[128,768]{1,0:T(8,128)(2,1)S(1)} %copy-done.15), channel_id=1, source_target_pairs={{0,4},{2,6},{4,0},{6,2},{8,12},{10,14},{12,8},{14,10},{16,20},{18,... | collective-permute-start | bytes 589832 | tf_op jit(solution)/shard_map/ppermute | solution.py:32
  105.1 23.9 %collective-permute-start.26 = (bf16[192,768]{1,0:T(8,128)(2,1)S(1)}, bf16[192,768]{1,0:T(8,128)(2,1)}, u32[]{:S(2)}, u32[]{:S(2)}) collective-permute-start(bf16[192,768]{1,0:T(8,128)(2,1)S(1)} %fusion.1.refs_0_), channel_id=1, source_target_pairs={{0,14},{2,12},{4,10},{6,8},{8,6},{10,4},{12,2},{14,0},{16,30},{18,... | collective-permute-start | bytes 884744 | tf_op jit(solution)/shard_map/ppermute | solution.py:32
  108.3 20.8 %collective-permute-start.22 = (bf16[192,768]{1,0:T(8,128)(2,1)S(1)}, bf16[192,768]{1,0:T(8,128)(2,1)}, u32[]{:S(2)}, u32[]{:S(2)}) collective-permute-start(bf16[192,768]{1,0:T(8,128)(2,1)S(1)} %collective-permute-done.21.refs_2_), channel_id=1, source_target_pairs={{0,2},{2,0},{4,6},{6,4},{8,10},{10,8},{12,14},{14,12},{16,18},{18,... | collective-permute-start | bytes 884744 | tf_op jit(solution)/shard_map/ppermute | solution.py:32
  108.6 20.5 %collective-permute-start.24 = (bf16[192,768]{1,0:T(8,128)(2,1)S(1)}, bf16[192,768]{1,0:T(8,128)(2,1)}, u32[]{:S(2)}, u32[]{:S(2)}) collective-permute-start(bf16[192,768]{1,0:T(8,128)(2,1)S(1)} %collective-permute-done.20.refs_1_), channel_id=1, source_target_pairs={{0,8},{2,10},{4,12},{6,14},{8,0},{10,2},{12,4},{14,6},{16,24},{18,... | collective-permute-start | bytes 884744 | tf_op jit(solution)/shard_map/ppermute | solution.py:32
  109.0 20.0 %collective-permute-start.25 = (bf16[192,768]{1,0:T(8,128)(2,1)}, bf16[192,768]{1,0:T(8,128)(2,1)}, u32[]{:S(2)}, u32[]{:S(2)}) collective-permute-start(bf16[192,768]{1,0:T(8,128)(2,1)} %collective-permute-done.23.refs_4_), channel_id=1, source_target_pairs={{0,4},{2,6},{4,0},{6,2},{8,12},{10,14},{12,8},{14,10},{16,20},{18,... | collective-permute-start | bytes 884744 | tf_op jit(solution)/shard_map/ppermute | solution.py:32
  110.3 14.0 %collective-permute-start.29 = (bf16[128,768]{1,0:T(8,128)(2,1)S(1)}, bf16[128,768]{1,0:T(8,128)(2,1)S(1)}, u32[]{:S(2)}, u32[]{:S(2)}) collective-permute-start(bf16[128,768]{1,0:T(8,128)(2,1)S(1)} %copy-done.13), channel_id=1, source_target_pairs={{0,6},{2,4},{4,2},{6,0},{8,14},{10,12},{12,10},{14,8},{16,22},{18,... | collective-permute-start | bytes 589832 | tf_op jit(solution)/shard_map/ppermute | solution.py:32
  137.4 9.8 %collective-permute-start.30 = (bf16[48,1536]{1,0:T(8,128)(2,1)S(1)}, bf16[48,1536]{1,0:T(8,128)(2,1)S(1)}, u32[]{:S(2)}, u32[]{:S(2)}) collective-permute-start(bf16[48,1536]{1,0:T(8,128)(2,1)S(1)} %get-tuple-element.89), channel_id=1, source_target_pairs={{0,16},{2,18},{4,20},{6,22},{8,24},{10,26},{12,28},{14,30},{16,0},... | collective-permute-start | bytes 442376 | tf_op jit(solution)/shard_map/ppermute | solution.py:32
  (7 other events, 4.7 us)
